TPU v7x, 32 devices: a whole 2x2x4 slice. The times are simulated.
32 devices in a mesh: groups: 2 (over y), row: 16 (over z, x, core).
Axes of the slice: x: 2, y: 2, z: 4, core: 2. Of those that a mesh axis runs over, the one named last changes fastest.
Arguments:
- decoder: bfloat16 [65536, 4096], P(('groups', 'row')), parts along dimension 0, may hold values from -130 to 130
- quarter: int32 [2], P('groups'), parts along dimension 0, may hold values from 0 to 3
Outputs:
- penalty: float32 [2], P('groups'), parts along dimension 0
- decoder_grad: float32 [65536, 4096], P(('groups', 'row')), parts along dimension 0
There are 2 independent parts, one for each index of `groups`. A program takes and returns all parts, laid end to end along the dimension named above; each array names one. Nothing has to cross between parts.
All inputs are finite; a program needn't handle non-finite values.
Results may differ from a plain program's by a relative error of at most 0.0004.
The roundings to bfloat16 on the way count: a program that leaves them out, or rounds other values in their place, can miss the bound.
Values may be sent and summed in bfloat16 or wider, within the bound.
No kernel may reach another device: no remote copies, remote signals or barrier semaphores. Data moves between devices by JAX's collectives and lax.ppermute only.
A program may use at most 192 MiB of HBM per device.

v0:
```python
import math

import jax
import jax.numpy as jnp
from jax import lax
from jax.sharding import PartitionSpec as P

DW = 4096
ROWS = 256


def from_root(value, axis, source):
    kept = jnp.where(lax.axis_index(axis) == source, value, 0).astype(value.dtype)
    return lax.psum(kept, axis)


def on_device(decoder, quarter):
    shard = decoder.shape[0]
    width = decoder.shape[1]
    devices = lax.axis_size("row")
    index = lax.axis_index("row")
    latents = shard * devices
    quarter_len = latents // 4
    values = decoder.astype(jnp.float32)
    norms = jnp.sqrt(jnp.sum(values * values, axis=1) + 1e-06)
    directions = values / norms[:, None]
    units = directions.astype(jnp.bfloat16)
    start = quarter[0] * quarter_len
    first_root = start // shard
    piece = min(ROWS, shard)
    received = from_root(units[:piece], "row", first_root + 0)
    cosines = jnp.dot(received, units.T, preferred_element_type=jnp.float32)
    row_ids = start + jnp.arange(ROWS, dtype=jnp.int32)
    col_ids = index * shard + jnp.arange(shard, dtype=jnp.int32)
    inside = (col_ids >= start) & (col_ids < start + ROWS)
    pair_weight = jnp.where(
        col_ids[None, :] == row_ids[:, None],
        jnp.float32(0.0),
        jnp.where(inside[None, :], jnp.float32(0.5), jnp.float32(1.0)),
    )
    products = pair_weight * cosines
    weighted = products.astype(jnp.bfloat16)
    local_penalty = jnp.sum(products * cosines)
    column_part = jnp.dot(weighted.T, received, preferred_element_type=jnp.float32)
    row_part = jnp.dot(weighted, units, preferred_element_type=jnp.float32)
    reduced = lax.psum_scatter(row_part, "row", scatter_dimension=0, tiled=True)
    row_sum = lax.all_gather(reduced, "row", axis=0, tiled=True)
    total_penalty = lax.psum(local_penalty, "row")
    blank = jnp.zeros((shard, width), jnp.float32)
    padded = jnp.concatenate([blank, row_sum, blank], axis=0)
    position = jnp.clip(index * shard - start + shard, 0, ROWS + shard)
    owned = lax.dynamic_slice_in_dim(padded, position, shard, 0)
    unit_grad = 2.0 * math.sqrt(DW) * (column_part + owned)
    along = jnp.sum(unit_grad * directions, axis=1)
    decoder_grad = (unit_grad - along[:, None] * directions) / norms[:, None]
    penalty = total_penalty * (DW / (ROWS * latents))
    return (jnp.reshape(penalty, (1,)), decoder_grad)


def solution(mesh):
    in_specs = (P(("groups", "row"), None), P("groups"))
    out_specs = (P("groups"), P(("groups", "row"), None))
    return jax.shard_map(
        on_device, mesh=mesh, in_specs=in_specs, out_specs=out_specs, check_vma=False
    )
```

profile of v0, /device:TPU:0, one launch (start us, length us, event | category | flops | bytes accessed | tf_op | source)
XLA Modules:
  0.0 359.1 jit_solution(1384268015980109912)
XLA Ops:
  7.2 0.0 all-reduce.2.cloned.1.call-start
  7.9 0.0 copy-start
  7.9 7.5 %fusion = f32[2048]{0:T(1024)S(1)} fusion(bf16[2048,4096]{1,0:T(8,128)(2,1)} %param.2), kind=kLoop, calls=%fused_computation.5 | loop fusion | flops 25163776 | bytes 16785408 | tf_op jit(solution)/shard_map/reduce_sum | solution.py:25
  15.4 3.2 copy-done
  18.5 8.3 %fusion.9 = bf16[2048,4096]{1,0:T(8,128)(2,1)} fusion(f32[2048]{0:T(1024)S(1)} %add_sqrt_fusion, bf16[2048,4096]{1,0:T(8,128)(2,1)S(1)} %copy-done), kind=kLoop, calls=%fused_computation.21 | loop fusion | flops 25165824 | bytes 33562624 | tf_op jit(solution)/shard_map/convert_element_type | solution.py:27
  26.8 3.1 slice_select_fusion
  29.9 0.0 all-reduce.2.cloned.1.call-update
  29.9 0.0 reduce-scatter.2.cloned.1.call-start
  30.0 100.5 %all-reduce.2.cloned.1.call-done = bf16[256,4096]{1,0:T(8,128)(2,1)} async-done(((bf16[256,4096]{1,0:T(8,128)(2,1)}), bf16[256,4096]{1,0:T(8,128)(2,1)}) %all-reduce.2.cloned.1.call-update) | async-done | bytes 2097168 | tf_op jit(solution)/shard_map/psum | solution.py:14
  130.5 9.5 %multiply_reduce_fusion.1 = (f32[]{:T(128)}, f32[256,2048]{1,0:T(8,128)S(1)}) fusion(f32[2048]{0:T(1024)S(1)} %and_select_fusion, s32[2048]{0:T(1024)S(1)} %iota_add_fusion, s32[256]{0:T(256)S(1)} %iota_add_fusion.1, bf16[256,4096]{1,0:T(8,128)(2,1)} %all-reduce.2.cloned.1.call-done, bf16[2048,4096]{1,0:T(8,128)(2,1)} %fusion.9), kind=kOutput, calls=%fused_computation.13 | convolution fusion | flops 4297588736 | bytes 20988932 | tf_op jit(solution)/shard_map/dot_general | solution.py:32
  140.0 0.0 copy-start.3
  140.0 11.0 %fusion.6 = f32[256,4096]{1,0:T(8,128)} fusion(bf16[2048,4096]{1,0:T(8,128)(2,1)} %fusion.9, f32[256,2048]{1,0:T(8,128)S(1)} %get-tuple-element.3, f32[2048]{0:T(1024)S(1)} %and_select_fusion, s32[2048]{0:T(1024)S(1)} %iota_add_fusion, s32[256]{0:T(256)S(1)} %iota_add_fusion.1), kind=kOutput, calls=%fused_computation.20 | convolution fusion | flops 4297064448 | bytes 23086080 | tf_op jit(solution)/shard_map/dot_general | solution.py:45
  151.0 0.0 copy-done.3
  151.0 0.0 reduce-scatter.2.cloned.1.call-update
  151.0 0.0 all-gather.2.cloned.1.call-start
  151.1 72.0 %reduce-scatter.2.cloned.1.call-done = f32[16,4096]{1,0:T(8,128)} async-done(((f32[256,4096]{1,0:T(8,128)}), f32[16,4096]{1,0:T(8,128)}) %reduce-scatter.2.cloned.1.call-update) | async-done | bytes 262160 | tf_op jit(solution)/shard_map/reduce_scatter | solution.py:46
  223.1 0.0 all-gather.2.cloned.1.call-update
  223.1 30.8 %psum.15 = f32[]{:T(128)} all-reduce(f32[]{:T(128)} %get-tuple-element.2), channel_id=1, replica_groups=mesh['groups'=2,'row'=16] {'row'}, use_global_device_ids=true, to_apply=%region_3.4 | all-reduce | flops 1 | bytes 8 | tf_op jit(solution)/shard_map/psum | solution.py:48
  254.5 0.0 copy-start.2
  254.5 20.6 %all-gather.2.cloned.1.call-done = f32[256,4096]{1,0:T(8,128)} async-done(((f32[16,4096]{1,0:T(8,128)}), f32[256,4096]{1,0:T(8,128)}) %all-gather.2.cloned.1.call-update) | async-done | bytes 4194320 | tf_op jit(solution)/shard_map/all_gather | solution.py:47
  275.2 0.0 copy-start.1
  275.2 0.0 copy-start.4
  275.2 12.4 %broadcast_in_dim.38 = f32[2048,4096]{1,0:T(8,128)} broadcast(f32[]{:T(128)} %constant.15.clone.1), dimensions={} | broadcast | bytes 33554436 | tf_op jit(solution)/shard_map/broadcast_in_dim | solution.py:49
  287.6 0.0 copy-done.2
  287.6 0.0 copy-done.1
  287.6 0.0 copy-done.4
  287.6 35.1 %multiply_reduce_fusion = (f32[2048]{0:T(1024)S(1)}, f32[2048,4096]{1,0:T(8,128)}) fusion(f32[2048]{0:T(1024)S(1)} %add_sqrt_fusion, bf16[2048,4096]{1,0:T(8,128)(2,1)} %param.2, s32[]{:T(128)S(6)} %min.4, f32[2048,4096]{1,0:T(8,128)} %broadcast_in_dim.38, f32[256,4096]{1,0:T(8,128)S(1)} %copy-done.1, bf16[256,4096]{1,0:T(8,128)(2,1)S(1)} %copy-done.2, ...), kind=kOutput, calls=%fused_computation.11 | convolution fusion | flops 4364171264 | bytes 92308480 | tf_op jit(solution)/shard_map/dot_general | solution.py:44
  322.7 28.8 %subtract_divide_fusion = f32[2048,4096]{1,0:T(8,128)} fusion(f32[2048,4096]{1,0:T(8,128)} %get-tuple-element.5, f32[2048]{0:T(1024)S(1)} %get-tuple-element.4, f32[2048]{0:T(1024)S(1)} %add_sqrt_fusion, bf16[2048,4096]{1,0:T(8,128)(2,1)} %param.2), kind=kLoop, calls=%fused_computation.10 | loop fusion | flops 41943040 | bytes 83902464 | tf_op jit(solution)/shard_map/div | solution.py:55
  (4 shorter events, 0.0 us)
Async XLA Ops:
  7.2 123.4 %all-reduce.2.cloned.1.call-start = ((), (), s32[]{:S(2)}) async-start(), calls=%async_computation.1 | async-start | bytes 4194304 | tf_op jit(solution)/shard_map/psum | solution.py:14
  7.9 10.7 %copy-start = (bf16[2048,4096]{1,0:T(8,128)(2,1)S(1)}, bf16[2048,4096]{1,0:T(8,128)(2,1)}, u32[]{:S(2)}) copy-start(bf16[2048,4096]{1,0:T(8,128)(2,1)} %param.2) | copy-start | bytes 50331652
  29.9 193.2 %reduce-scatter.2.cloned.1.call-start = ((), (), s32[]{:S(2)}) async-start(), calls=%async_computation.2 | async-start | bytes 4456448 | tf_op jit(solution)/shard_map/reduce_scatter | solution.py:46
  140.0 11.0 %copy-start.3 = (f32[256,2048]{1,0:T(8,128)}, f32[256,2048]{1,0:T(8,128)S(1)}, u32[]{:S(2)}) copy-start(f32[256,2048]{1,0:T(8,128)S(1)} %get-tuple-element.3) | copy-start | bytes 6291460
  151.0 124.2 %all-gather.2.cloned.1.call-start = ((), (), s32[]{:S(2)}) async-start(), calls=%async_computation.3 | async-start | bytes 4456448 | tf_op jit(solution)/shard_map/all_gather | solution.py:47
  254.5 33.0 %copy-start.2 = (bf16[256,4096]{1,0:T(8,128)(2,1)S(1)}, bf16[256,4096]{1,0:T(8,128)(2,1)}, u32[]{:S(2)}) copy-start(bf16[256,4096]{1,0:T(8,128)(2,1)} %all-reduce.2.cloned.1.call-done) | copy-start | bytes 6291460
  275.2 12.4 %copy-start.1 = (f32[256,4096]{1,0:T(8,128)S(1)}, f32[256,4096]{1,0:T(8,128)}, u32[]{:S(2)}) copy-start(f32[256,4096]{1,0:T(8,128)} %all-gather.2.cloned.1.call-done) | copy-start | bytes 12582916
  275.2 12.4 %copy-start.4 = (f32[256,2048]{1,0:T(8,128)S(1)}, f32[256,2048]{1,0:T(8,128)}, u32[]{:S(2)}) copy-start(f32[256,2048]{1,0:T(8,128)} %copy-done.3) | copy-start | bytes 6291460
Sparse Core Ops, SparseCore 0:
  30.0 100.4 all-reduce.1
  151.1 71.9 reduce-scatter.1
  225.3 49.8 all-gather.1
where the time goes:
time: 359 us
  waiting for transfers between devices  193 us (54%)
  matrix products  55.5 us (15%)
  other arithmetic  47.6 us (13%)
  blocking collectives  30.8 us (9%)
  between operations  16.3 us (5%)
  local copies, waits for them, and re-layouts  15.6 us (4%)
    psum x1, waiting for transfers between devices, from_root(): return lax.psum(kept, axis)  101 us
    reduce_scatter x1, waiting for transfers between devices, on_device(): reduced = lax.psum_scatter(row_part, 'row', scatter_dimension=0, tiled=True)  72 us
    dot_general x1, matrix products, on_device(): jnp.dot(weighted.T, received, preferred_element_type=jnp.float32)  35.1 us
    psum x1, blocking collectives, on_device(): total_penalty = lax.psum(local_penalty, 'row')  30.8 us
    div x1, other arithmetic, on_device(): decoder_grad = (unit_grad - along[:, None] * directions) / norms[:, None]  28.8 us
    all_gather x1, waiting for transfers between devices, on_device(): row_sum = lax.all_gather(reduced, 'row', axis=0, tiled=True)  20.6 us
    broadcast_in_dim x1, local copies, waits for them, and re-layouts, on_device(): blank = jnp.zeros((shard, width), jnp.float32)  12.4 us
    dot_general x1, matrix products, on_device(): row_part = jnp.dot(weighted, units, preferred_element_type=jnp.float32)  11 us
  transfers between devices with their start and end apart: 3, of which 3 were waited for; matrix products, arithmetic and copies ran while one was open for 0% of the time, Pallas kernels for 0%

commit v1 on v0

v1 whole, which is shorter than its diff:
```python
import functools
import math

import jax
import jax.numpy as jnp
from jax import lax
from jax.experimental import pallas as pl
from jax.experimental.pallas import tpu as pltpu
from jax.sharding import PartitionSpec as P

DW = 4096
ROWS = 256
BLOCK = 256
HALF_CHUNKS = 4
VMEM_LIMIT = 56 * 1024 * 1024
NT = (((1,), (1,)), ((), ()))


def params():
    return pltpu.CompilerParams(vmem_limit_bytes=VMEM_LIMIT)


def unit_block(block):
    values = block.astype(jnp.float32)
    norms = jnp.sqrt(jnp.sum(values * values, axis=1, keepdims=True) + 1e-06)
    inverse = 1.0 / norms
    return (values * inverse).astype(jnp.bfloat16), inverse


def head_kernel(decoder_ref, *chunk_refs):
    units, _ = unit_block(decoder_ref[...])
    step = chunk_refs[0].shape[1]
    for k, ref in enumerate(chunk_refs):
        ref[...] = units[:, k * step : (k + 1) * step]


def units_kernel(decoder_ref, units_ref, inverse_ref):
    units, inverse = unit_block(decoder_ref[...])
    units_ref[...] = units
    inverse_ref[...] = jnp.broadcast_to(inverse, inverse_ref.shape)


def cosine_kernel(delta_ref, *refs):
    count = len(refs) - 4
    chunks = refs[:count]
    units_ref, by_row_ref, by_col_ref, penalty_ref = refs[count:]
    step = chunks[0].shape[1]
    j = pl.program_id(0)
    cosines = jnp.zeros((ROWS, BLOCK), jnp.float32)
    for k in range(count):
        cosines += lax.dot_general(
            chunks[k][...],
            units_ref[:, k * step : (k + 1) * step],
            NT,
            preferred_element_type=jnp.float32,
        )
    rows = lax.broadcasted_iota(jnp.int32, (ROWS, BLOCK), 0)
    cols = lax.broadcasted_iota(jnp.int32, (ROWS, BLOCK), 1)
    cols = cols + (delta_ref[0] + j * BLOCK)
    inside = (cols >= 0) & (cols < ROWS)
    weight = jnp.where(cols == rows, 0.0, jnp.where(inside, 0.5, 1.0))
    products = weight * cosines
    by_row_ref[...] = products.astype(jnp.bfloat16)
    by_col_ref[...] = products.T.astype(jnp.bfloat16)

    @pl.when(j == 0)
    def _():
        penalty_ref[...] = jnp.zeros_like(penalty_ref)

    squares = (products * cosines).reshape(ROWS // 8, 8, BLOCK // 128, 128)
    penalty_ref[...] += jnp.sum(squares, axis=(0, 2))


def row_kernel(by_row_ref, units_ref, out_ref):
    out_ref[...] = jnp.dot(
        by_row_ref[...], units_ref[...], preferred_element_type=jnp.float32
    )


def finish_block(column, decoder_ref, inverse_ref, out_ref):
    inverse = inverse_ref[:, :1]
    values = decoder_ref[...].astype(jnp.float32)
    along = jnp.sum(column[...] * values, axis=1, keepdims=True)
    scale = (2.0 * math.sqrt(DW)) * inverse
    back = scale * (along * inverse * inverse)
    out_ref[...] = scale * column[...] - back * values


def finish_kernel(count, by_col_ref, decoder_ref, inverse_ref, *refs):
    chunks = refs[:count]
    out_ref, column = refs[count:]
    step = chunks[0].shape[1]
    for k in range(count):
        column[:, k * step : (k + 1) * step] = jnp.dot(
            by_col_ref[...], chunks[k][...], preferred_element_type=jnp.float32
        )
    finish_block(column, decoder_ref, inverse_ref, out_ref)


def last_kernel(count, owner_ref, by_col_ref, decoder_ref, inverse_ref, *refs):
    chunks, sums = refs[:count], refs[count : 2 * count]
    out_ref, column = refs[-2:]
    step = chunks[0].shape[1]
    owner = owner_ref[0] == 1
    for k in range(count):
        part = jnp.dot(by_col_ref[...], chunks[k][...], preferred_element_type=jnp.float32)
        column[:, k * step : (k + 1) * step] = part + jnp.where(owner, sums[k][...], 0.0)
    finish_block(column, decoder_ref, inverse_ref, out_ref)


def on_device(decoder, quarter):
    shard, width = decoder.shape
    devices = lax.axis_size("row")
    index = lax.axis_index("row")
    per = devices // 4
    latents = shard * devices
    blocks = shard // BLOCK
    count = 2 * HALF_CHUNKS
    step = width // count
    chosen_quarter = quarter[0]
    start = chosen_quarter * (latents // 4)
    place = index // per
    within = index % per
    here = place == chosen_quarter
    smem = pl.BlockSpec(memory_space=pltpu.SMEM)

    def send(value, pairs):
        return lax.ppermute(value, "row", pairs)

    def hop(level, lanes):
        moves = (((0, 1), (3, 2)), ((1, 2), (2, 1)), ((2, 3), (1, 0)))[level]
        return [(a * per + w, b * per + w) for a, b in moves for w in lanes]

    def each(moves):
        return [(z * per + a, z * per + b) for z in range(4) for a, b in moves]

    own = pl.pallas_call(
        head_kernel,
        grid=(1,),
        in_specs=[pl.BlockSpec((ROWS, width), lambda i: (0, 0))],
        out_specs=[pl.BlockSpec((ROWS, step), lambda i: (0, 0))] * count,
        out_shape=[jax.ShapeDtypeStruct((ROWS, step), jnp.bfloat16)] * count,
        compiler_params=params(),
        name="head_units",
    )(decoder)

    units, inverse = pl.pallas_call(
        units_kernel,
        grid=(blocks,),
        in_specs=[pl.BlockSpec((BLOCK, width), lambda i: (i, 0))],
        out_specs=[
            pl.BlockSpec((BLOCK, width), lambda i: (i, 0)),
            pl.BlockSpec((BLOCK, 128), lambda i: (i, 0)),
        ],
        out_shape=[
            jax.ShapeDtypeStruct((shard, width), jnp.bfloat16),
            jax.ShapeDtypeStruct((shard, 128), jnp.float32),
        ],
        compiler_params=params(),
        cost_estimate=pl.CostEstimate(
            flops=4 * shard * width, bytes_accessed=4 * shard * width, transcendentals=0
        ),
        name="units",
    )(decoder)

    chosen = [None] * count
    for k in range(HALF_CHUNKS):
        across = send(own[k + HALF_CHUNKS], each([(0, 2)]))
        mine = jnp.where(within == 2, across, own[k])
        first = send(mine, hop(0, (0, 2)))
        second = send(jnp.where(here, mine, first), hop(1, (0, 2)))
        third = send(jnp.where(here, mine, second), hop(2, (0, 2)))
        near = jnp.where(place == 1, chosen_quarter == 0, chosen_quarter == 3)
        middle = (place == 1) | (place == 2)
        held = jnp.where(
            here, mine, jnp.where(middle, jnp.where(near, first, second), third)
        )
        other = send(held, each([(0, 2), (2, 0)]))
        core_held = send(held, each([(0, 1), (2, 3)]))
        core_other = send(other, each([(0, 1), (2, 3)]))
        odd = (within % 2) == 1
        low = (within // 2) % 2 == 0
        one = jnp.where(odd, core_held, held)
        two = jnp.where(odd, core_other, other)
        chosen[k] = jnp.where(low, one, two)
        chosen[k + HALF_CHUNKS] = jnp.where(low, two, one)
        far = 4
        while far < per:
            moves = each([(w, w + far) for w in range(far)])
            fresh = (within >= far) & (within < 2 * far)
            for c in (k, k + HALF_CHUNKS):
                chosen[c] = jnp.where(fresh, send(chosen[c], moves), chosen[c])
            far *= 2

    delta = jnp.reshape(index * shard - start, (1,)).astype(jnp.int32)
    whole_chunk = pl.BlockSpec((ROWS, step), lambda i: (0, 0))
    by_row, by_col, local_penalty = pl.pallas_call(
        cosine_kernel,
        grid=(blocks,),
        in_specs=[smem]
        + [whole_chunk] * count
        + [pl.BlockSpec((BLOCK, width), lambda i: (i, 0))],
        out_specs=[
            pl.BlockSpec((ROWS, BLOCK), lambda i: (0, i)),
            pl.BlockSpec((BLOCK, ROWS), lambda i: (i, 0)),
            pl.BlockSpec((8, 128), lambda i: (0, 0)),
        ],
        out_shape=[
            jax.ShapeDtypeStruct((ROWS, shard), jnp.bfloat16),
            jax.ShapeDtypeStruct((shard, ROWS), jnp.bfloat16),
            jax.ShapeDtypeStruct((8, 128), jnp.float32),
        ],
        compiler_params=params(),
        cost_estimate=pl.CostEstimate(
            flops=2 * ROWS * shard * width, bytes_accessed=2 * shard * width, transcendentals=0
        ),
        name="cosines",
    )(delta, *chosen, units)

    penalties = lax.all_gather(local_penalty, "row", axis=0, tiled=True)

    row_parts = []
    for k in range(count):
        row_parts.append(
            pl.pallas_call(
                row_kernel,
                grid=(1,),
                in_specs=[
                    pl.BlockSpec((ROWS, shard), lambda i: (0, 0)),
                    pl.BlockSpec((shard, step), lambda i, k=k: (0, k)),
                ],
                out_specs=pl.BlockSpec((ROWS, step), lambda i: (0, 0)),
                out_shape=jax.ShapeDtypeStruct((ROWS, step), jnp.float32),
                compiler_params=params(),
                cost_estimate=pl.CostEstimate(
                    flops=2 * ROWS * shard * step,
                    bytes_accessed=2 * shard * step,
                    transcendentals=0,
                ),
                name="row_part",
            )(by_row, units)
        )

    sums = [None] * count
    for k in range(HALF_CHUNKS):
        pair = []
        for c in (k, k + HALF_CHUNKS):
            value = row_parts[c]
            far = per // 2
            while far >= 4:
                value = value + send(value, each([(w + far, w) for w in range(far)]))
                far //= 2
            pair.append(value + send(value, each([(1, 0), (3, 2)])))
        low = within == 0
        away = jnp.where(low, pair[1], pair[0])
        held = jnp.where(low, pair[0], pair[1]) + send(away, each([(0, 2), (2, 0)]))
        first = send(held, hop(0, (0, 2)))
        second = send(held + first, hop(1, (0, 2)))
        third = send(held + second, hop(2, (0, 2)))
        total = held + first + second + third
        sums[k] = total
        sums[k + HALF_CHUNKS] = send(total, each([(2, 0)]))

    out_type = jax.ShapeDtypeStruct((shard, width), jnp.float32)
    scratch = [pltpu.VMEM((BLOCK, width), jnp.float32)]

    def block_specs(first_block):
        return [
            pl.BlockSpec((BLOCK, ROWS), lambda i: (i + first_block, 0)),
            pl.BlockSpec((BLOCK, width), lambda i: (i + first_block, 0)),
            pl.BlockSpec((BLOCK, 128), lambda i: (i + first_block, 0)),
        ]

    grad = None
    if blocks > 1:
        grad = pl.pallas_call(
            functools.partial(finish_kernel, count),
            grid=(blocks - 1,),
            in_specs=block_specs(1) + [whole_chunk] * count,
            out_specs=pl.BlockSpec((BLOCK, width), lambda i: (i + 1, 0)),
            out_shape=out_type,
            scratch_shapes=scratch,
            compiler_params=params(),
            cost_estimate=pl.CostEstimate(
                flops=2 * ROWS * shard * width,
                bytes_accessed=6 * shard * width,
                transcendentals=0,
            ),
            name="finish",
        )(by_col, decoder, inverse, *chosen)

    owner = jnp.reshape(here & (within == 0), (1,)).astype(jnp.int32)
    operands = [owner, by_col, decoder, inverse, *chosen, *sums]
    specs = [smem] + block_specs(0) + [whole_chunk] * (2 * count)
    aliases = {}
    body = functools.partial(last_kernel, count)
    if grad is not None:
        aliases = {len(operands): 0}
        operands.append(grad)
        specs.append(pl.BlockSpec(memory_space=pl.ANY))
    decoder_grad = pl.pallas_call(
        body,
        grid=(1,),
        in_specs=specs,
        out_specs=pl.BlockSpec((BLOCK, width), lambda i: (0, 0)),
        out_shape=out_type,
        scratch_shapes=scratch,
        input_output_aliases=aliases,
        compiler_params=params(),
        name="finish_rows",
    )(*operands)

    penalty = jnp.sum(penalties) * (DW / (ROWS * latents))
    return (jnp.reshape(penalty, (1,)), decoder_grad)


def solution(mesh):
    in_specs = (P(("groups", "row"), None), P("groups"))
    out_specs = (P("groups"), P(("groups", "row"), None))
    return jax.shard_map(
        on_device, mesh=mesh, in_specs=in_specs, out_specs=out_specs, check_vma=False
    )
```

time: 359 us -> 269 us (0.75)
  waiting for transfers between devices: 193 us -> 40.2 us
  starting transfers between devices: 0.12 us -> 95.9 us
  Pallas kernels: 0 us -> 88.9 us
  matrix products: 55.5 us -> 0 us
  other arithmetic: 47.6 us -> 14.9 us
  local copies, waits for them, and re-layouts: 15.6 us -> 0.96 us
  between operations: 16.3 us -> 4.29 us
  blocking collectives: 30.8 us -> 21.9 us
    psum x1 -> x0, waiting for transfers between devices: 101 us -> none  [from_root(): return lax.psum(kept, axis)]
    ppermute x0 -> x56, starting transfers between devices: none -> 95.9 us  [send(): return lax.ppermute(value, 'row', pairs)]
    pallas_call x0 -> x13, Pallas kernels: none -> 88.9 us  [the longest x8 27.7 us: on_device(): pl.pallas_call(row_kernel, grid=(1,), in_specs=[pl.BlockSpec((ROWS, shard...]
    reduce_scatter x1 -> x0, waiting for transfers between devices: 72 us -> none  [on_device(): reduced = lax.psum_scatter(row_part, 'row', scatter_dimension=0, tiled=True)]
    dot_general x3 -> x0, matrix products: 55.5 us -> none  [the longest x1 35.1 us: on_device(): jnp.dot(weighted.T, received, preferred_element_type=jnp.float32)]
    ppermute x0 -> x56, waiting for transfers between devices: none -> 40.2 us  [send(): return lax.ppermute(value, 'row', pairs)]
    psum x1 -> x0, blocking collectives: 30.8 us -> none  [on_device(): total_penalty = lax.psum(local_penalty, 'row')]
    div x1 -> x0, other arithmetic: 28.8 us -> none  [on_device(): decoder_grad = (unit_grad - along[:, None] * directions) / norms[:, None]]
  transfers between devices with their start and end apart: 3 -> 56, of which waited for: 3 -> 11; matrix products, arithmetic and copies ran while one was open for 0% -> 5% of each run, Pallas kernels for 0% -> 23%
where the time goes in v1:
time: 269 us; the launch traced here: 267 us
  starting transfers between devices  95.9 us (36%)
  Pallas kernels  88.9 us (33%)
  waiting for transfers between devices  40.2 us (15%)
  blocking collectives  21.9 us (8%)
  other arithmetic  14.9 us (6%)
  between operations  4.29 us (2%)
    ppermute x56, starting transfers between devices, send(): return lax.ppermute(value, 'row', pairs)  95.9 us
    ppermute x56, waiting for transfers between devices, send(): return lax.ppermute(value, 'row', pairs)  40.2 us
    pallas_call x8, Pallas kernels, on_device(): pl.pallas_call(row_kernel, grid=(1,), in_specs=[pl.BlockSpec((ROWS, shard...  27.7 us
    all_gather x1, blocking collectives, on_device(): penalties = lax.all_gather(local_penalty, 'row', axis=0, tiled=True)  21.9 us
    pallas_call x1, Pallas kernels, on_device(): pl.pallas_call(functools.partial(finish_kernel, count), grid=(blocks - 1,...  20.7 us
    pallas_call x1, Pallas kernels, on_device(): pl.pallas_call(units_kernel, grid=(blocks,), in_specs=[pl.BlockSpec((BLOC...  17.1 us
    pallas_call x1, Pallas kernels, on_device(): pl.pallas_call(cosine_kernel, grid=(blocks,), in_specs=[smem] + [whole_ch...  12.9 us
    pallas_call x1, Pallas kernels, on_device(): pl.pallas_call(body, grid=(1,), in_specs=specs, out_specs=pl.BlockSpec((B...  7.04 us
  transfers between devices with their start and end apart: 56, of which 11 were waited for; matrix products, arithmetic and copies ran while one was open for 5% of the time, Pallas kernels for 23%

profile of v1, /device:TPU:0, one launch (start us, length us, event | category | flops | bytes accessed | tf_op | source)
XLA Modules:
  0.0 267.1 jit_solution(15034764768275227667)
XLA Ops:
  0.6 3.5 %head_units.1 = (bf16[256,512]{1,0:T(8,128)(2,1)}, bf16[256,512]{1,0:T(8,128)(2,1)}, bf16[256,512]{1,0:T(8,128)(2,1)}, bf16[256,512]{1,0:T(8,128)(2,1)}, bf16[25...) custom-call(bf16[2048,4096]{1,0:T(8,128)(2,1)} %decoder_ref.7), custom_call_target="tpu_custom_call" | custom-call | tf_op jit(solution)/shard_map/head_units/pallas_call | solution.py:137
  4.1 4.8 %collective-permute-start = (bf16[256,512]{1,0:T(8,128)(2,1)}, bf16[256,512]{1,0:T(8,128)(2,1)S(1)}, u32[]{:S(2)}, u32[]{:S(2)}) collective-permute-start(bf16[256,512]{1,0:T(8,128)(2,1)} %get-tuple-element.15), channel_id=1, source_target_pairs={{0,2},{4,6},{8,10},{12,14},{16,18},{20,22},{24,26},{28,30}} | collective-permute-start | bytes 786440 | tf_op jit(solution)/shard_map/ppermute | solution.py:128
  13.7 17.1 %units.1 = (bf16[2048,4096]{1,0:T(8,128)(2,1)}, f32[2048,128]{1,0:T(8,128)}) custom-call(bf16[2048,4096]{1,0:T(8,128)(2,1)} %decoder_ref.7), custom_call_target="tpu_custom_call" | custom-call | flops 33554432 | bytes 33554432 | tf_op jit(solution)/shard_map/units/pallas_call | solution.py:147
  31.7 3.5 %collective-permute-start.1 = (bf16[256,512]{1,0:T(8,128)(2,1)S(1)}, bf16[256,512]{1,0:T(8,128)(2,1)S(1)}, u32[]{:S(2)}, u32[]{:S(2)}) collective-permute-start(bf16[256,512]{1,0:T(8,128)(2,1)S(1)} %broadcast_select_fusion.7), channel_id=1, source_target_pairs={{0,4},{2,6},{12,8},{14,10},{16,20},{18,22},{28,24},{30,26}} | collective-permute-start | bytes 786440 | tf_op jit(solution)/shard_map/ppermute | solution.py:128
  52.3 7.3 %collective-permute-done.3 = bf16[256,512]{1,0:T(8,128)(2,1)S(1)} collective-permute-done((bf16[256,512]{1,0:T(8,128)(2,1)S(1)}, bf16[256,512]{1,0:T(8,128)(2,1)S(1)}, u32[]{:S(2)}, u32[]{:S(2)}) %collective-permute-start.3) | collective-permute-done | bytes 262176 | tf_op jit(solution)/shard_map/ppermute | solution.py:128
  64.2 3.9 %collective-permute-start.12 = (bf16[256,512]{1,0:T(8,128)(2,1)S(1)}, bf16[256,512]{1,0:T(8,128)(2,1)S(1)}, u32[]{:S(2)}, u32[]{:S(2)}) collective-permute-start(bf16[256,512]{1,0:T(8,128)(2,1)S(1)} %select_select_fusion.2), channel_id=1, source_target_pairs={{0,2},{2,0},{4,6},{6,4},{8,10},{10,8},{12,14},{14,12},{16,18},{18,... | collective-permute-start | bytes 786440 | tf_op jit(solution)/shard_map/ppermute | solution.py:128
  70.9 2.8 %collective-permute-start.19 = (bf16[256,512]{1,0:T(8,128)(2,1)S(1)}, bf16[256,512]{1,0:T(8,128)(2,1)S(1)}, u32[]{:S(2)}, u32[]{:S(2)}) collective-permute-start(bf16[256,512]{1,0:T(8,128)(2,1)S(1)} %select_select_fusion.1), channel_id=1, source_target_pairs={{0,2},{2,0},{4,6},{6,4},{8,10},{10,8},{12,14},{14,12},{16,18},{18,... | collective-permute-start | bytes 786440 | tf_op jit(solution)/shard_map/ppermute | solution.py:128
  75.1 3.0 %collective-permute-start.26 = (bf16[256,512]{1,0:T(8,128)(2,1)S(1)}, bf16[256,512]{1,0:T(8,128)(2,1)S(1)}, u32[]{:S(2)}, u32[]{:S(2)}) collective-permute-start(bf16[256,512]{1,0:T(8,128)(2,1)S(1)} %select_select_fusion), channel_id=1, source_target_pairs={{0,2},{2,0},{4,6},{6,4},{8,10},{10,8},{12,14},{14,12},{16,18},{18,... | collective-permute-start | bytes 786440 | tf_op jit(solution)/shard_map/ppermute | solution.py:128
  87.4 12.9 %cosines.1 = (bf16[256,2048]{1,0:T(8,128)(2,1)}, bf16[2048,256]{1,0:T(8,128)(2,1)}, f32[8,128]{1,0:T(8,128)}) custom-call(s32[1]{0:T(128)} %bitcast.1.delta_ref, bf16[256,512]{1,0:T(8,128)(2,1)} %get-tuple-element.35.refs_0_, bf16[256,512]{1,0:T(8,128)(2,1)} %get-tuple-element.33.refs_1_, bf16[256,512]{1,0:T(8,128)(2,1)} %get-tuple-element.31.refs_2_, ...), custom_call_target="tpu_custom_call" | custom-call | flops 4294967296 | bytes 16777216 | tf_op jit(solution)/shard_map/cosines/pallas_call | solution.py:197
  100.3 3.4 %row_part.8 = f32[256,512]{1,0:T(8,128)} custom-call(bf16[256,2048]{1,0:T(8,128)(2,1)} %get-tuple-element.27.by_row_ref, bf16[2048,4096]{1,0:T(8,128)(2,1)} %get-tuple-element.23.refs_8_.units_ref), custom_call_target="tpu_custom_call" | custom-call | flops 536870912 | bytes 2097152 | tf_op jit(solution)/shard_map/row_part/pallas_call | solution.py:225
  105.0 3.4 %row_part.9 = f32[256,512]{1,0:T(8,128)} custom-call(bf16[256,2048]{1,0:T(8,128)(2,1)} %get-tuple-element.27.by_row_ref, bf16[2048,4096]{1,0:T(8,128)(2,1)} %get-tuple-element.23.refs_8_.units_ref), custom_call_target="tpu_custom_call" | custom-call | flops 536870912 | bytes 2097152 | tf_op jit(solution)/shard_map/row_part/pallas_call | solution.py:225
  109.7 3.4 %row_part.10 = f32[256,512]{1,0:T(8,128)} custom-call(bf16[256,2048]{1,0:T(8,128)(2,1)} %get-tuple-element.27.by_row_ref, bf16[2048,4096]{1,0:T(8,128)(2,1)} %get-tuple-element.23.refs_8_.units_ref), custom_call_target="tpu_custom_call" | custom-call | flops 536870912 | bytes 2097152 | tf_op jit(solution)/shard_map/row_part/pallas_call | solution.py:225
  114.4 3.4 %row_part.11 = f32[256,512]{1,0:T(8,128)} custom-call(bf16[256,2048]{1,0:T(8,128)(2,1)} %get-tuple-element.27.by_row_ref, bf16[2048,4096]{1,0:T(8,128)(2,1)} %get-tuple-element.23.refs_8_.units_ref), custom_call_target="tpu_custom_call" | custom-call | flops 536870912 | bytes 2097152 | tf_op jit(solution)/shard_map/row_part/pallas_call | solution.py:225
  119.2 3.6 %row_part.12 = f32[256,512]{1,0:T(8,128)} custom-call(bf16[256,2048]{1,0:T(8,128)(2,1)} %get-tuple-element.27.by_row_ref, bf16[2048,4096]{1,0:T(8,128)(2,1)} %get-tuple-element.23.refs_8_.units_ref), custom_call_target="tpu_custom_call" | custom-call | flops 536870912 | bytes 2097152 | tf_op jit(solution)/shard_map/row_part/pallas_call | solution.py:225
  124.2 3.5 %row_part.15 = f32[256,512]{1,0:T(8,128)} custom-call(bf16[256,2048]{1,0:T(8,128)(2,1)} %get-tuple-element.27.by_row_ref, bf16[2048,4096]{1,0:T(8,128)(2,1)} %get-tuple-element.23.refs_8_.units_ref), custom_call_target="tpu_custom_call" | custom-call | flops 536870912 | bytes 2097152 | tf_op jit(solution)/shard_map/row_part/pallas_call | solution.py:225
  127.7 3.5 %row_part.14 = f32[256,512]{1,0:T(8,128)} custom-call(bf16[256,2048]{1,0:T(8,128)(2,1)} %get-tuple-element.27.by_row_ref, bf16[2048,4096]{1,0:T(8,128)(2,1)} %get-tuple-element.23.refs_8_.units_ref), custom_call_target="tpu_custom_call" | custom-call | flops 536870912 | bytes 2097152 | tf_op jit(solution)/shard_map/row_part/pallas_call | solution.py:225
  131.2 3.5 %row_part.13 = f32[256,512]{1,0:T(8,128)} custom-call(bf16[256,2048]{1,0:T(8,128)(2,1)} %get-tuple-element.27.by_row_ref, bf16[2048,4096]{1,0:T(8,128)(2,1)} %get-tuple-element.23.refs_8_.units_ref), custom_call_target="tpu_custom_call" | custom-call | flops 536870912 | bytes 2097152 | tf_op jit(solution)/shard_map/row_part/pallas_call | solution.py:225
  138.8 3.0 %collective-permute-start.30 = (f32[256,512]{1,0:T(8,128)S(1)}, f32[256,512]{1,0:T(8,128)S(1)}, u32[]{:S(2)}, u32[]{:S(2)}) collective-permute-start(f32[256,512]{1,0:T(8,128)S(1)} %broadcast_select_fusion.3), channel_id=1, source_target_pairs={{0,2},{2,0},{4,6},{6,4},{8,10},{10,8},{12,14},{14,12},{16,18},{18,... | collective-permute-start | bytes 1572872 | tf_op jit(solution)/shard_map/ppermute | solution.py:128
  146.2 3.0 %collective-permute-start.42 = (f32[256,512]{1,0:T(8,128)S(1)}, f32[256,512]{1,0:T(8,128)S(1)}, u32[]{:S(2)}, u32[]{:S(2)}) collective-permute-start(f32[256,512]{1,0:T(8,128)S(1)} %broadcast_select_fusion.1), channel_id=1, source_target_pairs={{0,2},{2,0},{4,6},{6,4},{8,10},{10,8},{12,14},{14,12},{16,18},{18,... | collective-permute-start | bytes 1572872 | tf_op jit(solution)/shard_map/ppermute | solution.py:128
  150.6 3.0 %collective-permute-start.48 = (f32[256,512]{1,0:T(8,128)S(1)}, f32[256,512]{1,0:T(8,128)S(1)}, u32[]{:S(2)}, u32[]{:S(2)}) collective-permute-start(f32[256,512]{1,0:T(8,128)S(1)} %broadcast_select_fusion), channel_id=1, source_target_pairs={{0,2},{2,0},{4,6},{6,4},{8,10},{10,8},{12,14},{14,12},{16,18},{18,... | collective-permute-start | bytes 1572872 | tf_op jit(solution)/shard_map/ppermute | solution.py:128
  153.9 4.3 %collective-permute-start.31 = (f32[256,512]{1,0:T(8,128)S(1)}, f32[256,512]{1,0:T(8,128)S(1)}, u32[]{:S(2)}, u32[]{:S(2)}) collective-permute-start(f32[256,512]{1,0:T(8,128)S(1)} %select_add_fusion.3), channel_id=1, source_target_pairs={{0,4},{2,6},{12,8},{14,10},{16,20},{18,22},{28,24},{30,26}} | collective-permute-start | bytes 1572872 | tf_op jit(solution)/shard_map/ppermute | solution.py:128
  162.5 4.3 %collective-permute-start.43 = (f32[256,512]{1,0:T(8,128)S(1)}, f32[256,512]{1,0:T(8,128)S(1)}, u32[]{:S(2)}, u32[]{:S(2)}) collective-permute-start(f32[256,512]{1,0:T(8,128)S(1)} %select_add_fusion.1), channel_id=1, source_target_pairs={{0,4},{2,6},{12,8},{14,10},{16,20},{18,22},{28,24},{30,26}} | collective-permute-start | bytes 1572872 | tf_op jit(solution)/shard_map/ppermute | solution.py:128
  167.1 4.3 %collective-permute-start.49 = (f32[256,512]{1,0:T(8,128)S(1)}, f32[256,512]{1,0:T(8,128)S(1)}, u32[]{:S(2)}, u32[]{:S(2)}) collective-permute-start(f32[256,512]{1,0:T(8,128)S(1)} %select_add_fusion), channel_id=1, source_target_pairs={{0,4},{2,6},{12,8},{14,10},{16,20},{18,22},{28,24},{30,26}} | collective-permute-start | bytes 1572872 | tf_op jit(solution)/shard_map/ppermute | solution.py:128
  172.9 3.1 %collective-permute-done.43 = f32[256,512]{1,0:T(8,128)S(1)} collective-permute-done((f32[256,512]{1,0:T(8,128)S(1)}, f32[256,512]{1,0:T(8,128)S(1)}, u32[]{:S(2)}, u32[]{:S(2)}) %collective-permute-start.43) | collective-permute-done | bytes 524320 | tf_op jit(solution)/shard_map/ppermute | solution.py:128
  176.8 4.8 %collective-permute-done.49 = f32[256,512]{1,0:T(8,128)S(1)} collective-permute-done((f32[256,512]{1,0:T(8,128)S(1)}, f32[256,512]{1,0:T(8,128)S(1)}, u32[]{:S(2)}, u32[]{:S(2)}) %collective-permute-start.49) | collective-permute-done | bytes 524320 | tf_op jit(solution)/shard_map/ppermute | solution.py:128
  188.0 7.8 %collective-permute-done.33 = f32[256,512]{1,0:T(8,128)S(1)} collective-permute-done((f32[256,512]{1,0:T(8,128)S(1)}, f32[256,512]{1,0:T(8,128)S(1)}, u32[]{:S(2)}, u32[]{:S(2)}) %collective-permute-start.33) | collective-permute-done | bytes 524320 | tf_op jit(solution)/shard_map/ppermute | solution.py:128
  197.2 4.2 %collective-permute-done.39 = f32[256,512]{1,0:T(8,128)S(1)} collective-permute-done((f32[256,512]{1,0:T(8,128)S(1)}, f32[256,512]{1,0:T(8,128)S(1)}, u32[]{:S(2)}, u32[]{:S(2)}) %collective-permute-start.39) | collective-permute-done | bytes 524320 | tf_op jit(solution)/shard_map/ppermute | solution.py:128
  202.9 4.2 %collective-permute-done.45 = f32[256,512]{1,0:T(8,128)S(1)} collective-permute-done((f32[256,512]{1,0:T(8,128)S(1)}, f32[256,512]{1,0:T(8,128)S(1)}, u32[]{:S(2)}, u32[]{:S(2)}) %collective-permute-start.45) | collective-permute-done | bytes 524320 | tf_op jit(solution)/shard_map/ppermute | solution.py:128
  208.5 4.2 %collective-permute-done.51 = f32[256,512]{1,0:T(8,128)S(1)} collective-permute-done((f32[256,512]{1,0:T(8,128)S(1)}, f32[256,512]{1,0:T(8,128)S(1)}, u32[]{:S(2)}, u32[]{:S(2)}) %collective-permute-start.51) | collective-permute-done | bytes 524320 | tf_op jit(solution)/shard_map/ppermute | solution.py:128
  214.1 21.9 %all_gather.3 = f32[128,128]{1,0:T(8,128)S(1)} all-gather(f32[8,128]{1,0:T(8,128)S(1)} %copy-done.13), channel_id=1, replica_groups=mesh['groups'=2,'row'=16] {'row'}, dimensions={0}, use_global_device_ids=true | all-gather | bytes 69632 | tf_op jit(solution)/shard_map/all_gather | solution.py:220
  237.3 20.7 %finish.1.refs_16_ = f32[2048,4096]{1,0:T(8,128)} custom-call(bf16[2048,256]{1,0:T(8,128)(2,1)} %get-tuple-element.25.by_col_ref, bf16[2048,4096]{1,0:T(8,128)(2,1)} %decoder_ref.7, f32[2048,128]{1,0:T(8,128)} %get-tuple-element.26.inverse_ref, bf16[256,512]{1,0:T(8,128)(2,1)} %get-tuple-element.35.refs_0_, bf16[256,512]{1,0:T(8,128)(2,1)} %get-tuple-element.33.refs_1_, ...), custom_call_target="tpu_custom_call" | custom-call | flops 4294967296 | bytes 50331648 | tf_op jit(solution)/shard_map/finish/pallas_call | solution.py:276
  258.9 7.0 %finish_rows.1 = f32[2048,4096]{1,0:T(8,128)} custom-call(s32[1]{0:T(128)} %bitcast.3.owner_ref, bf16[2048,256]{1,0:T(8,128)(2,1)} %get-tuple-element.25.by_col_ref, bf16[2048,4096]{1,0:T(8,128)(2,1)} %decoder_ref.7, f32[2048,128]{1,0:T(8,128)} %get-tuple-element.26.inverse_ref, ...), custom_call_target="tpu_custom_call", output_to_operand_aliasing={{}: (20, {})} | custom-call | tf_op jit(solution)/shard_map/finish_rows/pallas_call | solution.py:301
  (163 shorter events, 76.6 us)
Async XLA Ops:
  4.1 26.6 %collective-permute-start = (bf16[256,512]{1,0:T(8,128)(2,1)}, bf16[256,512]{1,0:T(8,128)(2,1)S(1)}, u32[]{:S(2)}, u32[]{:S(2)}) collective-permute-start(bf16[256,512]{1,0:T(8,128)(2,1)} %get-tuple-element.15), channel_id=1, source_target_pairs={{0,2},{4,6},{8,10},{12,14},{16,18},{20,22},{24,26},{28,30}} | collective-permute-start | bytes 786440 | tf_op jit(solution)/shard_map/ppermute | solution.py:128
  9.0 26.2 %collective-permute-start.7 = (bf16[256,512]{1,0:T(8,128)(2,1)}, bf16[256,512]{1,0:T(8,128)(2,1)S(1)}, u32[]{:S(2)}, u32[]{:S(2)}) collective-permute-start(bf16[256,512]{1,0:T(8,128)(2,1)} %get-tuple-element.17), channel_id=1, source_target_pairs={{0,2},{4,6},{8,10},{12,14},{16,18},{20,22},{24,26},{28,30}} | collective-permute-start | bytes 786440 | tf_op jit(solution)/shard_map/ppermute | solution.py:128
  10.3 27.2 %collective-permute-start.14 = (bf16[256,512]{1,0:T(8,128)(2,1)}, bf16[256,512]{1,0:T(8,128)(2,1)S(1)}, u32[]{:S(2)}, u32[]{:S(2)}) collective-permute-start(bf16[256,512]{1,0:T(8,128)(2,1)} %get-tuple-element.19), channel_id=1, source_target_pairs={{0,2},{4,6},{8,10},{12,14},{16,18},{20,22},{24,26},{28,30}} | collective-permute-start | bytes 786440 | tf_op jit(solution)/shard_map/ppermute | solution.py:128
  11.6 28.3 %collective-permute-start.21 = (bf16[256,512]{1,0:T(8,128)(2,1)}, bf16[256,512]{1,0:T(8,128)(2,1)S(1)}, u32[]{:S(2)}, u32[]{:S(2)}) collective-permute-start(bf16[256,512]{1,0:T(8,128)(2,1)} %get-tuple-element.21), channel_id=1, source_target_pairs={{0,2},{4,6},{8,10},{12,14},{16,18},{20,22},{24,26},{28,30}} | collective-permute-start | bytes 786440 | tf_op jit(solution)/shard_map/ppermute | solution.py:128
  47.5 14.0 %collective-permute-start.23 = (bf16[256,512]{1,0:T(8,128)(2,1)S(1)}, bf16[256,512]{1,0:T(8,128)(2,1)S(1)}, u32[]{:S(2)}, u32[]{:S(2)}) collective-permute-start(bf16[256,512]{1,0:T(8,128)(2,1)S(1)} %broadcast_select_fusion.9), channel_id=1, source_target_pairs={{4,8},{6,10},{8,4},{10,6},{20,24},{22,26},{24,20},{26,22}} | collective-permute-start | bytes 786440 | tf_op jit(solution)/shard_map/ppermute | solution.py:128
  49.6 14.6 %collective-permute-start.10 = (bf16[256,512]{1,0:T(8,128)(2,1)S(1)}, bf16[256,512]{1,0:T(8,128)(2,1)S(1)}, u32[]{:S(2)}, u32[]{:S(2)}) collective-permute-start(bf16[256,512]{1,0:T(8,128)(2,1)S(1)} %broadcast_select_fusion.12), channel_id=1, source_target_pairs={{8,12},{10,14},{4,0},{6,2},{24,28},{26,30},{20,16},{22,18}} | collective-permute-start | bytes 786440 | tf_op jit(solution)/shard_map/ppermute | solution.py:128
  51.0 17.2 %collective-permute-start.17 = (bf16[256,512]{1,0:T(8,128)(2,1)S(1)}, bf16[256,512]{1,0:T(8,128)(2,1)S(1)}, u32[]{:S(2)}, u32[]{:S(2)}) collective-permute-start(bf16[256,512]{1,0:T(8,128)(2,1)S(1)} %broadcast_select_fusion.10), channel_id=1, source_target_pairs={{8,12},{10,14},{4,0},{6,2},{24,28},{26,30},{20,16},{22,18}} | collective-permute-start | bytes 786440 | tf_op jit(solution)/shard_map/ppermute | solution.py:128
  68.2 12.2 %collective-permute-start.11 = (bf16[256,512]{1,0:T(8,128)(2,1)S(1)}, bf16[256,512]{1,0:T(8,128)(2,1)S(1)}, u32[]{:S(2)}, u32[]{:S(2)}) collective-permute-start(bf16[256,512]{1,0:T(8,128)(2,1)S(1)} %select_select_fusion.2), channel_id=1, source_target_pairs={{0,1},{2,3},{4,5},{6,7},{8,9},{10,11},{12,13},{14,15},{16,17},{18,... | collective-permute-start | bytes 786440 | tf_op jit(solution)/shard_map/ppermute | solution.py:128
  73.8 11.8 %collective-permute-start.18 = (bf16[256,512]{1,0:T(8,128)(2,1)S(1)}, bf16[256,512]{1,0:T(8,128)(2,1)S(1)}, u32[]{:S(2)}, u32[]{:S(2)}) collective-permute-start(bf16[256,512]{1,0:T(8,128)(2,1)S(1)} %select_select_fusion.1), channel_id=1, source_target_pairs={{0,1},{2,3},{4,5},{6,7},{8,9},{10,11},{12,13},{14,15},{16,17},{18,... | collective-permute-start | bytes 786440 | tf_op jit(solution)/shard_map/ppermute | solution.py:128
  103.7 30.9 %collective-permute-start.28 = (f32[256,512]{1,0:T(8,128)}, f32[256,512]{1,0:T(8,128)S(1)}, u32[]{:S(2)}, u32[]{:S(2)}) collective-permute-start(f32[256,512]{1,0:T(8,128)} %row_part.8), channel_id=1, source_target_pairs={{1,0},{3,2},{5,4},{7,6},{9,8},{11,10},{13,12},{15,14},{17,16},{19,... | collective-permute-start | bytes 1572872 | tf_op jit(solution)/shard_map/ppermute | solution.py:128
  108.5 27.5 %collective-permute-start.29 = (f32[256,512]{1,0:T(8,128)}, f32[256,512]{1,0:T(8,128)S(1)}, u32[]{:S(2)}, u32[]{:S(2)}) collective-permute-start(f32[256,512]{1,0:T(8,128)} %row_part.9), channel_id=1, source_target_pairs={{1,0},{3,2},{5,4},{7,6},{9,8},{11,10},{13,12},{15,14},{17,16},{19,... | collective-permute-start | bytes 1572872 | tf_op jit(solution)/shard_map/ppermute | solution.py:128
  113.2 24.3 %collective-permute-start.34 = (f32[256,512]{1,0:T(8,128)}, f32[256,512]{1,0:T(8,128)S(1)}, u32[]{:S(2)}, u32[]{:S(2)}) collective-permute-start(f32[256,512]{1,0:T(8,128)} %row_part.10), channel_id=1, source_target_pairs={{1,0},{3,2},{5,4},{7,6},{9,8},{11,10},{13,12},{15,14},{17,16},{19,... | collective-permute-start | bytes 1572872 | tf_op jit(solution)/shard_map/ppermute | solution.py:128
  117.9 20.9 %collective-permute-start.35 = (f32[256,512]{1,0:T(8,128)}, f32[256,512]{1,0:T(8,128)S(1)}, u32[]{:S(2)}, u32[]{:S(2)}) collective-permute-start(f32[256,512]{1,0:T(8,128)} %row_part.11), channel_id=1, source_target_pairs={{1,0},{3,2},{5,4},{7,6},{9,8},{11,10},{13,12},{15,14},{17,16},{19,... | collective-permute-start | bytes 1572872 | tf_op jit(solution)/shard_map/ppermute | solution.py:128
  122.8 19.3 %collective-permute-start.40 = (f32[256,512]{1,0:T(8,128)}, f32[256,512]{1,0:T(8,128)S(1)}, u32[]{:S(2)}, u32[]{:S(2)}) collective-permute-start(f32[256,512]{1,0:T(8,128)} %row_part.12), channel_id=1, source_target_pairs={{1,0},{3,2},{5,4},{7,6},{9,8},{11,10},{13,12},{15,14},{17,16},{19,... | collective-permute-start | bytes 1572872 | tf_op jit(solution)/shard_map/ppermute | solution.py:128
  136.0 13.3 %collective-permute-start.46 = (f32[256,512]{1,0:T(8,128)}, f32[256,512]{1,0:T(8,128)S(1)}, u32[]{:S(2)}, u32[]{:S(2)}) collective-permute-start(f32[256,512]{1,0:T(8,128)} %row_part.14), channel_id=1, source_target_pairs={{1,0},{3,2},{5,4},{7,6},{9,8},{11,10},{13,12},{15,14},{17,16},{19,... | collective-permute-start | bytes 1572872 | tf_op jit(solution)/shard_map/ppermute | solution.py:128
  137.5 11.8 %collective-permute-start.47 = (f32[256,512]{1,0:T(8,128)S(1)}, f32[256,512]{1,0:T(8,128)S(1)}, u32[]{:S(2)}, u32[]{:S(2)}) collective-permute-start(f32[256,512]{1,0:T(8,128)S(1)} %copy-done), channel_id=1, source_target_pairs={{1,0},{3,2},{5,4},{7,6},{9,8},{11,10},{13,12},{15,14},{17,16},{19,... | collective-permute-start | bytes 1572872 | tf_op jit(solution)/shard_map/ppermute | solution.py:128
  138.8 14.7 %collective-permute-start.30 = (f32[256,512]{1,0:T(8,128)S(1)}, f32[256,512]{1,0:T(8,128)S(1)}, u32[]{:S(2)}, u32[]{:S(2)}) collective-permute-start(f32[256,512]{1,0:T(8,128)S(1)} %broadcast_select_fusion.3), channel_id=1, source_target_pairs={{0,2},{2,0},{4,6},{6,4},{8,10},{10,8},{12,14},{14,12},{16,18},{18,... | collective-permute-start | bytes 1572872 | tf_op jit(solution)/shard_map/ppermute | solution.py:128
  142.1 16.0 %collective-permute-start.36 = (f32[256,512]{1,0:T(8,128)S(1)}, f32[256,512]{1,0:T(8,128)S(1)}, u32[]{:S(2)}, u32[]{:S(2)}) collective-permute-start(f32[256,512]{1,0:T(8,128)S(1)} %broadcast_select_fusion.2), channel_id=1, source_target_pairs={{0,2},{2,0},{4,6},{6,4},{8,10},{10,8},{12,14},{14,12},{16,18},{18,... | collective-permute-start | bytes 1572872 | tf_op jit(solution)/shard_map/ppermute | solution.py:128
  146.2 14.9 %collective-permute-start.42 = (f32[256,512]{1,0:T(8,128)S(1)}, f32[256,512]{1,0:T(8,128)S(1)}, u32[]{:S(2)}, u32[]{:S(2)}) collective-permute-start(f32[256,512]{1,0:T(8,128)S(1)} %broadcast_select_fusion.1), channel_id=1, source_target_pairs={{0,2},{2,0},{4,6},{6,4},{8,10},{10,8},{12,14},{14,12},{16,18},{18,... | collective-permute-start | bytes 1572872 | tf_op jit(solution)/shard_map/ppermute | solution.py:128
  150.6 16.2 %collective-permute-start.48 = (f32[256,512]{1,0:T(8,128)S(1)}, f32[256,512]{1,0:T(8,128)S(1)}, u32[]{:S(2)}, u32[]{:S(2)}) collective-permute-start(f32[256,512]{1,0:T(8,128)S(1)} %broadcast_select_fusion), channel_id=1, source_target_pairs={{0,2},{2,0},{4,6},{6,4},{8,10},{10,8},{12,14},{14,12},{16,18},{18,... | collective-permute-start | bytes 1572872 | tf_op jit(solution)/shard_map/ppermute | solution.py:128
  153.9 17.5 %collective-permute-start.31 = (f32[256,512]{1,0:T(8,128)S(1)}, f32[256,512]{1,0:T(8,128)S(1)}, u32[]{:S(2)}, u32[]{:S(2)}) collective-permute-start(f32[256,512]{1,0:T(8,128)S(1)} %select_add_fusion.3), channel_id=1, source_target_pairs={{0,4},{2,6},{12,8},{14,10},{16,20},{18,22},{28,24},{30,26}} | collective-permute-start | bytes 1572872 | tf_op jit(solution)/shard_map/ppermute | solution.py:128
  158.5 13.7 %collective-permute-start.37 = (f32[256,512]{1,0:T(8,128)S(1)}, f32[256,512]{1,0:T(8,128)S(1)}, u32[]{:S(2)}, u32[]{:S(2)}) collective-permute-start(f32[256,512]{1,0:T(8,128)S(1)} %select_add_fusion.2), channel_id=1, source_target_pairs={{0,4},{2,6},{12,8},{14,10},{16,20},{18,22},{28,24},{30,26}} | collective-permute-start | bytes 1572872 | tf_op jit(solution)/shard_map/ppermute | solution.py:128
  162.5 13.6 %collective-permute-start.43 = (f32[256,512]{1,0:T(8,128)S(1)}, f32[256,512]{1,0:T(8,128)S(1)}, u32[]{:S(2)}, u32[]{:S(2)}) collective-permute-start(f32[256,512]{1,0:T(8,128)S(1)} %select_add_fusion.1), channel_id=1, source_target_pairs={{0,4},{2,6},{12,8},{14,10},{16,20},{18,22},{28,24},{30,26}} | collective-permute-start | bytes 1572872 | tf_op jit(solution)/shard_map/ppermute | solution.py:128
  167.1 14.6 %collective-permute-start.49 = (f32[256,512]{1,0:T(8,128)S(1)}, f32[256,512]{1,0:T(8,128)S(1)}, u32[]{:S(2)}, u32[]{:S(2)}) collective-permute-start(f32[256,512]{1,0:T(8,128)S(1)} %select_add_fusion), channel_id=1, source_target_pairs={{0,4},{2,6},{12,8},{14,10},{16,20},{18,22},{28,24},{30,26}} | collective-permute-start | bytes 1572872 | tf_op jit(solution)/shard_map/ppermute | solution.py:128
  182.5 13.3 %collective-permute-start.33 = (f32[256,512]{1,0:T(8,128)S(1)}, f32[256,512]{1,0:T(8,128)S(1)}, u32[]{:S(2)}, u32[]{:S(2)}) collective-permute-start(f32[256,512]{1,0:T(8,128)S(1)} %add.114), channel_id=1, source_target_pairs={{8,12},{10,14},{4,0},{6,2},{24,28},{26,30},{20,16},{22,18}} | collective-permute-start | bytes 1572872 | tf_op jit(solution)/shard_map/ppermute | solution.py:128
  183.9 17.5 %collective-permute-start.39 = (f32[256,512]{1,0:T(8,128)S(1)}, f32[256,512]{1,0:T(8,128)S(1)}, u32[]{:S(2)}, u32[]{:S(2)}) collective-permute-start(f32[256,512]{1,0:T(8,128)S(1)} %add.121), channel_id=1, source_target_pairs={{8,12},{10,14},{4,0},{6,2},{24,28},{26,30},{20,16},{22,18}} | collective-permute-start | bytes 1572872 | tf_op jit(solution)/shard_map/ppermute | solution.py:128
  185.3 21.7 %collective-permute-start.45 = (f32[256,512]{1,0:T(8,128)S(1)}, f32[256,512]{1,0:T(8,128)S(1)}, u32[]{:S(2)}, u32[]{:S(2)}) collective-permute-start(f32[256,512]{1,0:T(8,128)S(1)} %add.128), channel_id=1, source_target_pairs={{8,12},{10,14},{4,0},{6,2},{24,28},{26,30},{20,16},{22,18}} | collective-permute-start | bytes 1572872 | tf_op jit(solution)/shard_map/ppermute | solution.py:128
  186.7 25.9 %collective-permute-start.51 = (f32[256,512]{1,0:T(8,128)S(1)}, f32[256,512]{1,0:T(8,128)S(1)}, u32[]{:S(2)}, u32[]{:S(2)}) collective-permute-start(f32[256,512]{1,0:T(8,128)S(1)} %add.135), channel_id=1, source_target_pairs={{8,12},{10,14},{4,0},{6,2},{24,28},{26,30},{20,16},{22,18}} | collective-permute-start | bytes 1572872 | tf_op jit(solution)/shard_map/ppermute | solution.py:128
  195.9 62.0 %collective-permute-start.52 = (f32[256,512]{1,0:T(8,128)S(1)}, f32[256,512]{1,0:T(8,128)S(1)}, u32[]{:S(2)}, u32[]{:S(2)}) collective-permute-start(f32[256,512]{1,0:T(8,128)S(1)} %add_add_fusion.3.refs_8_), channel_id=1, source_target_pairs={{2,0},{6,4},{10,8},{14,12},{18,16},{22,20},{26,24},{30,28}} | collective-permute-start | bytes 1572872 | tf_op jit(solution)/shard_map/ppermute | solution.py:128
  201.6 56.4 %collective-permute-start.53 = (f32[256,512]{1,0:T(8,128)S(1)}, f32[256,512]{1,0:T(8,128)S(1)}, u32[]{:S(2)}, u32[]{:S(2)}) collective-permute-start(f32[256,512]{1,0:T(8,128)S(1)} %add_add_fusion.2.refs_9_), channel_id=1, source_target_pairs={{2,0},{6,4},{10,8},{14,12},{18,16},{22,20},{26,24},{30,28}} | collective-permute-start | bytes 1572872 | tf_op jit(solution)/shard_map/ppermute | solution.py:128
  207.2 50.8 %collective-permute-start.54 = (f32[256,512]{1,0:T(8,128)S(1)}, f32[256,512]{1,0:T(8,128)}, u32[]{:S(2)}, u32[]{:S(2)}) collective-permute-start(f32[256,512]{1,0:T(8,128)S(1)} %add_add_fusion.1.refs_10_), channel_id=1, source_target_pairs={{2,0},{6,4},{10,8},{14,12},{18,16},{22,20},{26,24},{30,28}} | collective-permute-start | bytes 1572872 | tf_op jit(solution)/shard_map/ppermute | solution.py:128
  212.8 45.2 %collective-permute-start.55 = (f32[256,512]{1,0:T(8,128)S(1)}, f32[256,512]{1,0:T(8,128)}, u32[]{:S(2)}, u32[]{:S(2)}) collective-permute-start(f32[256,512]{1,0:T(8,128)S(1)} %add_add_fusion.refs_11_), channel_id=1, source_target_pairs={{2,0},{6,4},{10,8},{14,12},{18,16},{22,20},{26,24},{30,28}} | collective-permute-start | bytes 1572872 | tf_op jit(solution)/shard_map/ppermute | solution.py:128
  (38 other events, 643.9 us)

commit v2 on v0

v2 whole, which is shorter than its diff:
```python
import functools
import math

import jax
import jax.numpy as jnp
from jax import lax
from jax.experimental import pallas as pl
from jax.experimental.pallas import tpu as pltpu
from jax.sharding import PartitionSpec as P

DW = 4096
ROWS = 256
BLOCK = 256
WIDE = 512
PAIRS = 2
COUNT = 2 * PAIRS
VMEM_LIMIT = 32 * 1024 * 1024
NT = (((1,), (1,)), ((), ()))


def params():
    return pltpu.CompilerParams(vmem_limit_bytes=VMEM_LIMIT)


def cost(flops, moved):
    return pl.CostEstimate(flops=flops, bytes_accessed=moved, transcendentals=0)


def strip_inverse(ref, rows):
    width = ref.shape[1]
    total = None
    for t in range(0, width, 128):
        v = ref[rows, t : t + 128].astype(jnp.float32)
        total = v * v if total is None else total + v * v
    return 1.0 / jnp.sqrt(jnp.sum(total, axis=1, keepdims=True) + 1e-06)


def head_kernel(decoder_ref, *chunk_refs):
    step = chunk_refs[0].shape[1]
    rows = slice(0, decoder_ref.shape[0])
    inverse = strip_inverse(decoder_ref, rows)
    for k, ref in enumerate(chunk_refs):
        for t in range(0, step, 128):
            v = decoder_ref[rows, k * step + t : k * step + t + 128].astype(jnp.float32)
            ref[rows, t : t + 128] = (v * inverse).astype(jnp.bfloat16)


def units_kernel(decoder_ref, units_ref, inverse_ref):
    strip = 64

    def body(s, carry):
        rows = pl.ds(pl.multiple_of(s * strip, strip), strip)
        inverse = strip_inverse(decoder_ref, rows)
        inverse_ref[rows, :] = jnp.broadcast_to(inverse, (strip, 128))
        for t in range(0, decoder_ref.shape[1], 128):
            v = decoder_ref[rows, t : t + 128].astype(jnp.float32)
            units_ref[rows, t : t + 128] = (v * inverse).astype(jnp.bfloat16)
        return carry

    lax.fori_loop(0, decoder_ref.shape[0] // strip, body, 0)


def pair_cosines(units_ref, low_ref, high_ref):
    step = low_ref.shape[1]
    low = lax.dot_general(
        units_ref[:, :step], low_ref[...], NT, preferred_element_type=jnp.float32
    )
    high = lax.dot_general(
        units_ref[:, step:], high_ref[...], NT, preferred_element_type=jnp.float32
    )
    return low + high


def partial_kernel(units_ref, low_ref, high_ref, out_ref):
    out_ref[...] = pair_cosines(units_ref, low_ref, high_ref)


def weight_kernel(
    delta_ref, units_ref, low_ref, high_ref, partial_ref, col_ref, row_ref, along_ref, penalty_ref
):
    size = units_ref.shape[0]
    j = pl.program_id(0)
    cosines = partial_ref[...] + pair_cosines(units_ref, low_ref, high_ref)
    latents = lax.broadcasted_iota(jnp.int32, (size, ROWS), 0) + (delta_ref[0] + j * size)
    rows = lax.broadcasted_iota(jnp.int32, (size, ROWS), 1)
    inside = (latents >= 0) & (latents < ROWS)
    weight = jnp.where(latents == rows, 0.0, jnp.where(inside, 0.5, 1.0))
    products = weight * cosines
    weighted = products.astype(jnp.bfloat16)
    col_ref[...] = weighted
    row_ref[...] = products.T.astype(jnp.bfloat16)
    along = jnp.sum(weighted.astype(jnp.float32) * cosines, axis=1, keepdims=True)
    along_ref[...] = jnp.broadcast_to(along, along_ref.shape)

    @pl.when(j == 0)
    def _():
        penalty_ref[...] = jnp.zeros_like(penalty_ref)

    squares = products * cosines
    squares = squares[:, :128] + squares[:, 128:]
    penalty_ref[...] += jnp.sum(squares.reshape(size // 8, 8, 128), axis=0)


def row_kernel(row_ref, units_ref, out_ref):
    out_ref[...] = jnp.dot(row_ref[...], units_ref[...], preferred_element_type=jnp.float32)


def finish_kernel(col_ref, decoder_ref, inverse_ref, along_ref, *refs):
    chunks, out_ref = refs[:COUNT], refs[-1]
    step = chunks[0].shape[1]
    inverse = inverse_ref[:, :1]
    scale = (2.0 * math.sqrt(DW)) * inverse
    back = scale * (along_ref[:, :1] * inverse)
    for k in range(COUNT):
        span = slice(k * step, (k + 1) * step)
        part = jnp.dot(col_ref[...], chunks[k][...], preferred_element_type=jnp.float32)
        out_ref[:, span] = scale * part - back * decoder_ref[:, span].astype(jnp.float32)


def last_kernel(owner_ref, col_ref, decoder_ref, inverse_ref, *refs):
    chunks, sums = refs[:COUNT], refs[COUNT : 2 * COUNT]
    out_ref, column = refs[-2:]
    step = chunks[0].shape[1]
    owner = owner_ref[0] == 1
    total = jnp.zeros((col_ref.shape[0], 128), jnp.float32)
    for k in range(COUNT):
        span = slice(k * step, (k + 1) * step)
        part = jnp.dot(col_ref[...], chunks[k][...], preferred_element_type=jnp.float32)
        part = part + jnp.where(owner, sums[k][...], 0.0)
        column[:, span] = part
        along = part * decoder_ref[:, span].astype(jnp.float32)
        for t in range(0, step, 128):
            total = total + along[:, t : t + 128]
    inverse = inverse_ref[:, :1]
    scale = (2.0 * math.sqrt(DW)) * inverse
    back = scale * (jnp.sum(total, axis=1, keepdims=True) * inverse * inverse)
    for k in range(COUNT):
        span = slice(k * step, (k + 1) * step)
        out_ref[:, span] = scale * column[:, span] - back * decoder_ref[:, span].astype(
            jnp.float32
        )


def on_device(decoder, quarter):
    shard, width = decoder.shape
    devices = lax.axis_size("row")
    index = lax.axis_index("row")
    per = devices // 4
    latents = shard * devices
    blocks = shard // BLOCK
    wide = min(WIDE, shard)
    step = width // COUNT
    chosen_quarter = quarter[0]
    start = chosen_quarter * (latents // 4)
    place = index // per
    within = index % per
    here = place == chosen_quarter
    even_chip = (within // 2) % 2 == 0
    odd_core = (within % 2) == 1
    smem = pl.BlockSpec(memory_space=pltpu.SMEM)

    def send(value, pairs):
        return lax.ppermute(value, "row", pairs)

    def hop(level):
        moves = (((0, 1), (3, 2)), ((1, 2), (2, 1)), ((2, 3), (1, 0)))[level]
        return [(a * per + w, b * per + w) for a, b in moves for w in (0, 2)]

    def each(moves):
        return [(z * per + a, z * per + b) for z in range(4) for a, b in moves]

    own = pl.pallas_call(
        head_kernel,
        grid=(4,),
        in_specs=[pl.BlockSpec((ROWS // 4, width), lambda i: (i, 0))],
        out_specs=[pl.BlockSpec((ROWS // 4, step), lambda i: (i, 0))] * COUNT,
        out_shape=[jax.ShapeDtypeStruct((ROWS, step), jnp.bfloat16)] * COUNT,
        compiler_params=params(),
        cost_estimate=cost(4 * ROWS * width, 4 * ROWS * width),
        name="head_units",
    )(decoder)

    units, inverse = pl.pallas_call(
        units_kernel,
        grid=(blocks,),
        in_specs=[pl.BlockSpec((BLOCK, width), lambda i: (i, 0))],
        out_specs=[
            pl.BlockSpec((BLOCK, width), lambda i: (i, 0)),
            pl.BlockSpec((BLOCK, 128), lambda i: (i, 0)),
        ],
        out_shape=[
            jax.ShapeDtypeStruct((shard, width), jnp.bfloat16),
            jax.ShapeDtypeStruct((shard, 128), jnp.float32),
        ],
        compiler_params=params(),
        cost_estimate=cost(4 * shard * width, 4 * shard * width),
        name="units",
    )(decoder)

    near = jnp.where(place == 1, chosen_quarter == 0, chosen_quarter == 3)
    middle = (place == 1) | (place == 2)
    takes = (within == 2) & (inverse[0, 0] > 0)
    mine, first, second, third, held = ([None] * PAIRS for _ in range(5))
    for k in range(PAIRS):
        across = send(own[2 * k + 1], each([(0, 2)]))
        mine[k] = jnp.where(takes, across, own[2 * k])
        first[k] = send(mine[k], hop(0))
        second[k] = send(jnp.where(here, mine[k], first[k]), hop(1))
        third[k] = send(jnp.where(here, mine[k], second[k]), hop(2))
        inner = jnp.where(near, first[k], second[k])
        held[k] = jnp.where(here, mine[k], jnp.where(middle, inner, third[k]))
    chosen = []
    for k in range(PAIRS):
        other = send(held[k], each([(0, 2), (2, 0)]))
        core_held = send(held[k], each([(0, 1), (2, 3)]))
        core_other = send(other, each([(0, 1), (2, 3)]))
        one = jnp.where(odd_core, core_held, held[k])
        two = jnp.where(odd_core, core_other, other)
        pair = [jnp.where(even_chip, one, two), jnp.where(even_chip, two, one)]
        far = 4
        while far < per:
            moves = each([(w, w + far) for w in range(far)])
            fresh = (within >= far) & (within < 2 * far)
            pair = [jnp.where(fresh, send(value, moves), value) for value in pair]
            far *= 2
        chosen += pair

    delta = jnp.reshape(index * shard - start, (1,)).astype(jnp.int32)
    whole_chunk = pl.BlockSpec((ROWS, step), lambda i: (0, 0))
    half_flops = ROWS * shard * width
    partial = None
    for k in range(PAIRS):
        unit_spec = pl.BlockSpec((wide, 2 * step), lambda i, k=k: (i, k))
        wide_spec = pl.BlockSpec((wide, ROWS), lambda i: (i, 0))
        if k < PAIRS - 1:
            partial = pl.pallas_call(
                partial_kernel,
                grid=(shard // wide,),
                in_specs=[unit_spec, whole_chunk, whole_chunk],
                out_specs=wide_spec,
                out_shape=jax.ShapeDtypeStruct((shard, ROWS), jnp.float32),
                compiler_params=params(),
                cost_estimate=cost(half_flops, shard * width),
                name="part_cosines",
            )(units, chosen[2 * k], chosen[2 * k + 1])
            continue
        by_col, by_row, along, local_penalty = pl.pallas_call(
            weight_kernel,
            grid=(shard // wide,),
            in_specs=[smem, unit_spec, whole_chunk, whole_chunk, wide_spec],
            out_specs=[
                wide_spec,
                pl.BlockSpec((ROWS, wide), lambda i: (0, i)),
                pl.BlockSpec((wide, 128), lambda i: (i, 0)),
                pl.BlockSpec((8, 128), lambda i: (0, 0)),
            ],
            out_shape=[
                jax.ShapeDtypeStruct((shard, ROWS), jnp.bfloat16),
                jax.ShapeDtypeStruct((ROWS, shard), jnp.bfloat16),
                jax.ShapeDtypeStruct((shard, 128), jnp.float32),
                jax.ShapeDtypeStruct((8, 128), jnp.float32),
            ],
            compiler_params=params(),
            cost_estimate=cost(half_flops, shard * width),
            name="weights",
        )(delta, units, chosen[2 * k], chosen[2 * k + 1], partial)

    sums = [None] * COUNT
    for k in range(PAIRS):
        value = pl.pallas_call(
            row_kernel,
            grid=(4,),
            in_specs=[
                pl.BlockSpec((ROWS, shard), lambda i: (0, 0)),
                pl.BlockSpec((shard, step // 2), lambda i, k=k: (0, 4 * k + i)),
            ],
            out_specs=pl.BlockSpec((ROWS, step // 2), lambda i: (0, i)),
            out_shape=jax.ShapeDtypeStruct((ROWS, 2 * step), jnp.float32),
            compiler_params=params(),
            cost_estimate=cost(half_flops, shard * width),
            name="row_part",
        )(by_row, units)
        far = per // 2
        while far >= 4:
            value = value + send(value, each([(w + far, w) for w in range(far)]))
            far //= 2
        value = value + send(value, each([(1, 0), (3, 2)]))
        low, high = value[:, :step], value[:, step:]
        away = jnp.where(even_chip, high, low)
        kept = jnp.where(even_chip, low, high)
        kept = kept + send(away, each([(0, 2), (2, 0)]))
        first_sum = send(kept, hop(0))
        second_sum = send(kept + first_sum, hop(1))
        third_sum = send(kept + second_sum, hop(2))
        total = kept + first_sum + second_sum + third_sum
        sums[2 * k] = total
        sums[2 * k + 1] = send(total, each([(2, 0)]))

    penalties = local_penalty
    far = 1
    while far < devices:
        swap = [(i, i ^ far) for i in range(devices)]
        penalties = penalties + send(penalties, swap)
        far *= 2
    penalty = jnp.sum(penalties) * (DW / (ROWS * latents))

    out_type = jax.ShapeDtypeStruct((shard, width), jnp.float32)
    any_spec = pl.BlockSpec(memory_space=pl.ANY)
    grad = None
    bounds = [1, 1 + (blocks - 1) // 2, blocks] if blocks > 2 else [1, blocks]
    for low, high in zip(bounds[:-1], bounds[1:]):
        if high == low:
            continue
        operands = [by_col, decoder, inverse, along, *chosen]
        specs = [
            pl.BlockSpec((BLOCK, ROWS), lambda i, low=low: (i + low, 0)),
            pl.BlockSpec((BLOCK, width), lambda i, low=low: (i + low, 0)),
            pl.BlockSpec((BLOCK, 128), lambda i, low=low: (i + low, 0)),
            pl.BlockSpec((BLOCK, 128), lambda i, low=low: (i + low, 0)),
        ] + [whole_chunk] * COUNT
        aliases = {}
        if grad is not None:
            aliases = {len(operands): 0}
            operands.append(grad)
            specs.append(any_spec)
        rows = (high - low) * BLOCK
        grad = pl.pallas_call(
            finish_kernel,
            grid=(high - low,),
            in_specs=specs,
            out_specs=pl.BlockSpec((BLOCK, width), lambda i, low=low: (i + low, 0)),
            out_shape=out_type,
            input_output_aliases=aliases,
            compiler_params=params(),
            cost_estimate=cost(2 * ROWS * rows * width, 6 * rows * width),
            name="finish",
        )(*operands)

    owner = jnp.reshape(here & (within == 0), (1,)).astype(jnp.int32)
    narrow = BLOCK // 2
    operands = [owner, by_col, decoder, inverse, *chosen, *sums]
    specs = [
        smem,
        pl.BlockSpec((narrow, ROWS), lambda i: (i, 0)),
        pl.BlockSpec((narrow, width), lambda i: (i, 0)),
        pl.BlockSpec((narrow, 128), lambda i: (i, 0)),
    ]
    specs += [whole_chunk] * COUNT
    specs += [pl.BlockSpec((narrow, step), lambda i: (i, 0))] * COUNT
    aliases = {}
    if grad is not None:
        aliases = {len(operands): 0}
        operands.append(grad)
        specs.append(any_spec)
    decoder_grad = pl.pallas_call(
        last_kernel,
        grid=(2,),
        in_specs=specs,
        out_specs=pl.BlockSpec((narrow, width), lambda i: (i, 0)),
        out_shape=out_type,
        scratch_shapes=[pltpu.VMEM((narrow, width), jnp.float32)],
        input_output_aliases=aliases,
        compiler_params=params(),
        name="finish_rows",
    )(*operands)

    return (jnp.reshape(penalty, (1,)), decoder_grad)


def solution(mesh):
    in_specs = (P(("groups", "row"), None), P("groups"))
    out_specs = (P("groups"), P(("groups", "row"), None))
    return jax.shard_map(
        on_device, mesh=mesh, in_specs=in_specs, out_specs=out_specs, check_vma=False
    )
```

time: 359 us -> 255 us (0.71)
  waiting for transfers between devices: 193 us -> 99.1 us
  matrix products: 55.5 us -> 0 us
  starting transfers between devices: 0.12 us -> 50.3 us
  Pallas kernels: 0 us -> 48.2 us
  other arithmetic: 47.6 us -> 15.2 us
  blocking collectives: 30.8 us -> 0 us
  local copies, waits for them, and re-layouts: 15.6 us -> 37 us
  between operations: 16.3 us -> 4.24 us
    psum x1 -> x0, waiting for transfers between devices: 101 us -> none  [from_root(): return lax.psum(kept, axis)]
    ppermute x0 -> x30, waiting for transfers between devices: none -> 99.1 us  [send(): return lax.ppermute(value, 'row', pairs)]
    reduce_scatter x1 -> x0, waiting for transfers between devices: 72 us -> none  [on_device(): reduced = lax.psum_scatter(row_part, 'row', scatter_dimension=0, tiled=True)]
    dot_general x3 -> x0, matrix products: 55.5 us -> none  [the longest x1 35.1 us: on_device(): jnp.dot(weighted.T, received, preferred_element_type=jnp.float32)]
    ppermute x0 -> x30, starting transfers between devices: none -> 50.3 us  [send(): return lax.ppermute(value, 'row', pairs)]
    pallas_call x0 -> x9, Pallas kernels: none -> 48.2 us  [the longest x2 12.7 us: on_device(): pl.pallas_call(finish_kernel, grid=(high - low,), in_specs=specs, out_spe...]
    unnamed x10 -> x30, local copies, waits for them, and re-layouts: 3.19 us -> 36.5 us
    psum x1 -> x0, blocking collectives: 30.8 us -> none  [on_device(): total_penalty = lax.psum(local_penalty, 'row')]
  transfers between devices with their start and end apart: 3 -> 30, of which waited for: 3 -> 15; matrix products, arithmetic and copies ran while one was open for 0% -> 6% of each run, Pallas kernels for 0% -> 12%
where the time goes in v2:
time: 255 us; the launch traced here: 254 us
  waiting for transfers between devices  99.1 us (39%)
  starting transfers between devices  50.3 us (20%)
  Pallas kernels  48.2 us (19%)
  local copies, waits for them, and re-layouts  37 us (15%)
  other arithmetic  15.2 us (6%)
  between operations  4.24 us (2%)
    ppermute x30, waiting for transfers between devices, send(): return lax.ppermute(value, 'row', pairs)  99.1 us
    ppermute x30, starting transfers between devices, send(): return lax.ppermute(value, 'row', pairs)  50.3 us
    unnamed x30, local copies, waits for them, and re-layouts  36.5 us
    pallas_call x2, Pallas kernels, on_device(): pl.pallas_call(finish_kernel, grid=(high - low,), in_specs=specs, out_spe...  12.7 us
    pallas_call x1, Pallas kernels, on_device(): pl.pallas_call(units_kernel, grid=(blocks,), in_specs=[pl.BlockSpec((BLOC...  11.7 us
    pallas_call x2, Pallas kernels, on_device(): pl.pallas_call(row_kernel, grid=(4,), in_specs=[pl.BlockSpec((ROWS, shard...  7.53 us
    pallas_call x1, Pallas kernels, on_device(): pl.pallas_call(weight_kernel, grid=(shard // wide,), in_specs=[smem, unit...  6.48 us
    pallas_call x1, Pallas kernels, on_device(): pl.pallas_call(last_kernel, grid=(2,), in_specs=specs, out_specs=pl.Block...  5.19 us
  transfers between devices with their start and end apart: 30, of which 15 were waited for; matrix products, arithmetic and copies ran while one was open for 6% of the time, Pallas kernels for 12%

profile of v2, /device:TPU:0, one launch (start us, length us, event | category | flops | bytes accessed | tf_op | source)
XLA Modules:
  0.0 254.1 jit_solution(6026750220168826995)
XLA Ops:
  0.6 5.8 %copy-done = bf16[2048,4096]{1,0:T(8,128)(2,1)S(1)} copy-done((bf16[2048,4096]{1,0:T(8,128)(2,1)S(1)}, bf16[2048,4096]{1,0:T(8,128)(2,1)}, u32[]{:S(2)}) %copy-start) | copy-done | bytes 16777240
  7.4 5.7 %collective-permute-start.7 = (bf16[256,1024]{1,0:T(8,128)(2,1)S(1)}, bf16[256,1024]{1,0:T(8,128)(2,1)}, u32[]{:S(2)}, u32[]{:S(2)}) collective-permute-start(bf16[256,1024]{1,0:T(8,128)(2,1)S(1)} %get-tuple-element.16), channel_id=1, source_target_pairs={{0,2},{4,6},{8,10},{12,14},{16,18},{20,22},{24,26},{28,30}} | collective-permute-start | bytes 1572872 | tf_op jit(solution)/shard_map/ppermute | solution.py:163
  15.2 11.7 %units.1 = (bf16[2048,4096]{1,0:T(8,128)(2,1)S(1)}, f32[2048,128]{1,0:T(8,128)S(1)}) custom-call(bf16[2048,4096]{1,0:T(8,128)(2,1)} %decoder_ref.9), custom_call_target="tpu_custom_call" | custom-call | flops 33554432 | bytes 33554432 | tf_op jit(solution)/shard_map/units/pallas_call | solution.py:183
  27.0 6.2 %copy-done.2 = bf16[2048,4096]{1,0:T(8,128)(2,1)} copy-done((bf16[2048,4096]{1,0:T(8,128)(2,1)}, bf16[2048,4096]{1,0:T(8,128)(2,1)S(1)}, u32[]{:S(2)}) %copy-start.2) | copy-done | bytes 16777240
  34.4 4.3 %collective-permute-start.8 = (bf16[256,1024]{1,0:T(8,128)(2,1)S(1)}, bf16[256,1024]{1,0:T(8,128)(2,1)}, u32[]{:S(2)}, u32[]{:S(2)}) collective-permute-start(bf16[256,1024]{1,0:T(8,128)(2,1)S(1)} %broadcast_select_fusion), channel_id=1, source_target_pairs={{0,4},{2,6},{12,8},{14,10},{16,20},{18,22},{28,24},{30,26}} | collective-permute-start | bytes 1572872 | tf_op jit(solution)/shard_map/ppermute | solution.py:163
  40.7 3.8 %collective-permute-done.8 = bf16[256,1024]{1,0:T(8,128)(2,1)} collective-permute-done((bf16[256,1024]{1,0:T(8,128)(2,1)S(1)}, bf16[256,1024]{1,0:T(8,128)(2,1)}, u32[]{:S(2)}, u32[]{:S(2)}) %collective-permute-start.8) | collective-permute-done | bytes 524320 | tf_op jit(solution)/shard_map/ppermute | solution.py:163
  46.3 3.8 %collective-permute-done.1 = bf16[256,1024]{1,0:T(8,128)(2,1)S(1)} collective-permute-done((bf16[256,1024]{1,0:T(8,128)(2,1)S(1)}, bf16[256,1024]{1,0:T(8,128)(2,1)S(1)}, u32[]{:S(2)}, u32[]{:S(2)}) %collective-permute-start.1) | collective-permute-done | bytes 524320 | tf_op jit(solution)/shard_map/ppermute | solution.py:163
  55.4 13.6 %collective-permute-done.10 = bf16[256,1024]{1,0:T(8,128)(2,1)} collective-permute-done((bf16[256,1024]{1,0:T(8,128)(2,1)}, bf16[256,1024]{1,0:T(8,128)(2,1)}, u32[]{:S(2)}, u32[]{:S(2)}) %collective-permute-start.10) | collective-permute-done | bytes 524320 | tf_op jit(solution)/shard_map/ppermute | solution.py:163
  69.0 2.1 select_select_fusion
  76.5 2.4 collective-permute-start.5
  80.2 2.2 collective-permute-done.12
  85.8 2.2 collective-permute-done.5
  92.2 5.8 %copy-done.3 = bf16[2048,4096]{1,0:T(8,128)(2,1)S(1)} copy-done((bf16[2048,4096]{1,0:T(8,128)(2,1)S(1)}, bf16[2048,4096]{1,0:T(8,128)(2,1)}, u32[]{:S(2)}) %copy-start.3) | copy-done | bytes 16777240
  98.0 3.6 %part_cosines.1.partial_ref = f32[2048,256]{1,0:T(8,128)S(1)} custom-call(bf16[2048,4096]{1,0:T(8,128)(2,1)S(1)} %copy-done.3, bf16[256,1024]{1,0:T(8,128)(2,1)S(1)} %get-tuple-element.23.low_ref.refs_0_, bf16[256,1024]{1,0:T(8,128)(2,1)S(1)} %get-tuple-element.22.high_ref.refs_1_), custom_call_target="tpu_custom_call" | custom-call | flops 2147483648 | bytes 8388608 | tf_op jit(solution)/shard_map/part_cosines/pallas_call | solution.py:236
  103.7 6.5 %weights.1 = (bf16[2048,256]{1,0:T(8,128)(2,1)S(1)}, bf16[256,2048]{1,0:T(8,128)(2,1)S(1)}, f32[2048,128]{1,0:T(8,128)S(1)}, f32[8,128]{1,0:T(8,128)S(1)}) custom-call(s32[1]{0:T(128)} %bitcast.1.delta_ref, bf16[2048,4096]{1,0:T(8,128)(2,1)} %copy-done.2, bf16[256,1024]{1,0:T(8,128)(2,1)S(1)} %get-tuple-element.25.low_ref.refs_2_, ...), custom_call_target="tpu_custom_call" | custom-call | flops 2147483648 | bytes 8388608 | tf_op jit(solution)/shard_map/weights/pallas_call | solution.py:247
  112.2 5.8 %copy-done.4 = bf16[2048,4096]{1,0:T(8,128)(2,1)S(1)} copy-done((bf16[2048,4096]{1,0:T(8,128)(2,1)S(1)}, bf16[2048,4096]{1,0:T(8,128)(2,1)}, u32[]{:S(2)}) %copy-start.4) | copy-done | bytes 16777240
  118.0 3.7 %row_part.2 = f32[256,2048]{1,0:T(8,128)S(1)} custom-call(bf16[256,2048]{1,0:T(8,128)(2,1)S(1)} %get-tuple-element.20.row_ref, bf16[2048,4096]{1,0:T(8,128)(2,1)S(1)} %copy-done.4), custom_call_target="tpu_custom_call" | custom-call | flops 2147483648 | bytes 8388608 | tf_op jit(solution)/shard_map/row_part/pallas_call | solution.py:270
  123.0 3.8 %row_part.3 = f32[256,2048]{1,0:T(8,128)S(1)} custom-call(bf16[256,2048]{1,0:T(8,128)(2,1)S(1)} %get-tuple-element.20.row_ref, bf16[2048,4096]{1,0:T(8,128)(2,1)S(1)} %copy-done.4), custom_call_target="tpu_custom_call" | custom-call | flops 2147483648 | bytes 8388608 | tf_op jit(solution)/shard_map/row_part/pallas_call | solution.py:270
  128.6 2.2 collective-permute-start.19
  130.8 2.2 collective-permute-done.24
  133.5 2.2 collective-permute-start.25
  135.7 9.6 %collective-permute-done.19 = f32[256,1024]{1,0:T(8,128)S(1)} collective-permute-done((f32[256,1024]{1,0:T(8,128)S(1)}, f32[256,1024]{1,0:T(8,128)S(1)}, u32[]{:S(2)}, u32[]{:S(2)}) %collective-permute-start.19) | collective-permute-done | bytes 1048608 | tf_op jit(solution)/shard_map/ppermute | solution.py:163
  147.0 9.6 %collective-permute-done.25 = f32[256,1024]{1,0:T(8,128)S(1)} collective-permute-done((f32[256,1024]{1,0:T(8,128)S(1)}, f32[256,1024]{1,0:T(8,128)S(1)}, u32[]{:S(2)}, u32[]{:S(2)}) %collective-permute-start.25) | collective-permute-done | bytes 1048608 | tf_op jit(solution)/shard_map/ppermute | solution.py:163
  160.2 10.3 %collective-permute-done.26 = f32[256,1024]{1,0:T(8,128)S(1)} collective-permute-done((f32[256,1024]{1,0:T(8,128)S(1)}, f32[256,1024]{1,0:T(8,128)S(1)}, u32[]{:S(2)}, u32[]{:S(2)}) %collective-permute-start.26) | collective-permute-done | bytes 1048608 | tf_op jit(solution)/shard_map/ppermute | solution.py:163
  174.4 18.4 %collective-permute-done.22 = f32[256,1024]{1,0:T(8,128)S(1)} collective-permute-done((f32[256,1024]{1,0:T(8,128)S(1)}, f32[256,1024]{1,0:T(8,128)S(1)}, u32[]{:S(2)}, u32[]{:S(2)}) %collective-permute-start.22) | collective-permute-done | bytes 1048608 | tf_op jit(solution)/shard_map/ppermute | solution.py:163
  195.4 8.7 %collective-permute-done.28 = f32[256,1024]{1,0:T(8,128)S(1)} collective-permute-done((f32[256,1024]{1,0:T(8,128)S(1)}, f32[256,1024]{1,0:T(8,128)S(1)}, u32[]{:S(2)}, u32[]{:S(2)}) %collective-permute-start.28) | collective-permute-done | bytes 1048608 | tf_op jit(solution)/shard_map/ppermute | solution.py:163
  208.0 3.4 %collective-permute-start.15 = (f32[8,128]{1,0:T(8,128)S(1)}, f32[8,128]{1,0:T(8,128)S(1)}, u32[]{:S(2)}, u32[]{:S(2)}) collective-permute-start(f32[8,128]{1,0:T(8,128)S(1)} %add.65), channel_id=1, source_target_pairs={{0,2},{1,3},{2,0},{3,1},{4,6},{5,7},{6,4},{7,5},{8,10},{9,11},{10,... | collective-permute-start | bytes 12296 | tf_op jit(solution)/shard_map/ppermute | solution.py:163
  211.4 10.9 %collective-permute-done.15 = f32[8,128]{1,0:T(8,128)S(1)} collective-permute-done((f32[8,128]{1,0:T(8,128)S(1)}, f32[8,128]{1,0:T(8,128)S(1)}, u32[]{:S(2)}, u32[]{:S(2)}) %collective-permute-start.15) | collective-permute-done | bytes 4128 | tf_op jit(solution)/shard_map/ppermute | solution.py:163
  222.4 5.8 %copy-done.1 = bf16[2048,4096]{1,0:T(8,128)(2,1)S(1)} copy-done((bf16[2048,4096]{1,0:T(8,128)(2,1)S(1)}, bf16[2048,4096]{1,0:T(8,128)(2,1)}, u32[]{:S(2)}) %copy-start.1) | copy-done | bytes 16777240
  230.6 5.6 %finish.2.refs_4_ = f32[2048,4096]{1,0:T(8,128)} custom-call(bf16[2048,256]{1,0:T(8,128)(2,1)S(1)} %copy-done.6, bf16[2048,4096]{1,0:T(8,128)(2,1)S(1)} %copy-done.1, f32[2048,128]{1,0:T(8,128)S(1)} %get-tuple-element.13.inverse_ref, f32[2048,128]{1,0:T(8,128)S(1)} %copy-done.9, bf16[256,1024]{1,0:T(8,128)(2,1)S(1)} %get-tuple-element.23.low_ref.refs_0_, ...), custom_call_target="tpu_custom_call" | custom-call | flops 1610612736 | bytes 18874368 | tf_op jit(solution)/shard_map/finish/pallas_call | solution.py:327
  238.2 7.0 %finish.3.refs_8_ = f32[2048,4096]{1,0:T(8,128)} custom-call(bf16[2048,256]{1,0:T(8,128)(2,1)S(1)} %copy-done.6, bf16[2048,4096]{1,0:T(8,128)(2,1)S(1)} %copy-done.1, f32[2048,128]{1,0:T(8,128)S(1)} %get-tuple-element.13.inverse_ref, f32[2048,128]{1,0:T(8,128)S(1)} %copy-done.9, ...), custom_call_target="tpu_custom_call", output_to_operand_aliasing={{}: (8, {})} | custom-call | flops 2147483648 | bytes 25165824 | tf_op jit(solution)/shard_map/finish/pallas_call | solution.py:327
  247.8 5.2 %finish_rows.1 = f32[2048,4096]{1,0:T(8,128)} custom-call(s32[1]{0:T(128)} %bitcast.4.owner_ref, bf16[2048,256]{1,0:T(8,128)(2,1)S(1)} %copy-done.7, bf16[2048,4096]{1,0:T(8,128)(2,1)} %decoder_ref.9, f32[2048,128]{1,0:T(8,128)S(1)} %get-tuple-element.13.inverse_ref, ...), custom_call_target="tpu_custom_call", output_to_operand_aliasing={{}: (12, {})} | custom-call | tf_op jit(solution)/shard_map/finish_rows/pallas_call | solution.py:355
  (94 shorter events, 56.0 us)
Async XLA Ops:
  7.4 26.8 %collective-permute-start.7 = (bf16[256,1024]{1,0:T(8,128)(2,1)S(1)}, bf16[256,1024]{1,0:T(8,128)(2,1)}, u32[]{:S(2)}, u32[]{:S(2)}) collective-permute-start(bf16[256,1024]{1,0:T(8,128)(2,1)S(1)} %get-tuple-element.16), channel_id=1, source_target_pairs={{0,2},{4,6},{8,10},{12,14},{16,18},{20,22},{24,26},{28,30}} | collective-permute-start | bytes 1572872 | tf_op jit(solution)/shard_map/ppermute | solution.py:163
  13.1 25.6 %collective-permute-start = (bf16[256,1024]{1,0:T(8,128)(2,1)S(1)}, bf16[256,1024]{1,0:T(8,128)(2,1)}, u32[]{:S(2)}, u32[]{:S(2)}) collective-permute-start(bf16[256,1024]{1,0:T(8,128)(2,1)S(1)} %get-tuple-element.14), channel_id=1, source_target_pairs={{0,2},{4,6},{8,10},{12,14},{16,18},{20,22},{24,26},{28,30}} | collective-permute-start | bytes 1572872 | tf_op jit(solution)/shard_map/ppermute | solution.py:163
  34.4 10.2 %collective-permute-start.8 = (bf16[256,1024]{1,0:T(8,128)(2,1)S(1)}, bf16[256,1024]{1,0:T(8,128)(2,1)}, u32[]{:S(2)}, u32[]{:S(2)}) collective-permute-start(bf16[256,1024]{1,0:T(8,128)(2,1)S(1)} %broadcast_select_fusion), channel_id=1, source_target_pairs={{0,4},{2,6},{12,8},{14,10},{16,20},{18,22},{28,24},{30,26}} | collective-permute-start | bytes 1572872 | tf_op jit(solution)/shard_map/ppermute | solution.py:163
  38.7 11.4 %collective-permute-start.1 = (bf16[256,1024]{1,0:T(8,128)(2,1)S(1)}, bf16[256,1024]{1,0:T(8,128)(2,1)S(1)}, u32[]{:S(2)}, u32[]{:S(2)}) collective-permute-start(bf16[256,1024]{1,0:T(8,128)(2,1)S(1)} %broadcast_select_fusion.1), channel_id=1, source_target_pairs={{0,4},{2,6},{12,8},{14,10},{16,20},{18,22},{28,24},{30,26}} | collective-permute-start | bytes 1572872 | tf_op jit(solution)/shard_map/ppermute | solution.py:163
  45.6 5.3 %collective-permute-start.9 = (bf16[256,1024]{1,0:T(8,128)(2,1)S(1)}, bf16[256,1024]{1,0:T(8,128)(2,1)S(1)}, u32[]{:S(2)}, u32[]{:S(2)}) collective-permute-start(bf16[256,1024]{1,0:T(8,128)(2,1)S(1)} %broadcast_select_fusion.3), channel_id=1, source_target_pairs={{4,8},{6,10},{8,4},{10,6},{20,24},{22,26},{24,20},{26,22}} | collective-permute-start | bytes 1572872 | tf_op jit(solution)/shard_map/ppermute | solution.py:163
  50.2 3.0 %collective-permute-start.2 = (bf16[256,1024]{1,0:T(8,128)(2,1)S(1)}, bf16[256,1024]{1,0:T(8,128)(2,1)S(1)}, u32[]{:S(2)}, u32[]{:S(2)}) collective-permute-start(bf16[256,1024]{1,0:T(8,128)(2,1)S(1)} %broadcast_select_fusion.5), channel_id=1, source_target_pairs={{4,8},{6,10},{8,4},{10,6},{20,24},{22,26},{24,20},{26,22}} | collective-permute-start | bytes 1572872 | tf_op jit(solution)/shard_map/ppermute | solution.py:163
  51.9 17.1 %collective-permute-start.10 = (bf16[256,1024]{1,0:T(8,128)(2,1)}, bf16[256,1024]{1,0:T(8,128)(2,1)}, u32[]{:S(2)}, u32[]{:S(2)}) collective-permute-start(bf16[256,1024]{1,0:T(8,128)(2,1)} %broadcast_select_fusion.2), channel_id=1, source_target_pairs={{8,12},{10,14},{4,0},{6,2},{24,28},{26,30},{20,16},{22,18}} | collective-permute-start | bytes 1572872 | tf_op jit(solution)/shard_map/ppermute | solution.py:163
  54.1 20.5 %collective-permute-start.3 = (bf16[256,1024]{1,0:T(8,128)(2,1)}, bf16[256,1024]{1,0:T(8,128)(2,1)}, u32[]{:S(2)}, u32[]{:S(2)}) collective-permute-start(bf16[256,1024]{1,0:T(8,128)(2,1)} %broadcast_select_fusion.4), channel_id=1, source_target_pairs={{8,12},{10,14},{4,0},{6,2},{24,28},{26,30},{20,16},{22,18}} | collective-permute-start | bytes 1572872 | tf_op jit(solution)/shard_map/ppermute | solution.py:163
  71.1 11.3 %collective-permute-start.12 = (bf16[256,1024]{1,0:T(8,128)(2,1)}, bf16[256,1024]{1,0:T(8,128)(2,1)S(1)}, u32[]{:S(2)}, u32[]{:S(2)}) collective-permute-start(bf16[256,1024]{1,0:T(8,128)(2,1)} %select_select_fusion), channel_id=1, source_target_pairs={{0,2},{2,0},{4,6},{6,4},{8,10},{10,8},{12,14},{14,12},{16,18},{18,... | collective-permute-start | bytes 1572872 | tf_op jit(solution)/shard_map/ppermute | solution.py:163
  76.5 11.5 %collective-permute-start.5 = (bf16[256,1024]{1,0:T(8,128)(2,1)}, bf16[256,1024]{1,0:T(8,128)(2,1)S(1)}, u32[]{:S(2)}, u32[]{:S(2)}) collective-permute-start(bf16[256,1024]{1,0:T(8,128)(2,1)} %select_select_fusion.1), channel_id=1, source_target_pairs={{0,2},{2,0},{4,6},{6,4},{8,10},{10,8},{12,14},{14,12},{16,18},{18,... | collective-permute-start | bytes 1572872 | tf_op jit(solution)/shard_map/ppermute | solution.py:163
  78.9 11.2 %collective-permute-start.11 = (bf16[256,1024]{1,0:T(8,128)(2,1)}, bf16[256,1024]{1,0:T(8,128)(2,1)S(1)}, u32[]{:S(2)}, u32[]{:S(2)}) collective-permute-start(bf16[256,1024]{1,0:T(8,128)(2,1)} %select_select_fusion), channel_id=1, source_target_pairs={{0,1},{2,3},{4,5},{6,7},{8,9},{10,11},{12,13},{14,15},{16,17},{18,... | collective-permute-start | bytes 1572872 | tf_op jit(solution)/shard_map/ppermute | solution.py:163
  82.4 7.7 %copy-start.12 = (bf16[256,1024]{1,0:T(8,128)(2,1)}, bf16[256,1024]{1,0:T(8,128)(2,1)S(1)}, u32[]{:S(2)}) copy-start(bf16[256,1024]{1,0:T(8,128)(2,1)S(1)} %collective-permute-done.12) | copy-start | bytes 1572868
  82.4 8.5 %collective-permute-start.13 = (bf16[256,1024]{1,0:T(8,128)(2,1)S(1)}, bf16[256,1024]{1,0:T(8,128)(2,1)}, u32[]{:S(2)}, u32[]{:S(2)}) collective-permute-start(bf16[256,1024]{1,0:T(8,128)(2,1)S(1)} %collective-permute-done.12), channel_id=1, source_target_pairs={{0,1},{2,3},{4,5},{6,7},{8,9},{10,11},{12,13},{14,15},{16,17},{18,... | collective-permute-start | bytes 1572872 | tf_op jit(solution)/shard_map/ppermute | solution.py:163
  84.5 17.1 %collective-permute-start.4 = (bf16[256,1024]{1,0:T(8,128)(2,1)}, bf16[256,1024]{1,0:T(8,128)(2,1)S(1)}, u32[]{:S(2)}, u32[]{:S(2)}) collective-permute-start(bf16[256,1024]{1,0:T(8,128)(2,1)} %select_select_fusion.1), channel_id=1, source_target_pairs={{0,1},{2,3},{4,5},{6,7},{8,9},{10,11},{12,13},{14,15},{16,17},{18,... | collective-permute-start | bytes 1572872 | tf_op jit(solution)/shard_map/ppermute | solution.py:163
  88.0 13.6 %copy-start.11 = (bf16[256,1024]{1,0:T(8,128)(2,1)}, bf16[256,1024]{1,0:T(8,128)(2,1)S(1)}, u32[]{:S(2)}) copy-start(bf16[256,1024]{1,0:T(8,128)(2,1)S(1)} %collective-permute-done.5) | copy-start | bytes 1572868
  88.0 14.4 %collective-permute-start.6 = (bf16[256,1024]{1,0:T(8,128)(2,1)S(1)}, bf16[256,1024]{1,0:T(8,128)(2,1)}, u32[]{:S(2)}, u32[]{:S(2)}) collective-permute-start(bf16[256,1024]{1,0:T(8,128)(2,1)S(1)} %collective-permute-done.5), channel_id=1, source_target_pairs={{0,1},{2,3},{4,5},{6,7},{8,9},{10,11},{12,13},{14,15},{16,17},{18,... | collective-permute-start | bytes 1572872 | tf_op jit(solution)/shard_map/ppermute | solution.py:163
  121.7 6.4 %collective-permute-start.18 = (f32[256,2048]{1,0:T(8,128)S(1)}, f32[256,2048]{1,0:T(8,128)S(1)}, u32[]{:S(2)}, u32[]{:S(2)}) collective-permute-start(f32[256,2048]{1,0:T(8,128)S(1)} %row_part.2), channel_id=1, source_target_pairs={{1,0},{3,2},{5,4},{7,6},{9,8},{11,10},{13,12},{15,14},{17,16},{19,... | collective-permute-start | bytes 6291464 | tf_op jit(solution)/shard_map/ppermute | solution.py:163
  126.8 6.2 %collective-permute-start.24 = (f32[256,2048]{1,0:T(8,128)S(1)}, f32[256,2048]{1,0:T(8,128)S(1)}, u32[]{:S(2)}, u32[]{:S(2)}) collective-permute-start(f32[256,2048]{1,0:T(8,128)S(1)} %row_part.3), channel_id=1, source_target_pairs={{1,0},{3,2},{5,4},{7,6},{9,8},{11,10},{13,12},{15,14},{17,16},{19,... | collective-permute-start | bytes 6291464 | tf_op jit(solution)/shard_map/ppermute | solution.py:163
  128.6 16.7 %collective-permute-start.19 = (f32[256,1024]{1,0:T(8,128)S(1)}, f32[256,1024]{1,0:T(8,128)S(1)}, u32[]{:S(2)}, u32[]{:S(2)}) collective-permute-start(f32[256,1024]{1,0:T(8,128)S(1)} %slice_select_fusion.1), channel_id=1, source_target_pairs={{0,2},{2,0},{4,6},{6,4},{8,10},{10,8},{12,14},{14,12},{16,18},{18,... | collective-permute-start | bytes 3145736 | tf_op jit(solution)/shard_map/ppermute | solution.py:163
  133.5 23.0 %collective-permute-start.25 = (f32[256,1024]{1,0:T(8,128)S(1)}, f32[256,1024]{1,0:T(8,128)S(1)}, u32[]{:S(2)}, u32[]{:S(2)}) collective-permute-start(f32[256,1024]{1,0:T(8,128)S(1)} %slice_select_fusion), channel_id=1, source_target_pairs={{0,2},{2,0},{4,6},{6,4},{8,10},{10,8},{12,14},{14,12},{16,18},{18,... | collective-permute-start | bytes 3145736 | tf_op jit(solution)/shard_map/ppermute | solution.py:163
  145.6 13.6 %collective-permute-start.20 = (f32[256,1024]{1,0:T(8,128)S(1)}, f32[256,1024]{1,0:T(8,128)S(1)}, u32[]{:S(2)}, u32[]{:S(2)}) collective-permute-start(f32[256,1024]{1,0:T(8,128)S(1)} %select_add_fusion.1), channel_id=1, source_target_pairs={{0,4},{2,6},{12,8},{14,10},{16,20},{18,22},{28,24},{30,26}} | collective-permute-start | bytes 3145736 | tf_op jit(solution)/shard_map/ppermute | solution.py:163
  156.9 13.6 %collective-permute-start.26 = (f32[256,1024]{1,0:T(8,128)S(1)}, f32[256,1024]{1,0:T(8,128)S(1)}, u32[]{:S(2)}, u32[]{:S(2)}) collective-permute-start(f32[256,1024]{1,0:T(8,128)S(1)} %select_add_fusion), channel_id=1, source_target_pairs={{0,4},{2,6},{12,8},{14,10},{16,20},{18,22},{28,24},{30,26}} | collective-permute-start | bytes 3145736 | tf_op jit(solution)/shard_map/ppermute | solution.py:163
  159.4 12.0 %collective-permute-start.21 = (f32[256,1024]{1,0:T(8,128)S(1)}, f32[256,1024]{1,0:T(8,128)S(1)}, u32[]{:S(2)}, u32[]{:S(2)}) collective-permute-start(f32[256,1024]{1,0:T(8,128)S(1)} %add.71), channel_id=1, source_target_pairs={{4,8},{6,10},{8,4},{10,6},{20,24},{22,26},{24,20},{26,22}} | collective-permute-start | bytes 3145736 | tf_op jit(solution)/shard_map/ppermute | solution.py:163
  170.7 2.2 collective-permute-start.27
  171.6 21.2 %collective-permute-start.22 = (f32[256,1024]{1,0:T(8,128)S(1)}, f32[256,1024]{1,0:T(8,128)S(1)}, u32[]{:S(2)}, u32[]{:S(2)}) collective-permute-start(f32[256,1024]{1,0:T(8,128)S(1)} %add.73), channel_id=1, source_target_pairs={{8,12},{10,14},{4,0},{6,2},{24,28},{26,30},{20,16},{22,18}} | collective-permute-start | bytes 3145736 | tf_op jit(solution)/shard_map/ppermute | solution.py:163
  173.1 31.0 %collective-permute-start.28 = (f32[256,1024]{1,0:T(8,128)S(1)}, f32[256,1024]{1,0:T(8,128)S(1)}, u32[]{:S(2)}, u32[]{:S(2)}) collective-permute-start(f32[256,1024]{1,0:T(8,128)S(1)} %add.79), channel_id=1, source_target_pairs={{8,12},{10,14},{4,0},{6,2},{24,28},{26,30},{20,16},{22,18}} | collective-permute-start | bytes 3145736 | tf_op jit(solution)/shard_map/ppermute | solution.py:163
  194.1 52.4 %collective-permute-start.23 = (f32[256,1024]{1,0:T(8,128)}, f32[256,1024]{1,0:T(8,128)}, u32[]{:S(2)}, u32[]{:S(2)}) collective-permute-start(f32[256,1024]{1,0:T(8,128)} %add_add_fusion.1.refs_4_), channel_id=1, source_target_pairs={{2,0},{6,4},{10,8},{14,12},{18,16},{22,20},{26,24},{30,28}} | collective-permute-start | bytes 3145736 | tf_op jit(solution)/shard_map/ppermute | solution.py:163
  205.3 41.2 %collective-permute-start.29 = (f32[256,1024]{1,0:T(8,128)}, f32[256,1024]{1,0:T(8,128)}, u32[]{:S(2)}, u32[]{:S(2)}) collective-permute-start(f32[256,1024]{1,0:T(8,128)} %add_add_fusion.refs_6_), channel_id=1, source_target_pairs={{2,0},{6,4},{10,8},{14,12},{18,16},{22,20},{26,24},{30,28}} | collective-permute-start | bytes 3145736 | tf_op jit(solution)/shard_map/ppermute | solution.py:163
  206.8 1.2 collective-permute-start.14
  208.0 14.3 %collective-permute-start.15 = (f32[8,128]{1,0:T(8,128)S(1)}, f32[8,128]{1,0:T(8,128)S(1)}, u32[]{:S(2)}, u32[]{:S(2)}) collective-permute-start(f32[8,128]{1,0:T(8,128)S(1)} %add.65), channel_id=1, source_target_pairs={{0,2},{1,3},{2,0},{3,1},{4,6},{5,7},{6,4},{7,5},{8,10},{9,11},{10,... | collective-permute-start | bytes 12296 | tf_op jit(solution)/shard_map/ppermute | solution.py:163
  222.4 13.9 %collective-permute-start.16 = (f32[8,128]{1,0:T(8,128)S(1)}, f32[8,128]{1,0:T(8,128)S(1)}, u32[]{:S(2)}, u32[]{:S(2)}) collective-permute-start(f32[8,128]{1,0:T(8,128)S(1)} %add.66), channel_id=1, source_target_pairs={{0,4},{1,5},{2,6},{3,7},{4,0},{5,1},{6,2},{7,3},{8,12},{9,13},{10,... | collective-permute-start | bytes 12296 | tf_op jit(solution)/shard_map/ppermute | solution.py:163
  236.2 9.0 %collective-permute-start.17 = (f32[8,128]{1,0:T(8,128)S(1)}, f32[8,128]{1,0:T(8,128)S(1)}, u32[]{:S(2)}, u32[]{:S(2)}) collective-permute-start(f32[8,128]{1,0:T(8,128)S(1)} %add.67), channel_id=1, source_target_pairs={{0,8},{1,9},{2,10},{3,11},{4,12},{5,13},{6,14},{7,15},{8,0},{9,1},... | collective-permute-start | bytes 12296 | tf_op jit(solution)/shard_map/ppermute | solution.py:163
  (13 other events, 38.8 us)

commit v3 on v2

--- a/solution.py
+++ b/solution.py
@@ -14,7 +14,7 @@
 WIDE = 512
 PAIRS = 2
 COUNT = 2 * PAIRS
-VMEM_LIMIT = 32 * 1024 * 1024
+VMEM_LIMIT = 48 * 1024 * 1024
 NT = (((1,), (1,)), ((), ()))
 
 
@@ -106,7 +106,8 @@
 
 
 def finish_kernel(col_ref, decoder_ref, inverse_ref, along_ref, *refs):
-    chunks, out_ref = refs[:COUNT], refs[-1]
+    chunks = refs[:COUNT]
+    out_ref, mark_ref = refs[-2:]
     step = chunks[0].shape[1]
     inverse = inverse_ref[:, :1]
     scale = (2.0 * math.sqrt(DW)) * inverse
@@ -115,6 +116,55 @@
         span = slice(k * step, (k + 1) * step)
         part = jnp.dot(col_ref[...], chunks[k][...], preferred_element_type=jnp.float32)
         out_ref[:, span] = scale * part - back * decoder_ref[:, span].astype(jnp.float32)
+    mark_ref[...] = jnp.zeros_like(mark_ref)
+
+
+STEPS = 32000.0
+
+
+def encode(value, msg_ref):
+    size = value.shape[1]
+    top = jnp.max(jnp.abs(value), axis=1, keepdims=True)
+    power = jnp.ceil(jnp.log2(jnp.maximum(top, 1e-35)) * 8.0)
+    ratio = value * jnp.exp2(power * -0.125)
+    coded = ratio * lax.rsqrt(jnp.maximum(jnp.abs(ratio), 1e-30))
+    coded = jnp.round(coded * STEPS).astype(jnp.int32)
+    msg_ref[:, :size] = coded.astype(jnp.int16)
+    power = jnp.broadcast_to(power.astype(jnp.int32), (value.shape[0], 128))
+    msg_ref[:, size:] = power.astype(jnp.int16)
+
+
+def decode(msg_ref):
+    size = msg_ref.shape[1] - 128
+    power = msg_ref[:, size:].astype(jnp.int32).astype(jnp.float32)[:, :1]
+    coded = msg_ref[:, :size].astype(jnp.int32).astype(jnp.float32)
+    scale = jnp.exp2(power * 0.125) * (1.0 / (STEPS * STEPS))
+    return coded * jnp.abs(coded) * scale
+
+
+def split_kernel(even_ref, mine_ref, theirs_ref, *refs):
+    kept_ref, msg_ref = refs[-2:]
+    step = kept_ref.shape[1]
+    low, high = slice(0, step), slice(step, 2 * step)
+
+    @pl.when(even_ref[0] == 1)
+    def _():
+        kept_ref[...] = mine_ref[:, low] + theirs_ref[:, low]
+        encode(mine_ref[:, high] + theirs_ref[:, high], msg_ref)
+
+    @pl.when(even_ref[0] == 0)
+    def _():
+        kept_ref[...] = mine_ref[:, high] + theirs_ref[:, high]
+        encode(mine_ref[:, low] + theirs_ref[:, low], msg_ref)
+
+
+def merge_kernel(arrived, keep, kept_ref, *refs):
+    value = kept_ref[...]
+    for msg_ref in refs[:arrived]:
+        value = value + decode(msg_ref)
+    if keep:
+        refs[-2][...] = value
+    encode(value, refs[-1])
 
 
 def last_kernel(owner_ref, col_ref, decoder_ref, inverse_ref, *refs):
@@ -126,7 +176,8 @@
     for k in range(COUNT):
         span = slice(k * step, (k + 1) * step)
         part = jnp.dot(col_ref[...], chunks[k][...], preferred_element_type=jnp.float32)
-        part = part + jnp.where(owner, sums[k][...], 0.0)
+        row_sum = decode(sums[k]) if k % 2 else sums[k][...]
+        part = part + jnp.where(owner, row_sum, 0.0)
         column[:, span] = part
         along = part * decoder_ref[:, span].astype(jnp.float32)
         for t in range(0, step, 128):
@@ -265,7 +316,79 @@
             name="weights",
         )(delta, units, chosen[2 * k], chosen[2 * k + 1], partial)
 
-    sums = [None] * COUNT
+    penalties = [local_penalty]
+    far = 1
+    while far < devices:
+        swap = [(i, i ^ far) for i in range(devices)]
+        penalties.append(penalties[-1] + send(penalties[-1], swap))
+        far *= 2
+    penalty = jnp.sum(penalties[-1]) * (DW / (ROWS * latents))
+
+    out_type = jax.ShapeDtypeStruct((shard, width), jnp.float32)
+    mark_type = jax.ShapeDtypeStruct((8, 128), jnp.float32)
+    mark_spec = pl.BlockSpec((8, 128), lambda i: (0, 0))
+    any_spec = pl.BlockSpec(memory_space=pl.ANY)
+    grad = None
+    marks = []
+    bounds = [1 + (blocks - 1) * p // 3 for p in range(4)]
+    for low, high in zip(bounds[:-1], bounds[1:]):
+        if high == low:
+            continue
+        operands = [by_col, decoder, inverse, along, *chosen]
+        specs = [
+            pl.BlockSpec((BLOCK, ROWS), lambda i, low=low: (i + low, 0)),
+            pl.BlockSpec((BLOCK, width), lambda i, low=low: (i + low, 0)),
+            pl.BlockSpec((BLOCK, 128), lambda i, low=low: (i + low, 0)),
+            pl.BlockSpec((BLOCK, 128), lambda i, low=low: (i + low, 0)),
+        ] + [whole_chunk] * COUNT
+        aliases = {}
+        if grad is not None:
+            aliases = {len(operands): 0}
+            operands.append(grad)
+            specs.append(any_spec)
+        rows = (high - low) * BLOCK
+        grad, mark = pl.pallas_call(
+            finish_kernel,
+            grid=(high - low,),
+            in_specs=specs,
+            out_specs=[pl.BlockSpec((BLOCK, width), lambda i, low=low: (i + low, 0)), mark_spec],
+            out_shape=[out_type, mark_type],
+            input_output_aliases=aliases,
+            compiler_params=params(),
+            cost_estimate=cost(2 * ROWS * rows * width, 6 * rows * width),
+            name="finish",
+        )(*operands)
+        marks.append(mark)
+
+    quarter_rows = ROWS // 4
+    kept_spec = pl.BlockSpec((quarter_rows, step), lambda i: (i, 0))
+    msg_spec = pl.BlockSpec((quarter_rows, step + 128), lambda i: (i, 0))
+    both_spec = pl.BlockSpec((quarter_rows, 2 * step), lambda i: (i, 0))
+    kept_type = jax.ShapeDtypeStruct((ROWS, step), jnp.float32)
+    msg_type = jax.ShapeDtypeStruct((ROWS, step + 128), jnp.int16)
+    even_flag = jnp.reshape(even_chip, (1,)).astype(jnp.int32)
+    merge_cost = cost(20 * ROWS * step, 12 * ROWS * step)
+
+    def after(k, level):
+        if k:
+            return []
+        return penalties[level + 1 : level + 2] + (marks[level - 1 : level] if level else [])
+
+    def merge(kept, arrived, keep, ties):
+        result = pl.pallas_call(
+            functools.partial(merge_kernel, len(arrived), keep),
+            grid=(4,),
+            in_specs=[kept_spec] + [msg_spec] * len(arrived) + [any_spec] * len(ties),
+            out_specs=[kept_spec, msg_spec] if keep else [msg_spec],
+            out_shape=[kept_type, msg_type] if keep else [msg_type],
+            compiler_params=params(),
+            cost_estimate=merge_cost,
+            name="merge",
+        )(kept, *arrived, *ties)
+        return result if keep else result[0]
+
+    mine_row, kept, msg = ([None] * PAIRS for _ in range(3))
+    one_hop, two_hop, three_hop = ([None] * PAIRS for _ in range(3))
     for k in range(PAIRS):
         value = pl.pallas_call(
             row_kernel,
@@ -284,57 +407,34 @@
         while far >= 4:
             value = value + send(value, each([(w + far, w) for w in range(far)]))
             far //= 2
-        value = value + send(value, each([(1, 0), (3, 2)]))
-        low, high = value[:, :step], value[:, step:]
-        away = jnp.where(even_chip, high, low)
-        kept = jnp.where(even_chip, low, high)
-        kept = kept + send(away, each([(0, 2), (2, 0)]))
-        first_sum = send(kept, hop(0))
-        second_sum = send(kept + first_sum, hop(1))
-        third_sum = send(kept + second_sum, hop(2))
-        total = kept + first_sum + second_sum + third_sum
-        sums[2 * k] = total
-        sums[2 * k + 1] = send(total, each([(2, 0)]))
-
-    penalties = local_penalty
-    far = 1
-    while far < devices:
-        swap = [(i, i ^ far) for i in range(devices)]
-        penalties = penalties + send(penalties, swap)
-        far *= 2
-    penalty = jnp.sum(penalties) * (DW / (ROWS * latents))
-
-    out_type = jax.ShapeDtypeStruct((shard, width), jnp.float32)
-    any_spec = pl.BlockSpec(memory_space=pl.ANY)
-    grad = None
-    bounds = [1, 1 + (blocks - 1) // 2, blocks] if blocks > 2 else [1, blocks]
-    for low, high in zip(bounds[:-1], bounds[1:]):
-        if high == low:
-            continue
-        operands = [by_col, decoder, inverse, along, *chosen]
-        specs = [
-            pl.BlockSpec((BLOCK, ROWS), lambda i, low=low: (i + low, 0)),
-            pl.BlockSpec((BLOCK, width), lambda i, low=low: (i + low, 0)),
-            pl.BlockSpec((BLOCK, 128), lambda i, low=low: (i + low, 0)),
-            pl.BlockSpec((BLOCK, 128), lambda i, low=low: (i + low, 0)),
-        ] + [whole_chunk] * COUNT
-        aliases = {}
-        if grad is not None:
-            aliases = {len(operands): 0}
-            operands.append(grad)
-            specs.append(any_spec)
-        rows = (high - low) * BLOCK
-        grad = pl.pallas_call(
-            finish_kernel,
-            grid=(high - low,),
-            in_specs=specs,
-            out_specs=pl.BlockSpec((BLOCK, width), lambda i, low=low: (i + low, 0)),
-            out_shape=out_type,
-            input_output_aliases=aliases,
+        mine_row[k] = value
+    for k in range(PAIRS):
+        theirs = send(mine_row[k], each([(1, 0), (3, 2)]))
+        ties = after(k, 0)
+        kept[k], msg[k] = pl.pallas_call(
+            split_kernel,
+            grid=(4,),
+            in_specs=[smem, both_spec, both_spec] + [any_spec] * len(ties),
+            out_specs=[kept_spec, msg_spec],
+            out_shape=[kept_type, msg_type],
             compiler_params=params(),
-            cost_estimate=cost(2 * ROWS * rows * width, 6 * rows * width),
-            name="finish",
-        )(*operands)
+            cost_estimate=merge_cost,
+            name="split",
+        )(even_flag, mine_row[k], theirs, *ties)
+    for k in range(PAIRS):
+        across = send(msg[k], each([(0, 2), (2, 0)]))
+        kept[k], msg[k] = merge(kept[k], [across], True, after(k, 1))
+    for k in range(PAIRS):
+        one_hop[k] = send(msg[k], hop(0))
+        msg[k] = merge(kept[k], [one_hop[k]], False, after(k, 2))
+    for k in range(PAIRS):
+        two_hop[k] = send(msg[k], hop(1))
+        msg[k] = merge(kept[k], [two_hop[k]], False, after(k, 3))
+    sums = []
+    for k in range(PAIRS):
+        three_hop[k] = send(msg[k], hop(2))
+        total, coded = merge(kept[k], [one_hop[k], two_hop[k], three_hop[k]], True, [])
+        sums += [total, send(coded, each([(2, 0)]))]
 
     owner = jnp.reshape(here & (within == 0), (1,)).astype(jnp.int32)
     narrow = BLOCK // 2
@@ -346,7 +446,10 @@
         pl.BlockSpec((narrow, 128), lambda i: (i, 0)),
     ]
     specs += [whole_chunk] * COUNT
-    specs += [pl.BlockSpec((narrow, step), lambda i: (i, 0))] * COUNT
+    specs += [
+        pl.BlockSpec((narrow, step), lambda i: (i, 0)),
+        pl.BlockSpec((narrow, step + 128), lambda i: (i, 0)),
+    ] * PAIRS
     aliases = {}
     if grad is not None:
         aliases = {len(operands): 0}

time: 255 us -> 227 us (0.89)
  waiting for transfers between devices: 99.1 us -> 55.4 us
  Pallas kernels: 48.2 us -> 88.5 us
  local copies, waits for them, and re-layouts: 37 us -> 9.74 us
  starting transfers between devices: 50.3 us -> 57.1 us
  other arithmetic: 15.2 us -> 10.3 us
    ppermute x30, waiting for transfers between devices: 99.1 us -> 55.4 us  [send(): return lax.ppermute(value, 'row', pairs)]
    unnamed x30, local copies, waits for them, and re-layouts: 36.5 us -> 9.23 us
    pallas_call x0 -> x10, Pallas kernels: none -> 17.6 us  [the longest x8 11 us: merge(): pl.pallas_call(functools.partial(merge_kernel, len(arrived), keep), grid=...]
    pallas_call x2 -> x3, Pallas kernels: 12.7 us -> 20.1 us  [on_device(): pl.pallas_call(finish_kernel, grid=(high - low,), in_specs=specs, out_spe...]
    ppermute x30, starting transfers between devices: 50.3 us -> 57.1 us  [send(): return lax.ppermute(value, 'row', pairs)]
    pallas_call x2, Pallas kernels: 7.53 us -> 13.1 us  [on_device(): pl.pallas_call(row_kernel, grid=(4,), in_specs=[pl.BlockSpec((ROWS, shard...]
    pallas_call x1, Pallas kernels: 11.7 us -> 17.2 us  [on_device(): pl.pallas_call(units_kernel, grid=(blocks,), in_specs=[pl.BlockSpec((BLOC...]
    add x13 -> x3, other arithmetic: 4.48 us -> 0.01 us  [on_device(): penalties.append(penalties[-1] + send(penalties[-1], swap))]
  transfers between devices with their start and end apart: 30 -> 30, of which waited for: 15 -> 13; matrix products, arithmetic and copies ran while one was open for 6% -> 4% of each run, Pallas kernels for 12% -> 30%
where the time goes in v3:
time: 227 us; the launch traced here: 225 us
  Pallas kernels  88.5 us (39%)
  starting transfers between devices  57.1 us (25%)
  waiting for transfers between devices  55.4 us (24%)
  other arithmetic  10.3 us (5%)
  local copies, waits for them, and re-layouts  9.74 us (4%)
  between operations  4.22 us (2%)
    ppermute x30, starting transfers between devices, send(): return lax.ppermute(value, 'row', pairs)  57.1 us
    ppermute x30, waiting for transfers between devices, send(): return lax.ppermute(value, 'row', pairs)  55.4 us
    pallas_call x3, Pallas kernels, on_device(): pl.pallas_call(finish_kernel, grid=(high - low,), in_specs=specs, out_spe...  20.1 us
    pallas_call x1, Pallas kernels, on_device(): pl.pallas_call(units_kernel, grid=(blocks,), in_specs=[pl.BlockSpec((BLOC...  17.2 us
    pallas_call x2, Pallas kernels, on_device(): pl.pallas_call(row_kernel, grid=(4,), in_specs=[pl.BlockSpec((ROWS, shard...  13.1 us
    pallas_call x8, Pallas kernels, merge(): pl.pallas_call(functools.partial(merge_kernel, len(arrived), keep), grid=...  11 us
    unnamed x30, local copies, waits for them, and re-layouts  9.23 us
    pallas_call x1, Pallas kernels, on_device(): pl.pallas_call(weight_kernel, grid=(shard // wide,), in_specs=[smem, unit...  6.68 us
  transfers between devices with their start and end apart: 30, of which 13 were waited for; matrix products, arithmetic and copies ran while one was open for 4% of the time, Pallas kernels for 30%

profile of v3, /device:TPU:0, one launch (start us, length us, event | category | flops | bytes accessed | tf_op | source)
XLA Modules:
  0.0 225.3 jit_solution(10626394578674033691)
XLA Ops:
  0.6 2.9 %head_units.1 = (bf16[256,1024]{1,0:T(8,128)(2,1)S(1)}, bf16[256,1024]{1,0:T(8,128)(2,1)S(1)}, bf16[256,1024]{1,0:T(8,128)(2,1)S(1)}, bf16[256,1024]{1,0:T(8,128)(2,1)S(1)}) custom-call(bf16[2048,4096]{1,0:T(8,128)(2,1)} %decoder_ref.11), custom_call_target="tpu_custom_call" | custom-call | flops 4194304 | bytes 4194304 | tf_op jit(solution)/shard_map/head_units/pallas_call | solution.py:223
  3.5 5.7 %collective-permute-start.7 = (bf16[256,1024]{1,0:T(8,128)(2,1)S(1)}, bf16[256,1024]{1,0:T(8,128)(2,1)}, u32[]{:S(2)}, u32[]{:S(2)}) collective-permute-start(bf16[256,1024]{1,0:T(8,128)(2,1)S(1)} %get-tuple-element.34), channel_id=1, source_target_pairs={{0,2},{4,6},{8,10},{12,14},{16,18},{20,22},{24,26},{28,30}} | collective-permute-start | bytes 1572872 | tf_op jit(solution)/shard_map/ppermute | solution.py:214
  11.3 17.2 %units.1 = (bf16[2048,4096]{1,0:T(8,128)(2,1)}, f32[2048,128]{1,0:T(8,128)S(1)}) custom-call(bf16[2048,4096]{1,0:T(8,128)(2,1)} %decoder_ref.11), custom_call_target="tpu_custom_call" | custom-call | flops 33554432 | bytes 33554432 | tf_op jit(solution)/shard_map/units/pallas_call | solution.py:234
  29.8 4.3 %collective-permute-start.8 = (bf16[256,1024]{1,0:T(8,128)(2,1)S(1)}, bf16[256,1024]{1,0:T(8,128)(2,1)}, u32[]{:S(2)}, u32[]{:S(2)}) collective-permute-start(bf16[256,1024]{1,0:T(8,128)(2,1)S(1)} %broadcast_select_fusion), channel_id=1, source_target_pairs={{0,4},{2,6},{12,8},{14,10},{16,20},{18,22},{28,24},{30,26}} | collective-permute-start | bytes 1572872 | tf_op jit(solution)/shard_map/ppermute | solution.py:214
  36.1 3.8 %collective-permute-done.8 = bf16[256,1024]{1,0:T(8,128)(2,1)} collective-permute-done((bf16[256,1024]{1,0:T(8,128)(2,1)S(1)}, bf16[256,1024]{1,0:T(8,128)(2,1)}, u32[]{:S(2)}, u32[]{:S(2)}) %collective-permute-start.8) | collective-permute-done | bytes 524320 | tf_op jit(solution)/shard_map/ppermute | solution.py:214
  41.7 3.8 %collective-permute-done.1 = bf16[256,1024]{1,0:T(8,128)(2,1)S(1)} collective-permute-done((bf16[256,1024]{1,0:T(8,128)(2,1)S(1)}, bf16[256,1024]{1,0:T(8,128)(2,1)S(1)}, u32[]{:S(2)}, u32[]{:S(2)}) %collective-permute-start.1) | collective-permute-done | bytes 524320 | tf_op jit(solution)/shard_map/ppermute | solution.py:214
  50.7 13.6 %collective-permute-done.10 = bf16[256,1024]{1,0:T(8,128)(2,1)} collective-permute-done((bf16[256,1024]{1,0:T(8,128)(2,1)}, bf16[256,1024]{1,0:T(8,128)(2,1)}, u32[]{:S(2)}, u32[]{:S(2)}) %collective-permute-start.10) | collective-permute-done | bytes 524320 | tf_op jit(solution)/shard_map/ppermute | solution.py:214
  64.4 2.1 select_select_fusion
  71.9 2.3 %collective-permute-start.5 = (bf16[256,1024]{1,0:T(8,128)(2,1)}, bf16[256,1024]{1,0:T(8,128)(2,1)S(1)}, u32[]{:S(2)}, u32[]{:S(2)}) collective-permute-start(bf16[256,1024]{1,0:T(8,128)(2,1)} %select_select_fusion.1), channel_id=1, source_target_pairs={{0,2},{2,0},{4,6},{6,4},{8,10},{10,8},{12,14},{14,12},{16,18},{18,... | collective-permute-start | bytes 1572872 | tf_op jit(solution)/shard_map/ppermute | solution.py:214
  75.6 2.2 collective-permute-done.12
  81.1 2.2 collective-permute-done.5
  87.6 5.6 %part_cosines.1.partial_ref = f32[2048,256]{1,0:T(8,128)S(1)} custom-call(bf16[2048,4096]{1,0:T(8,128)(2,1)} %get-tuple-element.30.units_ref, bf16[256,1024]{1,0:T(8,128)(2,1)S(1)} %get-tuple-element.61.low_ref.refs_0_, bf16[256,1024]{1,0:T(8,128)(2,1)S(1)} %get-tuple-element.60.high_ref.refs_1_), custom_call_target="tpu_custom_call" | custom-call | flops 2147483648 | bytes 8388608 | tf_op jit(solution)/shard_map/part_cosines/pallas_call | solution.py:287
  95.4 6.7 %weights.1 = (bf16[2048,256]{1,0:T(8,128)(2,1)S(1)}, bf16[256,2048]{1,0:T(8,128)(2,1)S(1)}, f32[2048,128]{1,0:T(8,128)S(1)}, f32[8,128]{1,0:T(8,128)S(1)}) custom-call(s32[1]{0:T(128)} %bitcast.1.delta_ref, bf16[2048,4096]{1,0:T(8,128)(2,1)} %get-tuple-element.30.units_ref, bf16[256,1024]{1,0:T(8,128)(2,1)S(1)} %get-tuple-element.63.low_ref.refs_2_, ...), custom_call_target="tpu_custom_call" | custom-call | flops 2147483648 | bytes 8388608 | tf_op jit(solution)/shard_map/weights/pallas_call | solution.py:298
  104.0 6.6 %row_part.3.mine_ref = f32[256,2048]{1,0:T(8,128)} custom-call(bf16[256,2048]{1,0:T(8,128)(2,1)S(1)} %get-tuple-element.38.row_ref, bf16[2048,4096]{1,0:T(8,128)(2,1)} %get-tuple-element.30.units_ref), custom_call_target="tpu_custom_call" | custom-call | flops 2147483648 | bytes 8388608 | tf_op jit(solution)/shard_map/row_part/pallas_call | solution.py:393
  111.8 6.6 %row_part.2.mine_ref = f32[256,2048]{1,0:T(8,128)} custom-call(bf16[256,2048]{1,0:T(8,128)(2,1)S(1)} %get-tuple-element.38.row_ref, bf16[2048,4096]{1,0:T(8,128)(2,1)} %get-tuple-element.30.units_ref), custom_call_target="tpu_custom_call" | custom-call | flops 2147483648 | bytes 8388608 | tf_op jit(solution)/shard_map/row_part/pallas_call | solution.py:393
  119.7 3.9 %collective-permute-start.14 = (f32[8,128]{1,0:T(8,128)S(1)}, f32[8,128]{1,0:T(8,128)S(1)}, u32[]{:S(2)}, u32[]{:S(2)}) collective-permute-start(f32[8,128]{1,0:T(8,128)S(1)} %get-tuple-element.36), channel_id=1, source_target_pairs={{0,1},{1,0},{2,3},{3,2},{4,5},{5,4},{6,7},{7,6},{8,9},{9,8},{10,11... | collective-permute-start | bytes 12296 | tf_op jit(solution)/shard_map/ppermute | solution.py:214
  123.6 3.4 %split.3 = (f32[256,1024]{1,0:T(8,128)S(1)}, s16[256,1152]{1,0:T(8,128)(2,1)S(1)}) custom-call(s32[1]{0:T(128)} %bitcast.5.even_ref, f32[256,2048]{1,0:T(8,128)} %row_part.3.mine_ref, f32[256,2048]{1,0:T(8,128)} %collective-permute-done.24.theirs_ref), custom_call_target="tpu_custom_call" | custom-call | flops 5242880 | bytes 3145728 | tf_op jit(solution)/shard_map/split/pallas_call | solution.py:414
  127.0 2.2 collective-permute-start.25
  129.2 3.3 %split.2 = (f32[256,1024]{1,0:T(8,128)S(1)}, s16[256,1152]{1,0:T(8,128)(2,1)S(1)}) custom-call(s32[1]{0:T(128)} %bitcast.5.even_ref, f32[256,2048]{1,0:T(8,128)} %row_part.2.mine_ref, f32[256,2048]{1,0:T(8,128)} %collective-permute-done.18.theirs_ref, f32[8,128]{1,0:T(8,128)S(1)} %add.27.refs_0_), custom_call_target="tpu_custom_call" | custom-call | flops 5242880 | bytes 3145728 | tf_op jit(solution)/shard_map/split/pallas_call | solution.py:414
  132.4 3.7 %collective-permute-start.19 = (s16[256,1152]{1,0:T(8,128)(2,1)S(1)}, s16[256,1152]{1,0:T(8,128)(2,1)S(1)}, u32[]{:S(2)}, u32[]{:S(2)}) collective-permute-start(s16[256,1152]{1,0:T(8,128)(2,1)S(1)} %get-tuple-element.40), channel_id=1, source_target_pairs={{0,2},{2,0},{4,6},{6,4},{8,10},{10,8},{12,14},{14,12},{16,18},{18,... | collective-permute-start | bytes 1769480 | tf_op jit(solution)/shard_map/ppermute | solution.py:214
  138.9 5.9 %finish.3 = (f32[2048,4096]{1,0:T(8,128)}, f32[8,128]{1,0:T(8,128)S(1)}) custom-call(bf16[2048,256]{1,0:T(8,128)(2,1)S(1)} %copy-done.1, bf16[2048,4096]{1,0:T(8,128)(2,1)} %decoder_ref.11, f32[2048,128]{1,0:T(8,128)S(1)} %get-tuple-element.31.inverse_ref, f32[2048,128]{1,0:T(8,128)S(1)} %copy-done.5, ...), custom_call_target="tpu_custom_call" | custom-call | flops 1073741824 | bytes 12582912 | tf_op jit(solution)/shard_map/finish/pallas_call | solution.py:350
  150.2 5.8 %finish.4 = (f32[2048,4096]{1,0:T(8,128)}, f32[8,128]{1,0:T(8,128)S(1)}) custom-call(bf16[2048,256]{1,0:T(8,128)(2,1)S(1)} %copy-done.2, bf16[2048,4096]{1,0:T(8,128)(2,1)} %decoder_ref.11, f32[2048,128]{1,0:T(8,128)S(1)} %get-tuple-element.31.inverse_ref, f32[2048,128]{1,0:T(8,128)S(1)} %copy-done.6, ...), custom_call_target="tpu_custom_call", output_to_operand_aliasing={{0}: (8, {})} | custom-call | flops 1073741824 | bytes 12582912 | tf_op jit(solution)/shard_map/finish/pallas_call | solution.py:350
  156.0 5.4 %collective-permute-done.16 = f32[8,128]{1,0:T(8,128)S(1)} collective-permute-done((f32[8,128]{1,0:T(8,128)S(1)}, f32[8,128]{1,0:T(8,128)S(1)}, u32[]{:S(2)}, u32[]{:S(2)}) %collective-permute-start.16) | collective-permute-done | bytes 4128 | tf_op jit(solution)/shard_map/ppermute | solution.py:214
  165.0 7.0 %collective-permute-start.17 = (f32[8,128]{1,0:T(8,128)S(1)}, f32[8,128]{1,0:T(8,128)S(1)}, u32[]{:S(2)}, u32[]{:S(2)}) collective-permute-start(f32[8,128]{1,0:T(8,128)S(1)} %add.29.refs_1_), channel_id=1, source_target_pairs={{0,8},{1,9},{2,10},{3,11},{4,12},{5,13},{6,14},{7,15},{8,0},{9,1},... | collective-permute-start | bytes 12296 | tf_op jit(solution)/shard_map/ppermute | solution.py:214
  172.0 8.4 %finish.5 = (f32[2048,4096]{1,0:T(8,128)}, f32[8,128]{1,0:T(8,128)S(1)}) custom-call(bf16[2048,256]{1,0:T(8,128)(2,1)S(1)} %copy-done.2, bf16[2048,4096]{1,0:T(8,128)(2,1)} %decoder_ref.11, f32[2048,128]{1,0:T(8,128)S(1)} %get-tuple-element.31.inverse_ref, f32[2048,128]{1,0:T(8,128)S(1)} %copy-done.6, ...), custom_call_target="tpu_custom_call", output_to_operand_aliasing={{0}: (8, {})} | custom-call | flops 1610612736 | bytes 18874368 | tf_op jit(solution)/shard_map/finish/pallas_call | solution.py:350
  180.3 2.2 collective-permute-done.17
  188.0 8.1 %collective-permute-done.28.refs_2_ = s16[256,1152]{1,0:T(8,128)(2,1)S(1)} collective-permute-done((s16[256,1152]{1,0:T(8,128)(2,1)S(1)}, s16[256,1152]{1,0:T(8,128)(2,1)S(1)}, u32[]{:S(2)}, u32[]{:S(2)}) %collective-permute-start.28) | collective-permute-done | bytes 589856 | tf_op jit(solution)/shard_map/ppermute | solution.py:214
  196.0 2.2 merge.15
  202.3 2.2 merge.11
  207.5 3.9 %collective-permute-done.29.refs_7_ = s16[256,1152]{1,0:T(8,128)(2,1)} collective-permute-done((s16[256,1152]{1,0:T(8,128)(2,1)}, s16[256,1152]{1,0:T(8,128)(2,1)}, u32[]{:S(2)}, u32[]{:S(2)}) %collective-permute-start.29) | collective-permute-done | bytes 589856 | tf_op jit(solution)/shard_map/ppermute | solution.py:214
  211.3 6.3 %collective-permute-done.23.refs_5_ = s16[256,1152]{1,0:T(8,128)(2,1)} collective-permute-done((s16[256,1152]{1,0:T(8,128)(2,1)}, s16[256,1152]{1,0:T(8,128)(2,1)}, u32[]{:S(2)}, u32[]{:S(2)}) %collective-permute-start.23) | collective-permute-done | bytes 589856 | tf_op jit(solution)/shard_map/ppermute | solution.py:214
  218.9 5.3 %finish_rows.1 = f32[2048,4096]{1,0:T(8,128)} custom-call(s32[1]{0:T(128)} %bitcast.4.owner_ref, bf16[2048,256]{1,0:T(8,128)(2,1)S(1)} %copy-done.3, bf16[2048,4096]{1,0:T(8,128)(2,1)} %decoder_ref.11, f32[2048,128]{1,0:T(8,128)S(1)} %get-tuple-element.31.inverse_ref, ...), custom_call_target="tpu_custom_call", output_to_operand_aliasing={{}: (12, {})} | custom-call | tf_op jit(solution)/shard_map/finish_rows/pallas_call | solution.py:458
  (93 shorter events, 56.6 us)
Async XLA Ops:
  3.5 26.1 %collective-permute-start.7 = (bf16[256,1024]{1,0:T(8,128)(2,1)S(1)}, bf16[256,1024]{1,0:T(8,128)(2,1)}, u32[]{:S(2)}, u32[]{:S(2)}) collective-permute-start(bf16[256,1024]{1,0:T(8,128)(2,1)S(1)} %get-tuple-element.34), channel_id=1, source_target_pairs={{0,2},{4,6},{8,10},{12,14},{16,18},{20,22},{24,26},{28,30}} | collective-permute-start | bytes 1572872 | tf_op jit(solution)/shard_map/ppermute | solution.py:214
  9.2 24.9 %collective-permute-start = (bf16[256,1024]{1,0:T(8,128)(2,1)S(1)}, bf16[256,1024]{1,0:T(8,128)(2,1)}, u32[]{:S(2)}, u32[]{:S(2)}) collective-permute-start(bf16[256,1024]{1,0:T(8,128)(2,1)S(1)} %get-tuple-element.32), channel_id=1, source_target_pairs={{0,2},{4,6},{8,10},{12,14},{16,18},{20,22},{24,26},{28,30}} | collective-permute-start | bytes 1572872 | tf_op jit(solution)/shard_map/ppermute | solution.py:214
  29.8 10.2 %collective-permute-start.8 = (bf16[256,1024]{1,0:T(8,128)(2,1)S(1)}, bf16[256,1024]{1,0:T(8,128)(2,1)}, u32[]{:S(2)}, u32[]{:S(2)}) collective-permute-start(bf16[256,1024]{1,0:T(8,128)(2,1)S(1)} %broadcast_select_fusion), channel_id=1, source_target_pairs={{0,4},{2,6},{12,8},{14,10},{16,20},{18,22},{28,24},{30,26}} | collective-permute-start | bytes 1572872 | tf_op jit(solution)/shard_map/ppermute | solution.py:214
  34.1 11.4 %collective-permute-start.1 = (bf16[256,1024]{1,0:T(8,128)(2,1)S(1)}, bf16[256,1024]{1,0:T(8,128)(2,1)S(1)}, u32[]{:S(2)}, u32[]{:S(2)}) collective-permute-start(bf16[256,1024]{1,0:T(8,128)(2,1)S(1)} %broadcast_select_fusion.1), channel_id=1, source_target_pairs={{0,4},{2,6},{12,8},{14,10},{16,20},{18,22},{28,24},{30,26}} | collective-permute-start | bytes 1572872 | tf_op jit(solution)/shard_map/ppermute | solution.py:214
  41.0 5.3 %collective-permute-start.9 = (bf16[256,1024]{1,0:T(8,128)(2,1)S(1)}, bf16[256,1024]{1,0:T(8,128)(2,1)S(1)}, u32[]{:S(2)}, u32[]{:S(2)}) collective-permute-start(bf16[256,1024]{1,0:T(8,128)(2,1)S(1)} %broadcast_select_fusion.3), channel_id=1, source_target_pairs={{4,8},{6,10},{8,4},{10,6},{20,24},{22,26},{24,20},{26,22}} | collective-permute-start | bytes 1572872 | tf_op jit(solution)/shard_map/ppermute | solution.py:214
  45.6 3.0 %collective-permute-start.2 = (bf16[256,1024]{1,0:T(8,128)(2,1)S(1)}, bf16[256,1024]{1,0:T(8,128)(2,1)S(1)}, u32[]{:S(2)}, u32[]{:S(2)}) collective-permute-start(bf16[256,1024]{1,0:T(8,128)(2,1)S(1)} %broadcast_select_fusion.5), channel_id=1, source_target_pairs={{4,8},{6,10},{8,4},{10,6},{20,24},{22,26},{24,20},{26,22}} | collective-permute-start | bytes 1572872 | tf_op jit(solution)/shard_map/ppermute | solution.py:214
  47.3 17.1 %collective-permute-start.10 = (bf16[256,1024]{1,0:T(8,128)(2,1)}, bf16[256,1024]{1,0:T(8,128)(2,1)}, u32[]{:S(2)}, u32[]{:S(2)}) collective-permute-start(bf16[256,1024]{1,0:T(8,128)(2,1)} %broadcast_select_fusion.2), channel_id=1, source_target_pairs={{8,12},{10,14},{4,0},{6,2},{24,28},{26,30},{20,16},{22,18}} | collective-permute-start | bytes 1572872 | tf_op jit(solution)/shard_map/ppermute | solution.py:214
  49.4 20.6 %collective-permute-start.3 = (bf16[256,1024]{1,0:T(8,128)(2,1)}, bf16[256,1024]{1,0:T(8,128)(2,1)}, u32[]{:S(2)}, u32[]{:S(2)}) collective-permute-start(bf16[256,1024]{1,0:T(8,128)(2,1)} %broadcast_select_fusion.4), channel_id=1, source_target_pairs={{8,12},{10,14},{4,0},{6,2},{24,28},{26,30},{20,16},{22,18}} | collective-permute-start | bytes 1572872 | tf_op jit(solution)/shard_map/ppermute | solution.py:214
  66.5 11.3 %collective-permute-start.12 = (bf16[256,1024]{1,0:T(8,128)(2,1)}, bf16[256,1024]{1,0:T(8,128)(2,1)S(1)}, u32[]{:S(2)}, u32[]{:S(2)}) collective-permute-start(bf16[256,1024]{1,0:T(8,128)(2,1)} %select_select_fusion), channel_id=1, source_target_pairs={{0,2},{2,0},{4,6},{6,4},{8,10},{10,8},{12,14},{14,12},{16,18},{18,... | collective-permute-start | bytes 1572872 | tf_op jit(solution)/shard_map/ppermute | solution.py:214
  71.9 11.4 %collective-permute-start.5 = (bf16[256,1024]{1,0:T(8,128)(2,1)}, bf16[256,1024]{1,0:T(8,128)(2,1)S(1)}, u32[]{:S(2)}, u32[]{:S(2)}) collective-permute-start(bf16[256,1024]{1,0:T(8,128)(2,1)} %select_select_fusion.1), channel_id=1, source_target_pairs={{0,2},{2,0},{4,6},{6,4},{8,10},{10,8},{12,14},{14,12},{16,18},{18,... | collective-permute-start | bytes 1572872 | tf_op jit(solution)/shard_map/ppermute | solution.py:214
  74.2 11.2 %collective-permute-start.11 = (bf16[256,1024]{1,0:T(8,128)(2,1)}, bf16[256,1024]{1,0:T(8,128)(2,1)S(1)}, u32[]{:S(2)}, u32[]{:S(2)}) collective-permute-start(bf16[256,1024]{1,0:T(8,128)(2,1)} %select_select_fusion), channel_id=1, source_target_pairs={{0,1},{2,3},{4,5},{6,7},{8,9},{10,11},{12,13},{14,15},{16,17},{18,... | collective-permute-start | bytes 1572872 | tf_op jit(solution)/shard_map/ppermute | solution.py:214
  77.7 8.5 %collective-permute-start.13 = (bf16[256,1024]{1,0:T(8,128)(2,1)S(1)}, bf16[256,1024]{1,0:T(8,128)(2,1)}, u32[]{:S(2)}, u32[]{:S(2)}) collective-permute-start(bf16[256,1024]{1,0:T(8,128)(2,1)S(1)} %collective-permute-done.12), channel_id=1, source_target_pairs={{0,1},{2,3},{4,5},{6,7},{8,9},{10,11},{12,13},{14,15},{16,17},{18,... | collective-permute-start | bytes 1572872 | tf_op jit(solution)/shard_map/ppermute | solution.py:214
  79.8 13.4 %collective-permute-start.4 = (bf16[256,1024]{1,0:T(8,128)(2,1)}, bf16[256,1024]{1,0:T(8,128)(2,1)S(1)}, u32[]{:S(2)}, u32[]{:S(2)}) collective-permute-start(bf16[256,1024]{1,0:T(8,128)(2,1)} %select_select_fusion.1), channel_id=1, source_target_pairs={{0,1},{2,3},{4,5},{6,7},{8,9},{10,11},{12,13},{14,15},{16,17},{18,... | collective-permute-start | bytes 1572872 | tf_op jit(solution)/shard_map/ppermute | solution.py:214
  83.4 10.7 %collective-permute-start.6 = (bf16[256,1024]{1,0:T(8,128)(2,1)S(1)}, bf16[256,1024]{1,0:T(8,128)(2,1)}, u32[]{:S(2)}, u32[]{:S(2)}) collective-permute-start(bf16[256,1024]{1,0:T(8,128)(2,1)S(1)} %collective-permute-done.5), channel_id=1, source_target_pairs={{0,1},{2,3},{4,5},{6,7},{8,9},{10,11},{12,13},{14,15},{16,17},{18,... | collective-permute-start | bytes 1572872 | tf_op jit(solution)/shard_map/ppermute | solution.py:214
  110.6 13.0 %collective-permute-start.24 = (f32[256,2048]{1,0:T(8,128)}, f32[256,2048]{1,0:T(8,128)}, u32[]{:S(2)}, u32[]{:S(2)}) collective-permute-start(f32[256,2048]{1,0:T(8,128)} %row_part.3.mine_ref), channel_id=1, source_target_pairs={{1,0},{3,2},{5,4},{7,6},{9,8},{11,10},{13,12},{15,14},{17,16},{19,... | collective-permute-start | bytes 6291464 | tf_op jit(solution)/shard_map/ppermute | solution.py:214
  118.4 10.7 %collective-permute-start.18 = (f32[256,2048]{1,0:T(8,128)}, f32[256,2048]{1,0:T(8,128)}, u32[]{:S(2)}, u32[]{:S(2)}) collective-permute-start(f32[256,2048]{1,0:T(8,128)} %row_part.2.mine_ref), channel_id=1, source_target_pairs={{1,0},{3,2},{5,4},{7,6},{9,8},{11,10},{13,12},{15,14},{17,16},{19,... | collective-permute-start | bytes 6291464 | tf_op jit(solution)/shard_map/ppermute | solution.py:214
  119.7 9.4 %collective-permute-start.14 = (f32[8,128]{1,0:T(8,128)S(1)}, f32[8,128]{1,0:T(8,128)S(1)}, u32[]{:S(2)}, u32[]{:S(2)}) collective-permute-start(f32[8,128]{1,0:T(8,128)S(1)} %get-tuple-element.36), channel_id=1, source_target_pairs={{0,1},{1,0},{2,3},{3,2},{4,5},{5,4},{6,7},{7,6},{8,9},{9,8},{10,11... | collective-permute-start | bytes 12296 | tf_op jit(solution)/shard_map/ppermute | solution.py:214
  123.6 26.6 %copy-start.2 = (bf16[2048,256]{1,0:T(8,128)(2,1)S(1)}, bf16[2048,256]{1,0:T(8,128)(2,1)}, u32[]{:S(2)}) copy-start(bf16[2048,256]{1,0:T(8,128)(2,1)} %copy-done) | copy-start | bytes 3145732
  123.6 26.6 %copy-start.6 = (f32[2048,128]{1,0:T(8,128)S(1)}, f32[2048,128]{1,0:T(8,128)}, u32[]{:S(2)}) copy-start(f32[2048,128]{1,0:T(8,128)} %copy-done.4) | copy-start | bytes 3145732
  127.0 18.2 %collective-permute-start.25 = (s16[256,1152]{1,0:T(8,128)(2,1)S(1)}, s16[256,1152]{1,0:T(8,128)(2,1)S(1)}, u32[]{:S(2)}, u32[]{:S(2)}) collective-permute-start(s16[256,1152]{1,0:T(8,128)(2,1)S(1)} %get-tuple-element.52), channel_id=1, source_target_pairs={{0,2},{2,0},{4,6},{6,4},{8,10},{10,8},{12,14},{14,12},{16,18},{18,... | collective-permute-start | bytes 1769480 | tf_op jit(solution)/shard_map/ppermute | solution.py:214
  132.4 15.2 %collective-permute-start.19 = (s16[256,1152]{1,0:T(8,128)(2,1)S(1)}, s16[256,1152]{1,0:T(8,128)(2,1)S(1)}, u32[]{:S(2)}, u32[]{:S(2)}) collective-permute-start(s16[256,1152]{1,0:T(8,128)(2,1)S(1)} %get-tuple-element.40), channel_id=1, source_target_pairs={{0,2},{2,0},{4,6},{6,4},{8,10},{10,8},{12,14},{14,12},{16,18},{18,... | collective-permute-start | bytes 1769480 | tf_op jit(solution)/shard_map/ppermute | solution.py:214
  136.1 9.0 %collective-permute-start.15 = (f32[8,128]{1,0:T(8,128)S(1)}, f32[8,128]{1,0:T(8,128)S(1)}, u32[]{:S(2)}, u32[]{:S(2)}) collective-permute-start(f32[8,128]{1,0:T(8,128)S(1)} %add.27.refs_0_), channel_id=1, source_target_pairs={{0,2},{1,3},{2,0},{3,1},{4,6},{5,7},{6,4},{7,5},{8,10},{9,11},{10,... | collective-permute-start | bytes 12296 | tf_op jit(solution)/shard_map/ppermute | solution.py:214
  146.3 15.1 %collective-permute-start.26 = (s16[256,1152]{1,0:T(8,128)(2,1)S(1)}, s16[256,1152]{1,0:T(8,128)(2,1)S(1)}, u32[]{:S(2)}, u32[]{:S(2)}) collective-permute-start(s16[256,1152]{1,0:T(8,128)(2,1)S(1)} %get-tuple-element.54), channel_id=1, source_target_pairs={{0,4},{2,6},{12,8},{14,10},{16,20},{18,22},{28,24},{30,26}} | collective-permute-start | bytes 1769480 | tf_op jit(solution)/shard_map/ppermute | solution.py:214
  148.7 14.4 %collective-permute-start.20 = (s16[256,1152]{1,0:T(8,128)(2,1)S(1)}, s16[256,1152]{1,0:T(8,128)(2,1)S(1)}, u32[]{:S(2)}, u32[]{:S(2)}) collective-permute-start(s16[256,1152]{1,0:T(8,128)(2,1)S(1)} %get-tuple-element.44), channel_id=1, source_target_pairs={{0,4},{2,6},{12,8},{14,10},{16,20},{18,22},{28,24},{30,26}} | collective-permute-start | bytes 1769480 | tf_op jit(solution)/shard_map/ppermute | solution.py:214
  150.1 11.3 %collective-permute-start.16 = (f32[8,128]{1,0:T(8,128)S(1)}, f32[8,128]{1,0:T(8,128)S(1)}, u32[]{:S(2)}, u32[]{:S(2)}) collective-permute-start(f32[8,128]{1,0:T(8,128)S(1)} %add.28.refs_1_), channel_id=1, source_target_pairs={{0,4},{1,5},{2,6},{3,7},{4,0},{5,1},{6,2},{7,3},{8,12},{9,13},{10,... | collective-permute-start | bytes 12296 | tf_op jit(solution)/shard_map/ppermute | solution.py:214
  162.5 20.7 %collective-permute-start.27 = (s16[256,1152]{1,0:T(8,128)(2,1)S(1)}, s16[256,1152]{1,0:T(8,128)(2,1)S(1)}, u32[]{:S(2)}, u32[]{:S(2)}) collective-permute-start(s16[256,1152]{1,0:T(8,128)(2,1)S(1)} %merge.13), channel_id=1, source_target_pairs={{4,8},{6,10},{8,4},{10,6},{20,24},{22,26},{24,20},{26,22}} | collective-permute-start | bytes 1769480 | tf_op jit(solution)/shard_map/ppermute | solution.py:214
  164.3 21.3 %collective-permute-start.21 = (s16[256,1152]{1,0:T(8,128)(2,1)S(1)}, s16[256,1152]{1,0:T(8,128)(2,1)S(1)}, u32[]{:S(2)}, u32[]{:S(2)}) collective-permute-start(s16[256,1152]{1,0:T(8,128)(2,1)S(1)} %merge.9), channel_id=1, source_target_pairs={{4,8},{6,10},{8,4},{10,6},{20,24},{22,26},{24,20},{26,22}} | collective-permute-start | bytes 1769480 | tf_op jit(solution)/shard_map/ppermute | solution.py:214
  165.0 17.6 %collective-permute-start.17 = (f32[8,128]{1,0:T(8,128)S(1)}, f32[8,128]{1,0:T(8,128)S(1)}, u32[]{:S(2)}, u32[]{:S(2)}) collective-permute-start(f32[8,128]{1,0:T(8,128)S(1)} %add.29.refs_1_), channel_id=1, source_target_pairs={{0,8},{1,9},{2,10},{3,11},{4,12},{5,13},{6,14},{7,15},{8,0},{9,1},... | collective-permute-start | bytes 12296 | tf_op jit(solution)/shard_map/ppermute | solution.py:214
  184.3 11.8 %collective-permute-start.28 = (s16[256,1152]{1,0:T(8,128)(2,1)S(1)}, s16[256,1152]{1,0:T(8,128)(2,1)S(1)}, u32[]{:S(2)}, u32[]{:S(2)}) collective-permute-start(s16[256,1152]{1,0:T(8,128)(2,1)S(1)} %merge.14), channel_id=1, source_target_pairs={{8,12},{10,14},{4,0},{6,2},{24,28},{26,30},{20,16},{22,18}} | collective-permute-start | bytes 1769480 | tf_op jit(solution)/shard_map/ppermute | solution.py:214
  186.7 15.7 %collective-permute-start.22 = (s16[256,1152]{1,0:T(8,128)(2,1)S(1)}, s16[256,1152]{1,0:T(8,128)(2,1)S(1)}, u32[]{:S(2)}, u32[]{:S(2)}) collective-permute-start(s16[256,1152]{1,0:T(8,128)(2,1)S(1)} %merge.10), channel_id=1, source_target_pairs={{8,12},{10,14},{4,0},{6,2},{24,28},{26,30},{20,16},{22,18}} | collective-permute-start | bytes 1769480 | tf_op jit(solution)/shard_map/ppermute | solution.py:214
  199.3 12.1 %collective-permute-start.29 = (s16[256,1152]{1,0:T(8,128)(2,1)}, s16[256,1152]{1,0:T(8,128)(2,1)}, u32[]{:S(2)}, u32[]{:S(2)}) collective-permute-start(s16[256,1152]{1,0:T(8,128)(2,1)} %get-tuple-element.56), channel_id=1, source_target_pairs={{2,0},{6,4},{10,8},{14,12},{18,16},{22,20},{26,24},{30,28}} | collective-permute-start | bytes 1769480 | tf_op jit(solution)/shard_map/ppermute | solution.py:214
  205.5 12.1 %collective-permute-start.23 = (s16[256,1152]{1,0:T(8,128)(2,1)}, s16[256,1152]{1,0:T(8,128)(2,1)}, u32[]{:S(2)}, u32[]{:S(2)}) collective-permute-start(s16[256,1152]{1,0:T(8,128)(2,1)} %get-tuple-element.50), channel_id=1, source_target_pairs={{2,0},{6,4},{10,8},{14,12},{18,16},{22,20},{26,24},{30,28}} | collective-permute-start | bytes 1769480 | tf_op jit(solution)/shard_map/ppermute | solution.py:214
  (13 other events, 31.2 us)

commit v4 on v2

--- a/solution.py
+++ b/solution.py
@@ -14,7 +14,7 @@
 WIDE = 512
 PAIRS = 2
 COUNT = 2 * PAIRS
-VMEM_LIMIT = 32 * 1024 * 1024
+VMEM_LIMIT = 48 * 1024 * 1024
 NT = (((1,), (1,)), ((), ()))
 
 
@@ -39,13 +39,18 @@
     step = chunk_refs[0].shape[1]
     rows = slice(0, decoder_ref.shape[0])
     inverse = strip_inverse(decoder_ref, rows)
-    for k, ref in enumerate(chunk_refs):
-        for t in range(0, step, 128):
-            v = decoder_ref[rows, k * step + t : k * step + t + 128].astype(jnp.float32)
-            ref[rows, t : t + 128] = (v * inverse).astype(jnp.bfloat16)
-
-
-def units_kernel(decoder_ref, units_ref, inverse_ref):
+    piece = step // 2
+    for k in range(PAIRS):
+        for p in range(4):
+            ref, base = chunk_refs[2 * k + p % 2], (4 * k + p) * piece
+            for t in range(0, piece, 128):
+                v = decoder_ref[rows, base + t : base + t + 128].astype(jnp.float32)
+                to = (p // 2) * piece + t
+                ref[rows, to : to + 128] = (v * inverse).astype(jnp.bfloat16)
+
+
+def units_kernel(decoder_ref, *refs):
+    units_ref, inverse_ref = refs[-2:]
     strip = 64
 
     def body(s, carry):
@@ -101,12 +106,17 @@
     penalty_ref[...] += jnp.sum(squares.reshape(size // 8, 8, 128), axis=0)
 
 
-def row_kernel(row_ref, units_ref, out_ref):
-    out_ref[...] = jnp.dot(row_ref[...], units_ref[...], preferred_element_type=jnp.float32)
+def row_kernel(side_ref, row_ref, penalty_ref, units_ref, *refs):
+    out_ref = refs[-1]
+    out_ref[:ROWS, :] = jnp.dot(
+        row_ref[...], units_ref[...], preferred_element_type=jnp.float32
+    )
+    out_ref[ROWS:, :] = jnp.concatenate([penalty_ref[...]] * (out_ref.shape[1] // 128), axis=1)
 
 
 def finish_kernel(col_ref, decoder_ref, inverse_ref, along_ref, *refs):
-    chunks, out_ref = refs[:COUNT], refs[-1]
+    chunks = refs[:COUNT]
+    out_ref, mark_ref = refs[-2:]
     step = chunks[0].shape[1]
     inverse = inverse_ref[:, :1]
     scale = (2.0 * math.sqrt(DW)) * inverse
@@ -115,18 +125,104 @@
         span = slice(k * step, (k + 1) * step)
         part = jnp.dot(col_ref[...], chunks[k][...], preferred_element_type=jnp.float32)
         out_ref[:, span] = scale * part - back * decoder_ref[:, span].astype(jnp.float32)
+    mark_ref[...] = jnp.zeros_like(mark_ref)
+
+
+STEPS = 32000.0
+CODED_ROWS = ROWS + 16
+PENALTY_STEPS = float(1 << 23)
+
+
+def pack(coded):
+    half = coded.shape[1] // 2
+    return (coded[:, :half] << 16) | (coded[:, half:] & 0xFFFF)
+
+
+def unpack(words):
+    both = jnp.concatenate([words >> 16, (words << 16) >> 16], axis=1)
+    return both.astype(jnp.float32)
+
+
+def encode(value, penalty, msg_ref):
+    top = jnp.max(jnp.abs(value), axis=0, keepdims=True)
+    power = jnp.ceil(jnp.log2(jnp.maximum(top, 1e-35)) * 8.0)
+    ratio = value * jnp.exp2(power * -0.125)
+    coded = ratio * lax.rsqrt(jnp.maximum(jnp.abs(ratio), 1e-30))
+    msg_ref[:ROWS, :] = pack(jnp.round(coded * STEPS).astype(jnp.int32))
+    power = pack(power.astype(jnp.int32))
+    msg_ref[ROWS : ROWS + 8, :] = jnp.broadcast_to(power, (8, power.shape[1]))
+    top = jnp.max(jnp.max(penalty, axis=1, keepdims=True), axis=0, keepdims=True)
+    power = jnp.ceil(jnp.log2(jnp.maximum(top, 1e-35)))
+    coded = jnp.round(penalty * (jnp.exp2(-power) * PENALTY_STEPS)).astype(jnp.int32)
+    msg_ref[ROWS + 8 :, :128] = coded
+    msg_ref[ROWS + 8 :, 128:] = jnp.broadcast_to(power.astype(jnp.int32), (8, 128))
+
+
+def decode(words, powers):
+    coded = unpack(words)
+    scale = jnp.exp2(unpack(powers)[:1, :] * 0.125) * (1.0 / (STEPS * STEPS))
+    return coded * jnp.abs(coded) * scale
+
+
+def decode_at(msg_ref, base):
+    value = decode(msg_ref[base : base + ROWS, :], msg_ref[base + ROWS : base + ROWS + 8, :])
+    tail = slice(base + ROWS + 8, base + CODED_ROWS)
+    power = msg_ref[tail, 128:].astype(jnp.float32)
+    penalty = msg_ref[tail, :128].astype(jnp.float32) * (jnp.exp2(power) / PENALTY_STEPS)
+    return value, penalty
+
+
+def split_kernel(odd_ref, mine_ref, theirs_ref, kept_ref, penalty_ref, msg_ref):
+    piece = kept_ref.shape[1]
+    penalty = mine_ref[ROWS:, :128] + theirs_ref[ROWS:, :128]
+    penalty_ref[...] = penalty
+    low, high = slice(0, piece), slice(piece, 2 * piece)
+
+    def divide(keep, away):
+        kept_ref[...] = mine_ref[:ROWS, keep] + theirs_ref[:ROWS, keep]
+        encode(mine_ref[:ROWS, away] + theirs_ref[:ROWS, away], penalty, msg_ref)
+
+    @pl.when(odd_ref[0] == 0)
+    def _():
+        divide(low, high)
+
+    @pl.when(odd_ref[0] == 1)
+    def _():
+        divide(high, low)
+
+
+def merge_kernel(kept_ref, penalty_ref, arrived_ref, msg_ref):
+    value, penalty = decode_at(arrived_ref, 0)
+    encode(kept_ref[...] + value, penalty_ref[...] + penalty, msg_ref)
+
+
+def total_kernel(gathered_ref, *refs):
+    total_ref, penalty_ref, msg_ref = refs[-3:]
+    value, penalty = decode_at(gathered_ref, 0)
+    for z in range(1, 4):
+        more, more_penalty = decode_at(gathered_ref, z * CODED_ROWS)
+        value, penalty = value + more, penalty + more_penalty
+    total_ref[...] = value
+    penalty_ref[...] = penalty
+    encode(value, penalty, msg_ref)
 
 
 def last_kernel(owner_ref, col_ref, decoder_ref, inverse_ref, *refs):
-    chunks, sums = refs[:COUNT], refs[COUNT : 2 * COUNT]
+    chunks, sums = refs[:COUNT], refs[COUNT : COUNT + 7 * PAIRS]
     out_ref, column = refs[-2:]
     step = chunks[0].shape[1]
+    piece = step // 2
     owner = owner_ref[0] == 1
     total = jnp.zeros((col_ref.shape[0], 128), jnp.float32)
     for k in range(COUNT):
         span = slice(k * step, (k + 1) * step)
         part = jnp.dot(col_ref[...], chunks[k][...], preferred_element_type=jnp.float32)
-        part = part + jnp.where(owner, sums[k][...], 0.0)
+        own, *coded = sums[7 * (k // 2) : 7 * (k // 2) + 7]
+        pieces = [own[...]] + [
+            decode(coded[2 * p][...], coded[2 * p + 1][...]) for p in range(3)
+        ]
+        row_sum = jnp.concatenate(pieces[2 * (k % 2) : 2 * (k % 2) + 2], axis=1)
+        part = part + jnp.where(owner, row_sum, 0.0)
         column[:, span] = part
         along = part * decoder_ref[:, span].astype(jnp.float32)
         for t in range(0, step, 128):
@@ -162,10 +258,6 @@
     def send(value, pairs):
         return lax.ppermute(value, "row", pairs)
 
-    def hop(level):
-        moves = (((0, 1), (3, 2)), ((1, 2), (2, 1)), ((2, 3), (1, 0)))[level]
-        return [(a * per + w, b * per + w) for a, b in moves for w in (0, 2)]
-
     def each(moves):
         return [(z * per + a, z * per + b) for z in range(4) for a, b in moves]
 
@@ -180,43 +272,64 @@
         name="head_units",
     )(decoder)
 
-    units, inverse = pl.pallas_call(
-        units_kernel,
-        grid=(blocks,),
-        in_specs=[pl.BlockSpec((BLOCK, width), lambda i: (i, 0))],
-        out_specs=[
-            pl.BlockSpec((BLOCK, width), lambda i: (i, 0)),
-            pl.BlockSpec((BLOCK, 128), lambda i: (i, 0)),
-        ],
-        out_shape=[
-            jax.ShapeDtypeStruct((shard, width), jnp.bfloat16),
-            jax.ShapeDtypeStruct((shard, 128), jnp.float32),
-        ],
-        compiler_params=params(),
-        cost_estimate=cost(4 * shard * width, 4 * shard * width),
-        name="units",
-    )(decoder)
-
-    near = jnp.where(place == 1, chosen_quarter == 0, chosen_quarter == 3)
-    middle = (place == 1) | (place == 2)
-    takes = (within == 2) & (inverse[0, 0] > 0)
-    mine, first, second, third, held = ([None] * PAIRS for _ in range(5))
+    any_spec = pl.BlockSpec(memory_space=pl.ANY)
+    planes = [[z * per + w for z in range(4)] for w in range(per)]
+    across_x = each([(0, 2), (2, 0), (1, 3), (3, 1)])
+    across_core = each([(0, 1), (1, 0), (2, 3), (3, 2)])
+
+    def gather(value):
+        return lax.all_gather(value, "row", axis=0, tiled=True, axis_index_groups=planes)
+
+    piece = step // 2
+    pieces = []
     for k in range(PAIRS):
         across = send(own[2 * k + 1], each([(0, 2)]))
-        mine[k] = jnp.where(takes, across, own[2 * k])
-        first[k] = send(mine[k], hop(0))
-        second[k] = send(jnp.where(here, mine[k], first[k]), hop(1))
-        third[k] = send(jnp.where(here, mine[k], second[k]), hop(2))
-        inner = jnp.where(near, first[k], second[k])
-        held[k] = jnp.where(here, mine[k], jnp.where(middle, inner, third[k]))
+        mine = jnp.where(within == 2, across, own[2 * k])
+        moved = send(mine[:, piece:], each([(0, 1), (2, 3)]))
+        pieces.append(jnp.where(odd_core, moved, mine[:, :piece]))
+
+    units = inverse = None
+    ready = []
+    bounds = [0, blocks // 2, blocks]
+    for part, (low, high) in enumerate(zip(bounds[:-1], bounds[1:])):
+        if high == low:
+            continue
+        operands = [decoder, pieces[min(part, PAIRS - 1)]]
+        specs = [pl.BlockSpec((BLOCK, width), lambda i, low=low: (i + low, 0)), any_spec]
+        aliases = {}
+        if units is not None:
+            aliases = {2: 0, 3: 1}
+            operands += [units, inverse]
+            specs += [any_spec, any_spec]
+        units, inverse = pl.pallas_call(
+            units_kernel,
+            grid=(high - low,),
+            in_specs=specs,
+            out_specs=[
+                pl.BlockSpec((BLOCK, width), lambda i, low=low: (i + low, 0)),
+                pl.BlockSpec((BLOCK, 128), lambda i, low=low: (i + low, 0)),
+            ],
+            out_shape=[
+                jax.ShapeDtypeStruct((shard, width), jnp.bfloat16),
+                jax.ShapeDtypeStruct((shard, 128), jnp.float32),
+            ],
+            input_output_aliases=aliases,
+            compiler_params=params(),
+            cost_estimate=cost(4 * BLOCK * width, 4 * (high - low) * BLOCK * width),
+            name="units",
+        )(*operands)
+        ready.append((inverse[low * BLOCK, 0] < 0).astype(jnp.int32))
+
     chosen = []
     for k in range(PAIRS):
-        other = send(held[k], each([(0, 2), (2, 0)]))
-        core_held = send(held[k], each([(0, 1), (2, 3)]))
-        core_other = send(other, each([(0, 1), (2, 3)]))
-        one = jnp.where(odd_core, core_held, held[k])
-        two = jnp.where(odd_core, core_other, other)
-        pair = [jnp.where(even_chip, one, two), jnp.where(even_chip, two, one)]
+        first_row = chosen_quarter * ROWS + ready[min(k, len(ready) - 1)]
+        found = lax.dynamic_slice_in_dim(gather(pieces[k]), first_row, ROWS, 0)
+        other = send(found, across_x)
+        both = jnp.concatenate(
+            [jnp.where(even_chip, found, other), jnp.where(even_chip, other, found)], axis=1
+        )
+        theirs = send(both, across_core)
+        pair = [jnp.where(odd_core, theirs, both), jnp.where(odd_core, both, theirs)]
         far = 4
         while far < per:
             moves = each([(w, w + far) for w in range(far)])
@@ -265,50 +378,70 @@
             name="weights",
         )(delta, units, chosen[2 * k], chosen[2 * k + 1], partial)
 
-    sums = [None] * COUNT
+    core_side = within % 2
+    plane_x = jnp.reshape((within // 2) % 2, (1,)).astype(jnp.int32)
+    tall = ROWS + 8
+    coded_type = jax.ShapeDtypeStruct((CODED_ROWS, piece // 2), jnp.int32)
+    piece_type = jax.ShapeDtypeStruct((ROWS, piece), jnp.float32)
+    tile_type = jax.ShapeDtypeStruct((8, 128), jnp.float32)
+    vmem = pl.BlockSpec(memory_space=pltpu.VMEM)
+    merge_cost = cost(20 * ROWS * piece, 12 * ROWS * piece)
+
+    def row_part(k, side):
+        return pl.pallas_call(
+            row_kernel,
+            grid_spec=pltpu.PrefetchScalarGridSpec(
+                num_scalar_prefetch=1,
+                grid=(2,),
+                in_specs=[
+                    pl.BlockSpec((ROWS, shard), lambda i, s: (0, 0)),
+                    pl.BlockSpec((8, 128), lambda i, s: (0, 0)),
+                    pl.BlockSpec((shard, piece), lambda i, s: (0, 4 * k + 2 * s[0] + i)),
+                ],
+                out_specs=pl.BlockSpec((tall, piece), lambda i, s: (0, i)),
+            ),
+            out_shape=jax.ShapeDtypeStruct((tall, step), jnp.float32),
+            compiler_params=params(),
+            cost_estimate=cost(half_flops // 2, shard * width // 2),
+            name="row_part",
+        )(jnp.reshape(side, (1,)).astype(jnp.int32), by_row, local_penalty, units)
+
+    coded = []
     for k in range(PAIRS):
-        value = pl.pallas_call(
-            row_kernel,
-            grid=(4,),
-            in_specs=[
-                pl.BlockSpec((ROWS, shard), lambda i: (0, 0)),
-                pl.BlockSpec((shard, step // 2), lambda i, k=k: (0, 4 * k + i)),
-            ],
-            out_specs=pl.BlockSpec((ROWS, step // 2), lambda i: (0, i)),
-            out_shape=jax.ShapeDtypeStruct((ROWS, 2 * step), jnp.float32),
-            compiler_params=params(),
-            cost_estimate=cost(half_flops, shard * width),
-            name="row_part",
-        )(by_row, units)
+        away, near = row_part(k, 1 - core_side), row_part(k, core_side)
         far = per // 2
         while far >= 4:
-            value = value + send(value, each([(w + far, w) for w in range(far)]))
+            moves = each([(w + far, w) for w in range(far)])
+            away, near = away + send(away, moves), near + send(near, moves)
             far //= 2
-        value = value + send(value, each([(1, 0), (3, 2)]))
-        low, high = value[:, :step], value[:, step:]
-        away = jnp.where(even_chip, high, low)
-        kept = jnp.where(even_chip, low, high)
-        kept = kept + send(away, each([(0, 2), (2, 0)]))
-        first_sum = send(kept, hop(0))
-        second_sum = send(kept + first_sum, hop(1))
-        third_sum = send(kept + second_sum, hop(2))
-        total = kept + first_sum + second_sum + third_sum
-        sums[2 * k] = total
-        sums[2 * k + 1] = send(total, each([(2, 0)]))
-
-    penalties = local_penalty
-    far = 1
-    while far < devices:
-        swap = [(i, i ^ far) for i in range(devices)]
-        penalties = penalties + send(penalties, swap)
-        far *= 2
-    penalty = jnp.sum(penalties) * (DW / (ROWS * latents))
+        kept, tile, msg = pl.pallas_call(
+            split_kernel,
+            in_specs=[smem, vmem, vmem],
+            out_specs=[vmem, vmem, vmem],
+            out_shape=[piece_type, tile_type, coded_type],
+            compiler_params=params(),
+            cost_estimate=merge_cost,
+            name="split",
+        )(plane_x, near, send(away, across_core))
+        coded.append(
+            pl.pallas_call(
+                merge_kernel,
+                in_specs=[vmem, vmem, vmem],
+                out_specs=vmem,
+                out_shape=coded_type,
+                compiler_params=params(),
+                cost_estimate=merge_cost,
+                name="merge",
+            )(kept, tile, send(msg, across_x))
+        )
 
     out_type = jax.ShapeDtypeStruct((shard, width), jnp.float32)
-    any_spec = pl.BlockSpec(memory_space=pl.ANY)
+    mark_type = jax.ShapeDtypeStruct((8, 128), jnp.float32)
+    mark_spec = pl.BlockSpec((8, 128), lambda i: (0, 0))
     grad = None
-    bounds = [1, 1 + (blocks - 1) // 2, blocks] if blocks > 2 else [1, blocks]
-    for low, high in zip(bounds[:-1], bounds[1:]):
+    marks = []
+    bounds = [1 + (blocks - 1) * p // 3 for p in range(4)]
+    for part, (low, high) in enumerate(zip(bounds[:-1], bounds[1:])):
         if high == low:
             continue
         operands = [by_col, decoder, inverse, along, *chosen]
@@ -318,26 +451,59 @@
             pl.BlockSpec((BLOCK, 128), lambda i, low=low: (i + low, 0)),
             pl.BlockSpec((BLOCK, 128), lambda i, low=low: (i + low, 0)),
         ] + [whole_chunk] * COUNT
+        operands.append(coded[min(part, PAIRS - 1)])
+        specs.append(any_spec)
         aliases = {}
         if grad is not None:
             aliases = {len(operands): 0}
             operands.append(grad)
             specs.append(any_spec)
         rows = (high - low) * BLOCK
-        grad = pl.pallas_call(
+        grad, mark = pl.pallas_call(
             finish_kernel,
             grid=(high - low,),
             in_specs=specs,
-            out_specs=pl.BlockSpec((BLOCK, width), lambda i, low=low: (i + low, 0)),
-            out_shape=out_type,
+            out_specs=[pl.BlockSpec((BLOCK, width), lambda i, low=low: (i + low, 0)), mark_spec],
+            out_shape=[out_type, mark_type],
             input_output_aliases=aliases,
             compiler_params=params(),
             cost_estimate=cost(2 * ROWS * rows * width, 6 * rows * width),
             name="finish",
         )(*operands)
+        marks.append(mark)
+
+    sums, row_specs = [], []
+    narrow = BLOCK // 2
+    for k in range(PAIRS):
+        ties = marks[:2] if k == 0 else marks[2:]
+        total, tile, msg = pl.pallas_call(
+            total_kernel,
+            in_specs=[vmem] + [any_spec] * len(ties),
+            out_specs=[vmem, vmem, vmem],
+            out_shape=[piece_type, tile_type, coded_type],
+            compiler_params=params(),
+            cost_estimate=merge_cost,
+            name="total",
+        )(gather(coded[k]), *ties)
+        sums.append(total)
+        row_specs.append(pl.BlockSpec((narrow, piece), lambda i: (i, 0)))
+        for source in (2, 1, 3):
+            arrived = send(msg, each([(source, 0)]))
+            sums += [arrived, arrived]
+            row_specs += [
+                pl.BlockSpec((narrow, piece // 2), lambda i: (i, 0)),
+                pl.BlockSpec((8, piece // 2), lambda i: (ROWS // 8, 0)),
+            ]
+        if k == 0:
+            far = 4
+            while far < per:
+                moves = each([(w, w + far) for w in range(far)])
+                fresh = (within >= far) & (within < 2 * far)
+                tile = jnp.where(fresh, send(tile, moves), tile)
+                far *= 2
+            penalty = jnp.sum(tile) * (DW / (ROWS * latents))
 
     owner = jnp.reshape(here & (within == 0), (1,)).astype(jnp.int32)
-    narrow = BLOCK // 2
     operands = [owner, by_col, decoder, inverse, *chosen, *sums]
     specs = [
         smem,
@@ -346,7 +512,7 @@
         pl.BlockSpec((narrow, 128), lambda i: (i, 0)),
     ]
     specs += [whole_chunk] * COUNT
-    specs += [pl.BlockSpec((narrow, step), lambda i: (i, 0))] * COUNT
+    specs += row_specs
     aliases = {}
     if grad is not None:
         aliases = {len(operands): 0}

time: 255 us -> 221 us (0.87)
  Pallas kernels: 48.2 us -> 78 us
  waiting for transfers between devices: 99.1 us -> 73.4 us
  starting transfers between devices: 50.3 us -> 26.7 us
  local copies, waits for them, and re-layouts: 37 us -> 15.1 us
  between operations: 4.24 us -> 18 us
  other arithmetic: 15.2 us -> 8.52 us
    ppermute x30 -> x18, waiting for transfers between devices: 99.1 us -> 42 us  [send(): return lax.ppermute(value, 'row', pairs)]
    all_gather x0 -> x4, waiting for transfers between devices: none -> 31.4 us  [gather(): lax.all_gather(value, 'row', axis=0, tiled=True, axis_index_groups=planes)]
    unnamed x30 -> x36, local copies, waits for them, and re-layouts: 36.5 us -> 11.9 us
    ppermute x30 -> x18, starting transfers between devices: 50.3 us -> 26.5 us  [send(): return lax.ppermute(value, 'row', pairs)]
    pallas_call x3 -> x12, Pallas kernels: 19.3 us -> 37.4 us  [the longest x2 18.1 us: on_device(): pl.pallas_call(units_kernel, grid=(high - low,), in_specs=specs, out_spec...]
    pallas_call x2 -> x3, Pallas kernels: 12.7 us -> 20.1 us  [on_device(): pl.pallas_call(finish_kernel, grid=(high - low,), in_specs=specs, out_spe...]
    add x13 -> x0, other arithmetic: 4.48 us -> none  [the longest x4 2.85 us: on_device(): total = kept + first_sum + second_sum + third_sum]
    select_n x12 -> x8, other arithmetic: 10.2 us -> 6.97 us  [the longest x2 3.21 us: on_device(): jnp.where(odd_core, both, theirs)]
  transfers between devices with their start and end apart: 30 -> 22, of which waited for: 15 -> 12; matrix products, arithmetic and copies ran while one was open for 6% -> 4% of each run, Pallas kernels for 12% -> 27%
where the time goes in v4:
time: 221 us; the launch traced here: 220 us
  Pallas kernels  78 us (35%)
  waiting for transfers between devices  73.4 us (33%)
  starting transfers between devices  26.7 us (12%)
  between operations  18 us (8%)
  local copies, waits for them, and re-layouts  15.1 us (7%)
  other arithmetic  8.52 us (4%)
    ppermute x18, waiting for transfers between devices, send(): return lax.ppermute(value, 'row', pairs)  42 us
    all_gather x4, waiting for transfers between devices, gather(): lax.all_gather(value, 'row', axis=0, tiled=True, axis_index_groups=planes)  31.4 us
    ppermute x18, starting transfers between devices, send(): return lax.ppermute(value, 'row', pairs)  26.5 us
    pallas_call x3, Pallas kernels, on_device(): pl.pallas_call(finish_kernel, grid=(high - low,), in_specs=specs, out_spe...  20.1 us
    pallas_call x2, Pallas kernels, on_device(): pl.pallas_call(units_kernel, grid=(high - low,), in_specs=specs, out_spec...  18.1 us
    pallas_call x4, Pallas kernels, row_part(): pl.pallas_call(row_kernel, grid_spec=pltpu.PrefetchScalarGridSpec(num_sca...  12.8 us
    unnamed x36, local copies, waits for them, and re-layouts  11.9 us
    pallas_call x1, Pallas kernels, on_device(): pl.pallas_call(weight_kernel, grid=(shard // wide,), in_specs=[smem, unit...  6.68 us
  transfers between devices with their start and end apart: 22, of which 12 were waited for; matrix products, arithmetic and copies ran while one was open for 4% of the time, Pallas kernels for 27%

profile of v4, /device:TPU:0, one launch (start us, length us, event | category | flops | bytes accessed | tf_op | source)
XLA Modules:
  0.0 219.7 jit_solution(6282356208739824737)
XLA Ops:
  7.2 2.9 %head_units.1 = (bf16[256,1024]{1,0:T(8,128)(2,1)S(1)}, bf16[256,1024]{1,0:T(8,128)(2,1)S(1)}, bf16[256,1024]{1,0:T(8,128)(2,1)S(1)}, bf16[256,1024]{1,0:T(8,128)(2,1)S(1)}) custom-call(bf16[2048,4096]{1,0:T(8,128)(2,1)} %decoder_ref.13), custom_call_target="tpu_custom_call" | custom-call | flops 4194304 | bytes 4194304 | tf_op jit(solution)/shard_map/head_units/pallas_call | solution.py:264
  10.1 4.9 %collective-permute-start.2 = (bf16[256,1024]{1,0:T(8,128)(2,1)S(1)}, bf16[256,1024]{1,0:T(8,128)(2,1)S(1)}, u32[]{:S(2)}, u32[]{:S(2)}) collective-permute-start(bf16[256,1024]{1,0:T(8,128)(2,1)S(1)} %get-tuple-element.33), channel_id=1, source_target_pairs={{0,2},{4,6},{8,10},{12,14},{16,18},{20,22},{24,26},{28,30}} | collective-permute-start | bytes 1572872 | tf_op jit(solution)/shard_map/ppermute | solution.py:259
  15.0 6.6 %collective-permute-done.2 = bf16[256,1024]{1,0:T(8,128)(2,1)S(1)} collective-permute-done((bf16[256,1024]{1,0:T(8,128)(2,1)S(1)}, bf16[256,1024]{1,0:T(8,128)(2,1)S(1)}, u32[]{:S(2)}, u32[]{:S(2)}) %collective-permute-start.2) | collective-permute-done | bytes 524320 | tf_op jit(solution)/shard_map/ppermute | solution.py:259
  25.0 4.4 %collective-permute-start = (bf16[256,1024]{1,0:T(8,128)(2,1)S(1)}, bf16[256,1024]{1,0:T(8,128)(2,1)S(1)}, u32[]{:S(2)}, u32[]{:S(2)}) collective-permute-start(bf16[256,1024]{1,0:T(8,128)(2,1)S(1)} %get-tuple-element.31), channel_id=1, source_target_pairs={{0,2},{4,6},{8,10},{12,14},{16,18},{20,22},{24,26},{28,30}} | collective-permute-start | bytes 1572872 | tf_op jit(solution)/shard_map/ppermute | solution.py:259
  29.5 6.6 %collective-permute-done = bf16[256,1024]{1,0:T(8,128)(2,1)S(1)} collective-permute-done((bf16[256,1024]{1,0:T(8,128)(2,1)S(1)}, bf16[256,1024]{1,0:T(8,128)(2,1)S(1)}, u32[]{:S(2)}, u32[]{:S(2)}) %collective-permute-start) | collective-permute-done | bytes 524320 | tf_op jit(solution)/shard_map/ppermute | solution.py:259
  40.1 9.1 %units.2 = (bf16[2048,4096]{1,0:T(8,128)(2,1)}, f32[2048,128]{1,0:T(8,128)S(1)}) custom-call(bf16[2048,4096]{1,0:T(8,128)(2,1)} %decoder_ref.13, bf16[256,512]{1,0:T(8,128)(2,1)S(1)} %copy-done.10), custom_call_target="tpu_custom_call" | custom-call | flops 4194304 | bytes 16777216 | tf_op jit(solution)/shard_map/units/pallas_call | solution.py:304
  50.4 5.0 %all-gather.7.cloned.1.call-done = bf16[1024,512]{1,0:T(8,128)(2,1)} async-done(((bf16[256,512]{1,0:T(8,128)(2,1)}), bf16[1024,512]{1,0:T(8,128)(2,1)}) %all-gather.7.cloned.1.call-update) | async-done | bytes 1048592 | tf_op jit(solution)/shard_map/all_gather | solution.py:281
  56.4 1.5 collective-permute-start.6
  57.9 9.0 %units.3 = (bf16[2048,4096]{1,0:T(8,128)(2,1)}, f32[2048,128]{1,0:T(8,128)S(1)}) custom-call(bf16[2048,4096]{1,0:T(8,128)(2,1)} %decoder_ref.13, bf16[256,512]{1,0:T(8,128)(2,1)S(1)} %copy-done.9, bf16[2048,4096]{1,0:T(8,128)(2,1)} %get-tuple-element.35.refs_1_, f32[2048,128]{1,0:T(8,128)S(1)} %get-tuple-element.36.refs_2_), custom_call_target="tpu_custom_call", output_to_operand_aliasing={{0}: (2, {}), {1}: (3, {})} | custom-call | flops 4194304 | bytes 16777216 | tf_op jit(solution)/shard_map/units/pallas_call | solution.py:304
  68.2 16.1 %all-gather.5.cloned.1.call-done = bf16[1024,512]{1,0:T(8,128)(2,1)} async-done(((bf16[256,512]{1,0:T(8,128)(2,1)}), bf16[1024,512]{1,0:T(8,128)(2,1)}) %all-gather.5.cloned.1.call-update) | async-done | bytes 1048592 | tf_op jit(solution)/shard_map/all_gather | solution.py:281
  85.4 1.5 collective-permute-start.4
  88.1 5.2 %collective-permute-done.4 = bf16[256,512]{1,0:T(8,128)(2,1)S(1)} collective-permute-done((bf16[256,512]{1,0:T(8,128)(2,1)S(1)}, bf16[256,512]{1,0:T(8,128)(2,1)S(1)}, u32[]{:S(2)}, u32[]{:S(2)}) %collective-permute-start.4) | collective-permute-done | bytes 262176 | tf_op jit(solution)/shard_map/ppermute | solution.py:259
  96.6 5.6 %part_cosines.1.partial_ref = f32[2048,256]{1,0:T(8,128)S(1)} custom-call(bf16[2048,4096]{1,0:T(8,128)(2,1)} %get-tuple-element.37.units_ref, bf16[256,1024]{1,0:T(8,128)(2,1)S(1)} %get-tuple-element.61.low_ref.refs_0_, bf16[256,1024]{1,0:T(8,128)(2,1)S(1)} %get-tuple-element.60.high_ref.refs_1_), custom_call_target="tpu_custom_call" | custom-call | flops 2147483648 | bytes 8388608 | tf_op jit(solution)/shard_map/part_cosines/pallas_call | solution.py:349
  102.3 1.9 broadcast_select_fusion.2
  104.2 6.7 %weights.1 = (bf16[2048,256]{1,0:T(8,128)(2,1)S(1)}, bf16[256,2048]{1,0:T(8,128)(2,1)S(1)}, f32[2048,128]{1,0:T(8,128)S(1)}, f32[8,128]{1,0:T(8,128)S(1)}) custom-call(s32[1]{0:T(128)} %bitcast.3.delta_ref, bf16[2048,4096]{1,0:T(8,128)(2,1)} %get-tuple-element.37.units_ref, bf16[256,1024]{1,0:T(8,128)(2,1)S(1)} %get-tuple-element.63.low_ref.refs_2_, ...), custom_call_target="tpu_custom_call" | custom-call | flops 2147483648 | bytes 8388608 | tf_op jit(solution)/shard_map/weights/pallas_call | solution.py:360
  112.9 3.5 %row_part.7 = f32[264,1024]{1,0:T(8,128)S(1)} custom-call(s32[1]{0:T(128)} %bitcast.6.side_ref, bf16[256,2048]{1,0:T(8,128)(2,1)S(1)} %get-tuple-element.39.row_ref, f32[8,128]{1,0:T(8,128)S(1)} %get-tuple-element.40.penalty_ref, bf16[2048,4096]{1,0:T(8,128)(2,1)} %get-tuple-element.37.units_ref), custom_call_target="tpu_custom_call" | custom-call | flops 1073741824 | bytes 4194304 | tf_op jit(solution)/shard_map/row_part/pallas_call | solution.py:391
  117.0 3.1 %row_part.6.mine_ref = f32[264,1024]{1,0:T(8,128)S(1)} custom-call(s32[1]{0:T(128)} %bitcast.1.side_ref, bf16[256,2048]{1,0:T(8,128)(2,1)S(1)} %get-tuple-element.39.row_ref, f32[8,128]{1,0:T(8,128)S(1)} %get-tuple-element.40.penalty_ref, bf16[2048,4096]{1,0:T(8,128)(2,1)} %get-tuple-element.37.units_ref), custom_call_target="tpu_custom_call" | custom-call | flops 1073741824 | bytes 4194304 | tf_op jit(solution)/shard_map/row_part/pallas_call | solution.py:391
  120.4 1.5 collective-permute-start.11
  122.0 7.1 %collective-permute-done.11.arrived_ref = s32[272,256]{1,0:T(8,128)S(1)} collective-permute-done((s32[272,256]{1,0:T(8,128)S(1)}, s32[272,256]{1,0:T(8,128)S(1)}, u32[]{:S(2)}, u32[]{:S(2)}) %collective-permute-start.11) | collective-permute-done | bytes 278560 | tf_op jit(solution)/shard_map/ppermute | solution.py:259
  131.4 3.1 %row_part.5 = f32[264,1024]{1,0:T(8,128)S(1)} custom-call(s32[1]{0:T(128)} %bitcast.6.side_ref, bf16[256,2048]{1,0:T(8,128)(2,1)S(1)} %copy-done.5, f32[8,128]{1,0:T(8,128)S(1)} %get-tuple-element.40.penalty_ref, bf16[2048,4096]{1,0:T(8,128)(2,1)} %get-tuple-element.37.units_ref), custom_call_target="tpu_custom_call" | custom-call | flops 1073741824 | bytes 4194304 | tf_op jit(solution)/shard_map/row_part/pallas_call | solution.py:391
  134.6 3.1 %row_part.4.mine_ref = f32[264,1024]{1,0:T(8,128)S(1)} custom-call(s32[1]{0:T(128)} %bitcast.1.side_ref, bf16[256,2048]{1,0:T(8,128)(2,1)S(1)} %copy-done.5, f32[8,128]{1,0:T(8,128)S(1)} %get-tuple-element.40.penalty_ref, bf16[2048,4096]{1,0:T(8,128)(2,1)} %get-tuple-element.37.units_ref), custom_call_target="tpu_custom_call" | custom-call | flops 1073741824 | bytes 4194304 | tf_op jit(solution)/shard_map/row_part/pallas_call | solution.py:391
  138.3 1.5 collective-permute-start.9
  139.8 7.6 %collective-permute-done.9.arrived_ref = s32[272,256]{1,0:T(8,128)S(1)} collective-permute-done((s32[272,256]{1,0:T(8,128)S(1)}, s32[272,256]{1,0:T(8,128)S(1)}, u32[]{:S(2)}, u32[]{:S(2)}) %collective-permute-start.9) | collective-permute-done | bytes 278560 | tf_op jit(solution)/shard_map/ppermute | solution.py:259
  150.9 5.8 %finish.3 = (f32[2048,4096]{1,0:T(8,128)}, f32[8,128]{1,0:T(8,128)S(1)}) custom-call(bf16[2048,256]{1,0:T(8,128)(2,1)S(1)} %copy-done.2, bf16[2048,4096]{1,0:T(8,128)(2,1)} %decoder_ref.13, f32[2048,128]{1,0:T(8,128)S(1)} %get-tuple-element.38.inverse_ref, f32[2048,128]{1,0:T(8,128)S(1)} %copy-done.7, ...), custom_call_target="tpu_custom_call" | custom-call | flops 1073741824 | bytes 12582912 | tf_op jit(solution)/shard_map/finish/pallas_call | solution.py:462
  156.7 5.8 %finish.4 = (f32[2048,4096]{1,0:T(8,128)}, f32[8,128]{1,0:T(8,128)S(1)}) custom-call(bf16[2048,256]{1,0:T(8,128)(2,1)S(1)} %copy-done.2, bf16[2048,4096]{1,0:T(8,128)(2,1)} %decoder_ref.13, f32[2048,128]{1,0:T(8,128)S(1)} %get-tuple-element.38.inverse_ref, f32[2048,128]{1,0:T(8,128)S(1)} %copy-done.7, ...), custom_call_target="tpu_custom_call", output_to_operand_aliasing={{0}: (9, {})} | custom-call | flops 1073741824 | bytes 12582912 | tf_op jit(solution)/shard_map/finish/pallas_call | solution.py:462
  162.5 8.5 %finish.5 = (f32[2048,4096]{1,0:T(8,128)}, f32[8,128]{1,0:T(8,128)S(1)}) custom-call(bf16[2048,256]{1,0:T(8,128)(2,1)S(1)} %copy-done.2, bf16[2048,4096]{1,0:T(8,128)(2,1)} %decoder_ref.13, f32[2048,128]{1,0:T(8,128)S(1)} %get-tuple-element.38.inverse_ref, f32[2048,128]{1,0:T(8,128)S(1)} %copy-done.7, ...), custom_call_target="tpu_custom_call", output_to_operand_aliasing={{0}: (9, {})} | custom-call | flops 1610612736 | bytes 18874368 | tf_op jit(solution)/shard_map/finish/pallas_call | solution.py:462
  172.3 1.8 total.3
  178.8 10.2 %all-gather.9.cloned.1.call-done.gathered_ref = s32[1088,256]{1,0:T(8,128)} async-done(((s32[272,256]{1,0:T(8,128)}), s32[1088,256]{1,0:T(8,128)}) %all-gather.9.cloned.1.call-update) | async-done | bytes 1114128 | tf_op jit(solution)/shard_map/all_gather | solution.py:281
  190.3 1.8 total.2
  198.1 4.4 %collective-permute-done.12.refs_5_.refs_6_ = s32[272,256]{1,0:T(8,128)} collective-permute-done((s32[272,256]{1,0:T(8,128)}, s32[272,256]{1,0:T(8,128)}, u32[]{:S(2)}, u32[]{:S(2)}) %collective-permute-start.12) | collective-permute-done | bytes 278560 | tf_op jit(solution)/shard_map/ppermute | solution.py:259
  202.5 2.1 collective-permute-done.14.refs_9_.refs_10_
  206.7 5.3 %finish_rows.1 = f32[2048,4096]{1,0:T(8,128)} custom-call(s32[1]{0:T(128)} %bitcast.8.owner_ref, bf16[2048,256]{1,0:T(8,128)(2,1)S(1)} %copy-done.3, bf16[2048,4096]{1,0:T(8,128)(2,1)} %decoder_ref.13, f32[2048,128]{1,0:T(8,128)} %copy-done, bf16[256,1024]{1,0:T(8,128)(2,1)S(1)} %get-tuple-element.61.low_ref.refs_0_, ...), custom_call_target="tpu_custom_call", output_to_operand_aliasing={{}: (22, {})} | custom-call | tf_op jit(solution)/shard_map/finish_rows/pallas_call | solution.py:521
  (88 shorter events, 38.2 us)
Async XLA Ops:
  7.2 48.2 %all-gather.7.cloned.1.call-start = ((), (), s32[]{:S(2)}) async-start(), calls=%async_computation.1 | async-start | bytes 1310720 | tf_op jit(solution)/shard_map/all_gather | solution.py:281
  10.1 11.5 %collective-permute-start.2 = (bf16[256,1024]{1,0:T(8,128)(2,1)S(1)}, bf16[256,1024]{1,0:T(8,128)(2,1)S(1)}, u32[]{:S(2)}, u32[]{:S(2)}) collective-permute-start(bf16[256,1024]{1,0:T(8,128)(2,1)S(1)} %get-tuple-element.33), channel_id=1, source_target_pairs={{0,2},{4,6},{8,10},{12,14},{16,18},{20,22},{24,26},{28,30}} | collective-permute-start | bytes 1572872 | tf_op jit(solution)/shard_map/ppermute | solution.py:259
  21.7 2.4 %collective-permute-start.3 = (bf16[256,512]{1,0:T(8,128)(2,1)S(1)}, bf16[256,512]{1,0:T(8,128)(2,1)S(1)}, u32[]{:S(2)}, u32[]{:S(2)}) collective-permute-start(bf16[256,512]{1,0:T(8,128)(2,1)S(1)} %slice.26), channel_id=1, source_target_pairs={{0,1},{2,3},{4,5},{6,7},{8,9},{10,11},{12,13},{14,15},{16,17},{18,... | collective-permute-start | bytes 786440 | tf_op jit(solution)/shard_map/ppermute | solution.py:259
  24.9 15.1 %copy-start.10 = (bf16[256,512]{1,0:T(8,128)(2,1)S(1)}, bf16[256,512]{1,0:T(8,128)(2,1)}, u32[]{:S(2)}) copy-start(bf16[256,512]{1,0:T(8,128)(2,1)} %slice_select_fusion.refs_0_) | copy-start | bytes 786436
  25.0 59.4 %all-gather.5.cloned.1.call-start = ((), (), s32[]{:S(2)}) async-start(), calls=%async_computation | async-start | bytes 1310720 | tf_op jit(solution)/shard_map/all_gather | solution.py:281
  25.0 11.1 %collective-permute-start = (bf16[256,1024]{1,0:T(8,128)(2,1)S(1)}, bf16[256,1024]{1,0:T(8,128)(2,1)S(1)}, u32[]{:S(2)}, u32[]{:S(2)}) collective-permute-start(bf16[256,1024]{1,0:T(8,128)(2,1)S(1)} %get-tuple-element.31), channel_id=1, source_target_pairs={{0,2},{4,6},{8,10},{12,14},{16,18},{20,22},{24,26},{28,30}} | collective-permute-start | bytes 1572872 | tf_op jit(solution)/shard_map/ppermute | solution.py:259
  36.2 2.4 %collective-permute-start.1 = (bf16[256,512]{1,0:T(8,128)(2,1)S(1)}, bf16[256,512]{1,0:T(8,128)(2,1)S(1)}, u32[]{:S(2)}, u32[]{:S(2)}) collective-permute-start(bf16[256,512]{1,0:T(8,128)(2,1)S(1)} %slice.24), channel_id=1, source_target_pairs={{0,1},{2,3},{4,5},{6,7},{8,9},{10,11},{12,13},{14,15},{16,17},{18,... | collective-permute-start | bytes 786440 | tf_op jit(solution)/shard_map/ppermute | solution.py:259
  39.4 131.6 %all-gather.11.cloned.1.call-start = ((), (), s32[]{:S(2)}) async-start(), calls=%async_computation.3 | async-start | bytes 1392640 | tf_op jit(solution)/shard_map/all_gather | solution.py:281
  40.1 17.8 %copy-start.9 = (bf16[256,512]{1,0:T(8,128)(2,1)S(1)}, bf16[256,512]{1,0:T(8,128)(2,1)}, u32[]{:S(2)}) copy-start(bf16[256,512]{1,0:T(8,128)(2,1)} %slice_select_fusion.1.refs_0_) | copy-start | bytes 786436
  56.4 30.6 %collective-permute-start.6 = (bf16[256,512]{1,0:T(8,128)(2,1)S(1)}, bf16[256,512]{1,0:T(8,128)(2,1)S(1)}, u32[]{:S(2)}, u32[]{:S(2)}) collective-permute-start(bf16[256,512]{1,0:T(8,128)(2,1)S(1)} %constant_dynamic-slice_fusion), channel_id=1, source_target_pairs={{0,2},{2,0},{1,3},{3,1},{4,6},{6,4},{5,7},{7,5},{8,10},{10,8},{9,1... | collective-permute-start | bytes 786440 | tf_op jit(solution)/shard_map/ppermute | solution.py:259
  66.9 95.6 %copy-start = (f32[2048,128]{1,0:T(8,128)}, f32[2048,128]{1,0:T(8,128)S(1)}, u32[]{:S(2)}) copy-start(f32[2048,128]{1,0:T(8,128)S(1)} %get-tuple-element.38.inverse_ref) | copy-start | bytes 3145732
  85.4 8.0 %collective-permute-start.4 = (bf16[256,512]{1,0:T(8,128)(2,1)S(1)}, bf16[256,512]{1,0:T(8,128)(2,1)S(1)}, u32[]{:S(2)}, u32[]{:S(2)}) collective-permute-start(bf16[256,512]{1,0:T(8,128)(2,1)S(1)} %constant_dynamic-slice_fusion.1), channel_id=1, source_target_pairs={{0,2},{2,0},{1,3},{3,1},{4,6},{6,4},{5,7},{7,5},{8,10},{10,8},{9,1... | collective-permute-start | bytes 786440 | tf_op jit(solution)/shard_map/ppermute | solution.py:259
  88.1 7.3 %collective-permute-start.7 = (bf16[256,1024]{1,0:T(8,128)(2,1)S(1)}, bf16[256,1024]{1,0:T(8,128)(2,1)}, u32[]{:S(2)}, u32[]{:S(2)}) collective-permute-start(bf16[256,1024]{1,0:T(8,128)(2,1)S(1)} %pad_maximum_fusion.1), channel_id=1, source_target_pairs={{0,1},{1,0},{2,3},{3,2},{4,5},{5,4},{6,7},{7,6},{8,9},{9,8},{10,11... | collective-permute-start | bytes 1572872 | tf_op jit(solution)/shard_map/ppermute | solution.py:259
  94.4 7.8 %copy-start.17 = (bf16[256,512]{1,0:T(8,128)(2,1)}, bf16[256,512]{1,0:T(8,128)(2,1)S(1)}, u32[]{:S(2)}) copy-start(bf16[256,512]{1,0:T(8,128)(2,1)S(1)} %get-tuple-element.67) | copy-start | bytes 786436
  95.3 6.9 %collective-permute-start.5 = (bf16[256,1024]{1,0:T(8,128)(2,1)}, bf16[256,1024]{1,0:T(8,128)(2,1)}, u32[]{:S(2)}, u32[]{:S(2)}) collective-permute-start(bf16[256,1024]{1,0:T(8,128)(2,1)} %pad_maximum_fusion), channel_id=1, source_target_pairs={{0,1},{1,0},{2,3},{3,2},{4,5},{5,4},{6,7},{7,6},{8,9},{9,8},{10,11... | collective-permute-start | bytes 1572872 | tf_op jit(solution)/shard_map/ppermute | solution.py:259
  102.3 2.0 copy-start.8
  112.9 4.1 %copy-start.4 = (bf16[256,2048]{1,0:T(8,128)(2,1)}, bf16[256,2048]{1,0:T(8,128)(2,1)S(1)}, u32[]{:S(2)}) copy-start(bf16[256,2048]{1,0:T(8,128)(2,1)S(1)} %get-tuple-element.39.row_ref) | copy-start | bytes 3145732
  116.4 3.7 %collective-permute-start.10 = (f32[264,1024]{1,0:T(8,128)S(1)}, f32[264,1024]{1,0:T(8,128)S(1)}, u32[]{:S(2)}, u32[]{:S(2)}) collective-permute-start(f32[264,1024]{1,0:T(8,128)S(1)} %row_part.7), channel_id=1, source_target_pairs={{0,1},{1,0},{2,3},{3,2},{4,5},{5,4},{6,7},{7,6},{8,9},{9,8},{10,11... | collective-permute-start | bytes 3244040 | tf_op jit(solution)/shard_map/ppermute | solution.py:259
  120.4 8.7 %collective-permute-start.11 = (s32[272,256]{1,0:T(8,128)S(1)}, s32[272,256]{1,0:T(8,128)S(1)}, u32[]{:S(2)}, u32[]{:S(2)}) collective-permute-start(s32[272,256]{1,0:T(8,128)S(1)} %get-tuple-element.49), channel_id=1, source_target_pairs={{0,2},{2,0},{1,3},{3,1},{4,6},{6,4},{5,7},{7,5},{8,10},{10,8},{9,1... | collective-permute-start | bytes 835592 | tf_op jit(solution)/shard_map/ppermute | solution.py:259
  130.2 58.9 %all-gather.9.cloned.1.call-start = ((), (), s32[]{:S(2)}) async-start(), calls=%async_computation.2 | async-start | bytes 1392640 | tf_op jit(solution)/shard_map/all_gather | solution.py:281
  134.6 3.2 %collective-permute-start.8 = (f32[264,1024]{1,0:T(8,128)S(1)}, f32[264,1024]{1,0:T(8,128)S(1)}, u32[]{:S(2)}, u32[]{:S(2)}) collective-permute-start(f32[264,1024]{1,0:T(8,128)S(1)} %row_part.5), channel_id=1, source_target_pairs={{0,1},{1,0},{2,3},{3,2},{4,5},{5,4},{6,7},{7,6},{8,9},{9,8},{10,11... | collective-permute-start | bytes 3244040 | tf_op jit(solution)/shard_map/ppermute | solution.py:259
  138.3 9.1 %collective-permute-start.9 = (s32[272,256]{1,0:T(8,128)S(1)}, s32[272,256]{1,0:T(8,128)S(1)}, u32[]{:S(2)}, u32[]{:S(2)}) collective-permute-start(s32[272,256]{1,0:T(8,128)S(1)} %get-tuple-element.43), channel_id=1, source_target_pairs={{0,2},{2,0},{1,3},{3,1},{4,6},{6,4},{5,7},{7,5},{8,10},{10,8},{9,1... | collective-permute-start | bytes 835592 | tf_op jit(solution)/shard_map/ppermute | solution.py:259
  149.7 1.2 copy-start.7
  171.0 33.6 %copy-start.3 = (bf16[2048,256]{1,0:T(8,128)(2,1)S(1)}, bf16[2048,256]{1,0:T(8,128)(2,1)}, u32[]{:S(2)}) copy-start(bf16[2048,256]{1,0:T(8,128)(2,1)} %copy-done.1) | copy-start | bytes 3145732
  171.0 1.3 copy-start.11
  174.9 20.6 %collective-permute-start.15 = (s32[272,256]{1,0:T(8,128)}, s32[272,256]{1,0:T(8,128)S(1)}, u32[]{:S(2)}, u32[]{:S(2)}) collective-permute-start(s32[272,256]{1,0:T(8,128)} %get-tuple-element.58), channel_id=1, source_target_pairs={{2,0},{6,4},{10,8},{14,12},{18,16},{22,20},{26,24},{30,28}} | collective-permute-start | bytes 835592 | tf_op jit(solution)/shard_map/ppermute | solution.py:259
  176.2 21.9 %collective-permute-start.16 = (s32[272,256]{1,0:T(8,128)}, s32[272,256]{1,0:T(8,128)}, u32[]{:S(2)}, u32[]{:S(2)}) collective-permute-start(s32[272,256]{1,0:T(8,128)} %get-tuple-element.58), channel_id=1, source_target_pairs={{1,0},{5,4},{9,8},{13,12},{17,16},{21,20},{25,24},{29,28}} | collective-permute-start | bytes 835592 | tf_op jit(solution)/shard_map/ppermute | solution.py:259
  177.5 20.6 %collective-permute-start.17 = (s32[272,256]{1,0:T(8,128)}, s32[272,256]{1,0:T(8,128)}, u32[]{:S(2)}, u32[]{:S(2)}) collective-permute-start(s32[272,256]{1,0:T(8,128)} %get-tuple-element.58), channel_id=1, source_target_pairs={{3,0},{7,4},{11,8},{15,12},{19,16},{23,20},{27,24},{31,28}} | collective-permute-start | bytes 835592 | tf_op jit(solution)/shard_map/ppermute | solution.py:259
  189.1 1.2 copy-start.12
  192.9 9.6 %collective-permute-start.12 = (s32[272,256]{1,0:T(8,128)}, s32[272,256]{1,0:T(8,128)}, u32[]{:S(2)}, u32[]{:S(2)}) collective-permute-start(s32[272,256]{1,0:T(8,128)} %get-tuple-element.54), channel_id=1, source_target_pairs={{2,0},{6,4},{10,8},{14,12},{18,16},{22,20},{26,24},{30,28}} | collective-permute-start | bytes 835592 | tf_op jit(solution)/shard_map/ppermute | solution.py:259
  194.2 8.3 %collective-permute-start.13 = (s32[272,256]{1,0:T(8,128)}, s32[272,256]{1,0:T(8,128)}, u32[]{:S(2)}, u32[]{:S(2)}) collective-permute-start(s32[272,256]{1,0:T(8,128)} %get-tuple-element.54), channel_id=1, source_target_pairs={{1,0},{5,4},{9,8},{13,12},{17,16},{21,20},{25,24},{29,28}} | collective-permute-start | bytes 835592 | tf_op jit(solution)/shard_map/ppermute | solution.py:259
  195.5 9.1 %collective-permute-start.14 = (s32[272,256]{1,0:T(8,128)}, s32[272,256]{1,0:T(8,128)}, u32[]{:S(2)}, u32[]{:S(2)}) collective-permute-start(s32[272,256]{1,0:T(8,128)} %get-tuple-element.54), channel_id=1, source_target_pairs={{3,0},{7,4},{11,8},{15,12},{19,16},{23,20},{27,24},{31,28}} | collective-permute-start | bytes 835592 | tf_op jit(solution)/shard_map/ppermute | solution.py:259
  (8 other events, 8.1 us)
Sparse Core Ops, SparseCore 0:
  25.1 30.1 all-gather.6
  56.9 27.4 all-gather.4
  130.3 28.7 all-gather.10
  160.5 28.4 all-gather.8

commit v5 on v4

--- a/solution.py
+++ b/solution.py
@@ -39,30 +39,23 @@
     step = chunk_refs[0].shape[1]
     rows = slice(0, decoder_ref.shape[0])
     inverse = strip_inverse(decoder_ref, rows)
-    piece = step // 2
-    for k in range(PAIRS):
-        for p in range(4):
-            ref, base = chunk_refs[2 * k + p % 2], (4 * k + p) * piece
-            for t in range(0, piece, 128):
-                v = decoder_ref[rows, base + t : base + t + 128].astype(jnp.float32)
-                to = (p // 2) * piece + t
-                ref[rows, to : to + 128] = (v * inverse).astype(jnp.bfloat16)
+    for k, ref in enumerate(chunk_refs):
+        for t in range(0, step, 128):
+            v = decoder_ref[rows, k * step + t : k * step + t + 128].astype(jnp.float32)
+            ref[rows, t : t + 128] = (v * inverse).astype(jnp.bfloat16)
 
 
 def units_kernel(decoder_ref, *refs):
     units_ref, inverse_ref = refs[-2:]
     strip = 64
 
-    def body(s, carry):
-        rows = pl.ds(pl.multiple_of(s * strip, strip), strip)
+    for base in range(0, decoder_ref.shape[0], strip):
+        rows = slice(base, base + strip)
         inverse = strip_inverse(decoder_ref, rows)
         inverse_ref[rows, :] = jnp.broadcast_to(inverse, (strip, 128))
         for t in range(0, decoder_ref.shape[1], 128):
             v = decoder_ref[rows, t : t + 128].astype(jnp.float32)
             units_ref[rows, t : t + 128] = (v * inverse).astype(jnp.bfloat16)
-        return carry
-
-    lax.fori_loop(0, decoder_ref.shape[0] // strip, body, 0)
 
 
 def pair_cosines(units_ref, low_ref, high_ref):
@@ -164,11 +157,10 @@
     return coded * jnp.abs(coded) * scale
 
 
-def decode_at(msg_ref, base):
-    value = decode(msg_ref[base : base + ROWS, :], msg_ref[base + ROWS : base + ROWS + 8, :])
-    tail = slice(base + ROWS + 8, base + CODED_ROWS)
-    power = msg_ref[tail, 128:].astype(jnp.float32)
-    penalty = msg_ref[tail, :128].astype(jnp.float32) * (jnp.exp2(power) / PENALTY_STEPS)
+def decode_at(msg_ref):
+    value = decode(msg_ref[:ROWS, :], msg_ref[ROWS : ROWS + 8, :])
+    power = msg_ref[ROWS + 8 :, 128:].astype(jnp.float32)
+    penalty = msg_ref[ROWS + 8 :, :128].astype(jnp.float32) * (jnp.exp2(power) / PENALTY_STEPS)
     return value, penalty
 
 
@@ -191,20 +183,15 @@
         divide(high, low)
 
 
-def merge_kernel(kept_ref, penalty_ref, arrived_ref, msg_ref):
-    value, penalty = decode_at(arrived_ref, 0)
-    encode(kept_ref[...] + value, penalty_ref[...] + penalty, msg_ref)
-
-
-def total_kernel(gathered_ref, *refs):
-    total_ref, penalty_ref, msg_ref = refs[-3:]
-    value, penalty = decode_at(gathered_ref, 0)
-    for z in range(1, 4):
-        more, more_penalty = decode_at(gathered_ref, z * CODED_ROWS)
+def merge_kernel(arrived, keep, kept_ref, penalty_ref, *refs):
+    value, penalty = kept_ref[...], penalty_ref[...]
+    for msg_ref in refs[:arrived]:
+        more, more_penalty = decode_at(msg_ref)
         value, penalty = value + more, penalty + more_penalty
-    total_ref[...] = value
-    penalty_ref[...] = penalty
-    encode(value, penalty, msg_ref)
+    if keep:
+        refs[-3][...] = value
+        refs[-2][...] = penalty
+    encode(value, penalty, refs[-1])
 
 
 def last_kernel(owner_ref, col_ref, decoder_ref, inverse_ref, *refs):
@@ -273,41 +260,35 @@
     )(decoder)
 
     any_spec = pl.BlockSpec(memory_space=pl.ANY)
-    planes = [[z * per + w for z in range(4)] for w in range(per)]
     across_x = each([(0, 2), (2, 0), (1, 3), (3, 1)])
     across_core = each([(0, 1), (1, 0), (2, 3), (3, 2)])
-
-    def gather(value):
-        return lax.all_gather(value, "row", axis=0, tiled=True, axis_index_groups=planes)
-
     piece = step // 2
-    pieces = []
-    for k in range(PAIRS):
-        across = send(own[2 * k + 1], each([(0, 2)]))
-        mine = jnp.where(within == 2, across, own[2 * k])
-        moved = send(mine[:, piece:], each([(0, 1), (2, 3)]))
-        pieces.append(jnp.where(odd_core, moved, mine[:, :piece]))
-
-    units = inverse = None
-    ready = []
-    bounds = [0, blocks // 2, blocks]
-    for part, (low, high) in enumerate(zip(bounds[:-1], bounds[1:])):
+
+    def hop(level, lanes):
+        moves = (((0, 1), (3, 2)), ((1, 2), (2, 1)), ((2, 3), (1, 0)))[level]
+        return [(a * per + w, b * per + w) for a, b in moves for w in lanes]
+
+    unit_bounds = [0, blocks // 4, 5 * blocks // 8, blocks]
+    made = [None, None]
+
+    def make_units(part, tie):
+        low, high = unit_bounds[part], unit_bounds[part + 1]
         if high == low:
-            continue
-        operands = [decoder, pieces[min(part, PAIRS - 1)]]
-        specs = [pl.BlockSpec((BLOCK, width), lambda i, low=low: (i + low, 0)), any_spec]
+            return True
+        operands = [decoder, tie]
+        specs = [pl.BlockSpec((BLOCK, width), lambda i: (i + low, 0)), any_spec]
         aliases = {}
-        if units is not None:
+        if made[0] is not None:
             aliases = {2: 0, 3: 1}
-            operands += [units, inverse]
+            operands += made
             specs += [any_spec, any_spec]
-        units, inverse = pl.pallas_call(
+        made[:] = pl.pallas_call(
             units_kernel,
             grid=(high - low,),
             in_specs=specs,
             out_specs=[
-                pl.BlockSpec((BLOCK, width), lambda i, low=low: (i + low, 0)),
-                pl.BlockSpec((BLOCK, 128), lambda i, low=low: (i + low, 0)),
+                pl.BlockSpec((BLOCK, width), lambda i: (i + low, 0)),
+                pl.BlockSpec((BLOCK, 128), lambda i: (i + low, 0)),
             ],
             out_shape=[
                 jax.ShapeDtypeStruct((shard, width), jnp.bfloat16),
@@ -318,18 +299,41 @@
             cost_estimate=cost(4 * BLOCK * width, 4 * (high - low) * BLOCK * width),
             name="units",
         )(*operands)
-        ready.append((inverse[low * BLOCK, 0] < 0).astype(jnp.int32))
-
+        return made[1][low * BLOCK, 0] > 0
+
+    near = jnp.where(place == 1, chosen_quarter == 0, chosen_quarter == 3)
+    middle = (place == 1) | (place == 2)
+    mine, first, second, third, held = ([None] * PAIRS for _ in range(5))
+    across = [send(own[2 * k + 1], each([(0, 2)])) for k in range(PAIRS)]
+    done = make_units(0, own[0])
+    for k in range(PAIRS):
+        takes = (within == 2) & done if k == 0 else within == 2
+        mine[k] = jnp.where(takes, across[k], own[2 * k])
+    for k in range(PAIRS):
+        first[k] = send(mine[k], hop(0, (0, 2)))
+    done = make_units(1, mine[PAIRS - 1])
+    going = [None] * PAIRS
+    for k in range(PAIRS):
+        keeps = here & done if k == 0 else here
+        going[k] = jnp.where(keeps, mine[k], first[k])
+        second[k] = send(going[k], hop(1, (0, 2)))
+    for k in range(PAIRS):
+        going[k] = jnp.where(here, mine[k], second[k])
+        third[k] = send(going[k], hop(2, (0, 2)))
+    done = make_units(2, going[PAIRS - 1])
+    units, inverse = made
+    for k in range(PAIRS):
+        inner = jnp.where(near, first[k], second[k])
+        keeps = here & done if k == 0 else here
+        held[k] = jnp.where(keeps, mine[k], jnp.where(middle, inner, third[k]))
     chosen = []
     for k in range(PAIRS):
-        first_row = chosen_quarter * ROWS + ready[min(k, len(ready) - 1)]
-        found = lax.dynamic_slice_in_dim(gather(pieces[k]), first_row, ROWS, 0)
-        other = send(found, across_x)
-        both = jnp.concatenate(
-            [jnp.where(even_chip, found, other), jnp.where(even_chip, other, found)], axis=1
-        )
-        theirs = send(both, across_core)
-        pair = [jnp.where(odd_core, theirs, both), jnp.where(odd_core, both, theirs)]
+        other = send(held[k], each([(0, 2), (2, 0)]))
+        core_held = send(held[k], each([(0, 1), (2, 3)]))
+        core_other = send(other, each([(0, 1), (2, 3)]))
+        one = jnp.where(odd_core, core_held, held[k])
+        two = jnp.where(odd_core, core_other, other)
+        pair = [jnp.where(even_chip, one, two), jnp.where(even_chip, two, one)]
         far = 4
         while far < per:
             moves = each([(w, w + far) for w in range(far)])
@@ -406,7 +410,20 @@
             name="row_part",
         )(jnp.reshape(side, (1,)).astype(jnp.int32), by_row, local_penalty, units)
 
-    coded = []
+    def merge(kept, arrived, keep, ties=()):
+        tiles = [piece_type, tile_type, coded_type] if keep else [coded_type]
+        result = pl.pallas_call(
+            functools.partial(merge_kernel, len(arrived), keep),
+            in_specs=[vmem] * (2 + len(arrived)) + [any_spec] * len(ties),
+            out_specs=[vmem] * len(tiles),
+            out_shape=tiles,
+            compiler_params=params(),
+            cost_estimate=merge_cost,
+            name="merge",
+        )(*kept, *arrived, *ties)
+        return (tuple(result[:2]), result[2]) if keep else result[0]
+
+    kept, msg = [None] * PAIRS, [None] * PAIRS
     for k in range(PAIRS):
         away, near = row_part(k, 1 - core_side), row_part(k, core_side)
         far = per // 2
@@ -414,7 +431,7 @@
             moves = each([(w + far, w) for w in range(far)])
             away, near = away + send(away, moves), near + send(near, moves)
             far //= 2
-        kept, tile, msg = pl.pallas_call(
+        rest, tile, msg[k] = pl.pallas_call(
             split_kernel,
             in_specs=[smem, vmem, vmem],
             out_specs=[vmem, vmem, vmem],
@@ -423,35 +440,27 @@
             cost_estimate=merge_cost,
             name="split",
         )(plane_x, near, send(away, across_core))
-        coded.append(
-            pl.pallas_call(
-                merge_kernel,
-                in_specs=[vmem, vmem, vmem],
-                out_specs=vmem,
-                out_shape=coded_type,
-                compiler_params=params(),
-                cost_estimate=merge_cost,
-                name="merge",
-            )(kept, tile, send(msg, across_x))
-        )
+        kept[k] = (rest, tile)
 
     out_type = jax.ShapeDtypeStruct((shard, width), jnp.float32)
     mark_type = jax.ShapeDtypeStruct((8, 128), jnp.float32)
     mark_spec = pl.BlockSpec((8, 128), lambda i: (0, 0))
+    bounds = [1 + -(-(blocks - 1) * p // 4) for p in range(5)]
     grad = None
-    marks = []
-    bounds = [1 + (blocks - 1) * p // 3 for p in range(4)]
-    for part, (low, high) in enumerate(zip(bounds[:-1], bounds[1:])):
+
+    def finish(part, tie):
+        nonlocal grad
+        low, high = bounds[part], bounds[part + 1]
         if high == low:
-            continue
+            return []
         operands = [by_col, decoder, inverse, along, *chosen]
         specs = [
-            pl.BlockSpec((BLOCK, ROWS), lambda i, low=low: (i + low, 0)),
-            pl.BlockSpec((BLOCK, width), lambda i, low=low: (i + low, 0)),
-            pl.BlockSpec((BLOCK, 128), lambda i, low=low: (i + low, 0)),
-            pl.BlockSpec((BLOCK, 128), lambda i, low=low: (i + low, 0)),
+            pl.BlockSpec((BLOCK, ROWS), lambda i: (i + low, 0)),
+            pl.BlockSpec((BLOCK, width), lambda i: (i + low, 0)),
+            pl.BlockSpec((BLOCK, 128), lambda i: (i + low, 0)),
+            pl.BlockSpec((BLOCK, 128), lambda i: (i + low, 0)),
         ] + [whole_chunk] * COUNT
-        operands.append(coded[min(part, PAIRS - 1)])
+        operands.append(tie)
         specs.append(any_spec)
         aliases = {}
         if grad is not None:
@@ -463,45 +472,53 @@
             finish_kernel,
             grid=(high - low,),
             in_specs=specs,
-            out_specs=[pl.BlockSpec((BLOCK, width), lambda i, low=low: (i + low, 0)), mark_spec],
+            out_specs=[pl.BlockSpec((BLOCK, width), lambda i: (i + low, 0)), mark_spec],
             out_shape=[out_type, mark_type],
             input_output_aliases=aliases,
             compiler_params=params(),
             cost_estimate=cost(2 * ROWS * rows * width, 6 * rows * width),
             name="finish",
         )(*operands)
-        marks.append(mark)
+        return [mark]
+
+    lanes = range(4)
+    across = [send(msg[k], across_x) for k in range(PAIRS)]
+    ties = finish(0, msg[PAIRS - 1])
+    for k in range(PAIRS):
+        kept[k], msg[k] = merge(kept[k], [across[k]], True, () if k else ties)
+    arrivals = [[] for _ in range(PAIRS)]
+    for level in range(3):
+        for k in range(PAIRS):
+            arrivals[k].append(send(msg[k], hop(level, lanes)))
+        ties = finish(level + 1, msg[PAIRS - 1])
+        for k in range(PAIRS):
+            tied = () if k else ties
+            if level < 2:
+                msg[k] = merge(kept[k], arrivals[k][-1:], False, tied)
+            else:
+                kept[k], msg[k] = merge(kept[k], arrivals[k], True, tied)
+
+    tile = kept[0][1]
+    far = 4
+    while far < per:
+        moves = each([(w, w + far) for w in range(far)])
+        fresh = (within >= far) & (within < 2 * far)
+        tile = jnp.where(fresh, send(tile, moves), tile)
+        far *= 2
+    penalty = jnp.sum(tile) * (DW / (ROWS * latents))
 
     sums, row_specs = [], []
     narrow = BLOCK // 2
     for k in range(PAIRS):
-        ties = marks[:2] if k == 0 else marks[2:]
-        total, tile, msg = pl.pallas_call(
-            total_kernel,
-            in_specs=[vmem] + [any_spec] * len(ties),
-            out_specs=[vmem, vmem, vmem],
-            out_shape=[piece_type, tile_type, coded_type],
-            compiler_params=params(),
-            cost_estimate=merge_cost,
-            name="total",
-        )(gather(coded[k]), *ties)
-        sums.append(total)
+        sums.append(kept[k][0])
         row_specs.append(pl.BlockSpec((narrow, piece), lambda i: (i, 0)))
         for source in (2, 1, 3):
-            arrived = send(msg, each([(source, 0)]))
+            arrived = send(msg[k], each([(source, 0)]))
             sums += [arrived, arrived]
             row_specs += [
                 pl.BlockSpec((narrow, piece // 2), lambda i: (i, 0)),
                 pl.BlockSpec((8, piece // 2), lambda i: (ROWS // 8, 0)),
             ]
-        if k == 0:
-            far = 4
-            while far < per:
-                moves = each([(w, w + far) for w in range(far)])
-                fresh = (within >= far) & (within < 2 * far)
-                tile = jnp.where(fresh, send(tile, moves), tile)
-                far *= 2
-            penalty = jnp.sum(tile) * (DW / (ROWS * latents))
 
     owner = jnp.reshape(here & (within == 0), (1,)).astype(jnp.int32)
     operands = [owner, by_col, decoder, inverse, *chosen, *sums]

time: 221 us -> 190 us (0.86)
  waiting for transfers between devices: 73.4 us -> 22.6 us
  starting transfers between devices: 26.7 us -> 62.7 us
  between operations: 18 us -> 5.6 us
  local copies, waits for them, and re-layouts: 15.1 us -> 10.1 us
    ppermute x18 -> x30, starting transfers between devices: 26.5 us -> 62.7 us  [send(): return lax.ppermute(value, 'row', pairs)]
    all_gather x4 -> x0, waiting for transfers between devices: 31.4 us -> none  [gather(): lax.all_gather(value, 'row', axis=0, tiled=True, axis_index_groups=planes)]
    ppermute x18 -> x30, waiting for transfers between devices: 42 us -> 22.6 us  [send(): return lax.ppermute(value, 'row', pairs)]
    unnamed x36 -> x28, local copies, waits for them, and re-layouts: 11.9 us -> 8.54 us
    pallas_call x9 -> x15, Pallas kernels: 43.9 us -> 46.7 us  [the longest x4 21.8 us: finish(): pl.pallas_call(finish_kernel, grid=(high - low,), in_specs=specs, out_spe...]
    select_n x8 -> x10, other arithmetic: 6.97 us -> 7.16 us  [the longest x2 3.42 us: on_device(): held[k] = jnp.where(keeps, mine[k], jnp.where(middle, inner, third[k]))]
  transfers between devices with their start and end apart: 22 -> 30, of which waited for: 12 -> 8; matrix products, arithmetic and copies ran while one was open for 4% -> 5% of each run, Pallas kernels for 27% -> 33%
where the time goes in v5:
time: 190 us; the launch traced here: 189 us
  Pallas kernels  80.2 us (42%)
  starting transfers between devices  62.7 us (33%)
  waiting for transfers between devices  22.6 us (12%)
  local copies, waits for them, and re-layouts  10.1 us (5%)
  other arithmetic  7.76 us (4%)
  between operations  5.6 us (3%)
    ppermute x30, starting transfers between devices, send(): return lax.ppermute(value, 'row', pairs)  62.7 us
    ppermute x30, waiting for transfers between devices, send(): return lax.ppermute(value, 'row', pairs)  22.6 us
    pallas_call x4, Pallas kernels, finish(): pl.pallas_call(finish_kernel, grid=(high - low,), in_specs=specs, out_spe...  21.8 us
    pallas_call x3, Pallas kernels, make_units(): pl.pallas_call(units_kernel, grid=(high - low,), in_specs=specs, out_spec...  20.1 us
    pallas_call x4, Pallas kernels, row_part(): pl.pallas_call(row_kernel, grid_spec=pltpu.PrefetchScalarGridSpec(num_sca...  12.5 us
    unnamed x28, local copies, waits for them, and re-layouts  8.54 us
    pallas_call x1, Pallas kernels, on_device(): pl.pallas_call(weight_kernel, grid=(shard // wide,), in_specs=[smem, unit...  6.67 us
    pallas_call x1, Pallas kernels, on_device(): pl.pallas_call(partial_kernel, grid=(shard // wide,), in_specs=[unit_spec...  5.61 us
  transfers between devices with their start and end apart: 30, of which 8 were waited for; matrix products, arithmetic and copies ran while one was open for 5% of the time, Pallas kernels for 33%

profile of v5, /device:TPU:0, one launch (start us, length us, event | category | flops | bytes accessed | tf_op | source)
XLA Modules:
  0.0 189.0 jit_solution(15650371455355653991)
XLA Ops:
  0.6 2.9 %head_units.1 = (bf16[256,1024]{1,0:T(8,128)(2,1)S(1)}, bf16[256,1024]{1,0:T(8,128)(2,1)S(1)}, bf16[256,1024]{1,0:T(8,128)(2,1)S(1)}, bf16[256,1024]{1,0:T(8,128)(2,1)S(1)}) custom-call(bf16[2048,4096]{1,0:T(8,128)(2,1)} %decoder_ref.17), custom_call_target="tpu_custom_call" | custom-call | flops 4194304 | bytes 4194304 | tf_op jit(solution)/shard_map/head_units/pallas_call | solution.py:251
  3.5 5.7 %collective-permute-start.7 = (bf16[256,1024]{1,0:T(8,128)(2,1)S(1)}, bf16[256,1024]{1,0:T(8,128)(2,1)}, u32[]{:S(2)}, u32[]{:S(2)}) collective-permute-start(bf16[256,1024]{1,0:T(8,128)(2,1)S(1)} %get-tuple-element.50), channel_id=1, source_target_pairs={{0,2},{4,6},{8,10},{12,14},{16,18},{20,22},{24,26},{28,30}} | collective-permute-start | bytes 1572872 | tf_op jit(solution)/shard_map/ppermute | solution.py:246
  9.2 2.1 %collective-permute-start = (bf16[256,1024]{1,0:T(8,128)(2,1)S(1)}, bf16[256,1024]{1,0:T(8,128)(2,1)}, u32[]{:S(2)}, u32[]{:S(2)}) collective-permute-start(bf16[256,1024]{1,0:T(8,128)(2,1)S(1)} %get-tuple-element.41), channel_id=1, source_target_pairs={{0,2},{4,6},{8,10},{12,14},{16,18},{20,22},{24,26},{28,30}} | collective-permute-start | bytes 1572872 | tf_op jit(solution)/shard_map/ppermute | solution.py:246
  11.3 4.6 %units.3 = (bf16[2048,4096]{1,0:T(8,128)(2,1)}, f32[2048,128]{1,0:T(8,128)S(1)}) custom-call(bf16[2048,4096]{1,0:T(8,128)(2,1)} %decoder_ref.17, bf16[256,1024]{1,0:T(8,128)(2,1)S(1)} %get-tuple-element.43.refs_0_), custom_call_target="tpu_custom_call" | custom-call | flops 4194304 | bytes 8388608 | tf_op jit(solution)/shard_map/units/pallas_call | solution.py:285
  17.2 4.3 %collective-permute-start.8 = (bf16[256,1024]{1,0:T(8,128)(2,1)S(1)}, bf16[256,1024]{1,0:T(8,128)(2,1)}, u32[]{:S(2)}, u32[]{:S(2)}) collective-permute-start(bf16[256,1024]{1,0:T(8,128)(2,1)S(1)} %broadcast_select_fusion.1), channel_id=1, source_target_pairs={{0,4},{2,6},{12,8},{14,10},{16,20},{18,22},{28,24},{30,26}} | collective-permute-start | bytes 1572872 | tf_op jit(solution)/shard_map/ppermute | solution.py:246
  21.6 2.7 %collective-permute-start.1 = (bf16[256,1024]{1,0:T(8,128)(2,1)S(1)}, bf16[256,1024]{1,0:T(8,128)(2,1)S(1)}, u32[]{:S(2)}, u32[]{:S(2)}) collective-permute-start(bf16[256,1024]{1,0:T(8,128)(2,1)S(1)} %broadcast_select_fusion.10.refs_0_), channel_id=1, source_target_pairs={{0,4},{2,6},{12,8},{14,10},{16,20},{18,22},{28,24},{30,26}} | collective-permute-start | bytes 1572872 | tf_op jit(solution)/shard_map/ppermute | solution.py:246
  24.9 7.7 %units.4 = (bf16[2048,4096]{1,0:T(8,128)(2,1)}, f32[2048,128]{1,0:T(8,128)S(1)}) custom-call(bf16[2048,4096]{1,0:T(8,128)(2,1)} %decoder_ref.17, bf16[256,1024]{1,0:T(8,128)(2,1)S(1)} %broadcast_select_fusion.10.refs_0_, bf16[2048,4096]{1,0:T(8,128)(2,1)} %get-tuple-element.44.refs_1_, ...), custom_call_target="tpu_custom_call", output_to_operand_aliasing={{0}: (2, {}), {1}: (3, {})} | custom-call | flops 4194304 | bytes 12582912 | tf_op jit(solution)/shard_map/units/pallas_call | solution.py:285
  40.9 7.7 %units.5 = (bf16[2048,4096]{1,0:T(8,128)(2,1)}, f32[2048,128]{1,0:T(8,128)S(1)}) custom-call(bf16[2048,4096]{1,0:T(8,128)(2,1)} %decoder_ref.17, bf16[256,1024]{1,0:T(8,128)(2,1)S(1)} %broadcast_select_fusion.12.refs_0_, bf16[2048,4096]{1,0:T(8,128)(2,1)} %get-tuple-element.46.refs_1_, ...), custom_call_target="tpu_custom_call", output_to_operand_aliasing={{0}: (2, {}), {1}: (3, {})} | custom-call | flops 4194304 | bytes 12582912 | tf_op jit(solution)/shard_map/units/pallas_call | solution.py:285
  49.8 4.8 %collective-permute-done.10 = bf16[256,1024]{1,0:T(8,128)(2,1)} collective-permute-done((bf16[256,1024]{1,0:T(8,128)(2,1)}, bf16[256,1024]{1,0:T(8,128)(2,1)}, u32[]{:S(2)}, u32[]{:S(2)}) %collective-permute-start.10) | collective-permute-done | bytes 524320 | tf_op jit(solution)/shard_map/ppermute | solution.py:246
  54.7 2.1 %select_select_fusion = bf16[256,1024]{1,0:T(8,128)(2,1)} fusion(bf16[256,1024]{1,0:T(8,128)(2,1)S(1)} %broadcast_select_fusion.1, bf16[256,1024]{1,0:T(8,128)(2,1)} %collective-permute-done.10, bf16[256,1024]{1,0:T(8,128)(2,1)} %collective-permute-done.8, bf16[256,1024]{1,0:T(8,128)(2,1)} %copy-done.11, pred[]{:T(512)S(6)} %and.43, pred[]{:T(512)S(6)} %select_n.144, ...), kind=kLoop, calls=%fused_computation | loop fusion | flops 786432 | bytes 2621443 | tf_op jit(solution)/shard_map/jit(_where)/select_n | solution.py:328
  56.8 5.5 %collective-permute-start.12 = (bf16[256,1024]{1,0:T(8,128)(2,1)}, bf16[256,1024]{1,0:T(8,128)(2,1)S(1)}, u32[]{:S(2)}, u32[]{:S(2)}) collective-permute-start(bf16[256,1024]{1,0:T(8,128)(2,1)} %select_select_fusion), channel_id=1, source_target_pairs={{0,2},{2,0},{4,6},{6,4},{8,10},{10,8},{12,14},{14,12},{16,18},{18,... | collective-permute-start | bytes 1572872 | tf_op jit(solution)/shard_map/ppermute | solution.py:246
  63.6 3.5 %collective-permute-start.5 = (bf16[256,1024]{1,0:T(8,128)(2,1)S(1)}, bf16[256,1024]{1,0:T(8,128)(2,1)S(1)}, u32[]{:S(2)}, u32[]{:S(2)}) collective-permute-start(bf16[256,1024]{1,0:T(8,128)(2,1)S(1)} %select_select_fusion.1), channel_id=1, source_target_pairs={{0,2},{2,0},{4,6},{6,4},{8,10},{10,8},{12,14},{14,12},{16,18},{18,... | collective-permute-start | bytes 1572872 | tf_op jit(solution)/shard_map/ppermute | solution.py:246
  69.7 2.1 %collective-permute-start.13 = (bf16[256,1024]{1,0:T(8,128)(2,1)S(1)}, bf16[256,1024]{1,0:T(8,128)(2,1)}, u32[]{:S(2)}, u32[]{:S(2)}) collective-permute-start(bf16[256,1024]{1,0:T(8,128)(2,1)S(1)} %collective-permute-done.12), channel_id=1, source_target_pairs={{0,1},{2,3},{4,5},{6,7},{8,9},{10,11},{12,13},{14,15},{16,17},{18,... | collective-permute-start | bytes 1572872 | tf_op jit(solution)/shard_map/ppermute | solution.py:246
  71.7 2.1 %collective-permute-start.4 = (bf16[256,1024]{1,0:T(8,128)(2,1)S(1)}, bf16[256,1024]{1,0:T(8,128)(2,1)}, u32[]{:S(2)}, u32[]{:S(2)}) collective-permute-start(bf16[256,1024]{1,0:T(8,128)(2,1)S(1)} %select_select_fusion.1), channel_id=1, source_target_pairs={{0,1},{2,3},{4,5},{6,7},{8,9},{10,11},{12,13},{14,15},{16,17},{18,... | collective-permute-start | bytes 1572872 | tf_op jit(solution)/shard_map/ppermute | solution.py:246
  75.3 2.1 %collective-permute-start.6 = (bf16[256,1024]{1,0:T(8,128)(2,1)S(1)}, bf16[256,1024]{1,0:T(8,128)(2,1)}, u32[]{:S(2)}, u32[]{:S(2)}) collective-permute-start(bf16[256,1024]{1,0:T(8,128)(2,1)S(1)} %collective-permute-done.5), channel_id=1, source_target_pairs={{0,1},{2,3},{4,5},{6,7},{8,9},{10,11},{12,13},{14,15},{16,17},{18,... | collective-permute-start | bytes 1572872 | tf_op jit(solution)/shard_map/ppermute | solution.py:246
  79.5 5.6 %part_cosines.1.partial_ref = f32[2048,256]{1,0:T(8,128)S(1)} custom-call(bf16[2048,4096]{1,0:T(8,128)(2,1)} %get-tuple-element.48.units_ref, bf16[256,1024]{1,0:T(8,128)(2,1)S(1)} %get-tuple-element.81.low_ref.refs_0_, bf16[256,1024]{1,0:T(8,128)(2,1)S(1)} %get-tuple-element.80.high_ref.refs_1_), custom_call_target="tpu_custom_call" | custom-call | flops 2147483648 | bytes 8388608 | tf_op jit(solution)/shard_map/part_cosines/pallas_call | solution.py:353
  86.5 6.7 %weights.1 = (bf16[2048,256]{1,0:T(8,128)(2,1)S(1)}, bf16[256,2048]{1,0:T(8,128)(2,1)S(1)}, f32[2048,128]{1,0:T(8,128)S(1)}, f32[8,128]{1,0:T(8,128)S(1)}) custom-call(s32[1]{0:T(128)} %bitcast.3.delta_ref, bf16[2048,4096]{1,0:T(8,128)(2,1)} %get-tuple-element.48.units_ref, bf16[256,1024]{1,0:T(8,128)(2,1)S(1)} %get-tuple-element.83.low_ref.refs_2_, ...), custom_call_target="tpu_custom_call" | custom-call | flops 2147483648 | bytes 8388608 | tf_op jit(solution)/shard_map/weights/pallas_call | solution.py:364
  93.1 3.1 %row_part.5 = f32[264,1024]{1,0:T(8,128)S(1)} custom-call(s32[1]{0:T(128)} %bitcast.7.side_ref, bf16[256,2048]{1,0:T(8,128)(2,1)S(1)} %get-tuple-element.51.row_ref, f32[8,128]{1,0:T(8,128)S(1)} %get-tuple-element.52.penalty_ref, bf16[2048,4096]{1,0:T(8,128)(2,1)} %get-tuple-element.48.units_ref), custom_call_target="tpu_custom_call" | custom-call | flops 1073741824 | bytes 4194304 | tf_op jit(solution)/shard_map/row_part/pallas_call | solution.py:395
  96.3 3.1 %row_part.7 = f32[264,1024]{1,0:T(8,128)S(1)} custom-call(s32[1]{0:T(128)} %bitcast.7.side_ref, bf16[256,2048]{1,0:T(8,128)(2,1)S(1)} %get-tuple-element.51.row_ref, f32[8,128]{1,0:T(8,128)S(1)} %get-tuple-element.52.penalty_ref, bf16[2048,4096]{1,0:T(8,128)(2,1)} %get-tuple-element.48.units_ref), custom_call_target="tpu_custom_call" | custom-call | flops 1073741824 | bytes 4194304 | tf_op jit(solution)/shard_map/row_part/pallas_call | solution.py:395
  100.0 3.1 %row_part.4.mine_ref = f32[264,1024]{1,0:T(8,128)S(1)} custom-call(s32[1]{0:T(128)} %bitcast.1.side_ref, bf16[256,2048]{1,0:T(8,128)(2,1)S(1)} %get-tuple-element.51.row_ref, f32[8,128]{1,0:T(8,128)S(1)} %get-tuple-element.52.penalty_ref, bf16[2048,4096]{1,0:T(8,128)(2,1)} %get-tuple-element.48.units_ref), custom_call_target="tpu_custom_call" | custom-call | flops 1073741824 | bytes 4194304 | tf_op jit(solution)/shard_map/row_part/pallas_call | solution.py:395
  103.5 2.1 %collective-permute-start.15 = (s32[272,256]{1,0:T(8,128)S(1)}, s32[272,256]{1,0:T(8,128)S(1)}, u32[]{:S(2)}, u32[]{:S(2)}) collective-permute-start(s32[272,256]{1,0:T(8,128)S(1)} %get-tuple-element.55), channel_id=1, source_target_pairs={{0,2},{2,0},{1,3},{3,1},{4,6},{6,4},{5,7},{7,5},{8,10},{10,8},{9,1... | collective-permute-start | bytes 835592 | tf_op jit(solution)/shard_map/ppermute | solution.py:246
  105.6 3.1 %row_part.6.mine_ref = f32[264,1024]{1,0:T(8,128)S(1)} custom-call(s32[1]{0:T(128)} %bitcast.1.side_ref, bf16[256,2048]{1,0:T(8,128)(2,1)S(1)} %get-tuple-element.51.row_ref, f32[8,128]{1,0:T(8,128)S(1)} %get-tuple-element.52.penalty_ref, bf16[2048,4096]{1,0:T(8,128)(2,1)} %get-tuple-element.48.units_ref), custom_call_target="tpu_custom_call" | custom-call | flops 1073741824 | bytes 4194304 | tf_op jit(solution)/shard_map/row_part/pallas_call | solution.py:395
  109.1 5.8 %finish.4 = (f32[2048,4096]{1,0:T(8,128)}, f32[8,128]{1,0:T(8,128)S(1)}) custom-call(bf16[2048,256]{1,0:T(8,128)(2,1)S(1)} %get-tuple-element.56.col_ref, bf16[2048,4096]{1,0:T(8,128)(2,1)} %decoder_ref.17, f32[2048,128]{1,0:T(8,128)S(1)} %get-tuple-element.49.inverse_ref, f32[2048,128]{1,0:T(8,128)S(1)} %get-tuple-element.57.along_ref, ...), custom_call_target="tpu_custom_call" | custom-call | flops 1073741824 | bytes 12582912 | tf_op jit(solution)/shard_map/finish/pallas_call | solution.py:471
  115.2 9.6 %collective-permute-start.17 = (s32[272,256]{1,0:T(8,128)S(1)}, s32[272,256]{1,0:T(8,128)S(1)}, u32[]{:S(2)}, u32[]{:S(2)}) collective-permute-start(s32[272,256]{1,0:T(8,128)S(1)} %get-tuple-element.62), channel_id=1, source_target_pairs={{0,4},{1,5},{2,6},{3,7},{12,8},{13,9},{14,10},{15,11},{16,20},{17,... | collective-permute-start | bytes 835592 | tf_op jit(solution)/shard_map/ppermute | solution.py:246
  125.2 3.3 %collective-permute-start.20 = (s32[272,256]{1,0:T(8,128)S(1)}, s32[272,256]{1,0:T(8,128)S(1)}, u32[]{:S(2)}, u32[]{:S(2)}) collective-permute-start(s32[272,256]{1,0:T(8,128)S(1)} %get-tuple-element.65.refs_4_), channel_id=1, source_target_pairs={{0,4},{1,5},{2,6},{3,7},{12,8},{13,9},{14,10},{15,11},{16,20},{17,... | collective-permute-start | bytes 835592 | tf_op jit(solution)/shard_map/ppermute | solution.py:246
  128.5 5.8 %finish.5 = (f32[2048,4096]{1,0:T(8,128)}, f32[8,128]{1,0:T(8,128)S(1)}) custom-call(bf16[2048,256]{1,0:T(8,128)(2,1)S(1)} %get-tuple-element.56.col_ref, bf16[2048,4096]{1,0:T(8,128)(2,1)} %decoder_ref.17, f32[2048,128]{1,0:T(8,128)S(1)} %get-tuple-element.49.inverse_ref, ...), custom_call_target="tpu_custom_call", output_to_operand_aliasing={{0}: (9, {})} | custom-call | flops 1073741824 | bytes 12582912 | tf_op jit(solution)/shard_map/finish/pallas_call | solution.py:471
  137.6 5.8 %finish.6 = (f32[2048,4096]{1,0:T(8,128)}, f32[8,128]{1,0:T(8,128)S(1)}) custom-call(bf16[2048,256]{1,0:T(8,128)(2,1)S(1)} %get-tuple-element.56.col_ref, bf16[2048,4096]{1,0:T(8,128)(2,1)} %decoder_ref.17, f32[2048,128]{1,0:T(8,128)S(1)} %get-tuple-element.49.inverse_ref, ...), custom_call_target="tpu_custom_call", output_to_operand_aliasing={{0}: (9, {})} | custom-call | flops 1073741824 | bytes 12582912 | tf_op jit(solution)/shard_map/finish/pallas_call | solution.py:471
  146.7 4.4 %finish.7 = (f32[2048,4096]{1,0:T(8,128)}, f32[8,128]{1,0:T(8,128)S(1)}) custom-call(bf16[2048,256]{1,0:T(8,128)(2,1)S(1)} %get-tuple-element.56.col_ref, bf16[2048,4096]{1,0:T(8,128)(2,1)} %decoder_ref.17, f32[2048,128]{1,0:T(8,128)S(1)} %get-tuple-element.49.inverse_ref, ...), custom_call_target="tpu_custom_call", output_to_operand_aliasing={{0}: (9, {})} | custom-call | flops 536870912 | bytes 6291456 | tf_op jit(solution)/shard_map/finish/pallas_call | solution.py:471
  151.1 7.2 %collective-permute-done.21.refs_2_ = s32[272,256]{1,0:T(8,128)S(1)} collective-permute-done((s32[272,256]{1,0:T(8,128)S(1)}, s32[272,256]{1,0:T(8,128)S(1)}, u32[]{:S(2)}, u32[]{:S(2)}) %collective-permute-start.21) | collective-permute-done | bytes 278560 | tf_op jit(solution)/shard_map/ppermute | solution.py:246
  172.8 2.5 %collective-permute-done.27.refs_12_.refs_13_ = s32[272,256]{1,0:T(8,128)S(1)} collective-permute-done((s32[272,256]{1,0:T(8,128)}, s32[272,256]{1,0:T(8,128)S(1)}, u32[]{:S(2)}, u32[]{:S(2)}) %collective-permute-start.27) | collective-permute-done | bytes 278560 | tf_op jit(solution)/shard_map/ppermute | solution.py:246
  175.4 3.1 %collective-permute-done.29.refs_16_.refs_17_ = s32[272,256]{1,0:T(8,128)} collective-permute-done((s32[272,256]{1,0:T(8,128)}, s32[272,256]{1,0:T(8,128)}, u32[]{:S(2)}, u32[]{:S(2)}) %collective-permute-start.29) | collective-permute-done | bytes 278560 | tf_op jit(solution)/shard_map/ppermute | solution.py:246
  182.6 5.2 %finish_rows.1 = f32[2048,4096]{1,0:T(8,128)} custom-call(s32[1]{0:T(128)} %bitcast.9.owner_ref, bf16[2048,256]{1,0:T(8,128)(2,1)S(1)} %get-tuple-element.56.col_ref, bf16[2048,4096]{1,0:T(8,128)(2,1)} %decoder_ref.17, f32[2048,128]{1,0:T(8,128)} %copy-done, ...), custom_call_target="tpu_custom_call", output_to_operand_aliasing={{}: (22, {})} | custom-call | tf_op jit(solution)/shard_map/finish_rows/pallas_call | solution.py:538
  (95 shorter events, 43.7 us)
Async XLA Ops:
  3.5 13.6 %collective-permute-start.7 = (bf16[256,1024]{1,0:T(8,128)(2,1)S(1)}, bf16[256,1024]{1,0:T(8,128)(2,1)}, u32[]{:S(2)}, u32[]{:S(2)}) collective-permute-start(bf16[256,1024]{1,0:T(8,128)(2,1)S(1)} %get-tuple-element.50), channel_id=1, source_target_pairs={{0,2},{4,6},{8,10},{12,14},{16,18},{20,22},{24,26},{28,30}} | collective-permute-start | bytes 1572872 | tf_op jit(solution)/shard_map/ppermute | solution.py:246
  9.2 12.3 %collective-permute-start = (bf16[256,1024]{1,0:T(8,128)(2,1)S(1)}, bf16[256,1024]{1,0:T(8,128)(2,1)}, u32[]{:S(2)}, u32[]{:S(2)}) collective-permute-start(bf16[256,1024]{1,0:T(8,128)(2,1)S(1)} %get-tuple-element.41), channel_id=1, source_target_pairs={{0,2},{4,6},{8,10},{12,14},{16,18},{20,22},{24,26},{28,30}} | collective-permute-start | bytes 1572872 | tf_op jit(solution)/shard_map/ppermute | solution.py:246
  17.2 16.7 %collective-permute-start.8 = (bf16[256,1024]{1,0:T(8,128)(2,1)S(1)}, bf16[256,1024]{1,0:T(8,128)(2,1)}, u32[]{:S(2)}, u32[]{:S(2)}) collective-permute-start(bf16[256,1024]{1,0:T(8,128)(2,1)S(1)} %broadcast_select_fusion.1), channel_id=1, source_target_pairs={{0,4},{2,6},{12,8},{14,10},{16,20},{18,22},{28,24},{30,26}} | collective-permute-start | bytes 1572872 | tf_op jit(solution)/shard_map/ppermute | solution.py:246
  21.6 14.1 %collective-permute-start.1 = (bf16[256,1024]{1,0:T(8,128)(2,1)S(1)}, bf16[256,1024]{1,0:T(8,128)(2,1)S(1)}, u32[]{:S(2)}, u32[]{:S(2)}) collective-permute-start(bf16[256,1024]{1,0:T(8,128)(2,1)S(1)} %broadcast_select_fusion.10.refs_0_), channel_id=1, source_target_pairs={{0,4},{2,6},{12,8},{14,10},{16,20},{18,22},{28,24},{30,26}} | collective-permute-start | bytes 1572872 | tf_op jit(solution)/shard_map/ppermute | solution.py:246
  35.0 1.5 collective-permute-start.9
  35.8 3.0 %collective-permute-start.2 = (bf16[256,1024]{1,0:T(8,128)(2,1)S(1)}, bf16[256,1024]{1,0:T(8,128)(2,1)S(1)}, u32[]{:S(2)}, u32[]{:S(2)}) collective-permute-start(bf16[256,1024]{1,0:T(8,128)(2,1)S(1)} %broadcast_select_fusion.13), channel_id=1, source_target_pairs={{4,8},{6,10},{8,4},{10,6},{20,24},{22,26},{24,20},{26,22}} | collective-permute-start | bytes 1572872 | tf_op jit(solution)/shard_map/ppermute | solution.py:246
  37.4 17.2 %collective-permute-start.10 = (bf16[256,1024]{1,0:T(8,128)(2,1)}, bf16[256,1024]{1,0:T(8,128)(2,1)}, u32[]{:S(2)}, u32[]{:S(2)}) collective-permute-start(bf16[256,1024]{1,0:T(8,128)(2,1)} %broadcast_select_fusion.11), channel_id=1, source_target_pairs={{8,12},{10,14},{4,0},{6,2},{24,28},{26,30},{20,16},{22,18}} | collective-permute-start | bytes 1572872 | tf_op jit(solution)/shard_map/ppermute | solution.py:246
  39.6 22.7 %collective-permute-start.3 = (bf16[256,1024]{1,0:T(8,128)(2,1)S(1)}, bf16[256,1024]{1,0:T(8,128)(2,1)}, u32[]{:S(2)}, u32[]{:S(2)}) collective-permute-start(bf16[256,1024]{1,0:T(8,128)(2,1)S(1)} %broadcast_select_fusion.12.refs_0_), channel_id=1, source_target_pairs={{8,12},{10,14},{4,0},{6,2},{24,28},{26,30},{20,16},{22,18}} | collective-permute-start | bytes 1572872 | tf_op jit(solution)/shard_map/ppermute | solution.py:246
  48.6 98.0 %copy-start = (f32[2048,128]{1,0:T(8,128)}, f32[2048,128]{1,0:T(8,128)S(1)}, u32[]{:S(2)}) copy-start(f32[2048,128]{1,0:T(8,128)S(1)} %get-tuple-element.49.inverse_ref) | copy-start | bytes 3145732
  56.8 12.9 %collective-permute-start.12 = (bf16[256,1024]{1,0:T(8,128)(2,1)}, bf16[256,1024]{1,0:T(8,128)(2,1)S(1)}, u32[]{:S(2)}, u32[]{:S(2)}) collective-permute-start(bf16[256,1024]{1,0:T(8,128)(2,1)} %select_select_fusion), channel_id=1, source_target_pairs={{0,2},{2,0},{4,6},{6,4},{8,10},{10,8},{12,14},{14,12},{16,18},{18,... | collective-permute-start | bytes 1572872 | tf_op jit(solution)/shard_map/ppermute | solution.py:246
  63.6 11.7 %collective-permute-start.5 = (bf16[256,1024]{1,0:T(8,128)(2,1)S(1)}, bf16[256,1024]{1,0:T(8,128)(2,1)S(1)}, u32[]{:S(2)}, u32[]{:S(2)}) collective-permute-start(bf16[256,1024]{1,0:T(8,128)(2,1)S(1)} %select_select_fusion.1), channel_id=1, source_target_pairs={{0,2},{2,0},{4,6},{6,4},{8,10},{10,8},{12,14},{14,12},{16,18},{18,... | collective-permute-start | bytes 1572872 | tf_op jit(solution)/shard_map/ppermute | solution.py:246
  67.1 10.3 %collective-permute-start.11 = (bf16[256,1024]{1,0:T(8,128)(2,1)}, bf16[256,1024]{1,0:T(8,128)(2,1)S(1)}, u32[]{:S(2)}, u32[]{:S(2)}) collective-permute-start(bf16[256,1024]{1,0:T(8,128)(2,1)} %select_select_fusion), channel_id=1, source_target_pairs={{0,1},{2,3},{4,5},{6,7},{8,9},{10,11},{12,13},{14,15},{16,17},{18,... | collective-permute-start | bytes 1572872 | tf_op jit(solution)/shard_map/ppermute | solution.py:246
  69.7 8.5 %collective-permute-start.13 = (bf16[256,1024]{1,0:T(8,128)(2,1)S(1)}, bf16[256,1024]{1,0:T(8,128)(2,1)}, u32[]{:S(2)}, u32[]{:S(2)}) collective-permute-start(bf16[256,1024]{1,0:T(8,128)(2,1)S(1)} %collective-permute-done.12), channel_id=1, source_target_pairs={{0,1},{2,3},{4,5},{6,7},{8,9},{10,11},{12,13},{14,15},{16,17},{18,... | collective-permute-start | bytes 1572872 | tf_op jit(solution)/shard_map/ppermute | solution.py:246
  71.7 13.4 %collective-permute-start.4 = (bf16[256,1024]{1,0:T(8,128)(2,1)S(1)}, bf16[256,1024]{1,0:T(8,128)(2,1)}, u32[]{:S(2)}, u32[]{:S(2)}) collective-permute-start(bf16[256,1024]{1,0:T(8,128)(2,1)S(1)} %select_select_fusion.1), channel_id=1, source_target_pairs={{0,1},{2,3},{4,5},{6,7},{8,9},{10,11},{12,13},{14,15},{16,17},{18,... | collective-permute-start | bytes 1572872 | tf_op jit(solution)/shard_map/ppermute | solution.py:246
  75.3 9.9 %collective-permute-start.6 = (bf16[256,1024]{1,0:T(8,128)(2,1)S(1)}, bf16[256,1024]{1,0:T(8,128)(2,1)}, u32[]{:S(2)}, u32[]{:S(2)}) collective-permute-start(bf16[256,1024]{1,0:T(8,128)(2,1)S(1)} %collective-permute-done.5), channel_id=1, source_target_pairs={{0,1},{2,3},{4,5},{6,7},{8,9},{10,11},{12,13},{14,15},{16,17},{18,... | collective-permute-start | bytes 1572872 | tf_op jit(solution)/shard_map/ppermute | solution.py:246
  85.3 61.4 %copy-start.1 = (bf16[256,1024]{1,0:T(8,128)(2,1)}, bf16[256,1024]{1,0:T(8,128)(2,1)S(1)}, u32[]{:S(2)}) copy-start(bf16[256,1024]{1,0:T(8,128)(2,1)S(1)} %get-tuple-element.82.high_ref.refs_3_) | copy-start | bytes 1572868
  96.3 6.9 %collective-permute-start.14 = (f32[264,1024]{1,0:T(8,128)S(1)}, f32[264,1024]{1,0:T(8,128)S(1)}, u32[]{:S(2)}, u32[]{:S(2)}) collective-permute-start(f32[264,1024]{1,0:T(8,128)S(1)} %row_part.5), channel_id=1, source_target_pairs={{0,1},{1,0},{2,3},{3,2},{4,5},{5,4},{6,7},{7,6},{8,9},{9,8},{10,11... | collective-permute-start | bytes 3244040 | tf_op jit(solution)/shard_map/ppermute | solution.py:246
  99.5 9.2 %collective-permute-start.16 = (f32[264,1024]{1,0:T(8,128)S(1)}, f32[264,1024]{1,0:T(8,128)S(1)}, u32[]{:S(2)}, u32[]{:S(2)}) collective-permute-start(f32[264,1024]{1,0:T(8,128)S(1)} %row_part.7), channel_id=1, source_target_pairs={{0,1},{1,0},{2,3},{3,2},{4,5},{5,4},{6,7},{7,6},{8,9},{9,8},{10,11... | collective-permute-start | bytes 3244040 | tf_op jit(solution)/shard_map/ppermute | solution.py:246
  103.5 11.4 %collective-permute-start.15 = (s32[272,256]{1,0:T(8,128)S(1)}, s32[272,256]{1,0:T(8,128)S(1)}, u32[]{:S(2)}, u32[]{:S(2)}) collective-permute-start(s32[272,256]{1,0:T(8,128)S(1)} %get-tuple-element.55), channel_id=1, source_target_pairs={{0,2},{2,0},{1,3},{3,1},{4,6},{6,4},{5,7},{7,5},{8,10},{10,8},{9,1... | collective-permute-start | bytes 835592 | tf_op jit(solution)/shard_map/ppermute | solution.py:246
  109.0 15.8 %collective-permute-start.18 = (s32[272,256]{1,0:T(8,128)S(1)}, s32[272,256]{1,0:T(8,128)S(1)}, u32[]{:S(2)}, u32[]{:S(2)}) collective-permute-start(s32[272,256]{1,0:T(8,128)S(1)} %get-tuple-element.58.refs_4_), channel_id=1, source_target_pairs={{0,2},{2,0},{1,3},{3,1},{4,6},{6,4},{5,7},{7,5},{8,10},{10,8},{9,1... | collective-permute-start | bytes 835592 | tf_op jit(solution)/shard_map/ppermute | solution.py:246
  115.2 19.1 %collective-permute-start.17 = (s32[272,256]{1,0:T(8,128)S(1)}, s32[272,256]{1,0:T(8,128)S(1)}, u32[]{:S(2)}, u32[]{:S(2)}) collective-permute-start(s32[272,256]{1,0:T(8,128)S(1)} %get-tuple-element.62), channel_id=1, source_target_pairs={{0,4},{1,5},{2,6},{3,7},{12,8},{13,9},{14,10},{15,11},{16,20},{17,... | collective-permute-start | bytes 835592 | tf_op jit(solution)/shard_map/ppermute | solution.py:246
  125.2 11.4 %collective-permute-start.20 = (s32[272,256]{1,0:T(8,128)S(1)}, s32[272,256]{1,0:T(8,128)S(1)}, u32[]{:S(2)}, u32[]{:S(2)}) collective-permute-start(s32[272,256]{1,0:T(8,128)S(1)} %get-tuple-element.65.refs_4_), channel_id=1, source_target_pairs={{0,4},{1,5},{2,6},{3,7},{12,8},{13,9},{14,10},{15,11},{16,20},{17,... | collective-permute-start | bytes 835592 | tf_op jit(solution)/shard_map/ppermute | solution.py:246
  134.6 8.8 %collective-permute-start.19 = (s32[272,256]{1,0:T(8,128)S(1)}, s32[272,256]{1,0:T(8,128)S(1)}, u32[]{:S(2)}, u32[]{:S(2)}) collective-permute-start(s32[272,256]{1,0:T(8,128)S(1)} %merge.10), channel_id=1, source_target_pairs={{4,8},{5,9},{6,10},{7,11},{8,4},{9,5},{10,6},{11,7},{20,24},{21,25... | collective-permute-start | bytes 835592 | tf_op jit(solution)/shard_map/ppermute | solution.py:246
  136.9 8.1 %collective-permute-start.22 = (s32[272,256]{1,0:T(8,128)S(1)}, s32[272,256]{1,0:T(8,128)S(1)}, u32[]{:S(2)}, u32[]{:S(2)}) collective-permute-start(s32[272,256]{1,0:T(8,128)S(1)} %merge.11.refs_4_), channel_id=1, source_target_pairs={{4,8},{5,9},{6,10},{7,11},{8,4},{9,5},{10,6},{11,7},{20,24},{21,25... | collective-permute-start | bytes 835592 | tf_op jit(solution)/shard_map/ppermute | solution.py:246
  143.7 14.6 %collective-permute-start.21 = (s32[272,256]{1,0:T(8,128)S(1)}, s32[272,256]{1,0:T(8,128)S(1)}, u32[]{:S(2)}, u32[]{:S(2)}) collective-permute-start(s32[272,256]{1,0:T(8,128)S(1)} %merge.12), channel_id=1, source_target_pairs={{8,12},{9,13},{10,14},{11,15},{4,0},{5,1},{6,2},{7,3},{24,28},{25,... | collective-permute-start | bytes 835592 | tf_op jit(solution)/shard_map/ppermute | solution.py:246
  145.4 19.3 %collective-permute-start.26 = (s32[272,256]{1,0:T(8,128)S(1)}, s32[272,256]{1,0:T(8,128)S(1)}, u32[]{:S(2)}, u32[]{:S(2)}) collective-permute-start(s32[272,256]{1,0:T(8,128)S(1)} %merge.13.refs_4_), channel_id=1, source_target_pairs={{8,12},{9,13},{10,14},{11,15},{4,0},{5,1},{6,2},{7,3},{24,28},{25,... | collective-permute-start | bytes 835592 | tf_op jit(solution)/shard_map/ppermute | solution.py:246
  160.7 9.5 %collective-permute-start.23 = (s32[272,256]{1,0:T(8,128)}, s32[272,256]{1,0:T(8,128)S(1)}, u32[]{:S(2)}, u32[]{:S(2)}) collective-permute-start(s32[272,256]{1,0:T(8,128)} %get-tuple-element.76), channel_id=1, source_target_pairs={{2,0},{6,4},{10,8},{14,12},{18,16},{22,20},{26,24},{30,28}} | collective-permute-start | bytes 835592 | tf_op jit(solution)/shard_map/ppermute | solution.py:246
  162.0 10.8 %collective-permute-start.24 = (s32[272,256]{1,0:T(8,128)}, s32[272,256]{1,0:T(8,128)S(1)}, u32[]{:S(2)}, u32[]{:S(2)}) collective-permute-start(s32[272,256]{1,0:T(8,128)} %get-tuple-element.76), channel_id=1, source_target_pairs={{1,0},{5,4},{9,8},{13,12},{17,16},{21,20},{25,24},{29,28}} | collective-permute-start | bytes 835592 | tf_op jit(solution)/shard_map/ppermute | solution.py:246
  163.3 9.5 %collective-permute-start.25 = (s32[272,256]{1,0:T(8,128)}, s32[272,256]{1,0:T(8,128)S(1)}, u32[]{:S(2)}, u32[]{:S(2)}) collective-permute-start(s32[272,256]{1,0:T(8,128)} %get-tuple-element.76), channel_id=1, source_target_pairs={{3,0},{7,4},{11,8},{15,12},{19,16},{23,20},{27,24},{31,28}} | collective-permute-start | bytes 835592 | tf_op jit(solution)/shard_map/ppermute | solution.py:246
  166.7 8.6 %collective-permute-start.27 = (s32[272,256]{1,0:T(8,128)}, s32[272,256]{1,0:T(8,128)S(1)}, u32[]{:S(2)}, u32[]{:S(2)}) collective-permute-start(s32[272,256]{1,0:T(8,128)} %get-tuple-element.78), channel_id=1, source_target_pairs={{2,0},{6,4},{10,8},{14,12},{18,16},{22,20},{26,24},{30,28}} | collective-permute-start | bytes 835592 | tf_op jit(solution)/shard_map/ppermute | solution.py:246
  168.0 7.4 %collective-permute-start.28 = (s32[272,256]{1,0:T(8,128)}, s32[272,256]{1,0:T(8,128)}, u32[]{:S(2)}, u32[]{:S(2)}) collective-permute-start(s32[272,256]{1,0:T(8,128)} %get-tuple-element.78), channel_id=1, source_target_pairs={{1,0},{5,4},{9,8},{13,12},{17,16},{21,20},{25,24},{29,28}} | collective-permute-start | bytes 835592 | tf_op jit(solution)/shard_map/ppermute | solution.py:246
  170.3 8.2 %collective-permute-start.29 = (s32[272,256]{1,0:T(8,128)}, s32[272,256]{1,0:T(8,128)}, u32[]{:S(2)}, u32[]{:S(2)}) collective-permute-start(s32[272,256]{1,0:T(8,128)} %get-tuple-element.78), channel_id=1, source_target_pairs={{3,0},{7,4},{11,8},{15,12},{19,16},{23,20},{27,24},{31,28}} | collective-permute-start | bytes 835592 | tf_op jit(solution)/shard_map/ppermute | solution.py:246
  (12 other events, 80.9 us)

commit v6 on v5

--- a/solution.py
+++ b/solution.py
@@ -14,12 +14,12 @@
 WIDE = 512
 PAIRS = 2
 COUNT = 2 * PAIRS
-VMEM_LIMIT = 48 * 1024 * 1024
+MIB = 1024 * 1024
 NT = (((1,), (1,)), ((), ()))
 
 
-def params():
-    return pltpu.CompilerParams(vmem_limit_bytes=VMEM_LIMIT)
+def params(mib):
+    return pltpu.CompilerParams(vmem_limit_bytes=mib * MIB)
 
 
 def cost(flops, moved):
@@ -35,81 +35,152 @@
     return 1.0 / jnp.sqrt(jnp.sum(total, axis=1, keepdims=True) + 1e-06)
 
 
-def head_kernel(decoder_ref, *chunk_refs):
+def head_kernel(decoder_ref, *refs):
+    chunk_refs, (held, sems) = refs[:COUNT], refs[COUNT:]
     step = chunk_refs[0].shape[1]
-    rows = slice(0, decoder_ref.shape[0])
-    inverse = strip_inverse(decoder_ref, rows)
-    for k, ref in enumerate(chunk_refs):
-        for t in range(0, step, 128):
-            v = decoder_ref[rows, k * step + t : k * step + t + 128].astype(jnp.float32)
-            ref[rows, t : t + 128] = (v * inverse).astype(jnp.bfloat16)
-
-
-def units_kernel(decoder_ref, *refs):
-    units_ref, inverse_ref = refs[-2:]
+    strip = ROWS // 4
+
+    def fetch(j):
+        rows = pl.ds(j * strip, strip)
+        return pltpu.make_async_copy(decoder_ref.at[rows, :], held.at[rows, :], sems.at[j])
+
+    for j in range(4):
+        fetch(j).start()
+    for j in range(4):
+        fetch(j).wait()
+        rows = slice(j * strip, (j + 1) * strip)
+        inverse = strip_inverse(held, rows)
+        for k, ref in enumerate(chunk_refs):
+            for t in range(0, step, 128):
+                v = held[rows, k * step + t : k * step + t + 128].astype(jnp.float32)
+                ref[rows, t : t + 128] = (v * inverse).astype(jnp.bfloat16)
+
+
+def units_kernel(low, count, decoder_ref, *refs):
+    units_ref, inverse_ref, held, sems = refs[-4:]
     strip = 64
 
-    for base in range(0, decoder_ref.shape[0], strip):
-        rows = slice(base, base + strip)
-        inverse = strip_inverse(decoder_ref, rows)
-        inverse_ref[rows, :] = jnp.broadcast_to(inverse, (strip, 128))
-        for t in range(0, decoder_ref.shape[1], 128):
-            v = decoder_ref[rows, t : t + 128].astype(jnp.float32)
-            units_ref[rows, t : t + 128] = (v * inverse).astype(jnp.bfloat16)
-
-
-def pair_cosines(units_ref, low_ref, high_ref):
+    def fetch(j):
+        return pltpu.make_async_copy(
+            decoder_ref.at[pl.ds((low + j) * BLOCK, BLOCK), :], held.at[j % 2], sems.at[j % 2]
+        )
+
+    fetch(0).start()
+    for j in range(count):
+        if j + 1 < count:
+            fetch(j + 1).start()
+        fetch(j).wait()
+        block = held.at[j % 2]
+        for base in range(0, BLOCK, strip):
+            rows = slice(base, base + strip)
+            to = slice((low + j) * BLOCK + base, (low + j) * BLOCK + base + strip)
+            inverse = strip_inverse(block, rows)
+            inverse_ref[to, :] = jnp.broadcast_to(inverse, (strip, 128))
+            for t in range(0, block.shape[1], 128):
+                v = block[rows, t : t + 128].astype(jnp.float32)
+                units_ref[to, t : t + 128] = (v * inverse).astype(jnp.bfloat16)
+
+
+def pair_cosines(k, units_ref, rows, low_ref, high_ref):
     step = low_ref.shape[1]
+    base = 2 * k * step
     low = lax.dot_general(
-        units_ref[:, :step], low_ref[...], NT, preferred_element_type=jnp.float32
+        units_ref[rows, base : base + step],
+        low_ref[...],
+        NT,
+        preferred_element_type=jnp.float32,
     )
     high = lax.dot_general(
-        units_ref[:, step:], high_ref[...], NT, preferred_element_type=jnp.float32
+        units_ref[rows, base + step : base + 2 * step],
+        high_ref[...],
+        NT,
+        preferred_element_type=jnp.float32,
     )
     return low + high
 
 
-def partial_kernel(units_ref, low_ref, high_ref, out_ref):
-    out_ref[...] = pair_cosines(units_ref, low_ref, high_ref)
+def partial_kernel(k, units_ref, low_ref, high_ref, out_ref):
+    size = min(WIDE, units_ref.shape[0])
+
+    def body(j, carry):
+        rows = pl.ds(pl.multiple_of(j * size, size), size)
+        out_ref[rows, :] = pair_cosines(k, units_ref, rows, low_ref, high_ref)
+        return carry
+
+    lax.fori_loop(0, units_ref.shape[0] // size, body, 0)
 
 
 def weight_kernel(
-    delta_ref, units_ref, low_ref, high_ref, partial_ref, col_ref, row_ref, along_ref, penalty_ref
+    k,
+    delta_ref,
+    units_ref,
+    low_ref,
+    high_ref,
+    partial_ref,
+    col_ref,
+    row_ref,
+    along_ref,
+    penalty_ref,
 ):
-    size = units_ref.shape[0]
-    j = pl.program_id(0)
-    cosines = partial_ref[...] + pair_cosines(units_ref, low_ref, high_ref)
-    latents = lax.broadcasted_iota(jnp.int32, (size, ROWS), 0) + (delta_ref[0] + j * size)
-    rows = lax.broadcasted_iota(jnp.int32, (size, ROWS), 1)
-    inside = (latents >= 0) & (latents < ROWS)
-    weight = jnp.where(latents == rows, 0.0, jnp.where(inside, 0.5, 1.0))
-    products = weight * cosines
-    weighted = products.astype(jnp.bfloat16)
-    col_ref[...] = weighted
-    row_ref[...] = products.T.astype(jnp.bfloat16)
-    along = jnp.sum(weighted.astype(jnp.float32) * cosines, axis=1, keepdims=True)
-    along_ref[...] = jnp.broadcast_to(along, along_ref.shape)
-
-    @pl.when(j == 0)
+    size = min(WIDE, units_ref.shape[0])
+    penalty_ref[...] = jnp.zeros_like(penalty_ref)
+
+    def body(j, carry):
+        span = pl.ds(pl.multiple_of(j * size, size), size)
+        cosines = partial_ref[span, :] + pair_cosines(k, units_ref, span, low_ref, high_ref)
+        latents = lax.broadcasted_iota(jnp.int32, (size, ROWS), 0) + (delta_ref[0] + j * size)
+        rows = lax.broadcasted_iota(jnp.int32, (size, ROWS), 1)
+        inside = (latents >= 0) & (latents < ROWS)
+        weight = jnp.where(latents == rows, 0.0, jnp.where(inside, 0.5, 1.0))
+        products = weight * cosines
+        weighted = products.astype(jnp.bfloat16)
+        col_ref[span, :] = weighted
+        row_ref[:, span] = products.T.astype(jnp.bfloat16)
+        along = jnp.sum(weighted.astype(jnp.float32) * cosines, axis=1, keepdims=True)
+        along_ref[span, :] = jnp.broadcast_to(along, (size, 128))
+        squares = products * cosines
+        squares = squares[:, :128] + squares[:, 128:]
+        penalty_ref[...] += jnp.sum(squares.reshape(size // 8, 8, 128), axis=0)
+        return carry
+
+    lax.fori_loop(0, units_ref.shape[0] // size, body, 0)
+
+
+def row_kernel(k, side_ref, row_ref, penalty_ref, units_ref, out_ref):
+    tile = out_ref.shape[1] // 2
+    first = (2 * k + side_ref[0]) * out_ref.shape[1]
+    for i in range(2):
+        span = pl.ds(pl.multiple_of(first + i * tile, tile), tile)
+        out_ref[:ROWS, i * tile : (i + 1) * tile] = jnp.dot(
+            row_ref[...], units_ref[:, span], preferred_element_type=jnp.float32
+        )
+    out_ref[ROWS:, :] = jnp.concatenate([penalty_ref[...]] * (out_ref.shape[1] // 128), axis=1)
+
+
+def next_block(low, decoder_ref, held, sems):
+    i, size = pl.program_id(0), held.shape[1]
+
+    def fetch(j):
+        rows = pl.ds(pl.multiple_of((low + j) * size, size), size)
+        slot = lax.rem(j, 2)
+        return pltpu.make_async_copy(decoder_ref.at[rows, :], held.at[slot], sems.at[slot])
+
+    @pl.when(i == 0)
     def _():
-        penalty_ref[...] = jnp.zeros_like(penalty_ref)
-
-    squares = products * cosines
-    squares = squares[:, :128] + squares[:, 128:]
-    penalty_ref[...] += jnp.sum(squares.reshape(size // 8, 8, 128), axis=0)
-
-
-def row_kernel(side_ref, row_ref, penalty_ref, units_ref, *refs):
-    out_ref = refs[-1]
-    out_ref[:ROWS, :] = jnp.dot(
-        row_ref[...], units_ref[...], preferred_element_type=jnp.float32
-    )
-    out_ref[ROWS:, :] = jnp.concatenate([penalty_ref[...]] * (out_ref.shape[1] // 128), axis=1)
-
-
-def finish_kernel(col_ref, decoder_ref, inverse_ref, along_ref, *refs):
+        fetch(i).start()
+
+    @pl.when(i + 1 < pl.num_programs(0))
+    def _():
+        fetch(i + 1).start()
+
+    fetch(i).wait()
+    return held.at[lax.rem(i, 2)]
+
+
+def finish_kernel(low, pinned_ref, col_ref, inverse_ref, along_ref, *refs):
     chunks = refs[:COUNT]
-    out_ref, mark_ref = refs[-2:]
+    out_ref, mark_ref, held, sems = refs[-4:]
+    decoder_ref = next_block(low, pinned_ref, held, sems)
     step = chunks[0].shape[1]
     inverse = inverse_ref[:, :1]
     scale = (2.0 * math.sqrt(DW)) * inverse
@@ -194,9 +265,10 @@
     encode(value, penalty, refs[-1])
 
 
-def last_kernel(owner_ref, col_ref, decoder_ref, inverse_ref, *refs):
+def last_kernel(owner_ref, pinned_ref, col_ref, inverse_ref, *refs):
     chunks, sums = refs[:COUNT], refs[COUNT : COUNT + 7 * PAIRS]
-    out_ref, column = refs[-2:]
+    out_ref, column, held, sems = refs[-4:]
+    decoder_ref = next_block(0, pinned_ref, held, sems)
     step = chunks[0].shape[1]
     piece = step // 2
     owner = owner_ref[0] == 1
@@ -231,7 +303,6 @@
     per = devices // 4
     latents = shard * devices
     blocks = shard // BLOCK
-    wide = min(WIDE, shard)
     step = width // COUNT
     chosen_quarter = quarter[0]
     start = chosen_quarter * (latents // 4)
@@ -248,13 +319,18 @@
     def each(moves):
         return [(z * per + a, z * per + b) for z in range(4) for a, b in moves]
 
+    pinned = pl.BlockSpec(memory_space=pl.ANY)
+    vmem = pl.BlockSpec(memory_space=pltpu.VMEM)
     own = pl.pallas_call(
         head_kernel,
-        grid=(4,),
-        in_specs=[pl.BlockSpec((ROWS // 4, width), lambda i: (i, 0))],
-        out_specs=[pl.BlockSpec((ROWS // 4, step), lambda i: (i, 0))] * COUNT,
+        in_specs=[pinned],
+        out_specs=[vmem] * COUNT,
         out_shape=[jax.ShapeDtypeStruct((ROWS, step), jnp.bfloat16)] * COUNT,
-        compiler_params=params(),
+        scratch_shapes=[
+            pltpu.VMEM((ROWS, width), jnp.bfloat16),
+            pltpu.SemaphoreType.DMA((4,)),
+        ],
+        compiler_params=params(50),
         cost_estimate=cost(4 * ROWS * width, 4 * ROWS * width),
         name="head_units",
     )(decoder)
@@ -276,26 +352,26 @@
         if high == low:
             return True
         operands = [decoder, tie]
-        specs = [pl.BlockSpec((BLOCK, width), lambda i: (i + low, 0)), any_spec]
+        specs = [pinned, any_spec]
         aliases = {}
         if made[0] is not None:
             aliases = {2: 0, 3: 1}
             operands += made
-            specs += [any_spec, any_spec]
+            specs += [vmem, vmem]
         made[:] = pl.pallas_call(
-            units_kernel,
-            grid=(high - low,),
+            functools.partial(units_kernel, low, high - low),
             in_specs=specs,
-            out_specs=[
-                pl.BlockSpec((BLOCK, width), lambda i: (i + low, 0)),
-                pl.BlockSpec((BLOCK, 128), lambda i: (i + low, 0)),
-            ],
+            out_specs=[vmem, vmem],
             out_shape=[
                 jax.ShapeDtypeStruct((shard, width), jnp.bfloat16),
                 jax.ShapeDtypeStruct((shard, 128), jnp.float32),
             ],
+            scratch_shapes=[
+                pltpu.VMEM((2, BLOCK, width), jnp.bfloat16),
+                pltpu.SemaphoreType.DMA((2,)),
+            ],
             input_output_aliases=aliases,
-            compiler_params=params(),
+            compiler_params=params(24),
             cost_estimate=cost(4 * BLOCK * width, 4 * (high - low) * BLOCK * width),
             name="units",
         )(*operands)
@@ -345,42 +421,29 @@
     delta = jnp.reshape(index * shard - start, (1,)).astype(jnp.int32)
     whole_chunk = pl.BlockSpec((ROWS, step), lambda i: (0, 0))
     half_flops = ROWS * shard * width
-    partial = None
-    for k in range(PAIRS):
-        unit_spec = pl.BlockSpec((wide, 2 * step), lambda i, k=k: (i, k))
-        wide_spec = pl.BlockSpec((wide, ROWS), lambda i: (i, 0))
-        if k < PAIRS - 1:
-            partial = pl.pallas_call(
-                partial_kernel,
-                grid=(shard // wide,),
-                in_specs=[unit_spec, whole_chunk, whole_chunk],
-                out_specs=wide_spec,
-                out_shape=jax.ShapeDtypeStruct((shard, ROWS), jnp.float32),
-                compiler_params=params(),
-                cost_estimate=cost(half_flops, shard * width),
-                name="part_cosines",
-            )(units, chosen[2 * k], chosen[2 * k + 1])
-            continue
-        by_col, by_row, along, local_penalty = pl.pallas_call(
-            weight_kernel,
-            grid=(shard // wide,),
-            in_specs=[smem, unit_spec, whole_chunk, whole_chunk, wide_spec],
-            out_specs=[
-                wide_spec,
-                pl.BlockSpec((ROWS, wide), lambda i: (0, i)),
-                pl.BlockSpec((wide, 128), lambda i: (i, 0)),
-                pl.BlockSpec((8, 128), lambda i: (0, 0)),
-            ],
-            out_shape=[
-                jax.ShapeDtypeStruct((shard, ROWS), jnp.bfloat16),
-                jax.ShapeDtypeStruct((ROWS, shard), jnp.bfloat16),
-                jax.ShapeDtypeStruct((shard, 128), jnp.float32),
-                jax.ShapeDtypeStruct((8, 128), jnp.float32),
-            ],
-            compiler_params=params(),
-            cost_estimate=cost(half_flops, shard * width),
-            name="weights",
-        )(delta, units, chosen[2 * k], chosen[2 * k + 1], partial)
+    partial = pl.pallas_call(
+        functools.partial(partial_kernel, 0),
+        in_specs=[vmem] * 3,
+        out_specs=vmem,
+        out_shape=jax.ShapeDtypeStruct((shard, ROWS), jnp.float32),
+        compiler_params=params(24),
+        cost_estimate=cost(half_flops, shard * width),
+        name="part_cosines",
+    )(units, chosen[0], chosen[1])
+    by_col, by_row, along, local_penalty = pl.pallas_call(
+        functools.partial(weight_kernel, 1),
+        in_specs=[smem] + [vmem] * 4,
+        out_specs=[vmem] * 4,
+        out_shape=[
+            jax.ShapeDtypeStruct((shard, ROWS), jnp.bfloat16),
+            jax.ShapeDtypeStruct((ROWS, shard), jnp.bfloat16),
+            jax.ShapeDtypeStruct((shard, 128), jnp.float32),
+            jax.ShapeDtypeStruct((8, 128), jnp.float32),
+        ],
+        compiler_params=params(24),
+        cost_estimate=cost(half_flops, shard * width),
+        name="weights",
+    )(delta, units, chosen[2], chosen[3], partial)
 
     core_side = within % 2
     plane_x = jnp.reshape((within // 2) % 2, (1,)).astype(jnp.int32)
@@ -388,24 +451,15 @@
     coded_type = jax.ShapeDtypeStruct((CODED_ROWS, piece // 2), jnp.int32)
     piece_type = jax.ShapeDtypeStruct((ROWS, piece), jnp.float32)
     tile_type = jax.ShapeDtypeStruct((8, 128), jnp.float32)
-    vmem = pl.BlockSpec(memory_space=pltpu.VMEM)
     merge_cost = cost(20 * ROWS * piece, 12 * ROWS * piece)
 
     def row_part(k, side):
         return pl.pallas_call(
-            row_kernel,
-            grid_spec=pltpu.PrefetchScalarGridSpec(
-                num_scalar_prefetch=1,
-                grid=(2,),
-                in_specs=[
-                    pl.BlockSpec((ROWS, shard), lambda i, s: (0, 0)),
-                    pl.BlockSpec((8, 128), lambda i, s: (0, 0)),
-                    pl.BlockSpec((shard, piece), lambda i, s: (0, 4 * k + 2 * s[0] + i)),
-                ],
-                out_specs=pl.BlockSpec((tall, piece), lambda i, s: (0, i)),
-            ),
+            functools.partial(row_kernel, k),
+            in_specs=[smem, vmem, vmem, vmem],
+            out_specs=vmem,
             out_shape=jax.ShapeDtypeStruct((tall, step), jnp.float32),
-            compiler_params=params(),
+            compiler_params=params(24),
             cost_estimate=cost(half_flops // 2, shard * width // 2),
             name="row_part",
         )(jnp.reshape(side, (1,)).astype(jnp.int32), by_row, local_penalty, units)
@@ -417,7 +471,7 @@
             in_specs=[vmem] * (2 + len(arrived)) + [any_spec] * len(ties),
             out_specs=[vmem] * len(tiles),
             out_shape=tiles,
-            compiler_params=params(),
+            compiler_params=params(24),
             cost_estimate=merge_cost,
             name="merge",
         )(*kept, *arrived, *ties)
@@ -436,7 +490,7 @@
             in_specs=[smem, vmem, vmem],
             out_specs=[vmem, vmem, vmem],
             out_shape=[piece_type, tile_type, coded_type],
-            compiler_params=params(),
+            compiler_params=params(24),
             cost_estimate=merge_cost,
             name="split",
         )(plane_x, near, send(away, across_core))
@@ -453,10 +507,10 @@
         low, high = bounds[part], bounds[part + 1]
         if high == low:
             return []
-        operands = [by_col, decoder, inverse, along, *chosen]
+        operands = [decoder, by_col, inverse, along, *chosen]
         specs = [
+            pinned,
             pl.BlockSpec((BLOCK, ROWS), lambda i: (i + low, 0)),
-            pl.BlockSpec((BLOCK, width), lambda i: (i + low, 0)),
             pl.BlockSpec((BLOCK, 128), lambda i: (i + low, 0)),
             pl.BlockSpec((BLOCK, 128), lambda i: (i + low, 0)),
         ] + [whole_chunk] * COUNT
@@ -469,13 +523,17 @@
             specs.append(any_spec)
         rows = (high - low) * BLOCK
         grad, mark = pl.pallas_call(
-            finish_kernel,
+            functools.partial(finish_kernel, low),
             grid=(high - low,),
             in_specs=specs,
             out_specs=[pl.BlockSpec((BLOCK, width), lambda i: (i + low, 0)), mark_spec],
             out_shape=[out_type, mark_type],
+            scratch_shapes=[
+                pltpu.VMEM((2, BLOCK, width), jnp.bfloat16),
+                pltpu.SemaphoreType.DMA((2,)),
+            ],
             input_output_aliases=aliases,
-            compiler_params=params(),
+            compiler_params=params(50),
             cost_estimate=cost(2 * ROWS * rows * width, 6 * rows * width),
             name="finish",
         )(*operands)
@@ -521,11 +579,11 @@
             ]
 
     owner = jnp.reshape(here & (within == 0), (1,)).astype(jnp.int32)
-    operands = [owner, by_col, decoder, inverse, *chosen, *sums]
+    operands = [owner, decoder, by_col, inverse, *chosen, *sums]
     specs = [
         smem,
+        pinned,
         pl.BlockSpec((narrow, ROWS), lambda i: (i, 0)),
-        pl.BlockSpec((narrow, width), lambda i: (i, 0)),
         pl.BlockSpec((narrow, 128), lambda i: (i, 0)),
     ]
     specs += [whole_chunk] * COUNT
@@ -541,9 +599,13 @@
         in_specs=specs,
         out_specs=pl.BlockSpec((narrow, width), lambda i: (i, 0)),
         out_shape=out_type,
-        scratch_shapes=[pltpu.VMEM((narrow, width), jnp.float32)],
+        scratch_shapes=[
+            pltpu.VMEM((narrow, width), jnp.float32),
+            pltpu.VMEM((2, narrow, width), jnp.bfloat16),
+            pltpu.SemaphoreType.DMA((2,)),
+        ],
         input_output_aliases=aliases,
-        compiler_params=params(),
+        compiler_params=params(50),
         name="finish_rows",
     )(*operands)
 

time: 190 us -> 204 us (1.074)
  local copies, waits for them, and re-layouts: 10.1 us -> 41.9 us
  Pallas kernels: 80.2 us -> 68.4 us
  waiting for transfers between devices: 22.6 us -> 17.7 us
  starting transfers between devices: 62.7 us -> 60.5 us
    unnamed x28 -> x44, local copies, waits for them, and re-layouts: 8.54 us -> 40.3 us
    pallas_call x14, Pallas kernels: 69.6 us -> 54.1 us  [the longest x4 26 us: finish(): pl.pallas_call(functools.partial(finish_kernel, low), grid=(high - low,),...]
    ppermute x30, waiting for transfers between devices: 22.6 us -> 17.7 us  [send(): return lax.ppermute(value, 'row', pairs)]
    pallas_call x2, Pallas kernels: 0.64 us -> 3.94 us  [on_device(): pl.pallas_call(split_kernel, in_specs=[smem, vmem, vmem], out_specs=[vmem...]
    ppermute x30, starting transfers between devices: 62.7 us -> 60.5 us  [send(): return lax.ppermute(value, 'row', pairs)]
  transfers between devices with their start and end apart: 30 -> 30, of which waited for: 8 -> 7; matrix products, arithmetic and copies ran while one was open for 5% -> 5% of each run, Pallas kernels for 33% -> 26%
where the time goes in v6:
time: 204 us; the launch traced here: 203 us
  Pallas kernels  68.4 us (34%)
  starting transfers between devices  60.5 us (30%)
  local copies, waits for them, and re-layouts  41.9 us (21%)
  waiting for transfers between devices  17.7 us (9%)
  other arithmetic  8.77 us (4%)
  between operations  5.72 us (3%)
    ppermute x30, starting transfers between devices, send(): return lax.ppermute(value, 'row', pairs)  60.5 us
    unnamed x44, local copies, waits for them, and re-layouts  40.3 us
    pallas_call x4, Pallas kernels, finish(): pl.pallas_call(functools.partial(finish_kernel, low), grid=(high - low,),...  26 us
    ppermute x30, waiting for transfers between devices, send(): return lax.ppermute(value, 'row', pairs)  17.7 us
    pallas_call x3, Pallas kernels, make_units(): pl.pallas_call(functools.partial(units_kernel, low, high - low), in_specs...  13 us
    pallas_call x1, Pallas kernels, on_device(): pl.pallas_call(last_kernel, grid=(2,), in_specs=specs, out_specs=pl.Block...  6.34 us
    pallas_call x4, Pallas kernels, row_part(): pl.pallas_call(functools.partial(row_kernel, k), in_specs=[smem, vmem, vm...  6.02 us
  transfers between devices with their start and end apart: 30, of which 7 were waited for; matrix products, arithmetic and copies ran while one was open for 5% of the time, Pallas kernels for 26%

profile of v6, /device:TPU:0, one launch (start us, length us, event | category | flops | bytes accessed | tf_op | source)
XLA Modules:
  0.0 202.9 jit_solution(48656710701061208)
XLA Ops:
  2.7 5.7 %collective-permute-start.7 = (bf16[256,1024]{1,0:T(8,128)(2,1)S(1)}, bf16[256,1024]{1,0:T(8,128)(2,1)}, u32[]{:S(2)}, u32[]{:S(2)}) collective-permute-start(bf16[256,1024]{1,0:T(8,128)(2,1)S(1)} %get-tuple-element.50), channel_id=1, source_target_pairs={{0,2},{4,6},{8,10},{12,14},{16,18},{20,22},{24,26},{28,30}} | collective-permute-start | bytes 1572872 | tf_op jit(solution)/shard_map/ppermute | solution.py:317
  8.4 2.1 %collective-permute-start = (bf16[256,1024]{1,0:T(8,128)(2,1)S(1)}, bf16[256,1024]{1,0:T(8,128)(2,1)}, u32[]{:S(2)}, u32[]{:S(2)}) collective-permute-start(bf16[256,1024]{1,0:T(8,128)(2,1)S(1)} %get-tuple-element.41), channel_id=1, source_target_pairs={{0,2},{4,6},{8,10},{12,14},{16,18},{20,22},{24,26},{28,30}} | collective-permute-start | bytes 1572872 | tf_op jit(solution)/shard_map/ppermute | solution.py:317
  10.4 3.3 %units.3 = (bf16[2048,4096]{1,0:T(8,128)(2,1)S(1)}, f32[2048,128]{1,0:T(8,128)S(1)}) custom-call(bf16[2048,4096]{1,0:T(8,128)(2,1)} %pinned_ref.9, bf16[256,1024]{1,0:T(8,128)(2,1)S(1)} %get-tuple-element.43.refs_0_), custom_call_target="tpu_custom_call" | custom-call | flops 4194304 | bytes 8388608 | tf_op jit(solution)/shard_map/units/pallas_call | solution.py:361
  13.8 6.2 %copy-done = bf16[2048,4096]{1,0:T(8,128)(2,1)} copy-done((bf16[2048,4096]{1,0:T(8,128)(2,1)}, bf16[2048,4096]{1,0:T(8,128)(2,1)S(1)}, u32[]{:S(2)}) %copy-start) | copy-done | bytes 16777240
  21.2 4.3 %collective-permute-start.8 = (bf16[256,1024]{1,0:T(8,128)(2,1)S(1)}, bf16[256,1024]{1,0:T(8,128)(2,1)}, u32[]{:S(2)}, u32[]{:S(2)}) collective-permute-start(bf16[256,1024]{1,0:T(8,128)(2,1)S(1)} %broadcast_select_fusion.1), channel_id=1, source_target_pairs={{0,4},{2,6},{12,8},{14,10},{16,20},{18,22},{28,24},{30,26}} | collective-permute-start | bytes 1572872 | tf_op jit(solution)/shard_map/ppermute | solution.py:317
  27.6 5.8 %copy-done.1 = bf16[2048,4096]{1,0:T(8,128)(2,1)S(1)} copy-done((bf16[2048,4096]{1,0:T(8,128)(2,1)S(1)}, bf16[2048,4096]{1,0:T(8,128)(2,1)}, u32[]{:S(2)}) %copy-start.1) | copy-done | bytes 16777240
  33.3 4.9 %units.4 = (bf16[2048,4096]{1,0:T(8,128)(2,1)S(1)}, f32[2048,128]{1,0:T(8,128)S(1)}) custom-call(bf16[2048,4096]{1,0:T(8,128)(2,1)} %pinned_ref.9, bf16[256,1024]{1,0:T(8,128)(2,1)S(1)} %broadcast_select_fusion.10.refs_0_, bf16[2048,4096]{1,0:T(8,128)(2,1)S(1)} %copy-done.1, ...), custom_call_target="tpu_custom_call", output_to_operand_aliasing={{0}: (2, {}), {1}: (3, {})} | custom-call | flops 4194304 | bytes 12582912 | tf_op jit(solution)/shard_map/units/pallas_call | solution.py:361
  38.2 6.2 %copy-done.2 = bf16[2048,4096]{1,0:T(8,128)(2,1)} copy-done((bf16[2048,4096]{1,0:T(8,128)(2,1)}, bf16[2048,4096]{1,0:T(8,128)(2,1)S(1)}, u32[]{:S(2)}) %copy-start.2) | copy-done | bytes 16777240
  53.5 5.8 %copy-done.3 = bf16[2048,4096]{1,0:T(8,128)(2,1)S(1)} copy-done((bf16[2048,4096]{1,0:T(8,128)(2,1)S(1)}, bf16[2048,4096]{1,0:T(8,128)(2,1)}, u32[]{:S(2)}) %copy-start.3) | copy-done | bytes 16777240
  59.3 4.9 %units.5 = (bf16[2048,4096]{1,0:T(8,128)(2,1)S(1)}, f32[2048,128]{1,0:T(8,128)S(1)}) custom-call(bf16[2048,4096]{1,0:T(8,128)(2,1)} %pinned_ref.9, bf16[256,1024]{1,0:T(8,128)(2,1)S(1)} %broadcast_select_fusion.12.refs_0_, bf16[2048,4096]{1,0:T(8,128)(2,1)S(1)} %copy-done.3, ...), custom_call_target="tpu_custom_call", output_to_operand_aliasing={{0}: (2, {}), {1}: (3, {})} | custom-call | flops 4194304 | bytes 12582912 | tf_op jit(solution)/shard_map/units/pallas_call | solution.py:361
  64.2 6.2 %copy-done.4 = bf16[2048,4096]{1,0:T(8,128)(2,1)} copy-done((bf16[2048,4096]{1,0:T(8,128)(2,1)}, bf16[2048,4096]{1,0:T(8,128)(2,1)S(1)}, u32[]{:S(2)}) %copy-start.4) | copy-done | bytes 16777240
  71.5 2.1 %select_select_fusion = bf16[256,1024]{1,0:T(8,128)(2,1)} fusion(bf16[256,1024]{1,0:T(8,128)(2,1)S(1)} %broadcast_select_fusion.1, bf16[256,1024]{1,0:T(8,128)(2,1)} %collective-permute-done.10, bf16[256,1024]{1,0:T(8,128)(2,1)} %collective-permute-done.8, bf16[256,1024]{1,0:T(8,128)(2,1)} %copy-done.17, pred[]{:T(512)S(6)} %and.43, pred[]{:T(512)S(6)} %select_n.144, ...), kind=kLoop, calls=%fused_computation | loop fusion | flops 786432 | bytes 2621443 | tf_op jit(solution)/shard_map/jit(_where)/select_n | solution.py:404
  77.1 3.7 %collective-permute-start.5 = (bf16[256,1024]{1,0:T(8,128)(2,1)S(1)}, bf16[256,1024]{1,0:T(8,128)(2,1)S(1)}, u32[]{:S(2)}, u32[]{:S(2)}) collective-permute-start(bf16[256,1024]{1,0:T(8,128)(2,1)S(1)} %select_select_fusion.1), channel_id=1, source_target_pairs={{0,2},{2,0},{4,6},{6,4},{8,10},{10,8},{12,14},{14,12},{16,18},{18,... | collective-permute-start | bytes 1572872 | tf_op jit(solution)/shard_map/ppermute | solution.py:317
  80.8 2.1 %collective-permute-start.11 = (bf16[256,1024]{1,0:T(8,128)(2,1)}, bf16[256,1024]{1,0:T(8,128)(2,1)}, u32[]{:S(2)}, u32[]{:S(2)}) collective-permute-start(bf16[256,1024]{1,0:T(8,128)(2,1)} %select_select_fusion), channel_id=1, source_target_pairs={{0,1},{2,3},{4,5},{6,7},{8,9},{10,11},{12,13},{14,15},{16,17},{18,... | collective-permute-start | bytes 1572872 | tf_op jit(solution)/shard_map/ppermute | solution.py:317
  82.9 2.1 %collective-permute-done.12 = bf16[256,1024]{1,0:T(8,128)(2,1)} collective-permute-done((bf16[256,1024]{1,0:T(8,128)(2,1)}, bf16[256,1024]{1,0:T(8,128)(2,1)}, u32[]{:S(2)}, u32[]{:S(2)}) %collective-permute-start.12) | collective-permute-done | bytes 524320 | tf_op jit(solution)/shard_map/ppermute | solution.py:317
  87.1 2.1 %collective-permute-start.4 = (bf16[256,1024]{1,0:T(8,128)(2,1)S(1)}, bf16[256,1024]{1,0:T(8,128)(2,1)}, u32[]{:S(2)}, u32[]{:S(2)}) collective-permute-start(bf16[256,1024]{1,0:T(8,128)(2,1)S(1)} %select_select_fusion.1), channel_id=1, source_target_pairs={{0,1},{2,3},{4,5},{6,7},{8,9},{10,11},{12,13},{14,15},{16,17},{18,... | collective-permute-start | bytes 1572872 | tf_op jit(solution)/shard_map/ppermute | solution.py:317
  90.5 2.1 %collective-permute-start.6 = (bf16[256,1024]{1,0:T(8,128)(2,1)S(1)}, bf16[256,1024]{1,0:T(8,128)(2,1)}, u32[]{:S(2)}, u32[]{:S(2)}) collective-permute-start(bf16[256,1024]{1,0:T(8,128)(2,1)S(1)} %collective-permute-done.5), channel_id=1, source_target_pairs={{0,1},{2,3},{4,5},{6,7},{8,9},{10,11},{12,13},{14,15},{16,17},{18,... | collective-permute-start | bytes 1572872 | tf_op jit(solution)/shard_map/ppermute | solution.py:317
  94.0 5.8 %copy-done.5 = bf16[2048,4096]{1,0:T(8,128)(2,1)S(1)} copy-done((bf16[2048,4096]{1,0:T(8,128)(2,1)S(1)}, bf16[2048,4096]{1,0:T(8,128)(2,1)}, u32[]{:S(2)}) %copy-start.5) | copy-done | bytes 16777240
  99.7 3.0 %part_cosines.1.partial_ref = f32[2048,256]{1,0:T(8,128)S(1)} custom-call(bf16[2048,4096]{1,0:T(8,128)(2,1)S(1)} %copy-done.5, bf16[256,1024]{1,0:T(8,128)(2,1)S(1)} %get-tuple-element.81.low_ref.refs_0_, bf16[256,1024]{1,0:T(8,128)(2,1)S(1)} %get-tuple-element.80.high_ref.refs_1_), custom_call_target="tpu_custom_call" | custom-call | flops 2147483648 | bytes 8388608 | tf_op jit(solution)/shard_map/part_cosines/pallas_call | solution.py:424
  102.9 4.0 %weights.1 = (bf16[2048,256]{1,0:T(8,128)(2,1)S(1)}, bf16[256,2048]{1,0:T(8,128)(2,1)S(1)}, f32[2048,128]{1,0:T(8,128)S(1)}, f32[8,128]{1,0:T(8,128)S(1)}) custom-call(s32[1]{0:T(128)} %bitcast.3.delta_ref, bf16[2048,4096]{1,0:T(8,128)(2,1)S(1)} %copy-done.5, bf16[256,1024]{1,0:T(8,128)(2,1)S(1)} %get-tuple-element.83.low_ref.refs_2_, ...), custom_call_target="tpu_custom_call" | custom-call | flops 2147483648 | bytes 8388608 | tf_op jit(solution)/shard_map/weights/pallas_call | solution.py:433
  107.9 2.3 %row_part.5 = f32[264,1024]{1,0:T(8,128)} custom-call(s32[1]{0:T(128)} %bitcast.7.side_ref, bf16[256,2048]{1,0:T(8,128)(2,1)S(1)} %get-tuple-element.51.row_ref, f32[8,128]{1,0:T(8,128)S(1)} %get-tuple-element.52.penalty_ref, bf16[2048,4096]{1,0:T(8,128)(2,1)S(1)} %copy-done.5), custom_call_target="tpu_custom_call" | custom-call | flops 1073741824 | bytes 4194304 | tf_op jit(solution)/shard_map/row_part/pallas_call | solution.py:457
  113.2 2.3 %split.2 = (f32[256,512]{1,0:T(8,128)S(1)}, f32[8,128]{1,0:T(8,128)S(1)}, s32[272,256]{1,0:T(8,128)S(1)}) custom-call(s32[1]{0:T(128)} %bitcast.odd_ref, f32[264,1024]{1,0:T(8,128)S(1)} %row_part.4.mine_ref, f32[264,1024]{1,0:T(8,128)} %collective-permute-done.14.theirs_ref), custom_call_target="tpu_custom_call" | custom-call | flops 2621440 | bytes 1572864 | tf_op jit(solution)/shard_map/split/pallas_call | solution.py:488
  120.7 6.8 %finish.4 = (f32[2048,4096]{1,0:T(8,128)}, f32[8,128]{1,0:T(8,128)S(1)}) custom-call(bf16[2048,4096]{1,0:T(8,128)(2,1)} %pinned_ref.9, bf16[2048,256]{1,0:T(8,128)(2,1)S(1)} %get-tuple-element.56.col_ref, f32[2048,128]{1,0:T(8,128)} %copy-done.6, f32[2048,128]{1,0:T(8,128)} %copy-done.12, bf16[256,1024]{1,0:T(8,128)(2,1)S(1)} %get-tuple-element.81.low_ref.refs_0_, ...), custom_call_target="tpu_custom_call" | custom-call | flops 1073741824 | bytes 12582912 | tf_op jit(solution)/shard_map/finish/pallas_call | solution.py:525
  127.8 12.0 %collective-permute-start.17 = (s32[272,256]{1,0:T(8,128)S(1)}, s32[272,256]{1,0:T(8,128)S(1)}, u32[]{:S(2)}, u32[]{:S(2)}) collective-permute-start(s32[272,256]{1,0:T(8,128)S(1)} %get-tuple-element.62), channel_id=1, source_target_pairs={{0,4},{1,5},{2,6},{3,7},{12,8},{13,9},{14,10},{15,11},{16,20},{17,... | collective-permute-start | bytes 835592 | tf_op jit(solution)/shard_map/ppermute | solution.py:317
  140.2 2.2 %collective-permute-start.20 = (s32[272,256]{1,0:T(8,128)S(1)}, s32[272,256]{1,0:T(8,128)S(1)}, u32[]{:S(2)}, u32[]{:S(2)}) collective-permute-start(s32[272,256]{1,0:T(8,128)S(1)} %get-tuple-element.65.refs_4_), channel_id=1, source_target_pairs={{0,4},{1,5},{2,6},{3,7},{12,8},{13,9},{14,10},{15,11},{16,20},{17,... | collective-permute-start | bytes 835592 | tf_op jit(solution)/shard_map/ppermute | solution.py:317
  142.4 6.9 %finish.5 = (f32[2048,4096]{1,0:T(8,128)}, f32[8,128]{1,0:T(8,128)S(1)}) custom-call(bf16[2048,4096]{1,0:T(8,128)(2,1)} %pinned_ref.9, bf16[2048,256]{1,0:T(8,128)(2,1)S(1)} %get-tuple-element.56.col_ref, f32[2048,128]{1,0:T(8,128)} %copy-done.6, f32[2048,128]{1,0:T(8,128)} %copy-done.12, ...), custom_call_target="tpu_custom_call", output_to_operand_aliasing={{0}: (9, {})} | custom-call | flops 1073741824 | bytes 12582912 | tf_op jit(solution)/shard_map/finish/pallas_call | solution.py:525
  152.2 6.9 %finish.6 = (f32[2048,4096]{1,0:T(8,128)}, f32[8,128]{1,0:T(8,128)S(1)}) custom-call(bf16[2048,4096]{1,0:T(8,128)(2,1)} %pinned_ref.9, bf16[2048,256]{1,0:T(8,128)(2,1)S(1)} %get-tuple-element.56.col_ref, f32[2048,128]{1,0:T(8,128)} %copy-done.6, f32[2048,128]{1,0:T(8,128)} %copy-done.12, ...), custom_call_target="tpu_custom_call", output_to_operand_aliasing={{0}: (9, {})} | custom-call | flops 1073741824 | bytes 12582912 | tf_op jit(solution)/shard_map/finish/pallas_call | solution.py:525
  162.6 5.4 %finish.7 = (f32[2048,4096]{1,0:T(8,128)}, f32[8,128]{1,0:T(8,128)S(1)}) custom-call(bf16[2048,4096]{1,0:T(8,128)(2,1)} %pinned_ref.9, bf16[2048,256]{1,0:T(8,128)(2,1)S(1)} %get-tuple-element.56.col_ref, f32[2048,128]{1,0:T(8,128)} %copy-done.6, f32[2048,128]{1,0:T(8,128)} %copy-done.12, ...), custom_call_target="tpu_custom_call", output_to_operand_aliasing={{0}: (9, {})} | custom-call | flops 536870912 | bytes 6291456 | tf_op jit(solution)/shard_map/finish/pallas_call | solution.py:525
  168.0 7.0 %collective-permute-done.21.refs_2_ = s32[272,256]{1,0:T(8,128)S(1)} collective-permute-done((s32[272,256]{1,0:T(8,128)S(1)}, s32[272,256]{1,0:T(8,128)S(1)}, u32[]{:S(2)}, u32[]{:S(2)}) %collective-permute-start.21) | collective-permute-done | bytes 278560 | tf_op jit(solution)/shard_map/ppermute | solution.py:317
  187.9 2.6 %collective-permute-done.27.refs_12_.refs_13_ = s32[272,256]{1,0:T(8,128)S(1)} collective-permute-done((s32[272,256]{1,0:T(8,128)S(1)}, s32[272,256]{1,0:T(8,128)S(1)}, u32[]{:S(2)}, u32[]{:S(2)}) %collective-permute-start.27) | collective-permute-done | bytes 278560 | tf_op jit(solution)/shard_map/ppermute | solution.py:317
  190.5 2.8 %collective-permute-done.29.refs_16_.refs_17_ = s32[272,256]{1,0:T(8,128)S(1)} collective-permute-done((s32[272,256]{1,0:T(8,128)S(1)}, s32[272,256]{1,0:T(8,128)S(1)}, u32[]{:S(2)}, u32[]{:S(2)}) %collective-permute-start.29) | collective-permute-done | bytes 278560 | tf_op jit(solution)/shard_map/ppermute | solution.py:317
  195.5 6.3 %finish_rows.1 = f32[2048,4096]{1,0:T(8,128)} custom-call(s32[1]{0:T(128)} %bitcast.9.owner_ref, bf16[2048,4096]{1,0:T(8,128)(2,1)} %pinned_ref.9, bf16[2048,256]{1,0:T(8,128)(2,1)} %copy-done.7, f32[2048,128]{1,0:T(8,128)} %copy-done.6, bf16[256,1024]{1,0:T(8,128)(2,1)S(1)} %get-tuple-element.81.low_ref.refs_0_, ...), custom_call_target="tpu_custom_call", output_to_operand_aliasing={{}: (22, {})} | custom-call | tf_op jit(solution)/shard_map/finish_rows/pallas_call | solution.py:596
  (112 shorter events, 51.6 us)
Async XLA Ops:
  2.7 18.4 %collective-permute-start.7 = (bf16[256,1024]{1,0:T(8,128)(2,1)S(1)}, bf16[256,1024]{1,0:T(8,128)(2,1)}, u32[]{:S(2)}, u32[]{:S(2)}) collective-permute-start(bf16[256,1024]{1,0:T(8,128)(2,1)S(1)} %get-tuple-element.50), channel_id=1, source_target_pairs={{0,2},{4,6},{8,10},{12,14},{16,18},{20,22},{24,26},{28,30}} | collective-permute-start | bytes 1572872 | tf_op jit(solution)/shard_map/ppermute | solution.py:317
  8.4 17.1 %collective-permute-start = (bf16[256,1024]{1,0:T(8,128)(2,1)S(1)}, bf16[256,1024]{1,0:T(8,128)(2,1)}, u32[]{:S(2)}, u32[]{:S(2)}) collective-permute-start(bf16[256,1024]{1,0:T(8,128)(2,1)S(1)} %get-tuple-element.41), channel_id=1, source_target_pairs={{0,2},{4,6},{8,10},{12,14},{16,18},{20,22},{24,26},{28,30}} | collective-permute-start | bytes 1572872 | tf_op jit(solution)/shard_map/ppermute | solution.py:317
  21.2 24.3 %collective-permute-start.8 = (bf16[256,1024]{1,0:T(8,128)(2,1)S(1)}, bf16[256,1024]{1,0:T(8,128)(2,1)}, u32[]{:S(2)}, u32[]{:S(2)}) collective-permute-start(bf16[256,1024]{1,0:T(8,128)(2,1)S(1)} %broadcast_select_fusion.1), channel_id=1, source_target_pairs={{0,4},{2,6},{12,8},{14,10},{16,20},{18,22},{28,24},{30,26}} | collective-permute-start | bytes 1572872 | tf_op jit(solution)/shard_map/ppermute | solution.py:317
  25.6 21.8 %collective-permute-start.1 = (bf16[256,1024]{1,0:T(8,128)(2,1)S(1)}, bf16[256,1024]{1,0:T(8,128)(2,1)S(1)}, u32[]{:S(2)}, u32[]{:S(2)}) collective-permute-start(bf16[256,1024]{1,0:T(8,128)(2,1)S(1)} %broadcast_select_fusion.10.refs_0_), channel_id=1, source_target_pairs={{0,4},{2,6},{12,8},{14,10},{16,20},{18,22},{28,24},{30,26}} | collective-permute-start | bytes 1572872 | tf_op jit(solution)/shard_map/ppermute | solution.py:317
  46.6 2.3 %collective-permute-start.9 = (bf16[256,1024]{1,0:T(8,128)(2,1)S(1)}, bf16[256,1024]{1,0:T(8,128)(2,1)S(1)}, u32[]{:S(2)}, u32[]{:S(2)}) collective-permute-start(bf16[256,1024]{1,0:T(8,128)(2,1)S(1)} %broadcast_select_fusion), channel_id=1, source_target_pairs={{4,8},{6,10},{8,4},{10,6},{20,24},{22,26},{24,20},{26,22}} | collective-permute-start | bytes 1572872 | tf_op jit(solution)/shard_map/ppermute | solution.py:317
  47.4 3.7 %collective-permute-start.2 = (bf16[256,1024]{1,0:T(8,128)(2,1)S(1)}, bf16[256,1024]{1,0:T(8,128)(2,1)}, u32[]{:S(2)}, u32[]{:S(2)}) collective-permute-start(bf16[256,1024]{1,0:T(8,128)(2,1)S(1)} %broadcast_select_fusion.13), channel_id=1, source_target_pairs={{4,8},{6,10},{8,4},{10,6},{20,24},{22,26},{24,20},{26,22}} | collective-permute-start | bytes 1572872 | tf_op jit(solution)/shard_map/ppermute | solution.py:317
  49.8 21.7 %collective-permute-start.10 = (bf16[256,1024]{1,0:T(8,128)(2,1)}, bf16[256,1024]{1,0:T(8,128)(2,1)}, u32[]{:S(2)}, u32[]{:S(2)}) collective-permute-start(bf16[256,1024]{1,0:T(8,128)(2,1)} %broadcast_select_fusion.11), channel_id=1, source_target_pairs={{8,12},{10,14},{4,0},{6,2},{24,28},{26,30},{20,16},{22,18}} | collective-permute-start | bytes 1572872 | tf_op jit(solution)/shard_map/ppermute | solution.py:317
  52.2 23.5 %collective-permute-start.3 = (bf16[256,1024]{1,0:T(8,128)(2,1)S(1)}, bf16[256,1024]{1,0:T(8,128)(2,1)}, u32[]{:S(2)}, u32[]{:S(2)}) collective-permute-start(bf16[256,1024]{1,0:T(8,128)(2,1)S(1)} %broadcast_select_fusion.12.refs_0_), channel_id=1, source_target_pairs={{8,12},{10,14},{4,0},{6,2},{24,28},{26,30},{20,16},{22,18}} | collective-permute-start | bytes 1572872 | tf_op jit(solution)/shard_map/ppermute | solution.py:317
  73.7 11.4 %collective-permute-start.12 = (bf16[256,1024]{1,0:T(8,128)(2,1)}, bf16[256,1024]{1,0:T(8,128)(2,1)}, u32[]{:S(2)}, u32[]{:S(2)}) collective-permute-start(bf16[256,1024]{1,0:T(8,128)(2,1)} %select_select_fusion), channel_id=1, source_target_pairs={{0,2},{2,0},{4,6},{6,4},{8,10},{10,8},{12,14},{14,12},{16,18},{18,... | collective-permute-start | bytes 1572872 | tf_op jit(solution)/shard_map/ppermute | solution.py:317
  77.1 13.5 %collective-permute-start.5 = (bf16[256,1024]{1,0:T(8,128)(2,1)S(1)}, bf16[256,1024]{1,0:T(8,128)(2,1)S(1)}, u32[]{:S(2)}, u32[]{:S(2)}) collective-permute-start(bf16[256,1024]{1,0:T(8,128)(2,1)S(1)} %select_select_fusion.1), channel_id=1, source_target_pairs={{0,2},{2,0},{4,6},{6,4},{8,10},{10,8},{12,14},{14,12},{16,18},{18,... | collective-permute-start | bytes 1572872 | tf_op jit(solution)/shard_map/ppermute | solution.py:317
  80.8 11.8 %collective-permute-start.11 = (bf16[256,1024]{1,0:T(8,128)(2,1)}, bf16[256,1024]{1,0:T(8,128)(2,1)}, u32[]{:S(2)}, u32[]{:S(2)}) collective-permute-start(bf16[256,1024]{1,0:T(8,128)(2,1)} %select_select_fusion), channel_id=1, source_target_pairs={{0,1},{2,3},{4,5},{6,7},{8,9},{10,11},{12,13},{14,15},{16,17},{18,... | collective-permute-start | bytes 1572872 | tf_op jit(solution)/shard_map/ppermute | solution.py:317
  85.0 7.6 %collective-permute-start.13 = (bf16[256,1024]{1,0:T(8,128)(2,1)}, bf16[256,1024]{1,0:T(8,128)(2,1)}, u32[]{:S(2)}, u32[]{:S(2)}) collective-permute-start(bf16[256,1024]{1,0:T(8,128)(2,1)} %collective-permute-done.12), channel_id=1, source_target_pairs={{0,1},{2,3},{4,5},{6,7},{8,9},{10,11},{12,13},{14,15},{16,17},{18,... | collective-permute-start | bytes 1572872 | tf_op jit(solution)/shard_map/ppermute | solution.py:317
  87.1 15.6 %collective-permute-start.4 = (bf16[256,1024]{1,0:T(8,128)(2,1)S(1)}, bf16[256,1024]{1,0:T(8,128)(2,1)}, u32[]{:S(2)}, u32[]{:S(2)}) collective-permute-start(bf16[256,1024]{1,0:T(8,128)(2,1)S(1)} %select_select_fusion.1), channel_id=1, source_target_pairs={{0,1},{2,3},{4,5},{6,7},{8,9},{10,11},{12,13},{14,15},{16,17},{18,... | collective-permute-start | bytes 1572872 | tf_op jit(solution)/shard_map/ppermute | solution.py:317
  90.5 12.2 %collective-permute-start.6 = (bf16[256,1024]{1,0:T(8,128)(2,1)S(1)}, bf16[256,1024]{1,0:T(8,128)(2,1)}, u32[]{:S(2)}, u32[]{:S(2)}) collective-permute-start(bf16[256,1024]{1,0:T(8,128)(2,1)S(1)} %collective-permute-done.5), channel_id=1, source_target_pairs={{0,1},{2,3},{4,5},{6,7},{8,9},{10,11},{12,13},{14,15},{16,17},{18,... | collective-permute-start | bytes 1572872 | tf_op jit(solution)/shard_map/ppermute | solution.py:317
  102.9 59.7 %copy-start.8 = (bf16[256,1024]{1,0:T(8,128)(2,1)}, bf16[256,1024]{1,0:T(8,128)(2,1)S(1)}, u32[]{:S(2)}) copy-start(bf16[256,1024]{1,0:T(8,128)(2,1)S(1)} %get-tuple-element.82.high_ref.refs_3_) | copy-start | bytes 1572868
  102.9 59.7 %copy-start.10 = (bf16[256,1024]{1,0:T(8,128)(2,1)}, bf16[256,1024]{1,0:T(8,128)(2,1)S(1)}, u32[]{:S(2)}) copy-start(bf16[256,1024]{1,0:T(8,128)(2,1)S(1)} %get-tuple-element.83.low_ref.refs_2_) | copy-start | bytes 1572868
  110.1 3.1 %collective-permute-start.14 = (f32[264,1024]{1,0:T(8,128)}, f32[264,1024]{1,0:T(8,128)}, u32[]{:S(2)}, u32[]{:S(2)}) collective-permute-start(f32[264,1024]{1,0:T(8,128)} %row_part.5), channel_id=1, source_target_pairs={{0,1},{1,0},{2,3},{3,2},{4,5},{5,4},{6,7},{7,6},{8,9},{9,8},{10,11... | collective-permute-start | bytes 3244040 | tf_op jit(solution)/shard_map/ppermute | solution.py:317
  111.4 6.4 %collective-permute-start.16 = (f32[264,1024]{1,0:T(8,128)S(1)}, f32[264,1024]{1,0:T(8,128)}, u32[]{:S(2)}, u32[]{:S(2)}) collective-permute-start(f32[264,1024]{1,0:T(8,128)S(1)} %row_part.7), channel_id=1, source_target_pairs={{0,1},{1,0},{2,3},{3,2},{4,5},{5,4},{6,7},{7,6},{8,9},{9,8},{10,11... | collective-permute-start | bytes 3244040 | tf_op jit(solution)/shard_map/ppermute | solution.py:317
  115.6 11.9 %collective-permute-start.15 = (s32[272,256]{1,0:T(8,128)S(1)}, s32[272,256]{1,0:T(8,128)S(1)}, u32[]{:S(2)}, u32[]{:S(2)}) collective-permute-start(s32[272,256]{1,0:T(8,128)S(1)} %get-tuple-element.55), channel_id=1, source_target_pairs={{0,2},{2,0},{1,3},{3,1},{4,6},{6,4},{5,7},{7,5},{8,10},{10,8},{9,1... | collective-permute-start | bytes 835592 | tf_op jit(solution)/shard_map/ppermute | solution.py:317
  119.4 20.4 %collective-permute-start.18 = (s32[272,256]{1,0:T(8,128)S(1)}, s32[272,256]{1,0:T(8,128)S(1)}, u32[]{:S(2)}, u32[]{:S(2)}) collective-permute-start(s32[272,256]{1,0:T(8,128)S(1)} %get-tuple-element.58.refs_4_), channel_id=1, source_target_pairs={{0,2},{2,0},{1,3},{3,1},{4,6},{6,4},{5,7},{7,5},{8,10},{10,8},{9,1... | collective-permute-start | bytes 835592 | tf_op jit(solution)/shard_map/ppermute | solution.py:317
  127.8 21.4 %collective-permute-start.17 = (s32[272,256]{1,0:T(8,128)S(1)}, s32[272,256]{1,0:T(8,128)S(1)}, u32[]{:S(2)}, u32[]{:S(2)}) collective-permute-start(s32[272,256]{1,0:T(8,128)S(1)} %get-tuple-element.62), channel_id=1, source_target_pairs={{0,4},{1,5},{2,6},{3,7},{12,8},{13,9},{14,10},{15,11},{16,20},{17,... | collective-permute-start | bytes 835592 | tf_op jit(solution)/shard_map/ppermute | solution.py:317
  140.2 11.1 %collective-permute-start.20 = (s32[272,256]{1,0:T(8,128)S(1)}, s32[272,256]{1,0:T(8,128)S(1)}, u32[]{:S(2)}, u32[]{:S(2)}) collective-permute-start(s32[272,256]{1,0:T(8,128)S(1)} %get-tuple-element.65.refs_4_), channel_id=1, source_target_pairs={{0,4},{1,5},{2,6},{3,7},{12,8},{13,9},{14,10},{15,11},{16,20},{17,... | collective-permute-start | bytes 835592 | tf_op jit(solution)/shard_map/ppermute | solution.py:317
  149.6 9.5 %collective-permute-start.19 = (s32[272,256]{1,0:T(8,128)S(1)}, s32[272,256]{1,0:T(8,128)S(1)}, u32[]{:S(2)}, u32[]{:S(2)}) collective-permute-start(s32[272,256]{1,0:T(8,128)S(1)} %merge.10), channel_id=1, source_target_pairs={{4,8},{5,9},{6,10},{7,11},{8,4},{9,5},{10,6},{11,7},{20,24},{21,25... | collective-permute-start | bytes 835592 | tf_op jit(solution)/shard_map/ppermute | solution.py:317
  151.5 9.2 %collective-permute-start.22 = (s32[272,256]{1,0:T(8,128)S(1)}, s32[272,256]{1,0:T(8,128)S(1)}, u32[]{:S(2)}, u32[]{:S(2)}) collective-permute-start(s32[272,256]{1,0:T(8,128)S(1)} %merge.11.refs_4_), channel_id=1, source_target_pairs={{4,8},{5,9},{6,10},{7,11},{8,4},{9,5},{10,6},{11,7},{20,24},{21,25... | collective-permute-start | bytes 835592 | tf_op jit(solution)/shard_map/ppermute | solution.py:317
  159.4 15.6 %collective-permute-start.21 = (s32[272,256]{1,0:T(8,128)S(1)}, s32[272,256]{1,0:T(8,128)S(1)}, u32[]{:S(2)}, u32[]{:S(2)}) collective-permute-start(s32[272,256]{1,0:T(8,128)S(1)} %merge.12), channel_id=1, source_target_pairs={{8,12},{9,13},{10,14},{11,15},{4,0},{5,1},{6,2},{7,3},{24,28},{25,... | collective-permute-start | bytes 835592 | tf_op jit(solution)/shard_map/ppermute | solution.py:317
  161.0 18.8 %collective-permute-start.26 = (s32[272,256]{1,0:T(8,128)S(1)}, s32[272,256]{1,0:T(8,128)S(1)}, u32[]{:S(2)}, u32[]{:S(2)}) collective-permute-start(s32[272,256]{1,0:T(8,128)S(1)} %merge.13.refs_4_), channel_id=1, source_target_pairs={{8,12},{9,13},{10,14},{11,15},{4,0},{5,1},{6,2},{7,3},{24,28},{25,... | collective-permute-start | bytes 835592 | tf_op jit(solution)/shard_map/ppermute | solution.py:317
  176.0 9.3 %collective-permute-start.23 = (s32[272,256]{1,0:T(8,128)S(1)}, s32[272,256]{1,0:T(8,128)S(1)}, u32[]{:S(2)}, u32[]{:S(2)}) collective-permute-start(s32[272,256]{1,0:T(8,128)S(1)} %get-tuple-element.76), channel_id=1, source_target_pairs={{2,0},{6,4},{10,8},{14,12},{18,16},{22,20},{26,24},{30,28}} | collective-permute-start | bytes 835592 | tf_op jit(solution)/shard_map/ppermute | solution.py:317
  177.3 10.6 %collective-permute-start.24 = (s32[272,256]{1,0:T(8,128)S(1)}, s32[272,256]{1,0:T(8,128)S(1)}, u32[]{:S(2)}, u32[]{:S(2)}) collective-permute-start(s32[272,256]{1,0:T(8,128)S(1)} %get-tuple-element.76), channel_id=1, source_target_pairs={{1,0},{5,4},{9,8},{13,12},{17,16},{21,20},{25,24},{29,28}} | collective-permute-start | bytes 835592 | tf_op jit(solution)/shard_map/ppermute | solution.py:317
  178.6 9.3 %collective-permute-start.25 = (s32[272,256]{1,0:T(8,128)S(1)}, s32[272,256]{1,0:T(8,128)S(1)}, u32[]{:S(2)}, u32[]{:S(2)}) collective-permute-start(s32[272,256]{1,0:T(8,128)S(1)} %get-tuple-element.76), channel_id=1, source_target_pairs={{3,0},{7,4},{11,8},{15,12},{19,16},{23,20},{27,24},{31,28}} | collective-permute-start | bytes 835592 | tf_op jit(solution)/shard_map/ppermute | solution.py:317
  181.9 8.6 %collective-permute-start.27 = (s32[272,256]{1,0:T(8,128)S(1)}, s32[272,256]{1,0:T(8,128)S(1)}, u32[]{:S(2)}, u32[]{:S(2)}) collective-permute-start(s32[272,256]{1,0:T(8,128)S(1)} %get-tuple-element.78), channel_id=1, source_target_pairs={{2,0},{6,4},{10,8},{14,12},{18,16},{22,20},{26,24},{30,28}} | collective-permute-start | bytes 835592 | tf_op jit(solution)/shard_map/ppermute | solution.py:317
  183.2 7.3 %collective-permute-start.28 = (s32[272,256]{1,0:T(8,128)S(1)}, s32[272,256]{1,0:T(8,128)S(1)}, u32[]{:S(2)}, u32[]{:S(2)}) collective-permute-start(s32[272,256]{1,0:T(8,128)S(1)} %get-tuple-element.78), channel_id=1, source_target_pairs={{1,0},{5,4},{9,8},{13,12},{17,16},{21,20},{25,24},{29,28}} | collective-permute-start | bytes 835592 | tf_op jit(solution)/shard_map/ppermute | solution.py:317
  185.3 8.1 %collective-permute-start.29 = (s32[272,256]{1,0:T(8,128)S(1)}, s32[272,256]{1,0:T(8,128)S(1)}, u32[]{:S(2)}, u32[]{:S(2)}) collective-permute-start(s32[272,256]{1,0:T(8,128)S(1)} %get-tuple-element.78), channel_id=1, source_target_pairs={{3,0},{7,4},{11,8},{15,12},{19,16},{23,20},{27,24},{31,28}} | collective-permute-start | bytes 835592 | tf_op jit(solution)/shard_map/ppermute | solution.py:317
  (20 other events, 174.3 us)

commit v7 on v6

--- a/solution.py
+++ b/solution.py
@@ -35,7 +35,7 @@
     return 1.0 / jnp.sqrt(jnp.sum(total, axis=1, keepdims=True) + 1e-06)
 
 
-def head_kernel(decoder_ref, *refs):
+def head_kernel(flags_ref, decoder_ref, *refs):
     chunk_refs, (held, sems) = refs[:COUNT], refs[COUNT:]
     step = chunk_refs[0].shape[1]
     strip = ROWS // 4
@@ -73,7 +73,7 @@
         block = held.at[j % 2]
         for base in range(0, BLOCK, strip):
             rows = slice(base, base + strip)
-            to = slice((low + j) * BLOCK + base, (low + j) * BLOCK + base + strip)
+            to = slice(j * BLOCK + base, j * BLOCK + base + strip)
             inverse = strip_inverse(block, rows)
             inverse_ref[to, :] = jnp.broadcast_to(inverse, (strip, 128))
             for t in range(0, block.shape[1], 128):
@@ -99,92 +99,92 @@
     return low + high
 
 
-def partial_kernel(k, units_ref, low_ref, high_ref, out_ref):
-    size = min(WIDE, units_ref.shape[0])
-
-    def body(j, carry):
-        rows = pl.ds(pl.multiple_of(j * size, size), size)
-        out_ref[rows, :] = pair_cosines(k, units_ref, rows, low_ref, high_ref)
-        return carry
-
-    lax.fori_loop(0, units_ref.shape[0] // size, body, 0)
-
-
-def weight_kernel(
-    k,
-    delta_ref,
-    units_ref,
-    low_ref,
-    high_ref,
-    partial_ref,
-    col_ref,
-    row_ref,
-    along_ref,
-    penalty_ref,
-):
-    size = min(WIDE, units_ref.shape[0])
+def pick_kernel(slots, count, flags_ref, *refs):
+    for slot, out_ref in zip(slots, refs[-len(slots) :]):
+        for c in range(count):
+
+            @pl.when(flags_ref[slot] == c)
+            def _(out_ref=out_ref, c=c):
+                out_ref[...] = refs[c][...]
+
+
+def partial_kernel(k, parts, low_ref, high_ref, *refs):
+    out_ref = refs[-1]
+    base = 0
+    for units_ref in refs[:parts]:
+        count = units_ref.shape[0]
+        size = min(WIDE, count)
+
+        def body(j, carry, units_ref=units_ref, size=size, base=base):
+            rows = pl.ds(pl.multiple_of(j * size, size), size)
+            to = pl.ds(pl.multiple_of(base + j * size, size), size)
+            out_ref[to, :] = pair_cosines(k, units_ref, rows, low_ref, high_ref)
+            return carry
+
+        lax.fori_loop(0, count // size, body, 0)
+        base += count
+
+
+def weight_kernel(k, parts, delta_ref, low_ref, high_ref, partial_ref, *refs):
+    col_ref, row_ref, factor_ref, penalty_ref = refs[-4:]
     penalty_ref[...] = jnp.zeros_like(penalty_ref)
-
-    def body(j, carry):
-        span = pl.ds(pl.multiple_of(j * size, size), size)
-        cosines = partial_ref[span, :] + pair_cosines(k, units_ref, span, low_ref, high_ref)
-        latents = lax.broadcasted_iota(jnp.int32, (size, ROWS), 0) + (delta_ref[0] + j * size)
-        rows = lax.broadcasted_iota(jnp.int32, (size, ROWS), 1)
-        inside = (latents >= 0) & (latents < ROWS)
-        weight = jnp.where(latents == rows, 0.0, jnp.where(inside, 0.5, 1.0))
-        products = weight * cosines
-        weighted = products.astype(jnp.bfloat16)
-        col_ref[span, :] = weighted
-        row_ref[:, span] = products.T.astype(jnp.bfloat16)
-        along = jnp.sum(weighted.astype(jnp.float32) * cosines, axis=1, keepdims=True)
-        along_ref[span, :] = jnp.broadcast_to(along, (size, 128))
-        squares = products * cosines
-        squares = squares[:, :128] + squares[:, 128:]
-        penalty_ref[...] += jnp.sum(squares.reshape(size // 8, 8, 128), axis=0)
-        return carry
-
-    lax.fori_loop(0, units_ref.shape[0] // size, body, 0)
-
-
-def row_kernel(k, side_ref, row_ref, penalty_ref, units_ref, out_ref):
+    base = 0
+    for units_ref, inverse_ref in zip(refs[:parts], refs[parts : 2 * parts]):
+        count = units_ref.shape[0]
+        size = min(WIDE, count)
+
+        def body(j, carry, units_ref=units_ref, inverse_ref=inverse_ref, size=size, base=base):
+            here = pl.ds(pl.multiple_of(j * size, size), size)
+            first = base + j * size
+            span = pl.ds(pl.multiple_of(first, size), size)
+            cosines = partial_ref[span, :] + pair_cosines(k, units_ref, here, low_ref, high_ref)
+            latents = lax.broadcasted_iota(jnp.int32, (size, ROWS), 0) + (delta_ref[0] + first)
+            rows = lax.broadcasted_iota(jnp.int32, (size, ROWS), 1)
+            inside = (latents >= 0) & (latents < ROWS)
+            weight = jnp.where(latents == rows, 0.0, jnp.where(inside, 0.5, 1.0))
+            products = weight * cosines
+            weighted = products.astype(jnp.bfloat16)
+            col_ref[span, :] = weighted
+            row_ref[:, span] = products.T.astype(jnp.bfloat16)
+            along = jnp.sum(weighted.astype(jnp.float32) * cosines, axis=1, keepdims=True)
+            inverse = inverse_ref[here, :]
+            lanes = lax.broadcasted_iota(jnp.int32, (size, 128), 1)
+            factor_ref[span, :] = jnp.where(lanes < 64, inverse, along * inverse)
+            squares = products * cosines
+            squares = squares[:, :128] + squares[:, 128:]
+            penalty_ref[...] += jnp.sum(squares.reshape(size // 8, 8, 128), axis=0)
+            return carry
+
+        lax.fori_loop(0, count // size, body, 0)
+        base += count
+
+
+def row_kernel(k, parts, side_ref, row_ref, penalty_ref, *refs):
+    out_ref = refs[-1]
     tile = out_ref.shape[1] // 2
     first = (2 * k + side_ref[0]) * out_ref.shape[1]
     for i in range(2):
         span = pl.ds(pl.multiple_of(first + i * tile, tile), tile)
-        out_ref[:ROWS, i * tile : (i + 1) * tile] = jnp.dot(
-            row_ref[...], units_ref[:, span], preferred_element_type=jnp.float32
-        )
+        total, base = None, 0
+        for units_ref in refs[:parts]:
+            count = units_ref.shape[0]
+            part = jnp.dot(
+                row_ref[:, base : base + count],
+                units_ref[:, span],
+                preferred_element_type=jnp.float32,
+            )
+            total = part if total is None else total + part
+            base += count
+        out_ref[:ROWS, i * tile : (i + 1) * tile] = total
     out_ref[ROWS:, :] = jnp.concatenate([penalty_ref[...]] * (out_ref.shape[1] // 128), axis=1)
 
 
-def next_block(low, decoder_ref, held, sems):
-    i, size = pl.program_id(0), held.shape[1]
-
-    def fetch(j):
-        rows = pl.ds(pl.multiple_of((low + j) * size, size), size)
-        slot = lax.rem(j, 2)
-        return pltpu.make_async_copy(decoder_ref.at[rows, :], held.at[slot], sems.at[slot])
-
-    @pl.when(i == 0)
-    def _():
-        fetch(i).start()
-
-    @pl.when(i + 1 < pl.num_programs(0))
-    def _():
-        fetch(i + 1).start()
-
-    fetch(i).wait()
-    return held.at[lax.rem(i, 2)]
-
-
-def finish_kernel(low, pinned_ref, col_ref, inverse_ref, along_ref, *refs):
+def finish_kernel(col_ref, decoder_ref, factor_ref, *refs):
     chunks = refs[:COUNT]
-    out_ref, mark_ref, held, sems = refs[-4:]
-    decoder_ref = next_block(low, pinned_ref, held, sems)
+    out_ref, mark_ref = refs[-2:]
     step = chunks[0].shape[1]
-    inverse = inverse_ref[:, :1]
-    scale = (2.0 * math.sqrt(DW)) * inverse
-    back = scale * (along_ref[:, :1] * inverse)
+    scale = (2.0 * math.sqrt(DW)) * factor_ref[:, :1]
+    back = scale * factor_ref[:, 64:65]
     for k in range(COUNT):
         span = slice(k * step, (k + 1) * step)
         part = jnp.dot(col_ref[...], chunks[k][...], preferred_element_type=jnp.float32)
@@ -265,10 +265,10 @@
     encode(value, penalty, refs[-1])
 
 
-def last_kernel(owner_ref, pinned_ref, col_ref, inverse_ref, *refs):
+def last_kernel(share, owner_ref, col_ref, decoder_ref, factor_ref, tile_ref, *refs):
     chunks, sums = refs[:COUNT], refs[COUNT : COUNT + 7 * PAIRS]
-    out_ref, column, held, sems = refs[-4:]
-    decoder_ref = next_block(0, pinned_ref, held, sems)
+    out_ref, penalty_ref, column = refs[-3:]
+    penalty_ref[0] = jnp.sum(tile_ref[...]) * share
     step = chunks[0].shape[1]
     piece = step // 2
     owner = owner_ref[0] == 1
@@ -286,7 +286,7 @@
         along = part * decoder_ref[:, span].astype(jnp.float32)
         for t in range(0, step, 128):
             total = total + along[:, t : t + 128]
-    inverse = inverse_ref[:, :1]
+    inverse = factor_ref[:, :1]
     scale = (2.0 * math.sqrt(DW)) * inverse
     back = scale * (jnp.sum(total, axis=1, keepdims=True) * inverse * inverse)
     for k in range(COUNT):
@@ -310,7 +310,6 @@
     within = index % per
     here = place == chosen_quarter
     even_chip = (within // 2) % 2 == 0
-    odd_core = (within % 2) == 1
     smem = pl.BlockSpec(memory_space=pltpu.SMEM)
 
     def send(value, pairs):
@@ -319,13 +318,32 @@
     def each(moves):
         return [(z * per + a, z * per + b) for z in range(4) for a, b in moves]
 
+    near = jnp.where(place == 1, chosen_quarter == 0, chosen_quarter == 3)
+    middle = (place == 1) | (place == 2)
+    reached = jnp.where(here, 0, jnp.where(middle, jnp.where(near, 1, 2), 3))
+    core_index = within % 2
+    fresh = [(within >= 4 << n) & (within < 8 << n) for n in range((per // 4).bit_length() - 1)]
+    TAKES, WAITS, REACHED, LOW, HIGH, FRESH = range(6)
+    flags = jnp.stack(
+        [
+            jnp.where(within == 2, 1, 0),
+            jnp.where(here, 0, 1),
+            reached,
+            jnp.where(even_chip, 0, 2) + core_index,
+            jnp.where(even_chip, 2, 0) + core_index,
+        ]
+        + [jnp.where(value, 1, 0) for value in fresh]
+    ).astype(jnp.int32)
+
     pinned = pl.BlockSpec(memory_space=pl.ANY)
+    any_spec = pinned
     vmem = pl.BlockSpec(memory_space=pltpu.VMEM)
+    chunk_type = jax.ShapeDtypeStruct((ROWS, step), jnp.bfloat16)
     own = pl.pallas_call(
         head_kernel,
-        in_specs=[pinned],
+        in_specs=[smem, pinned],
         out_specs=[vmem] * COUNT,
-        out_shape=[jax.ShapeDtypeStruct((ROWS, step), jnp.bfloat16)] * COUNT,
+        out_shape=[chunk_type] * COUNT,
         scratch_shapes=[
             pltpu.VMEM((ROWS, width), jnp.bfloat16),
             pltpu.SemaphoreType.DMA((4,)),
@@ -333,9 +351,8 @@
         compiler_params=params(50),
         cost_estimate=cost(4 * ROWS * width, 4 * ROWS * width),
         name="head_units",
-    )(decoder)
-
-    any_spec = pl.BlockSpec(memory_space=pl.ANY)
+    )(flags, decoder)
+
     across_x = each([(0, 2), (2, 0), (1, 3), (3, 1)])
     across_core = each([(0, 1), (1, 0), (2, 3), (3, 2)])
     piece = step // 2
@@ -344,95 +361,90 @@
         moves = (((0, 1), (3, 2)), ((1, 2), (2, 1)), ((2, 3), (1, 0)))[level]
         return [(a * per + w, b * per + w) for a, b in moves for w in lanes]
 
-    unit_bounds = [0, blocks // 4, 5 * blocks // 8, blocks]
-    made = [None, None]
+    def pick(slots, candidates, ties=()):
+        return pl.pallas_call(
+            functools.partial(pick_kernel, slots, len(candidates)),
+            in_specs=[smem] + [vmem] * len(candidates) + [any_spec] * len(ties),
+            out_specs=[vmem] * len(slots),
+            out_shape=[chunk_type] * len(slots),
+            compiler_params=params(12),
+            cost_estimate=cost(ROWS * step, 4 * ROWS * step),
+            name="pick",
+        )(flags, *candidates, *ties)
+
+    unit_bounds = [0, blocks // 4, blocks // 2, blocks]
+    units, inverses = [], []
 
     def make_units(part, tie):
         low, high = unit_bounds[part], unit_bounds[part + 1]
         if high == low:
-            return True
-        operands = [decoder, tie]
-        specs = [pinned, any_spec]
-        aliases = {}
-        if made[0] is not None:
-            aliases = {2: 0, 3: 1}
-            operands += made
-            specs += [vmem, vmem]
-        made[:] = pl.pallas_call(
+            return []
+        rows = (high - low) * BLOCK
+        made = pl.pallas_call(
             functools.partial(units_kernel, low, high - low),
-            in_specs=specs,
+            in_specs=[pinned, any_spec],
             out_specs=[vmem, vmem],
             out_shape=[
-                jax.ShapeDtypeStruct((shard, width), jnp.bfloat16),
-                jax.ShapeDtypeStruct((shard, 128), jnp.float32),
+                jax.ShapeDtypeStruct((rows, width), jnp.bfloat16),
+                jax.ShapeDtypeStruct((rows, 128), jnp.float32),
             ],
             scratch_shapes=[
                 pltpu.VMEM((2, BLOCK, width), jnp.bfloat16),
                 pltpu.SemaphoreType.DMA((2,)),
             ],
-            input_output_aliases=aliases,
-            compiler_params=params(24),
-            cost_estimate=cost(4 * BLOCK * width, 4 * (high - low) * BLOCK * width),
+            compiler_params=params((46, 44, 34)[part]),
+            cost_estimate=cost(4 * rows * width, 4 * rows * width),
             name="units",
-        )(*operands)
-        return made[1][low * BLOCK, 0] > 0
-
-    near = jnp.where(place == 1, chosen_quarter == 0, chosen_quarter == 3)
-    middle = (place == 1) | (place == 2)
+        )(decoder, tie)
+        units.append(made[0])
+        inverses.append(made[1])
+        return [made[1]]
+
     mine, first, second, third, held = ([None] * PAIRS for _ in range(5))
     across = [send(own[2 * k + 1], each([(0, 2)])) for k in range(PAIRS)]
     done = make_units(0, own[0])
     for k in range(PAIRS):
-        takes = (within == 2) & done if k == 0 else within == 2
-        mine[k] = jnp.where(takes, across[k], own[2 * k])
-    for k in range(PAIRS):
+        [mine[k]] = pick([TAKES], [own[2 * k], across[k]], () if k else done)
         first[k] = send(mine[k], hop(0, (0, 2)))
     done = make_units(1, mine[PAIRS - 1])
-    going = [None] * PAIRS
-    for k in range(PAIRS):
-        keeps = here & done if k == 0 else here
-        going[k] = jnp.where(keeps, mine[k], first[k])
-        second[k] = send(going[k], hop(1, (0, 2)))
-    for k in range(PAIRS):
-        going[k] = jnp.where(here, mine[k], second[k])
-        third[k] = send(going[k], hop(2, (0, 2)))
-    done = make_units(2, going[PAIRS - 1])
-    units, inverse = made
-    for k in range(PAIRS):
-        inner = jnp.where(near, first[k], second[k])
-        keeps = here & done if k == 0 else here
-        held[k] = jnp.where(keeps, mine[k], jnp.where(middle, inner, third[k]))
+    for k in range(PAIRS):
+        [going] = pick([WAITS], [mine[k], first[k]], () if k else done)
+        second[k] = send(going, hop(1, (0, 2)))
+    for k in range(PAIRS):
+        [going] = pick([WAITS], [mine[k], second[k]])
+        third[k] = send(going, hop(2, (0, 2)))
+    for k in range(PAIRS):
+        [held[k]] = pick([REACHED], [mine[k], first[k], second[k], third[k]])
+    done = make_units(2, held[PAIRS - 1])
     chosen = []
     for k in range(PAIRS):
         other = send(held[k], each([(0, 2), (2, 0)]))
         core_held = send(held[k], each([(0, 1), (2, 3)]))
         core_other = send(other, each([(0, 1), (2, 3)]))
-        one = jnp.where(odd_core, core_held, held[k])
-        two = jnp.where(odd_core, core_other, other)
-        pair = [jnp.where(even_chip, one, two), jnp.where(even_chip, two, one)]
-        far = 4
-        while far < per:
-            moves = each([(w, w + far) for w in range(far)])
-            fresh = (within >= far) & (within < 2 * far)
-            pair = [jnp.where(fresh, send(value, moves), value) for value in pair]
-            far *= 2
+        pair = pick(
+            [LOW, HIGH], [held[k], core_held, other, core_other], () if k else done
+        )
+        for n in range(len(fresh)):
+            moves = each([(w, w + (4 << n)) for w in range(4 << n)])
+            pair = [pick([FRESH + n], [value, send(value, moves)])[0] for value in pair]
         chosen += pair
 
     delta = jnp.reshape(index * shard - start, (1,)).astype(jnp.int32)
     whole_chunk = pl.BlockSpec((ROWS, step), lambda i: (0, 0))
     half_flops = ROWS * shard * width
+    parts = len(units)
     partial = pl.pallas_call(
-        functools.partial(partial_kernel, 0),
-        in_specs=[vmem] * 3,
+        functools.partial(partial_kernel, 0, parts),
+        in_specs=[vmem] * (2 + parts),
         out_specs=vmem,
         out_shape=jax.ShapeDtypeStruct((shard, ROWS), jnp.float32),
-        compiler_params=params(24),
+        compiler_params=params(16),
         cost_estimate=cost(half_flops, shard * width),
         name="part_cosines",
-    )(units, chosen[0], chosen[1])
-    by_col, by_row, along, local_penalty = pl.pallas_call(
-        functools.partial(weight_kernel, 1),
-        in_specs=[smem] + [vmem] * 4,
+    )(chosen[0], chosen[1], *units)
+    by_col, by_row, factors, local_penalty = pl.pallas_call(
+        functools.partial(weight_kernel, 1, parts),
+        in_specs=[smem] + [vmem] * (3 + 2 * parts),
         out_specs=[vmem] * 4,
         out_shape=[
             jax.ShapeDtypeStruct((shard, ROWS), jnp.bfloat16),
@@ -440,10 +452,10 @@
             jax.ShapeDtypeStruct((shard, 128), jnp.float32),
             jax.ShapeDtypeStruct((8, 128), jnp.float32),
         ],
-        compiler_params=params(24),
+        compiler_params=params(16),
         cost_estimate=cost(half_flops, shard * width),
         name="weights",
-    )(delta, units, chosen[2], chosen[3], partial)
+    )(delta, chosen[2], chosen[3], partial, *units, *inverses)
 
     core_side = within % 2
     plane_x = jnp.reshape((within // 2) % 2, (1,)).astype(jnp.int32)
@@ -455,14 +467,14 @@
 
     def row_part(k, side):
         return pl.pallas_call(
-            functools.partial(row_kernel, k),
-            in_specs=[smem, vmem, vmem, vmem],
+            functools.partial(row_kernel, k, parts),
+            in_specs=[smem] + [vmem] * (2 + parts),
             out_specs=vmem,
             out_shape=jax.ShapeDtypeStruct((tall, step), jnp.float32),
             compiler_params=params(24),
             cost_estimate=cost(half_flops // 2, shard * width // 2),
             name="row_part",
-        )(jnp.reshape(side, (1,)).astype(jnp.int32), by_row, local_penalty, units)
+        )(jnp.reshape(side, (1,)).astype(jnp.int32), by_row, local_penalty, *units)
 
     def merge(kept, arrived, keep, ties=()):
         tiles = [piece_type, tile_type, coded_type] if keep else [coded_type]
@@ -507,11 +519,10 @@
         low, high = bounds[part], bounds[part + 1]
         if high == low:
             return []
-        operands = [decoder, by_col, inverse, along, *chosen]
+        operands = [by_col, decoder, factors, *chosen]
         specs = [
-            pinned,
             pl.BlockSpec((BLOCK, ROWS), lambda i: (i + low, 0)),
-            pl.BlockSpec((BLOCK, 128), lambda i: (i + low, 0)),
+            pl.BlockSpec((BLOCK, width), lambda i: (i + low, 0)),
             pl.BlockSpec((BLOCK, 128), lambda i: (i + low, 0)),
         ] + [whole_chunk] * COUNT
         operands.append(tie)
@@ -523,15 +534,11 @@
             specs.append(any_spec)
         rows = (high - low) * BLOCK
         grad, mark = pl.pallas_call(
-            functools.partial(finish_kernel, low),
+            finish_kernel,
             grid=(high - low,),
             in_specs=specs,
             out_specs=[pl.BlockSpec((BLOCK, width), lambda i: (i + low, 0)), mark_spec],
             out_shape=[out_type, mark_type],
-            scratch_shapes=[
-                pltpu.VMEM((2, BLOCK, width), jnp.bfloat16),
-                pltpu.SemaphoreType.DMA((2,)),
-            ],
             input_output_aliases=aliases,
             compiler_params=params(50),
             cost_estimate=cost(2 * ROWS * rows * width, 6 * rows * width),
@@ -563,7 +570,6 @@
         fresh = (within >= far) & (within < 2 * far)
         tile = jnp.where(fresh, send(tile, moves), tile)
         far *= 2
-    penalty = jnp.sum(tile) * (DW / (ROWS * latents))
 
     sums, row_specs = [], []
     narrow = BLOCK // 2
@@ -579,12 +585,13 @@
             ]
 
     owner = jnp.reshape(here & (within == 0), (1,)).astype(jnp.int32)
-    operands = [owner, decoder, by_col, inverse, *chosen, *sums]
+    operands = [owner, by_col, decoder, factors, tile, *chosen, *sums]
     specs = [
         smem,
-        pinned,
         pl.BlockSpec((narrow, ROWS), lambda i: (i, 0)),
+        pl.BlockSpec((narrow, width), lambda i: (i, 0)),
         pl.BlockSpec((narrow, 128), lambda i: (i, 0)),
+        pl.BlockSpec((8, 128), lambda i: (0, 0)),
     ]
     specs += [whole_chunk] * COUNT
     specs += row_specs
@@ -593,23 +600,19 @@
         aliases = {len(operands): 0}
         operands.append(grad)
         specs.append(any_spec)
-    decoder_grad = pl.pallas_call(
-        last_kernel,
+    decoder_grad, penalty = pl.pallas_call(
+        functools.partial(last_kernel, DW / (ROWS * latents)),
         grid=(2,),
         in_specs=specs,
-        out_specs=pl.BlockSpec((narrow, width), lambda i: (i, 0)),
-        out_shape=out_type,
-        scratch_shapes=[
-            pltpu.VMEM((narrow, width), jnp.float32),
-            pltpu.VMEM((2, narrow, width), jnp.bfloat16),
-            pltpu.SemaphoreType.DMA((2,)),
-        ],
+        out_specs=[pl.BlockSpec((narrow, width), lambda i: (i, 0)), smem],
+        out_shape=[out_type, jax.ShapeDtypeStruct((1,), jnp.float32)],
+        scratch_shapes=[pltpu.VMEM((narrow, width), jnp.float32)],
         input_output_aliases=aliases,
         compiler_params=params(50),
         name="finish_rows",
     )(*operands)
 
-    return (jnp.reshape(penalty, (1,)), decoder_grad)
+    return (penalty, decoder_grad)
 
 
 def solution(mesh):

time: 204 us -> 166 us (0.81)
  local copies, waits for them, and re-layouts: 41.9 us -> 7.62 us
  waiting for transfers between devices: 17.7 us -> 37 us
  starting transfers between devices: 60.5 us -> 50.2 us
  other arithmetic: 8.77 us -> 0 us
  between operations: 5.72 us -> 2.03 us
    unnamed x44 -> x36, local copies, waits for them, and re-layouts: 40.3 us -> 7.54 us
    ppermute x30, waiting for transfers between devices: 17.7 us -> 37 us  [send(): return lax.ppermute(value, 'row', pairs)]
    ppermute x30, starting transfers between devices: 60.5 us -> 50.2 us  [send(): return lax.ppermute(value, 'row', pairs)]
    select_n x10 -> x0, other arithmetic: 8.17 us -> none  [the longest x2 3.41 us: on_device(): held[k] = jnp.where(keeps, mine[k], jnp.where(middle, inner, third[k]))]
    pallas_call x2, Pallas kernels: 3.94 us -> 1.37 us  [on_device(): pl.pallas_call(split_kernel, in_specs=[smem, vmem, vmem], out_specs=[vmem...]
    pallas_call x12 -> x22, Pallas kernels: 47.4 us -> 48.7 us  [the longest x4 21.8 us: finish(): pl.pallas_call(finish_kernel, grid=(high - low,), in_specs=specs, out_spe...]
  transfers between devices with their start and end apart: 30 -> 30, of which waited for: 7 -> 13; matrix products, arithmetic and copies ran while one was open for 5% -> 0% of each run, Pallas kernels for 26% -> 33%
where the time goes in v7:
time: 166 us; the launch traced here: 165 us
  Pallas kernels  68.1 us (41%)
  starting transfers between devices  50.2 us (30%)
  waiting for transfers between devices  37 us (22%)
  local copies, waits for them, and re-layouts  7.62 us (5%)
  between operations  2.03 us (1%)
    ppermute x30, starting transfers between devices, send(): return lax.ppermute(value, 'row', pairs)  50.2 us
    ppermute x30, waiting for transfers between devices, send(): return lax.ppermute(value, 'row', pairs)  37 us
    pallas_call x4, Pallas kernels, finish(): pl.pallas_call(finish_kernel, grid=(high - low,), in_specs=specs, out_spe...  21.8 us
    pallas_call x3, Pallas kernels, make_units(): pl.pallas_call(functools.partial(units_kernel, low, high - low), in_specs...  13.3 us
    unnamed x36, local copies, waits for them, and re-layouts  7.54 us
    pallas_call x10, Pallas kernels, pick(): pl.pallas_call(functools.partial(pick_kernel, slots, len(candidates)), in...  7.25 us
    pallas_call x1, Pallas kernels, on_device(): pl.pallas_call(functools.partial(last_kernel, DW / (ROWS * latents)), gri...  5.45 us
    pallas_call x4, Pallas kernels, row_part(): pl.pallas_call(functools.partial(row_kernel, k, parts), in_specs=[smem] +...  5.02 us
  transfers between devices with their start and end apart: 30, of which 13 were waited for; matrix products, arithmetic and copies ran while one was open for 0% of the time, Pallas kernels for 33%

profile of v7, /device:TPU:0, one launch (start us, length us, event | category | flops | bytes accessed | tf_op | source)
XLA Modules:
  0.0 164.9 jit_solution(11675129193033706708)
XLA Ops:
  1.5 2.6 %head_units.1 = (bf16[256,1024]{1,0:T(8,128)(2,1)S(1)}, bf16[256,1024]{1,0:T(8,128)(2,1)S(1)}, bf16[256,1024]{1,0:T(8,128)(2,1)S(1)}, bf16[256,1024]{1,0:T(8,128)(2,1)S(1)}) custom-call(s32[5]{0:T(128)S(1)} %stack.23.flags_ref, bf16[2048,4096]{1,0:T(8,128)(2,1)} %decoder_ref.17), custom_call_target="tpu_custom_call" | custom-call | flops 4194304 | bytes 4194304 | tf_op jit(solution)/shard_map/head_units/pallas_call | solution.py:342
  4.1 4.9 %collective-permute-start.7 = (bf16[256,1024]{1,0:T(8,128)(2,1)S(1)}, bf16[256,1024]{1,0:T(8,128)(2,1)S(1)}, u32[]{:S(2)}, u32[]{:S(2)}) collective-permute-start(bf16[256,1024]{1,0:T(8,128)(2,1)S(1)} %get-tuple-element.52), channel_id=1, source_target_pairs={{0,2},{4,6},{8,10},{12,14},{16,18},{20,22},{24,26},{28,30}} | collective-permute-start | bytes 1572872 | tf_op jit(solution)/shard_map/ppermute | solution.py:316
  10.3 3.3 %units.3 = (bf16[512,4096]{1,0:T(8,128)(2,1)S(1)}, f32[512,128]{1,0:T(8,128)S(1)}) custom-call(bf16[2048,4096]{1,0:T(8,128)(2,1)} %decoder_ref.17, bf16[256,1024]{1,0:T(8,128)(2,1)S(1)} %get-tuple-element.51.refs_0_), custom_call_target="tpu_custom_call" | custom-call | flops 8388608 | bytes 8388608 | tf_op jit(solution)/shard_map/units/pallas_call | solution.py:383
  13.6 2.0 %copy-done = bf16[512,4096]{1,0:T(8,128)(2,1)} copy-done((bf16[512,4096]{1,0:T(8,128)(2,1)}, bf16[512,4096]{1,0:T(8,128)(2,1)S(1)}, u32[]{:S(2)}) %copy-start) | copy-done | bytes 4194328
  16.2 3.5 %collective-permute-start.8 = (bf16[256,1024]{1,0:T(8,128)(2,1)S(1)}, bf16[256,1024]{1,0:T(8,128)(2,1)S(1)}, u32[]{:S(2)}, u32[]{:S(2)}) collective-permute-start(bf16[256,1024]{1,0:T(8,128)(2,1)S(1)} %pick.15.refs_0_), channel_id=1, source_target_pairs={{0,4},{2,6},{12,8},{14,10},{16,20},{18,22},{28,24},{30,26}} | collective-permute-start | bytes 1572872 | tf_op jit(solution)/shard_map/ppermute | solution.py:316
  19.8 1.5 collective-permute-done.refs_1_
  21.8 3.5 %collective-permute-start.1 = (bf16[256,1024]{1,0:T(8,128)(2,1)S(1)}, bf16[256,1024]{1,0:T(8,128)(2,1)S(1)}, u32[]{:S(2)}, u32[]{:S(2)}) collective-permute-start(bf16[256,1024]{1,0:T(8,128)(2,1)S(1)} %pick.10.refs_0_), channel_id=1, source_target_pairs={{0,4},{2,6},{12,8},{14,10},{16,20},{18,22},{28,24},{30,26}} | collective-permute-start | bytes 1572872 | tf_op jit(solution)/shard_map/ppermute | solution.py:316
  25.3 3.3 %units.4 = (bf16[512,4096]{1,0:T(8,128)(2,1)S(1)}, f32[512,128]{1,0:T(8,128)S(1)}) custom-call(bf16[2048,4096]{1,0:T(8,128)(2,1)} %decoder_ref.17, bf16[256,1024]{1,0:T(8,128)(2,1)S(1)} %pick.10.refs_0_), custom_call_target="tpu_custom_call" | custom-call | flops 8388608 | bytes 8388608 | tf_op jit(solution)/shard_map/units/pallas_call | solution.py:383
  30.0 2.0 %collective-permute-done.1.refs_1_ = bf16[256,1024]{1,0:T(8,128)(2,1)S(1)} collective-permute-done((bf16[256,1024]{1,0:T(8,128)(2,1)S(1)}, bf16[256,1024]{1,0:T(8,128)(2,1)S(1)}, u32[]{:S(2)}, u32[]{:S(2)}) %collective-permute-start.1) | collective-permute-done | bytes 524320 | tf_op jit(solution)/shard_map/ppermute | solution.py:316
  37.1 12.5 %collective-permute-done.10.refs_3_ = bf16[256,1024]{1,0:T(8,128)(2,1)S(1)} collective-permute-done((bf16[256,1024]{1,0:T(8,128)(2,1)S(1)}, bf16[256,1024]{1,0:T(8,128)(2,1)S(1)}, u32[]{:S(2)}, u32[]{:S(2)}) %collective-permute-start.10) | collective-permute-done | bytes 524320 | tf_op jit(solution)/shard_map/ppermute | solution.py:316
  50.2 4.4 %collective-permute-start.12 = (bf16[256,1024]{1,0:T(8,128)(2,1)S(1)}, bf16[256,1024]{1,0:T(8,128)(2,1)S(1)}, u32[]{:S(2)}, u32[]{:S(2)}) collective-permute-start(bf16[256,1024]{1,0:T(8,128)(2,1)S(1)} %pick.18.refs_0_), channel_id=1, source_target_pairs={{0,2},{2,0},{4,6},{6,4},{8,10},{10,8},{12,14},{14,12},{16,18},{18,... | collective-permute-start | bytes 1572872 | tf_op jit(solution)/shard_map/ppermute | solution.py:316
  55.8 4.4 %collective-permute-start.5 = (bf16[256,1024]{1,0:T(8,128)(2,1)S(1)}, bf16[256,1024]{1,0:T(8,128)(2,1)S(1)}, u32[]{:S(2)}, u32[]{:S(2)}) collective-permute-start(bf16[256,1024]{1,0:T(8,128)(2,1)S(1)} %pick.13.refs_0_), channel_id=1, source_target_pairs={{0,2},{2,0},{4,6},{6,4},{8,10},{10,8},{12,14},{14,12},{16,18},{18,... | collective-permute-start | bytes 1572872 | tf_op jit(solution)/shard_map/ppermute | solution.py:316
  61.7 2.1 %collective-permute-start.13 = (bf16[256,1024]{1,0:T(8,128)(2,1)S(1)}, bf16[256,1024]{1,0:T(8,128)(2,1)}, u32[]{:S(2)}, u32[]{:S(2)}) collective-permute-start(bf16[256,1024]{1,0:T(8,128)(2,1)S(1)} %collective-permute-done.12.refs_2_), channel_id=1, source_target_pairs={{0,1},{2,3},{4,5},{6,7},{8,9},{10,11},{12,13},{14,15},{16,17},{18,... | collective-permute-start | bytes 1572872 | tf_op jit(solution)/shard_map/ppermute | solution.py:316
  65.1 2.2 %collective-permute-done.5.refs_2_ = bf16[256,1024]{1,0:T(8,128)(2,1)S(1)} collective-permute-done((bf16[256,1024]{1,0:T(8,128)(2,1)S(1)}, bf16[256,1024]{1,0:T(8,128)(2,1)S(1)}, u32[]{:S(2)}, u32[]{:S(2)}) %collective-permute-start.5) | collective-permute-done | bytes 524320 | tf_op jit(solution)/shard_map/ppermute | solution.py:316
  67.3 2.1 %collective-permute-start.6 = (bf16[256,1024]{1,0:T(8,128)(2,1)S(1)}, bf16[256,1024]{1,0:T(8,128)(2,1)}, u32[]{:S(2)}, u32[]{:S(2)}) collective-permute-start(bf16[256,1024]{1,0:T(8,128)(2,1)S(1)} %collective-permute-done.5.refs_2_), channel_id=1, source_target_pairs={{0,1},{2,3},{4,5},{6,7},{8,9},{10,11},{12,13},{14,15},{16,17},{18,... | collective-permute-start | bytes 1572872 | tf_op jit(solution)/shard_map/ppermute | solution.py:316
  69.4 6.6 %units.5 = (bf16[1024,4096]{1,0:T(8,128)(2,1)S(1)}, f32[1024,128]{1,0:T(8,128)S(1)}) custom-call(bf16[2048,4096]{1,0:T(8,128)(2,1)} %decoder_ref.17, bf16[256,1024]{1,0:T(8,128)(2,1)S(1)} %pick.13.refs_0_), custom_call_target="tpu_custom_call" | custom-call | flops 16777216 | bytes 16777216 | tf_op jit(solution)/shard_map/units/pallas_call | solution.py:383
  79.0 1.4 pick.19
  80.4 2.8 %part_cosines.1.partial_ref = f32[2048,256]{1,0:T(8,128)S(1)} custom-call(bf16[256,1024]{1,0:T(8,128)(2,1)S(1)} %get-tuple-element.56.low_ref.refs_0_, bf16[256,1024]{1,0:T(8,128)(2,1)S(1)} %get-tuple-element.57.high_ref.refs_1_, bf16[512,4096]{1,0:T(8,128)(2,1)S(1)} %copy-done.1, bf16[512,4096]{1,0:T(8,128)(2,1)S(1)} %copy-done.3, ...), custom_call_target="tpu_custom_call" | custom-call | flops 2147483648 | bytes 8388608 | tf_op jit(solution)/shard_map/part_cosines/pallas_call | solution.py:436
  86.2 3.9 %weights.1 = (bf16[2048,256]{1,0:T(8,128)(2,1)S(1)}, bf16[256,2048]{1,0:T(8,128)(2,1)S(1)}, f32[2048,128]{1,0:T(8,128)S(1)}, f32[8,128]{1,0:T(8,128)S(1)}) custom-call(s32[1]{0:T(128)} %bitcast.2.delta_ref, bf16[256,1024]{1,0:T(8,128)(2,1)S(1)} %get-tuple-element.49.low_ref.refs_2_, bf16[256,1024]{1,0:T(8,128)(2,1)S(1)} %get-tuple-element.50.high_ref.refs_3_, ...), custom_call_target="tpu_custom_call" | custom-call | flops 2147483648 | bytes 8388608 | tf_op jit(solution)/shard_map/weights/pallas_call | solution.py:445
  95.6 2.0 %collective-permute-start.15 = (s32[272,256]{1,0:T(8,128)}, s32[272,256]{1,0:T(8,128)S(1)}, u32[]{:S(2)}, u32[]{:S(2)}) collective-permute-start(s32[272,256]{1,0:T(8,128)} %get-tuple-element.67), channel_id=1, source_target_pairs={{0,2},{2,0},{1,3},{3,1},{4,6},{6,4},{5,7},{7,5},{8,10},{10,8},{9,1... | collective-permute-start | bytes 835592 | tf_op jit(solution)/shard_map/ppermute | solution.py:316
  99.2 5.8 %finish.4 = (f32[2048,4096]{1,0:T(8,128)}, f32[8,128]{1,0:T(8,128)S(1)}) custom-call(bf16[2048,256]{1,0:T(8,128)(2,1)S(1)} %get-tuple-element.61.col_ref, bf16[2048,4096]{1,0:T(8,128)(2,1)} %decoder_ref.17, f32[2048,128]{1,0:T(8,128)} %copy-done.5, bf16[256,1024]{1,0:T(8,128)(2,1)S(1)} %get-tuple-element.56.low_ref.refs_0_, ...), custom_call_target="tpu_custom_call" | custom-call | flops 1073741824 | bytes 12582912 | tf_op jit(solution)/shard_map/finish/pallas_call | solution.py:536
  105.6 1.5 collective-permute-start.17
  107.0 3.6 %collective-permute-done.18.refs_0_ = s32[272,256]{1,0:T(8,128)S(1)} collective-permute-done((s32[272,256]{1,0:T(8,128)S(1)}, s32[272,256]{1,0:T(8,128)S(1)}, u32[]{:S(2)}, u32[]{:S(2)}) %collective-permute-start.18) | collective-permute-done | bytes 278560 | tf_op jit(solution)/shard_map/ppermute | solution.py:316
  110.9 1.5 collective-permute-start.20
  112.4 5.8 %finish.5 = (f32[2048,4096]{1,0:T(8,128)}, f32[8,128]{1,0:T(8,128)S(1)}) custom-call(bf16[2048,256]{1,0:T(8,128)(2,1)S(1)} %get-tuple-element.61.col_ref, bf16[2048,4096]{1,0:T(8,128)(2,1)} %decoder_ref.17, f32[2048,128]{1,0:T(8,128)} %copy-done.5, bf16[256,1024]{1,0:T(8,128)(2,1)S(1)} %get-tuple-element.56.low_ref.refs_0_, ...), custom_call_target="tpu_custom_call", output_to_operand_aliasing={{0}: (8, {})} | custom-call | flops 1073741824 | bytes 12582912 | tf_op jit(solution)/shard_map/finish/pallas_call | solution.py:536
  120.4 5.8 %finish.6 = (f32[2048,4096]{1,0:T(8,128)}, f32[8,128]{1,0:T(8,128)S(1)}) custom-call(bf16[2048,256]{1,0:T(8,128)(2,1)S(1)} %get-tuple-element.61.col_ref, bf16[2048,4096]{1,0:T(8,128)(2,1)} %decoder_ref.17, f32[2048,128]{1,0:T(8,128)} %copy-done.5, bf16[256,1024]{1,0:T(8,128)(2,1)S(1)} %get-tuple-element.56.low_ref.refs_0_, ...), custom_call_target="tpu_custom_call", output_to_operand_aliasing={{0}: (8, {})} | custom-call | flops 1073741824 | bytes 12582912 | tf_op jit(solution)/shard_map/finish/pallas_call | solution.py:536
  129.4 4.4 %finish.7 = (f32[2048,4096]{1,0:T(8,128)}, f32[8,128]{1,0:T(8,128)S(1)}) custom-call(bf16[2048,256]{1,0:T(8,128)(2,1)S(1)} %get-tuple-element.61.col_ref, bf16[2048,4096]{1,0:T(8,128)(2,1)} %decoder_ref.17, f32[2048,128]{1,0:T(8,128)} %copy-done.5, bf16[256,1024]{1,0:T(8,128)(2,1)S(1)} %get-tuple-element.56.low_ref.refs_0_, ...), custom_call_target="tpu_custom_call", output_to_operand_aliasing={{0}: (8, {})} | custom-call | flops 536870912 | bytes 6291456 | tf_op jit(solution)/shard_map/finish/pallas_call | solution.py:536
  133.8 6.3 %collective-permute-done.21.refs_2_ = s32[272,256]{1,0:T(8,128)S(1)} collective-permute-done((s32[272,256]{1,0:T(8,128)S(1)}, s32[272,256]{1,0:T(8,128)S(1)}, u32[]{:S(2)}, u32[]{:S(2)}) %collective-permute-start.21) | collective-permute-done | bytes 278560 | tf_op jit(solution)/shard_map/ppermute | solution.py:316
  140.2 1.6 merge.14
  153.4 3.0 %collective-permute-done.27.refs_12_.refs_13_ = s32[272,256]{1,0:T(8,128)S(1)} collective-permute-done((s32[272,256]{1,0:T(8,128)}, s32[272,256]{1,0:T(8,128)S(1)}, u32[]{:S(2)}, u32[]{:S(2)}) %collective-permute-start.27) | collective-permute-done | bytes 278560 | tf_op jit(solution)/shard_map/ppermute | solution.py:316
  156.4 3.1 %collective-permute-done.29.refs_16_.refs_17_ = s32[272,256]{1,0:T(8,128)} collective-permute-done((s32[272,256]{1,0:T(8,128)}, s32[272,256]{1,0:T(8,128)}, u32[]{:S(2)}, u32[]{:S(2)}) %collective-permute-start.29) | collective-permute-done | bytes 278560 | tf_op jit(solution)/shard_map/ppermute | solution.py:316
  159.5 5.4 %finish_rows.1 = (f32[2048,4096]{1,0:T(8,128)}, f32[1]{0:T(128)}) custom-call(s32[1]{0:T(128)} %bitcast.1.owner_ref, bf16[2048,256]{1,0:T(8,128)(2,1)} %copy-done.4, bf16[2048,4096]{1,0:T(8,128)(2,1)} %decoder_ref.17, f32[2048,128]{1,0:T(8,128)} %copy-done.5, f32[8,128]{1,0:T(8,128)S(1)} %get-tuple-element.84.tile_ref, ...), custom_call_target="tpu_custom_call", output_to_operand_aliasing={{0}: (23, {})} | custom-call | tf_op jit(solution)/shard_map/finish_rows/pallas_call | solution.py:603
  (100 shorter events, 44.4 us)
Async XLA Ops:
  4.1 11.6 %collective-permute-start.7 = (bf16[256,1024]{1,0:T(8,128)(2,1)S(1)}, bf16[256,1024]{1,0:T(8,128)(2,1)S(1)}, u32[]{:S(2)}, u32[]{:S(2)}) collective-permute-start(bf16[256,1024]{1,0:T(8,128)(2,1)S(1)} %get-tuple-element.52), channel_id=1, source_target_pairs={{0,2},{4,6},{8,10},{12,14},{16,18},{20,22},{24,26},{28,30}} | collective-permute-start | bytes 1572872 | tf_op jit(solution)/shard_map/ppermute | solution.py:316
  9.0 12.3 %collective-permute-start = (bf16[256,1024]{1,0:T(8,128)(2,1)S(1)}, bf16[256,1024]{1,0:T(8,128)(2,1)S(1)}, u32[]{:S(2)}, u32[]{:S(2)}) collective-permute-start(bf16[256,1024]{1,0:T(8,128)(2,1)S(1)} %get-tuple-element.48), channel_id=1, source_target_pairs={{0,2},{4,6},{8,10},{12,14},{16,18},{20,22},{24,26},{28,30}} | collective-permute-start | bytes 1572872 | tf_op jit(solution)/shard_map/ppermute | solution.py:316
  16.2 12.5 %collective-permute-start.8 = (bf16[256,1024]{1,0:T(8,128)(2,1)S(1)}, bf16[256,1024]{1,0:T(8,128)(2,1)S(1)}, u32[]{:S(2)}, u32[]{:S(2)}) collective-permute-start(bf16[256,1024]{1,0:T(8,128)(2,1)S(1)} %pick.15.refs_0_), channel_id=1, source_target_pairs={{0,4},{2,6},{12,8},{14,10},{16,20},{18,22},{28,24},{30,26}} | collective-permute-start | bytes 1572872 | tf_op jit(solution)/shard_map/ppermute | solution.py:316
  21.8 10.2 %collective-permute-start.1 = (bf16[256,1024]{1,0:T(8,128)(2,1)S(1)}, bf16[256,1024]{1,0:T(8,128)(2,1)S(1)}, u32[]{:S(2)}, u32[]{:S(2)}) collective-permute-start(bf16[256,1024]{1,0:T(8,128)(2,1)S(1)} %pick.10.refs_0_), channel_id=1, source_target_pairs={{0,4},{2,6},{12,8},{14,10},{16,20},{18,22},{28,24},{30,26}} | collective-permute-start | bytes 1572872 | tf_op jit(solution)/shard_map/ppermute | solution.py:316
  28.7 21.5 %copy-start.2 = (bf16[512,4096]{1,0:T(8,128)(2,1)}, bf16[512,4096]{1,0:T(8,128)(2,1)S(1)}, u32[]{:S(2)}) copy-start(bf16[512,4096]{1,0:T(8,128)(2,1)S(1)} %get-tuple-element.59.refs_1_) | copy-start | bytes 12582916
  29.3 4.0 %collective-permute-start.9 = (bf16[256,1024]{1,0:T(8,128)(2,1)S(1)}, bf16[256,1024]{1,0:T(8,128)(2,1)S(1)}, u32[]{:S(2)}, u32[]{:S(2)}) collective-permute-start(bf16[256,1024]{1,0:T(8,128)(2,1)S(1)} %pick.16), channel_id=1, source_target_pairs={{4,8},{6,10},{8,4},{10,6},{20,24},{22,26},{24,20},{26,22}} | collective-permute-start | bytes 1572872 | tf_op jit(solution)/shard_map/ppermute | solution.py:316
  32.6 2.6 %collective-permute-start.2 = (bf16[256,1024]{1,0:T(8,128)(2,1)S(1)}, bf16[256,1024]{1,0:T(8,128)(2,1)S(1)}, u32[]{:S(2)}, u32[]{:S(2)}) collective-permute-start(bf16[256,1024]{1,0:T(8,128)(2,1)S(1)} %pick.11), channel_id=1, source_target_pairs={{4,8},{6,10},{8,4},{10,6},{20,24},{22,26},{24,20},{26,22}} | collective-permute-start | bytes 1572872 | tf_op jit(solution)/shard_map/ppermute | solution.py:316
  33.9 15.7 %collective-permute-start.10 = (bf16[256,1024]{1,0:T(8,128)(2,1)S(1)}, bf16[256,1024]{1,0:T(8,128)(2,1)S(1)}, u32[]{:S(2)}, u32[]{:S(2)}) collective-permute-start(bf16[256,1024]{1,0:T(8,128)(2,1)S(1)} %pick.17), channel_id=1, source_target_pairs={{8,12},{10,14},{4,0},{6,2},{24,28},{26,30},{20,16},{22,18}} | collective-permute-start | bytes 1572872 | tf_op jit(solution)/shard_map/ppermute | solution.py:316
  35.8 19.4 %collective-permute-start.3 = (bf16[256,1024]{1,0:T(8,128)(2,1)S(1)}, bf16[256,1024]{1,0:T(8,128)(2,1)S(1)}, u32[]{:S(2)}, u32[]{:S(2)}) collective-permute-start(bf16[256,1024]{1,0:T(8,128)(2,1)S(1)} %pick.12), channel_id=1, source_target_pairs={{8,12},{10,14},{4,0},{6,2},{24,28},{26,30},{20,16},{22,18}} | collective-permute-start | bytes 1572872 | tf_op jit(solution)/shard_map/ppermute | solution.py:316
  50.2 11.5 %collective-permute-start.12 = (bf16[256,1024]{1,0:T(8,128)(2,1)S(1)}, bf16[256,1024]{1,0:T(8,128)(2,1)S(1)}, u32[]{:S(2)}, u32[]{:S(2)}) collective-permute-start(bf16[256,1024]{1,0:T(8,128)(2,1)S(1)} %pick.18.refs_0_), channel_id=1, source_target_pairs={{0,2},{2,0},{4,6},{6,4},{8,10},{10,8},{12,14},{14,12},{16,18},{18,... | collective-permute-start | bytes 1572872 | tf_op jit(solution)/shard_map/ppermute | solution.py:316
  55.8 11.5 %collective-permute-start.5 = (bf16[256,1024]{1,0:T(8,128)(2,1)S(1)}, bf16[256,1024]{1,0:T(8,128)(2,1)S(1)}, u32[]{:S(2)}, u32[]{:S(2)}) collective-permute-start(bf16[256,1024]{1,0:T(8,128)(2,1)S(1)} %pick.13.refs_0_), channel_id=1, source_target_pairs={{0,2},{2,0},{4,6},{6,4},{8,10},{10,8},{12,14},{14,12},{16,18},{18,... | collective-permute-start | bytes 1572872 | tf_op jit(solution)/shard_map/ppermute | solution.py:316
  60.2 15.9 %collective-permute-start.11 = (bf16[256,1024]{1,0:T(8,128)(2,1)S(1)}, bf16[256,1024]{1,0:T(8,128)(2,1)S(1)}, u32[]{:S(2)}, u32[]{:S(2)}) collective-permute-start(bf16[256,1024]{1,0:T(8,128)(2,1)S(1)} %pick.18.refs_0_), channel_id=1, source_target_pairs={{0,1},{2,3},{4,5},{6,7},{8,9},{10,11},{12,13},{14,15},{16,17},{18,... | collective-permute-start | bytes 1572872 | tf_op jit(solution)/shard_map/ppermute | solution.py:316
  61.7 15.1 %collective-permute-start.13 = (bf16[256,1024]{1,0:T(8,128)(2,1)S(1)}, bf16[256,1024]{1,0:T(8,128)(2,1)}, u32[]{:S(2)}, u32[]{:S(2)}) collective-permute-start(bf16[256,1024]{1,0:T(8,128)(2,1)S(1)} %collective-permute-done.12.refs_2_), channel_id=1, source_target_pairs={{0,1},{2,3},{4,5},{6,7},{8,9},{10,11},{12,13},{14,15},{16,17},{18,... | collective-permute-start | bytes 1572872 | tf_op jit(solution)/shard_map/ppermute | solution.py:316
  63.8 19.3 %collective-permute-start.4 = (bf16[256,1024]{1,0:T(8,128)(2,1)S(1)}, bf16[256,1024]{1,0:T(8,128)(2,1)S(1)}, u32[]{:S(2)}, u32[]{:S(2)}) collective-permute-start(bf16[256,1024]{1,0:T(8,128)(2,1)S(1)} %pick.13.refs_0_), channel_id=1, source_target_pairs={{0,1},{2,3},{4,5},{6,7},{8,9},{10,11},{12,13},{14,15},{16,17},{18,... | collective-permute-start | bytes 1572872 | tf_op jit(solution)/shard_map/ppermute | solution.py:316
  67.3 16.6 %collective-permute-start.6 = (bf16[256,1024]{1,0:T(8,128)(2,1)S(1)}, bf16[256,1024]{1,0:T(8,128)(2,1)}, u32[]{:S(2)}, u32[]{:S(2)}) collective-permute-start(bf16[256,1024]{1,0:T(8,128)(2,1)S(1)} %collective-permute-done.5.refs_2_), channel_id=1, source_target_pairs={{0,1},{2,3},{4,5},{6,7},{8,9},{10,11},{12,13},{14,15},{16,17},{18,... | collective-permute-start | bytes 1572872 | tf_op jit(solution)/shard_map/ppermute | solution.py:316
  90.0 39.4 %copy-start.4 = (bf16[2048,256]{1,0:T(8,128)(2,1)}, bf16[2048,256]{1,0:T(8,128)(2,1)S(1)}, u32[]{:S(2)}) copy-start(bf16[2048,256]{1,0:T(8,128)(2,1)S(1)} %get-tuple-element.61.col_ref) | copy-start | bytes 3145732
  91.3 3.2 %collective-permute-start.14 = (f32[264,1024]{1,0:T(8,128)S(1)}, f32[264,1024]{1,0:T(8,128)S(1)}, u32[]{:S(2)}, u32[]{:S(2)}) collective-permute-start(f32[264,1024]{1,0:T(8,128)S(1)} %row_part.5), channel_id=1, source_target_pairs={{0,1},{1,0},{2,3},{3,2},{4,5},{5,4},{6,7},{7,6},{8,9},{9,8},{10,11... | collective-permute-start | bytes 3244040 | tf_op jit(solution)/shard_map/ppermute | solution.py:316
  92.7 6.2 %collective-permute-start.16 = (f32[264,1024]{1,0:T(8,128)S(1)}, f32[264,1024]{1,0:T(8,128)S(1)}, u32[]{:S(2)}, u32[]{:S(2)}) collective-permute-start(f32[264,1024]{1,0:T(8,128)S(1)} %row_part.7), channel_id=1, source_target_pairs={{0,1},{1,0},{2,3},{3,2},{4,5},{5,4},{6,7},{7,6},{8,9},{9,8},{10,11... | collective-permute-start | bytes 3244040 | tf_op jit(solution)/shard_map/ppermute | solution.py:316
  95.6 9.7 %collective-permute-start.15 = (s32[272,256]{1,0:T(8,128)}, s32[272,256]{1,0:T(8,128)S(1)}, u32[]{:S(2)}, u32[]{:S(2)}) collective-permute-start(s32[272,256]{1,0:T(8,128)} %get-tuple-element.67), channel_id=1, source_target_pairs={{0,2},{2,0},{1,3},{3,1},{4,6},{6,4},{5,7},{7,5},{8,10},{10,8},{9,1... | collective-permute-start | bytes 835592 | tf_op jit(solution)/shard_map/ppermute | solution.py:316
  99.2 11.4 %collective-permute-start.18 = (s32[272,256]{1,0:T(8,128)S(1)}, s32[272,256]{1,0:T(8,128)S(1)}, u32[]{:S(2)}, u32[]{:S(2)}) collective-permute-start(s32[272,256]{1,0:T(8,128)S(1)} %get-tuple-element.68.refs_4_), channel_id=1, source_target_pairs={{0,2},{2,0},{1,3},{3,1},{4,6},{6,4},{5,7},{7,5},{8,10},{10,8},{9,1... | collective-permute-start | bytes 835592 | tf_op jit(solution)/shard_map/ppermute | solution.py:316
  105.6 12.6 %collective-permute-start.17 = (s32[272,256]{1,0:T(8,128)S(1)}, s32[272,256]{1,0:T(8,128)S(1)}, u32[]{:S(2)}, u32[]{:S(2)}) collective-permute-start(s32[272,256]{1,0:T(8,128)S(1)} %get-tuple-element.72), channel_id=1, source_target_pairs={{0,4},{1,5},{2,6},{3,7},{12,8},{13,9},{14,10},{15,11},{16,20},{17,... | collective-permute-start | bytes 835592 | tf_op jit(solution)/shard_map/ppermute | solution.py:316
  110.9 8.3 %collective-permute-start.20 = (s32[272,256]{1,0:T(8,128)S(1)}, s32[272,256]{1,0:T(8,128)S(1)}, u32[]{:S(2)}, u32[]{:S(2)}) collective-permute-start(s32[272,256]{1,0:T(8,128)S(1)} %get-tuple-element.75.refs_4_), channel_id=1, source_target_pairs={{0,4},{1,5},{2,6},{3,7},{12,8},{13,9},{14,10},{15,11},{16,20},{17,... | collective-permute-start | bytes 835592 | tf_op jit(solution)/shard_map/ppermute | solution.py:316
  118.5 7.7 %collective-permute-start.19 = (s32[272,256]{1,0:T(8,128)S(1)}, s32[272,256]{1,0:T(8,128)S(1)}, u32[]{:S(2)}, u32[]{:S(2)}) collective-permute-start(s32[272,256]{1,0:T(8,128)S(1)} %merge.10), channel_id=1, source_target_pairs={{4,8},{5,9},{6,10},{7,11},{8,4},{9,5},{10,6},{11,7},{20,24},{21,25... | collective-permute-start | bytes 835592 | tf_op jit(solution)/shard_map/ppermute | solution.py:316
  119.5 8.3 %collective-permute-start.22 = (s32[272,256]{1,0:T(8,128)S(1)}, s32[272,256]{1,0:T(8,128)S(1)}, u32[]{:S(2)}, u32[]{:S(2)}) collective-permute-start(s32[272,256]{1,0:T(8,128)S(1)} %merge.11.refs_4_), channel_id=1, source_target_pairs={{4,8},{5,9},{6,10},{7,11},{8,4},{9,5},{10,6},{11,7},{20,24},{21,25... | collective-permute-start | bytes 835592 | tf_op jit(solution)/shard_map/ppermute | solution.py:316
  126.5 13.6 %collective-permute-start.21 = (s32[272,256]{1,0:T(8,128)S(1)}, s32[272,256]{1,0:T(8,128)S(1)}, u32[]{:S(2)}, u32[]{:S(2)}) collective-permute-start(s32[272,256]{1,0:T(8,128)S(1)} %merge.12), channel_id=1, source_target_pairs={{8,12},{9,13},{10,14},{11,15},{4,0},{5,1},{6,2},{7,3},{24,28},{25,... | collective-permute-start | bytes 835592 | tf_op jit(solution)/shard_map/ppermute | solution.py:316
  128.1 17.5 %collective-permute-start.26 = (s32[272,256]{1,0:T(8,128)S(1)}, s32[272,256]{1,0:T(8,128)S(1)}, u32[]{:S(2)}, u32[]{:S(2)}) collective-permute-start(s32[272,256]{1,0:T(8,128)S(1)} %merge.13.refs_4_), channel_id=1, source_target_pairs={{8,12},{9,13},{10,14},{11,15},{4,0},{5,1},{6,2},{7,3},{24,28},{25,... | collective-permute-start | bytes 835592 | tf_op jit(solution)/shard_map/ppermute | solution.py:316
  141.8 9.5 %collective-permute-start.23 = (s32[272,256]{1,0:T(8,128)}, s32[272,256]{1,0:T(8,128)S(1)}, u32[]{:S(2)}, u32[]{:S(2)}) collective-permute-start(s32[272,256]{1,0:T(8,128)} %get-tuple-element.86), channel_id=1, source_target_pairs={{2,0},{6,4},{10,8},{14,12},{18,16},{22,20},{26,24},{30,28}} | collective-permute-start | bytes 835592 | tf_op jit(solution)/shard_map/ppermute | solution.py:316
  143.1 9.5 %collective-permute-start.24 = (s32[272,256]{1,0:T(8,128)}, s32[272,256]{1,0:T(8,128)S(1)}, u32[]{:S(2)}, u32[]{:S(2)}) collective-permute-start(s32[272,256]{1,0:T(8,128)} %get-tuple-element.86), channel_id=1, source_target_pairs={{1,0},{5,4},{9,8},{13,12},{17,16},{21,20},{25,24},{29,28}} | collective-permute-start | bytes 835592 | tf_op jit(solution)/shard_map/ppermute | solution.py:316
  144.4 9.0 %collective-permute-start.25 = (s32[272,256]{1,0:T(8,128)}, s32[272,256]{1,0:T(8,128)S(1)}, u32[]{:S(2)}, u32[]{:S(2)}) collective-permute-start(s32[272,256]{1,0:T(8,128)} %get-tuple-element.86), channel_id=1, source_target_pairs={{3,0},{7,4},{11,8},{15,12},{19,16},{23,20},{27,24},{31,28}} | collective-permute-start | bytes 835592 | tf_op jit(solution)/shard_map/ppermute | solution.py:316
  147.8 8.6 %collective-permute-start.27 = (s32[272,256]{1,0:T(8,128)}, s32[272,256]{1,0:T(8,128)S(1)}, u32[]{:S(2)}, u32[]{:S(2)}) collective-permute-start(s32[272,256]{1,0:T(8,128)} %get-tuple-element.88), channel_id=1, source_target_pairs={{2,0},{6,4},{10,8},{14,12},{18,16},{22,20},{26,24},{30,28}} | collective-permute-start | bytes 835592 | tf_op jit(solution)/shard_map/ppermute | solution.py:316
  149.1 7.4 %collective-permute-start.28 = (s32[272,256]{1,0:T(8,128)}, s32[272,256]{1,0:T(8,128)}, u32[]{:S(2)}, u32[]{:S(2)}) collective-permute-start(s32[272,256]{1,0:T(8,128)} %get-tuple-element.88), channel_id=1, source_target_pairs={{1,0},{5,4},{9,8},{13,12},{17,16},{21,20},{25,24},{29,28}} | collective-permute-start | bytes 835592 | tf_op jit(solution)/shard_map/ppermute | solution.py:316
  151.3 8.2 %collective-permute-start.29 = (s32[272,256]{1,0:T(8,128)}, s32[272,256]{1,0:T(8,128)}, u32[]{:S(2)}, u32[]{:S(2)}) collective-permute-start(s32[272,256]{1,0:T(8,128)} %get-tuple-element.88), channel_id=1, source_target_pairs={{3,0},{7,4},{11,8},{15,12},{19,16},{23,20},{27,24},{31,28}} | collective-permute-start | bytes 835592 | tf_op jit(solution)/shard_map/ppermute | solution.py:316
  (16 other events, 94.1 us)

commit v8 on v7

--- a/solution.py
+++ b/solution.py
@@ -100,12 +100,16 @@
 
 
 def pick_kernel(slots, count, flags_ref, *refs):
-    for slot, out_ref in zip(slots, refs[-len(slots) :]):
+    out_refs, sems = refs[-len(slots) - 1 : -1], refs[-1]
+    for n, (slot, out_ref) in enumerate(zip(slots, out_refs)):
         for c in range(count):
 
             @pl.when(flags_ref[slot] == c)
-            def _(out_ref=out_ref, c=c):
-                out_ref[...] = refs[c][...]
+            def _(out_ref=out_ref, c=c, n=n):
+                pltpu.make_async_copy(refs[c], out_ref, sems.at[n]).start()
+
+    for n, out_ref in enumerate(out_refs):
+        pltpu.make_async_copy(refs[0], out_ref, sems.at[n]).wait()
 
 
 def partial_kernel(k, parts, low_ref, high_ref, *refs):
@@ -364,15 +368,16 @@
     def pick(slots, candidates, ties=()):
         return pl.pallas_call(
             functools.partial(pick_kernel, slots, len(candidates)),
-            in_specs=[smem] + [vmem] * len(candidates) + [any_spec] * len(ties),
+            in_specs=[smem] + [any_spec] * (len(candidates) + len(ties)),
             out_specs=[vmem] * len(slots),
             out_shape=[chunk_type] * len(slots),
+            scratch_shapes=[pltpu.SemaphoreType.DMA((len(slots),))],
             compiler_params=params(12),
             cost_estimate=cost(ROWS * step, 4 * ROWS * step),
             name="pick",
         )(flags, *candidates, *ties)
 
-    unit_bounds = [0, blocks // 4, blocks // 2, blocks]
+    unit_bounds = [blocks * p // 4 for p in range(5)]
     units, inverses = [], []
 
     def make_units(part, tie):
@@ -392,7 +397,7 @@
                 pltpu.VMEM((2, BLOCK, width), jnp.bfloat16),
                 pltpu.SemaphoreType.DMA((2,)),
             ],
-            compiler_params=params((46, 44, 34)[part]),
+            compiler_params=params((46, 44, 40, 36)[part]),
             cost_estimate=cost(4 * rows * width, 4 * rows * width),
             name="units",
         )(decoder, tie)
@@ -411,11 +416,13 @@
         [going] = pick([WAITS], [mine[k], first[k]], () if k else done)
         second[k] = send(going, hop(1, (0, 2)))
     for k in range(PAIRS):
-        [going] = pick([WAITS], [mine[k], second[k]])
+        [going] = pick([WAITS], [mine[k], second[k]], done if k else ())
         third[k] = send(going, hop(2, (0, 2)))
+        if k == 0:
+            done = make_units(2, going)
     for k in range(PAIRS):
         [held[k]] = pick([REACHED], [mine[k], first[k], second[k], third[k]])
-    done = make_units(2, held[PAIRS - 1])
+    done = make_units(3, held[PAIRS - 1])
     chosen = []
     for k in range(PAIRS):
         other = send(held[k], each([(0, 2), (2, 0)]))
@@ -511,7 +518,7 @@
     out_type = jax.ShapeDtypeStruct((shard, width), jnp.float32)
     mark_type = jax.ShapeDtypeStruct((8, 128), jnp.float32)
     mark_spec = pl.BlockSpec((8, 128), lambda i: (0, 0))
-    bounds = [1 + -(-(blocks - 1) * p // 4) for p in range(5)]
+    bounds = [1 + (blocks - 1) * p // 7 for p in (0, 2, 4, 5, 5, 7)]
     grad = None
 
     def finish(part, tie):
@@ -571,13 +578,14 @@
         tile = jnp.where(fresh, send(tile, moves), tile)
         far *= 2
 
+    finish(4, msg[PAIRS - 1])
     sums, row_specs = [], []
     narrow = BLOCK // 2
     for k in range(PAIRS):
         sums.append(kept[k][0])
         row_specs.append(pl.BlockSpec((narrow, piece), lambda i: (i, 0)))
-        for source in (2, 1, 3):
-            arrived = send(msg[k], each([(source, 0)]))
+        arrivals = [send(msg[k], each([(source, 0)])) for source in (2, 3, 1)]
+        for arrived in (arrivals[0], arrivals[2], arrivals[1]):
             sums += [arrived, arrived]
             row_specs += [
                 pl.BlockSpec((narrow, piece // 2), lambda i: (i, 0)),

time: 166 us -> 156 us (0.940)
  waiting for transfers between devices: 37 us -> 25.8 us
  local copies, waits for them, and re-layouts: 7.62 us -> 10.7 us
  Pallas kernels: 68.1 us -> 66 us
    ppermute x30, waiting for transfers between devices: 37 us -> 25.8 us  [send(): return lax.ppermute(value, 'row', pairs)]
    unnamed x36 -> x40, local copies, waits for them, and re-layouts: 7.54 us -> 10.6 us
    pallas_call x3 -> x4, Pallas kernels: 13.3 us -> 13.5 us  [make_units(): pl.pallas_call(functools.partial(units_kernel, low, high - low), in_specs...]
  transfers between devices with their start and end apart: 30 -> 30, of which waited for: 13 -> 8; matrix products, arithmetic and copies ran while one was open for 0% -> 0% of each run, Pallas kernels for 33% -> 34%
where the time goes in v8:
time: 156 us; the launch traced here: 155 us
  Pallas kernels  66 us (42%)
  starting transfers between devices  50.2 us (32%)
  waiting for transfers between devices  25.8 us (17%)
  local copies, waits for them, and re-layouts  10.7 us (7%)
  between operations  2.23 us (1%)
    ppermute x30, starting transfers between devices, send(): return lax.ppermute(value, 'row', pairs)  50.2 us
    ppermute x30, waiting for transfers between devices, send(): return lax.ppermute(value, 'row', pairs)  25.8 us
    pallas_call x4, Pallas kernels, finish(): pl.pallas_call(finish_kernel, grid=(high - low,), in_specs=specs, out_spe...  21.8 us
    pallas_call x4, Pallas kernels, make_units(): pl.pallas_call(functools.partial(units_kernel, low, high - low), in_specs...  13.5 us
    unnamed x40, local copies, waits for them, and re-layouts  10.6 us
    pallas_call x10, Pallas kernels, pick(): pl.pallas_call(functools.partial(pick_kernel, slots, len(candidates)), in...  6.38 us
    pallas_call x1, Pallas kernels, on_device(): pl.pallas_call(functools.partial(last_kernel, DW / (ROWS * latents)), gri...  5.58 us
    pallas_call x4, Pallas kernels, row_part(): pl.pallas_call(functools.partial(row_kernel, k, parts), in_specs=[smem] +...  5.02 us
  transfers between devices with their start and end apart: 30, of which 8 were waited for; matrix products, arithmetic and copies ran while one was open for 0% of the time, Pallas kernels for 34%

profile of v8, /device:TPU:0, one launch (start us, length us, event | category | flops | bytes accessed | tf_op | source)
XLA Modules:
  0.0 154.9 jit_solution(12218023759545114599)
XLA Ops:
  1.5 2.6 %head_units.1 = (bf16[256,1024]{1,0:T(8,128)(2,1)S(1)}, bf16[256,1024]{1,0:T(8,128)(2,1)S(1)}, bf16[256,1024]{1,0:T(8,128)(2,1)S(1)}, bf16[256,1024]{1,0:T(8,128)(2,1)S(1)}) custom-call(s32[5]{0:T(128)S(1)} %stack.23.flags_ref, bf16[2048,4096]{1,0:T(8,128)(2,1)} %decoder_ref.19), custom_call_target="tpu_custom_call" | custom-call | flops 4194304 | bytes 4194304 | tf_op jit(solution)/shard_map/head_units/pallas_call | solution.py:346
  4.1 4.9 %collective-permute-start.3 = (bf16[256,1024]{1,0:T(8,128)(2,1)S(1)}, bf16[256,1024]{1,0:T(8,128)(2,1)S(1)}, u32[]{:S(2)}, u32[]{:S(2)}) collective-permute-start(bf16[256,1024]{1,0:T(8,128)(2,1)S(1)} %get-tuple-element.51), channel_id=1, source_target_pairs={{0,2},{4,6},{8,10},{12,14},{16,18},{20,22},{24,26},{28,30}} | collective-permute-start | bytes 1572872 | tf_op jit(solution)/shard_map/ppermute | solution.py:320
  10.3 3.3 %units.4 = (bf16[512,4096]{1,0:T(8,128)(2,1)S(1)}, f32[512,128]{1,0:T(8,128)S(1)}) custom-call(bf16[2048,4096]{1,0:T(8,128)(2,1)} %decoder_ref.19, bf16[256,1024]{1,0:T(8,128)(2,1)S(1)} %get-tuple-element.50.refs_0_), custom_call_target="tpu_custom_call" | custom-call | flops 8388608 | bytes 8388608 | tf_op jit(solution)/shard_map/units/pallas_call | solution.py:388
  13.6 2.0 %copy-done = bf16[512,4096]{1,0:T(8,128)(2,1)} copy-done((bf16[512,4096]{1,0:T(8,128)(2,1)}, bf16[512,4096]{1,0:T(8,128)(2,1)S(1)}, u32[]{:S(2)}) %copy-start) | copy-done | bytes 4194328
  16.2 3.5 %collective-permute-start.4 = (bf16[256,1024]{1,0:T(8,128)(2,1)S(1)}, bf16[256,1024]{1,0:T(8,128)(2,1)S(1)}, u32[]{:S(2)}, u32[]{:S(2)}) collective-permute-start(bf16[256,1024]{1,0:T(8,128)(2,1)S(1)} %pick.12.refs_0_), channel_id=1, source_target_pairs={{0,4},{2,6},{12,8},{14,10},{16,20},{18,22},{28,24},{30,26}} | collective-permute-start | bytes 1572872 | tf_op jit(solution)/shard_map/ppermute | solution.py:320
  19.8 1.5 collective-permute-done.refs_1_
  21.8 3.5 %collective-permute-start.1 = (bf16[256,1024]{1,0:T(8,128)(2,1)S(1)}, bf16[256,1024]{1,0:T(8,128)(2,1)S(1)}, u32[]{:S(2)}, u32[]{:S(2)}) collective-permute-start(bf16[256,1024]{1,0:T(8,128)(2,1)S(1)} %pick.10.refs_0_), channel_id=1, source_target_pairs={{0,4},{2,6},{12,8},{14,10},{16,20},{18,22},{28,24},{30,26}} | collective-permute-start | bytes 1572872 | tf_op jit(solution)/shard_map/ppermute | solution.py:320
  25.4 3.3 %units.5 = (bf16[512,4096]{1,0:T(8,128)(2,1)S(1)}, f32[512,128]{1,0:T(8,128)S(1)}) custom-call(bf16[2048,4096]{1,0:T(8,128)(2,1)} %decoder_ref.19, bf16[256,1024]{1,0:T(8,128)(2,1)S(1)} %pick.10.refs_0_), custom_call_target="tpu_custom_call" | custom-call | flops 8388608 | bytes 8388608 | tf_op jit(solution)/shard_map/units/pallas_call | solution.py:388
  28.7 2.0 %copy-done.2 = bf16[512,4096]{1,0:T(8,128)(2,1)} copy-done((bf16[512,4096]{1,0:T(8,128)(2,1)}, bf16[512,4096]{1,0:T(8,128)(2,1)S(1)}, u32[]{:S(2)}) %copy-start.2) | copy-done | bytes 4194328
  35.3 3.3 %units.6 = (bf16[512,4096]{1,0:T(8,128)(2,1)S(1)}, f32[512,128]{1,0:T(8,128)S(1)}) custom-call(bf16[2048,4096]{1,0:T(8,128)(2,1)} %decoder_ref.19, bf16[256,1024]{1,0:T(8,128)(2,1)S(1)} %pick.14.refs_0_), custom_call_target="tpu_custom_call" | custom-call | flops 8388608 | bytes 8388608 | tf_op jit(solution)/shard_map/units/pallas_call | solution.py:388
  38.6 2.0 %copy-done.4 = bf16[512,4096]{1,0:T(8,128)(2,1)} copy-done((bf16[512,4096]{1,0:T(8,128)(2,1)}, bf16[512,4096]{1,0:T(8,128)(2,1)S(1)}, u32[]{:S(2)}) %copy-start.4) | copy-done | bytes 4194328
  42.5 8.2 %collective-permute-done.10.refs_3_ = bf16[256,1024]{1,0:T(8,128)(2,1)S(1)} collective-permute-done((bf16[256,1024]{1,0:T(8,128)(2,1)S(1)}, bf16[256,1024]{1,0:T(8,128)(2,1)S(1)}, u32[]{:S(2)}, u32[]{:S(2)}) %collective-permute-start.10) | collective-permute-done | bytes 524320 | tf_op jit(solution)/shard_map/ppermute | solution.py:320
  51.4 4.4 %collective-permute-start.12 = (bf16[256,1024]{1,0:T(8,128)(2,1)S(1)}, bf16[256,1024]{1,0:T(8,128)(2,1)S(1)}, u32[]{:S(2)}, u32[]{:S(2)}) collective-permute-start(bf16[256,1024]{1,0:T(8,128)(2,1)S(1)} %pick.18.refs_0_), channel_id=1, source_target_pairs={{0,2},{2,0},{4,6},{6,4},{8,10},{10,8},{12,14},{14,12},{16,18},{18,... | collective-permute-start | bytes 1572872 | tf_op jit(solution)/shard_map/ppermute | solution.py:320
  55.8 2.3 %collective-permute-done.6.refs_3_ = bf16[256,1024]{1,0:T(8,128)(2,1)S(1)} collective-permute-done((bf16[256,1024]{1,0:T(8,128)(2,1)S(1)}, bf16[256,1024]{1,0:T(8,128)(2,1)S(1)}, u32[]{:S(2)}, u32[]{:S(2)}) %collective-permute-start.6) | collective-permute-done | bytes 524320 | tf_op jit(solution)/shard_map/ppermute | solution.py:320
  58.7 4.4 %collective-permute-start.8 = (bf16[256,1024]{1,0:T(8,128)(2,1)S(1)}, bf16[256,1024]{1,0:T(8,128)(2,1)S(1)}, u32[]{:S(2)}, u32[]{:S(2)}) collective-permute-start(bf16[256,1024]{1,0:T(8,128)(2,1)S(1)} %pick.16.refs_0_), channel_id=1, source_target_pairs={{0,2},{2,0},{4,6},{6,4},{8,10},{10,8},{12,14},{14,12},{16,18},{18,... | collective-permute-start | bytes 1572872 | tf_op jit(solution)/shard_map/ppermute | solution.py:320
  65.8 2.1 %collective-permute-start.7 = (bf16[256,1024]{1,0:T(8,128)(2,1)S(1)}, bf16[256,1024]{1,0:T(8,128)(2,1)}, u32[]{:S(2)}, u32[]{:S(2)}) collective-permute-start(bf16[256,1024]{1,0:T(8,128)(2,1)S(1)} %pick.16.refs_0_), channel_id=1, source_target_pairs={{0,1},{2,3},{4,5},{6,7},{8,9},{10,11},{12,13},{14,15},{16,17},{18,... | collective-permute-start | bytes 1572872 | tf_op jit(solution)/shard_map/ppermute | solution.py:320
  67.8 2.4 %collective-permute-done.8.refs_2_ = bf16[256,1024]{1,0:T(8,128)(2,1)S(1)} collective-permute-done((bf16[256,1024]{1,0:T(8,128)(2,1)S(1)}, bf16[256,1024]{1,0:T(8,128)(2,1)S(1)}, u32[]{:S(2)}, u32[]{:S(2)}) %collective-permute-start.8) | collective-permute-done | bytes 524320 | tf_op jit(solution)/shard_map/ppermute | solution.py:320
  70.2 2.1 %collective-permute-start.9 = (bf16[256,1024]{1,0:T(8,128)(2,1)S(1)}, bf16[256,1024]{1,0:T(8,128)(2,1)}, u32[]{:S(2)}, u32[]{:S(2)}) collective-permute-start(bf16[256,1024]{1,0:T(8,128)(2,1)S(1)} %collective-permute-done.8.refs_2_), channel_id=1, source_target_pairs={{0,1},{2,3},{4,5},{6,7},{8,9},{10,11},{12,13},{14,15},{16,17},{18,... | collective-permute-start | bytes 1572872 | tf_op jit(solution)/shard_map/ppermute | solution.py:320
  72.3 3.5 %units.7 = (bf16[512,4096]{1,0:T(8,128)(2,1)S(1)}, f32[512,128]{1,0:T(8,128)S(1)}) custom-call(bf16[2048,4096]{1,0:T(8,128)(2,1)} %decoder_ref.19, bf16[256,1024]{1,0:T(8,128)(2,1)S(1)} %pick.16.refs_0_), custom_call_target="tpu_custom_call" | custom-call | flops 8388608 | bytes 8388608 | tf_op jit(solution)/shard_map/units/pallas_call | solution.py:388
  80.6 2.4 %part_cosines.1.partial_ref = f32[2048,256]{1,0:T(8,128)S(1)} custom-call(bf16[256,1024]{1,0:T(8,128)(2,1)S(1)} %get-tuple-element.58.low_ref.refs_0_, bf16[256,1024]{1,0:T(8,128)(2,1)S(1)} %get-tuple-element.59.high_ref.refs_1_, bf16[512,4096]{1,0:T(8,128)(2,1)S(1)} %copy-done.1, bf16[512,4096]{1,0:T(8,128)(2,1)S(1)} %copy-done.3, ...), custom_call_target="tpu_custom_call" | custom-call | flops 2147483648 | bytes 8388608 | tf_op jit(solution)/shard_map/part_cosines/pallas_call | solution.py:443
  83.7 3.3 %weights.1 = (bf16[2048,256]{1,0:T(8,128)(2,1)S(1)}, bf16[256,2048]{1,0:T(8,128)(2,1)S(1)}, f32[2048,128]{1,0:T(8,128)S(1)}, f32[8,128]{1,0:T(8,128)S(1)}) custom-call(s32[1]{0:T(128)} %bitcast.2.delta_ref, bf16[256,1024]{1,0:T(8,128)(2,1)S(1)} %get-tuple-element.55.low_ref.refs_2_, bf16[256,1024]{1,0:T(8,128)(2,1)S(1)} %get-tuple-element.56.high_ref.refs_3_, ...), custom_call_target="tpu_custom_call" | custom-call | flops 2147483648 | bytes 8388608 | tf_op jit(solution)/shard_map/weights/pallas_call | solution.py:452
  91.8 2.1 %collective-permute-start.18 = (s32[272,256]{1,0:T(8,128)S(1)}, s32[272,256]{1,0:T(8,128)S(1)}, u32[]{:S(2)}, u32[]{:S(2)}) collective-permute-start(s32[272,256]{1,0:T(8,128)S(1)} %get-tuple-element.71.refs_4_), channel_id=1, source_target_pairs={{0,2},{2,0},{1,3},{3,1},{4,6},{6,4},{5,7},{7,5},{8,10},{10,8},{9,1... | collective-permute-start | bytes 835592 | tf_op jit(solution)/shard_map/ppermute | solution.py:320
  95.6 5.8 %collective-permute-done.18.refs_0_ = s32[272,256]{1,0:T(8,128)S(1)} collective-permute-done((s32[272,256]{1,0:T(8,128)S(1)}, s32[272,256]{1,0:T(8,128)S(1)}, u32[]{:S(2)}, u32[]{:S(2)}) %collective-permute-start.18) | collective-permute-done | bytes 278560 | tf_op jit(solution)/shard_map/ppermute | solution.py:320
  101.7 1.5 collective-permute-start.20
  103.2 5.8 %finish.4 = (f32[2048,4096]{1,0:T(8,128)}, f32[8,128]{1,0:T(8,128)S(1)}) custom-call(bf16[2048,256]{1,0:T(8,128)(2,1)S(1)} %get-tuple-element.64.col_ref, bf16[2048,4096]{1,0:T(8,128)(2,1)} %decoder_ref.19, f32[2048,128]{1,0:T(8,128)} %copy-done.7, bf16[256,1024]{1,0:T(8,128)(2,1)S(1)} %get-tuple-element.58.low_ref.refs_0_, ...), custom_call_target="tpu_custom_call" | custom-call | flops 1073741824 | bytes 12582912 | tf_op jit(solution)/shard_map/finish/pallas_call | solution.py:543
  111.8 5.8 %finish.5 = (f32[2048,4096]{1,0:T(8,128)}, f32[8,128]{1,0:T(8,128)S(1)}) custom-call(bf16[2048,256]{1,0:T(8,128)(2,1)S(1)} %get-tuple-element.64.col_ref, bf16[2048,4096]{1,0:T(8,128)(2,1)} %decoder_ref.19, f32[2048,128]{1,0:T(8,128)} %copy-done.7, bf16[256,1024]{1,0:T(8,128)(2,1)S(1)} %get-tuple-element.58.low_ref.refs_0_, ...), custom_call_target="tpu_custom_call", output_to_operand_aliasing={{0}: (8, {})} | custom-call | flops 1073741824 | bytes 12582912 | tf_op jit(solution)/shard_map/finish/pallas_call | solution.py:543
  120.2 4.4 %finish.6 = (f32[2048,4096]{1,0:T(8,128)}, f32[8,128]{1,0:T(8,128)S(1)}) custom-call(bf16[2048,256]{1,0:T(8,128)(2,1)S(1)} %get-tuple-element.64.col_ref, bf16[2048,4096]{1,0:T(8,128)(2,1)} %decoder_ref.19, f32[2048,128]{1,0:T(8,128)} %copy-done.7, bf16[256,1024]{1,0:T(8,128)(2,1)S(1)} %get-tuple-element.58.low_ref.refs_0_, ...), custom_call_target="tpu_custom_call", output_to_operand_aliasing={{0}: (8, {})} | custom-call | flops 536870912 | bytes 6291456 | tf_op jit(solution)/shard_map/finish/pallas_call | solution.py:543
  126.2 3.0 %collective-permute-done.26.refs_2_ = s32[272,256]{1,0:T(8,128)S(1)} collective-permute-done((s32[272,256]{1,0:T(8,128)S(1)}, s32[272,256]{1,0:T(8,128)S(1)}, u32[]{:S(2)}, u32[]{:S(2)}) %collective-permute-start.26) | collective-permute-done | bytes 278560 | tf_op jit(solution)/shard_map/ppermute | solution.py:320
  135.3 1.6 %merge.13 = (f32[256,512]{1,0:T(8,128)S(1)}, f32[8,128]{1,0:T(8,128)S(1)}, s32[272,256]{1,0:T(8,128)}) custom-call(f32[256,512]{1,0:T(8,128)S(1)} %get-tuple-element.73.kept_ref, f32[8,128]{1,0:T(8,128)S(1)} %get-tuple-element.74.penalty_ref, s32[272,256]{1,0:T(8,128)S(1)} %collective-permute-done.17.refs_0_, ...), custom_call_target="tpu_custom_call" | custom-call | flops 2621440 | bytes 1572864 | tf_op jit(solution)/shard_map/merge/pallas_call | solution.py:488
  141.7 5.8 %finish.7 = (f32[2048,4096]{1,0:T(8,128)}, f32[8,128]{1,0:T(8,128)}) custom-call(bf16[2048,256]{1,0:T(8,128)(2,1)S(1)} %get-tuple-element.64.col_ref, bf16[2048,4096]{1,0:T(8,128)(2,1)} %decoder_ref.19, f32[2048,128]{1,0:T(8,128)} %copy-done.7, bf16[256,1024]{1,0:T(8,128)(2,1)S(1)} %get-tuple-element.58.low_ref.refs_0_, ...), custom_call_target="tpu_custom_call", output_to_operand_aliasing={{0}: (8, {})} | custom-call | flops 1073741824 | bytes 12582912 | tf_op jit(solution)/shard_map/finish/pallas_call | solution.py:543
  147.5 1.6 %collective-permute-done.22.refs_5_.refs_6_ = s32[272,256]{1,0:T(8,128)} collective-permute-done((s32[272,256]{1,0:T(8,128)}, s32[272,256]{1,0:T(8,128)}, u32[]{:S(2)}, u32[]{:S(2)}) %collective-permute-start.22) | collective-permute-done | bytes 278560 | tf_op jit(solution)/shard_map/ppermute | solution.py:320
  149.1 5.6 %finish_rows.1 = (f32[2048,4096]{1,0:T(8,128)}, f32[1]{0:T(128)}) custom-call(s32[1]{0:T(128)} %bitcast.1.owner_ref, bf16[2048,256]{1,0:T(8,128)(2,1)} %copy-done.6, bf16[2048,4096]{1,0:T(8,128)(2,1)} %decoder_ref.19, f32[2048,128]{1,0:T(8,128)} %copy-done.7, f32[8,128]{1,0:T(8,128)S(1)} %get-tuple-element.85.tile_ref, ...), custom_call_target="tpu_custom_call", output_to_operand_aliasing={{0}: (23, {})} | custom-call | tf_op jit(solution)/shard_map/finish_rows/pallas_call | solution.py:611
  (105 shorter events, 42.8 us)
Async XLA Ops:
  4.1 11.6 %collective-permute-start.3 = (bf16[256,1024]{1,0:T(8,128)(2,1)S(1)}, bf16[256,1024]{1,0:T(8,128)(2,1)S(1)}, u32[]{:S(2)}, u32[]{:S(2)}) collective-permute-start(bf16[256,1024]{1,0:T(8,128)(2,1)S(1)} %get-tuple-element.51), channel_id=1, source_target_pairs={{0,2},{4,6},{8,10},{12,14},{16,18},{20,22},{24,26},{28,30}} | collective-permute-start | bytes 1572872 | tf_op jit(solution)/shard_map/ppermute | solution.py:320
  9.0 12.3 %collective-permute-start = (bf16[256,1024]{1,0:T(8,128)(2,1)S(1)}, bf16[256,1024]{1,0:T(8,128)(2,1)S(1)}, u32[]{:S(2)}, u32[]{:S(2)}) collective-permute-start(bf16[256,1024]{1,0:T(8,128)(2,1)S(1)} %get-tuple-element.49), channel_id=1, source_target_pairs={{0,2},{4,6},{8,10},{12,14},{16,18},{20,22},{24,26},{28,30}} | collective-permute-start | bytes 1572872 | tf_op jit(solution)/shard_map/ppermute | solution.py:320
  16.2 14.4 %collective-permute-start.4 = (bf16[256,1024]{1,0:T(8,128)(2,1)S(1)}, bf16[256,1024]{1,0:T(8,128)(2,1)S(1)}, u32[]{:S(2)}, u32[]{:S(2)}) collective-permute-start(bf16[256,1024]{1,0:T(8,128)(2,1)S(1)} %pick.12.refs_0_), channel_id=1, source_target_pairs={{0,4},{2,6},{12,8},{14,10},{16,20},{18,22},{28,24},{30,26}} | collective-permute-start | bytes 1572872 | tf_op jit(solution)/shard_map/ppermute | solution.py:320
  21.8 10.2 %collective-permute-start.1 = (bf16[256,1024]{1,0:T(8,128)(2,1)S(1)}, bf16[256,1024]{1,0:T(8,128)(2,1)S(1)}, u32[]{:S(2)}, u32[]{:S(2)}) collective-permute-start(bf16[256,1024]{1,0:T(8,128)(2,1)S(1)} %pick.10.refs_0_), channel_id=1, source_target_pairs={{0,4},{2,6},{12,8},{14,10},{16,20},{18,22},{28,24},{30,26}} | collective-permute-start | bytes 1572872 | tf_op jit(solution)/shard_map/ppermute | solution.py:320
  31.3 2.1 %collective-permute-start.5 = (bf16[256,1024]{1,0:T(8,128)(2,1)S(1)}, bf16[256,1024]{1,0:T(8,128)(2,1)S(1)}, u32[]{:S(2)}, u32[]{:S(2)}) collective-permute-start(bf16[256,1024]{1,0:T(8,128)(2,1)S(1)} %pick.13), channel_id=1, source_target_pairs={{4,8},{6,10},{8,4},{10,6},{20,24},{22,26},{24,20},{26,22}} | collective-permute-start | bytes 1572872 | tf_op jit(solution)/shard_map/ppermute | solution.py:320
  32.6 8.0 %collective-permute-start.2 = (bf16[256,1024]{1,0:T(8,128)(2,1)S(1)}, bf16[256,1024]{1,0:T(8,128)(2,1)S(1)}, u32[]{:S(2)}, u32[]{:S(2)}) collective-permute-start(bf16[256,1024]{1,0:T(8,128)(2,1)S(1)} %pick.11), channel_id=1, source_target_pairs={{4,8},{6,10},{8,4},{10,6},{20,24},{22,26},{24,20},{26,22}} | collective-permute-start | bytes 1572872 | tf_op jit(solution)/shard_map/ppermute | solution.py:320
  34.0 16.8 %collective-permute-start.10 = (bf16[256,1024]{1,0:T(8,128)(2,1)S(1)}, bf16[256,1024]{1,0:T(8,128)(2,1)S(1)}, u32[]{:S(2)}, u32[]{:S(2)}) collective-permute-start(bf16[256,1024]{1,0:T(8,128)(2,1)S(1)} %pick.14.refs_0_), channel_id=1, source_target_pairs={{8,12},{10,14},{4,0},{6,2},{24,28},{26,30},{20,16},{22,18}} | collective-permute-start | bytes 1572872 | tf_op jit(solution)/shard_map/ppermute | solution.py:320
  40.6 29.6 %copy-start.10 = (f32[512,128]{1,0:T(8,128)}, f32[512,128]{1,0:T(8,128)S(1)}, u32[]{:S(2)}) copy-start(f32[512,128]{1,0:T(8,128)S(1)} %get-tuple-element.54.refs_2_.refs_6_) | copy-start | bytes 786436
  41.2 16.8 %collective-permute-start.6 = (bf16[256,1024]{1,0:T(8,128)(2,1)S(1)}, bf16[256,1024]{1,0:T(8,128)(2,1)S(1)}, u32[]{:S(2)}, u32[]{:S(2)}) collective-permute-start(bf16[256,1024]{1,0:T(8,128)(2,1)S(1)} %pick.15), channel_id=1, source_target_pairs={{8,12},{10,14},{4,0},{6,2},{24,28},{26,30},{20,16},{22,18}} | collective-permute-start | bytes 1572872 | tf_op jit(solution)/shard_map/ppermute | solution.py:320
  51.4 13.0 %collective-permute-start.12 = (bf16[256,1024]{1,0:T(8,128)(2,1)S(1)}, bf16[256,1024]{1,0:T(8,128)(2,1)S(1)}, u32[]{:S(2)}, u32[]{:S(2)}) collective-permute-start(bf16[256,1024]{1,0:T(8,128)(2,1)S(1)} %pick.18.refs_0_), channel_id=1, source_target_pairs={{0,2},{2,0},{4,6},{6,4},{8,10},{10,8},{12,14},{14,12},{16,18},{18,... | collective-permute-start | bytes 1572872 | tf_op jit(solution)/shard_map/ppermute | solution.py:320
  58.7 11.5 %collective-permute-start.8 = (bf16[256,1024]{1,0:T(8,128)(2,1)S(1)}, bf16[256,1024]{1,0:T(8,128)(2,1)S(1)}, u32[]{:S(2)}, u32[]{:S(2)}) collective-permute-start(bf16[256,1024]{1,0:T(8,128)(2,1)S(1)} %pick.16.refs_0_), channel_id=1, source_target_pairs={{0,2},{2,0},{4,6},{6,4},{8,10},{10,8},{12,14},{14,12},{16,18},{18,... | collective-permute-start | bytes 1572872 | tf_op jit(solution)/shard_map/ppermute | solution.py:320
  63.1 12.8 %collective-permute-start.11 = (bf16[256,1024]{1,0:T(8,128)(2,1)S(1)}, bf16[256,1024]{1,0:T(8,128)(2,1)S(1)}, u32[]{:S(2)}, u32[]{:S(2)}) collective-permute-start(bf16[256,1024]{1,0:T(8,128)(2,1)S(1)} %pick.18.refs_0_), channel_id=1, source_target_pairs={{0,1},{2,3},{4,5},{6,7},{8,9},{10,11},{12,13},{14,15},{16,17},{18,... | collective-permute-start | bytes 1572872 | tf_op jit(solution)/shard_map/ppermute | solution.py:320
  64.4 12.2 %collective-permute-start.13 = (bf16[256,1024]{1,0:T(8,128)(2,1)S(1)}, bf16[256,1024]{1,0:T(8,128)(2,1)S(1)}, u32[]{:S(2)}, u32[]{:S(2)}) collective-permute-start(bf16[256,1024]{1,0:T(8,128)(2,1)S(1)} %collective-permute-done.12.refs_2_), channel_id=1, source_target_pairs={{0,1},{2,3},{4,5},{6,7},{8,9},{10,11},{12,13},{14,15},{16,17},{18,... | collective-permute-start | bytes 1572872 | tf_op jit(solution)/shard_map/ppermute | solution.py:320
  65.8 17.2 %collective-permute-start.7 = (bf16[256,1024]{1,0:T(8,128)(2,1)S(1)}, bf16[256,1024]{1,0:T(8,128)(2,1)}, u32[]{:S(2)}, u32[]{:S(2)}) collective-permute-start(bf16[256,1024]{1,0:T(8,128)(2,1)S(1)} %pick.16.refs_0_), channel_id=1, source_target_pairs={{0,1},{2,3},{4,5},{6,7},{8,9},{10,11},{12,13},{14,15},{16,17},{18,... | collective-permute-start | bytes 1572872 | tf_op jit(solution)/shard_map/ppermute | solution.py:320
  70.2 12.8 %collective-permute-start.9 = (bf16[256,1024]{1,0:T(8,128)(2,1)S(1)}, bf16[256,1024]{1,0:T(8,128)(2,1)}, u32[]{:S(2)}, u32[]{:S(2)}) collective-permute-start(bf16[256,1024]{1,0:T(8,128)(2,1)S(1)} %collective-permute-done.8.refs_2_), channel_id=1, source_target_pairs={{0,1},{2,3},{4,5},{6,7},{8,9},{10,11},{12,13},{14,15},{16,17},{18,... | collective-permute-start | bytes 1572872 | tf_op jit(solution)/shard_map/ppermute | solution.py:320
  87.0 54.7 %copy-start.6 = (bf16[2048,256]{1,0:T(8,128)(2,1)}, bf16[2048,256]{1,0:T(8,128)(2,1)S(1)}, u32[]{:S(2)}) copy-start(bf16[2048,256]{1,0:T(8,128)(2,1)S(1)} %get-tuple-element.64.col_ref) | copy-start | bytes 3145732
  88.3 3.2 %collective-permute-start.16 = (f32[264,1024]{1,0:T(8,128)S(1)}, f32[264,1024]{1,0:T(8,128)S(1)}, u32[]{:S(2)}, u32[]{:S(2)}) collective-permute-start(f32[264,1024]{1,0:T(8,128)S(1)} %row_part.7), channel_id=1, source_target_pairs={{0,1},{1,0},{2,3},{3,2},{4,5},{5,4},{6,7},{7,6},{8,9},{9,8},{10,11... | collective-permute-start | bytes 3244040 | tf_op jit(solution)/shard_map/ppermute | solution.py:320
  89.7 5.5 %collective-permute-start.14 = (f32[264,1024]{1,0:T(8,128)S(1)}, f32[264,1024]{1,0:T(8,128)S(1)}, u32[]{:S(2)}, u32[]{:S(2)}) collective-permute-start(f32[264,1024]{1,0:T(8,128)S(1)} %row_part.5), channel_id=1, source_target_pairs={{0,1},{1,0},{2,3},{3,2},{4,5},{5,4},{6,7},{7,6},{8,9},{9,8},{10,11... | collective-permute-start | bytes 3244040 | tf_op jit(solution)/shard_map/ppermute | solution.py:320
  91.8 9.5 %collective-permute-start.18 = (s32[272,256]{1,0:T(8,128)S(1)}, s32[272,256]{1,0:T(8,128)S(1)}, u32[]{:S(2)}, u32[]{:S(2)}) collective-permute-start(s32[272,256]{1,0:T(8,128)S(1)} %get-tuple-element.71.refs_4_), channel_id=1, source_target_pairs={{0,2},{2,0},{1,3},{3,1},{4,6},{6,4},{5,7},{7,5},{8,10},{10,8},{9,1... | collective-permute-start | bytes 835592 | tf_op jit(solution)/shard_map/ppermute | solution.py:320
  95.5 13.4 %collective-permute-start.15 = (s32[272,256]{1,0:T(8,128)S(1)}, s32[272,256]{1,0:T(8,128)S(1)}, u32[]{:S(2)}, u32[]{:S(2)}) collective-permute-start(s32[272,256]{1,0:T(8,128)S(1)} %get-tuple-element.70), channel_id=1, source_target_pairs={{0,2},{2,0},{1,3},{3,1},{4,6},{6,4},{5,7},{7,5},{8,10},{10,8},{9,1... | collective-permute-start | bytes 835592 | tf_op jit(solution)/shard_map/ppermute | solution.py:320
  101.7 8.9 %collective-permute-start.20 = (s32[272,256]{1,0:T(8,128)S(1)}, s32[272,256]{1,0:T(8,128)S(1)}, u32[]{:S(2)}, u32[]{:S(2)}) collective-permute-start(s32[272,256]{1,0:T(8,128)S(1)} %get-tuple-element.78.refs_4_), channel_id=1, source_target_pairs={{0,4},{1,5},{2,6},{3,7},{12,8},{13,9},{14,10},{15,11},{16,20},{17,... | collective-permute-start | bytes 835592 | tf_op jit(solution)/shard_map/ppermute | solution.py:320
  109.3 8.3 %collective-permute-start.17 = (s32[272,256]{1,0:T(8,128)S(1)}, s32[272,256]{1,0:T(8,128)S(1)}, u32[]{:S(2)}, u32[]{:S(2)}) collective-permute-start(s32[272,256]{1,0:T(8,128)S(1)} %get-tuple-element.75), channel_id=1, source_target_pairs={{0,4},{1,5},{2,6},{3,7},{12,8},{13,9},{14,10},{15,11},{16,20},{17,... | collective-permute-start | bytes 835592 | tf_op jit(solution)/shard_map/ppermute | solution.py:320
  110.9 7.7 %collective-permute-start.25 = (s32[272,256]{1,0:T(8,128)S(1)}, s32[272,256]{1,0:T(8,128)S(1)}, u32[]{:S(2)}, u32[]{:S(2)}) collective-permute-start(s32[272,256]{1,0:T(8,128)S(1)} %merge.11.refs_4_), channel_id=1, source_target_pairs={{4,8},{5,9},{6,10},{7,11},{8,4},{9,5},{10,6},{11,7},{20,24},{21,25... | collective-permute-start | bytes 835592 | tf_op jit(solution)/shard_map/ppermute | solution.py:320
  117.9 6.7 %collective-permute-start.19 = (s32[272,256]{1,0:T(8,128)S(1)}, s32[272,256]{1,0:T(8,128)S(1)}, u32[]{:S(2)}, u32[]{:S(2)}) collective-permute-start(s32[272,256]{1,0:T(8,128)S(1)} %merge.10), channel_id=1, source_target_pairs={{4,8},{5,9},{6,10},{7,11},{8,4},{9,5},{10,6},{11,7},{20,24},{21,25... | collective-permute-start | bytes 835592 | tf_op jit(solution)/shard_map/ppermute | solution.py:320
  118.9 10.3 %collective-permute-start.26 = (s32[272,256]{1,0:T(8,128)S(1)}, s32[272,256]{1,0:T(8,128)S(1)}, u32[]{:S(2)}, u32[]{:S(2)}) collective-permute-start(s32[272,256]{1,0:T(8,128)S(1)} %merge.14), channel_id=1, source_target_pairs={{8,12},{9,13},{10,14},{11,15},{4,0},{5,1},{6,2},{7,3},{24,28},{25,... | collective-permute-start | bytes 835592 | tf_op jit(solution)/shard_map/ppermute | solution.py:320
  124.9 10.4 %collective-permute-start.21 = (s32[272,256]{1,0:T(8,128)S(1)}, s32[272,256]{1,0:T(8,128)S(1)}, u32[]{:S(2)}, u32[]{:S(2)}) collective-permute-start(s32[272,256]{1,0:T(8,128)S(1)} %merge.12), channel_id=1, source_target_pairs={{8,12},{9,13},{10,14},{11,15},{4,0},{5,1},{6,2},{7,3},{24,28},{25,... | collective-permute-start | bytes 835592 | tf_op jit(solution)/shard_map/ppermute | solution.py:320
  130.6 9.8 %collective-permute-start.29 = (s32[272,256]{1,0:T(8,128)}, s32[272,256]{1,0:T(8,128)S(1)}, u32[]{:S(2)}, u32[]{:S(2)}) collective-permute-start(s32[272,256]{1,0:T(8,128)} %get-tuple-element.89.refs_4_), channel_id=1, source_target_pairs={{3,0},{7,4},{11,8},{15,12},{19,16},{23,20},{27,24},{31,28}} | collective-permute-start | bytes 835592 | tf_op jit(solution)/shard_map/ppermute | solution.py:320
  131.8 15.7 %collective-permute-start.28 = (s32[272,256]{1,0:T(8,128)}, s32[272,256]{1,0:T(8,128)}, u32[]{:S(2)}, u32[]{:S(2)}) collective-permute-start(s32[272,256]{1,0:T(8,128)} %get-tuple-element.89.refs_4_), channel_id=1, source_target_pairs={{1,0},{5,4},{9,8},{13,12},{17,16},{21,20},{25,24},{29,28}} | collective-permute-start | bytes 835592 | tf_op jit(solution)/shard_map/ppermute | solution.py:320
  133.1 14.4 %collective-permute-start.27 = (s32[272,256]{1,0:T(8,128)}, s32[272,256]{1,0:T(8,128)}, u32[]{:S(2)}, u32[]{:S(2)}) collective-permute-start(s32[272,256]{1,0:T(8,128)} %get-tuple-element.89.refs_4_), channel_id=1, source_target_pairs={{2,0},{6,4},{10,8},{14,12},{18,16},{22,20},{26,24},{30,28}} | collective-permute-start | bytes 835592 | tf_op jit(solution)/shard_map/ppermute | solution.py:320
  137.8 9.7 %collective-permute-start.24 = (s32[272,256]{1,0:T(8,128)}, s32[272,256]{1,0:T(8,128)}, u32[]{:S(2)}, u32[]{:S(2)}) collective-permute-start(s32[272,256]{1,0:T(8,128)} %get-tuple-element.87), channel_id=1, source_target_pairs={{3,0},{7,4},{11,8},{15,12},{19,16},{23,20},{27,24},{31,28}} | collective-permute-start | bytes 835592 | tf_op jit(solution)/shard_map/ppermute | solution.py:320
  139.1 8.5 %collective-permute-start.23 = (s32[272,256]{1,0:T(8,128)}, s32[272,256]{1,0:T(8,128)}, u32[]{:S(2)}, u32[]{:S(2)}) collective-permute-start(s32[272,256]{1,0:T(8,128)} %get-tuple-element.87), channel_id=1, source_target_pairs={{1,0},{5,4},{9,8},{13,12},{17,16},{21,20},{25,24},{29,28}} | collective-permute-start | bytes 835592 | tf_op jit(solution)/shard_map/ppermute | solution.py:320
  140.4 8.8 %collective-permute-start.22 = (s32[272,256]{1,0:T(8,128)}, s32[272,256]{1,0:T(8,128)}, u32[]{:S(2)}, u32[]{:S(2)}) collective-permute-start(s32[272,256]{1,0:T(8,128)} %get-tuple-element.87), channel_id=1, source_target_pairs={{2,0},{6,4},{10,8},{14,12},{18,16},{22,20},{26,24},{30,28}} | collective-permute-start | bytes 835592 | tf_op jit(solution)/shard_map/ppermute | solution.py:320
  (18 other events, 68.7 us)

commit v9 on v8

--- a/solution.py
+++ b/solution.py
@@ -352,7 +352,7 @@
             pltpu.VMEM((ROWS, width), jnp.bfloat16),
             pltpu.SemaphoreType.DMA((4,)),
         ],
-        compiler_params=params(50),
+        compiler_params=params(44),
         cost_estimate=cost(4 * ROWS * width, 4 * ROWS * width),
         name="head_units",
     )(flags, decoder)
@@ -397,7 +397,7 @@
                 pltpu.VMEM((2, BLOCK, width), jnp.bfloat16),
                 pltpu.SemaphoreType.DMA((2,)),
             ],
-            compiler_params=params((46, 44, 40, 36)[part]),
+            compiler_params=params((43, 40, 37, 34)[part]),
             cost_estimate=cost(4 * rows * width, 4 * rows * width),
             name="units",
         )(decoder, tie)
@@ -521,7 +521,7 @@
     bounds = [1 + (blocks - 1) * p // 7 for p in (0, 2, 4, 5, 5, 7)]
     grad = None
 
-    def finish(part, tie):
+    def finish(part, ties):
         nonlocal grad
         low, high = bounds[part], bounds[part + 1]
         if high == low:
@@ -532,8 +532,8 @@
             pl.BlockSpec((BLOCK, width), lambda i: (i + low, 0)),
             pl.BlockSpec((BLOCK, 128), lambda i: (i + low, 0)),
         ] + [whole_chunk] * COUNT
-        operands.append(tie)
-        specs.append(any_spec)
+        operands += ties
+        specs += [any_spec] * len(ties)
         aliases = {}
         if grad is not None:
             aliases = {len(operands): 0}
@@ -547,7 +547,7 @@
             out_specs=[pl.BlockSpec((BLOCK, width), lambda i: (i + low, 0)), mark_spec],
             out_shape=[out_type, mark_type],
             input_output_aliases=aliases,
-            compiler_params=params(50),
+            compiler_params=params(44),
             cost_estimate=cost(2 * ROWS * rows * width, 6 * rows * width),
             name="finish",
         )(*operands)
@@ -555,20 +555,19 @@
 
     lanes = range(4)
     across = [send(msg[k], across_x) for k in range(PAIRS)]
-    ties = finish(0, msg[PAIRS - 1])
-    for k in range(PAIRS):
-        kept[k], msg[k] = merge(kept[k], [across[k]], True, () if k else ties)
+    ties = finish(0, msg)
+    for k in range(PAIRS):
+        kept[k], msg[k] = merge(kept[k], [across[k]], True, ties)
     arrivals = [[] for _ in range(PAIRS)]
     for level in range(3):
         for k in range(PAIRS):
             arrivals[k].append(send(msg[k], hop(level, lanes)))
-        ties = finish(level + 1, msg[PAIRS - 1])
+        ties = finish(level + 1, msg)
         for k in range(PAIRS):
-            tied = () if k else ties
             if level < 2:
-                msg[k] = merge(kept[k], arrivals[k][-1:], False, tied)
+                msg[k] = merge(kept[k], arrivals[k][-1:], False, ties)
             else:
-                kept[k], msg[k] = merge(kept[k], arrivals[k], True, tied)
+                kept[k], msg[k] = merge(kept[k], arrivals[k], True, ties)
 
     tile = kept[0][1]
     far = 4
@@ -578,7 +577,7 @@
         tile = jnp.where(fresh, send(tile, moves), tile)
         far *= 2
 
-    finish(4, msg[PAIRS - 1])
+    finish(4, msg)
     sums, row_specs = [], []
     narrow = BLOCK // 2
     for k in range(PAIRS):
@@ -616,7 +615,7 @@
         out_shape=[out_type, jax.ShapeDtypeStruct((1,), jnp.float32)],
         scratch_shapes=[pltpu.VMEM((narrow, width), jnp.float32)],
         input_output_aliases=aliases,
-        compiler_params=params(50),
+        compiler_params=params(44),
         name="finish_rows",
     )(*operands)
 

time: 156 us -> 164 us (1.051); the launches traced: 155 us -> 161 us
  waiting for transfers between devices: 25.8 us -> 29 us
  local copies, waits for them, and re-layouts: 10.7 us -> 12.8 us
    ppermute x30, waiting for transfers between devices: 25.8 us -> 29 us  [send(): return lax.ppermute(value, 'row', pairs)]
    unnamed x40 -> x44, local copies, waits for them, and re-layouts: 10.6 us -> 12.7 us
  transfers between devices with their start and end apart: 30 -> 30, of which waited for: 8 -> 8; matrix products, arithmetic and copies ran while one was open for 0% -> 0% of each run, Pallas kernels for 34% -> 33%
where the time goes in v9:
time: 164 us; the launch traced here: 161 us
  Pallas kernels  66.6 us (41%)
  starting transfers between devices  50.3 us (31%)
  waiting for transfers between devices  29 us (18%)
  local copies, waits for them, and re-layouts  12.8 us (8%)
  between operations  2.05 us (1%)
    ppermute x30, starting transfers between devices, send(): return lax.ppermute(value, 'row', pairs)  50.3 us
    ppermute x30, waiting for transfers between devices, send(): return lax.ppermute(value, 'row', pairs)  29 us
    pallas_call x4, Pallas kernels, finish(): pl.pallas_call(finish_kernel, grid=(high - low,), in_specs=specs, out_spe...  21.9 us
    pallas_call x4, Pallas kernels, make_units(): pl.pallas_call(functools.partial(units_kernel, low, high - low), in_specs...  13.5 us
    unnamed x44, local copies, waits for them, and re-layouts  12.7 us
    pallas_call x10, Pallas kernels, pick(): pl.pallas_call(functools.partial(pick_kernel, slots, len(candidates)), in...  6.38 us
    pallas_call x1, Pallas kernels, on_device(): pl.pallas_call(functools.partial(last_kernel, DW / (ROWS * latents)), gri...  5.35 us
    pallas_call x4, Pallas kernels, row_part(): pl.pallas_call(functools.partial(row_kernel, k, parts), in_specs=[smem] +...  5.02 us
  transfers between devices with their start and end apart: 30, of which 8 were waited for; matrix products, arithmetic and copies ran while one was open for 0% of the time, Pallas kernels for 33%

profile of v9, /device:TPU:0, one launch (start us, length us, event | category | flops | bytes accessed | tf_op | source)
XLA Modules:
  0.0 160.8 jit_solution(544711687937961200)
XLA Ops:
  1.5 2.6 %head_units.1 = (bf16[256,1024]{1,0:T(8,128)(2,1)S(1)}, bf16[256,1024]{1,0:T(8,128)(2,1)S(1)}, bf16[256,1024]{1,0:T(8,128)(2,1)S(1)}, bf16[256,1024]{1,0:T(8,128)(2,1)S(1)}) custom-call(s32[5]{0:T(128)S(1)} %stack.23.flags_ref, bf16[2048,4096]{1,0:T(8,128)(2,1)} %decoder_ref.19), custom_call_target="tpu_custom_call" | custom-call | flops 4194304 | bytes 4194304 | tf_op jit(solution)/shard_map/head_units/pallas_call | solution.py:346
  4.1 4.9 %collective-permute-start.3 = (bf16[256,1024]{1,0:T(8,128)(2,1)S(1)}, bf16[256,1024]{1,0:T(8,128)(2,1)S(1)}, u32[]{:S(2)}, u32[]{:S(2)}) collective-permute-start(bf16[256,1024]{1,0:T(8,128)(2,1)S(1)} %get-tuple-element.51), channel_id=1, source_target_pairs={{0,2},{4,6},{8,10},{12,14},{16,18},{20,22},{24,26},{28,30}} | collective-permute-start | bytes 1572872 | tf_op jit(solution)/shard_map/ppermute | solution.py:320
  10.3 3.3 %units.4 = (bf16[512,4096]{1,0:T(8,128)(2,1)S(1)}, f32[512,128]{1,0:T(8,128)S(1)}) custom-call(bf16[2048,4096]{1,0:T(8,128)(2,1)} %decoder_ref.19, bf16[256,1024]{1,0:T(8,128)(2,1)S(1)} %get-tuple-element.50.refs_0_), custom_call_target="tpu_custom_call" | custom-call | flops 8388608 | bytes 8388608 | tf_op jit(solution)/shard_map/units/pallas_call | solution.py:388
  13.6 2.0 %copy-done = bf16[512,4096]{1,0:T(8,128)(2,1)} copy-done((bf16[512,4096]{1,0:T(8,128)(2,1)}, bf16[512,4096]{1,0:T(8,128)(2,1)S(1)}, u32[]{:S(2)}) %copy-start) | copy-done | bytes 4194328
  16.2 3.5 %collective-permute-start.4 = (bf16[256,1024]{1,0:T(8,128)(2,1)S(1)}, bf16[256,1024]{1,0:T(8,128)(2,1)S(1)}, u32[]{:S(2)}, u32[]{:S(2)}) collective-permute-start(bf16[256,1024]{1,0:T(8,128)(2,1)S(1)} %pick.12.refs_0_), channel_id=1, source_target_pairs={{0,4},{2,6},{12,8},{14,10},{16,20},{18,22},{28,24},{30,26}} | collective-permute-start | bytes 1572872 | tf_op jit(solution)/shard_map/ppermute | solution.py:320
  19.8 1.5 collective-permute-done.refs_1_
  21.8 3.5 %collective-permute-start.1 = (bf16[256,1024]{1,0:T(8,128)(2,1)S(1)}, bf16[256,1024]{1,0:T(8,128)(2,1)S(1)}, u32[]{:S(2)}, u32[]{:S(2)}) collective-permute-start(bf16[256,1024]{1,0:T(8,128)(2,1)S(1)} %pick.10.refs_0_), channel_id=1, source_target_pairs={{0,4},{2,6},{12,8},{14,10},{16,20},{18,22},{28,24},{30,26}} | collective-permute-start | bytes 1572872 | tf_op jit(solution)/shard_map/ppermute | solution.py:320
  25.4 3.3 %units.5 = (bf16[512,4096]{1,0:T(8,128)(2,1)S(1)}, f32[512,128]{1,0:T(8,128)S(1)}) custom-call(bf16[2048,4096]{1,0:T(8,128)(2,1)} %decoder_ref.19, bf16[256,1024]{1,0:T(8,128)(2,1)S(1)} %pick.10.refs_0_), custom_call_target="tpu_custom_call" | custom-call | flops 8388608 | bytes 8388608 | tf_op jit(solution)/shard_map/units/pallas_call | solution.py:388
  28.7 2.0 %copy-done.2 = bf16[512,4096]{1,0:T(8,128)(2,1)} copy-done((bf16[512,4096]{1,0:T(8,128)(2,1)}, bf16[512,4096]{1,0:T(8,128)(2,1)S(1)}, u32[]{:S(2)}) %copy-start.2) | copy-done | bytes 4194328
  35.3 3.3 %units.6 = (bf16[512,4096]{1,0:T(8,128)(2,1)S(1)}, f32[512,128]{1,0:T(8,128)S(1)}) custom-call(bf16[2048,4096]{1,0:T(8,128)(2,1)} %decoder_ref.19, bf16[256,1024]{1,0:T(8,128)(2,1)S(1)} %pick.14.refs_0_), custom_call_target="tpu_custom_call" | custom-call | flops 8388608 | bytes 8388608 | tf_op jit(solution)/shard_map/units/pallas_call | solution.py:388
  38.6 2.0 %copy-done.4 = bf16[512,4096]{1,0:T(8,128)(2,1)} copy-done((bf16[512,4096]{1,0:T(8,128)(2,1)}, bf16[512,4096]{1,0:T(8,128)(2,1)S(1)}, u32[]{:S(2)}) %copy-start.4) | copy-done | bytes 4194328
  42.5 8.2 %collective-permute-done.10.refs_3_ = bf16[256,1024]{1,0:T(8,128)(2,1)S(1)} collective-permute-done((bf16[256,1024]{1,0:T(8,128)(2,1)S(1)}, bf16[256,1024]{1,0:T(8,128)(2,1)S(1)}, u32[]{:S(2)}, u32[]{:S(2)}) %collective-permute-start.10) | collective-permute-done | bytes 524320 | tf_op jit(solution)/shard_map/ppermute | solution.py:320
  51.4 4.4 %collective-permute-start.12 = (bf16[256,1024]{1,0:T(8,128)(2,1)S(1)}, bf16[256,1024]{1,0:T(8,128)(2,1)S(1)}, u32[]{:S(2)}, u32[]{:S(2)}) collective-permute-start(bf16[256,1024]{1,0:T(8,128)(2,1)S(1)} %pick.18.refs_0_), channel_id=1, source_target_pairs={{0,2},{2,0},{4,6},{6,4},{8,10},{10,8},{12,14},{14,12},{16,18},{18,... | collective-permute-start | bytes 1572872 | tf_op jit(solution)/shard_map/ppermute | solution.py:320
  55.8 2.3 %collective-permute-done.6.refs_3_ = bf16[256,1024]{1,0:T(8,128)(2,1)S(1)} collective-permute-done((bf16[256,1024]{1,0:T(8,128)(2,1)S(1)}, bf16[256,1024]{1,0:T(8,128)(2,1)S(1)}, u32[]{:S(2)}, u32[]{:S(2)}) %collective-permute-start.6) | collective-permute-done | bytes 524320 | tf_op jit(solution)/shard_map/ppermute | solution.py:320
  58.7 4.4 %collective-permute-start.8 = (bf16[256,1024]{1,0:T(8,128)(2,1)S(1)}, bf16[256,1024]{1,0:T(8,128)(2,1)S(1)}, u32[]{:S(2)}, u32[]{:S(2)}) collective-permute-start(bf16[256,1024]{1,0:T(8,128)(2,1)S(1)} %pick.16.refs_0_), channel_id=1, source_target_pairs={{0,2},{2,0},{4,6},{6,4},{8,10},{10,8},{12,14},{14,12},{16,18},{18,... | collective-permute-start | bytes 1572872 | tf_op jit(solution)/shard_map/ppermute | solution.py:320
  65.8 2.1 %collective-permute-start.7 = (bf16[256,1024]{1,0:T(8,128)(2,1)S(1)}, bf16[256,1024]{1,0:T(8,128)(2,1)}, u32[]{:S(2)}, u32[]{:S(2)}) collective-permute-start(bf16[256,1024]{1,0:T(8,128)(2,1)S(1)} %pick.16.refs_0_), channel_id=1, source_target_pairs={{0,1},{2,3},{4,5},{6,7},{8,9},{10,11},{12,13},{14,15},{16,17},{18,... | collective-permute-start | bytes 1572872 | tf_op jit(solution)/shard_map/ppermute | solution.py:320
  67.9 2.4 %collective-permute-done.8.refs_2_ = bf16[256,1024]{1,0:T(8,128)(2,1)S(1)} collective-permute-done((bf16[256,1024]{1,0:T(8,128)(2,1)S(1)}, bf16[256,1024]{1,0:T(8,128)(2,1)S(1)}, u32[]{:S(2)}, u32[]{:S(2)}) %collective-permute-start.8) | collective-permute-done | bytes 524320 | tf_op jit(solution)/shard_map/ppermute | solution.py:320
  70.2 2.1 %collective-permute-start.9 = (bf16[256,1024]{1,0:T(8,128)(2,1)S(1)}, bf16[256,1024]{1,0:T(8,128)(2,1)}, u32[]{:S(2)}, u32[]{:S(2)}) collective-permute-start(bf16[256,1024]{1,0:T(8,128)(2,1)S(1)} %collective-permute-done.8.refs_2_), channel_id=1, source_target_pairs={{0,1},{2,3},{4,5},{6,7},{8,9},{10,11},{12,13},{14,15},{16,17},{18,... | collective-permute-start | bytes 1572872 | tf_op jit(solution)/shard_map/ppermute | solution.py:320
  72.3 3.5 %units.7 = (bf16[512,4096]{1,0:T(8,128)(2,1)S(1)}, f32[512,128]{1,0:T(8,128)S(1)}) custom-call(bf16[2048,4096]{1,0:T(8,128)(2,1)} %decoder_ref.19, bf16[256,1024]{1,0:T(8,128)(2,1)S(1)} %pick.16.refs_0_), custom_call_target="tpu_custom_call" | custom-call | flops 8388608 | bytes 8388608 | tf_op jit(solution)/shard_map/units/pallas_call | solution.py:388
  80.6 2.4 %part_cosines.1.partial_ref = f32[2048,256]{1,0:T(8,128)S(1)} custom-call(bf16[256,1024]{1,0:T(8,128)(2,1)S(1)} %get-tuple-element.58.low_ref.refs_0_, bf16[256,1024]{1,0:T(8,128)(2,1)S(1)} %get-tuple-element.59.high_ref.refs_1_, bf16[512,4096]{1,0:T(8,128)(2,1)S(1)} %copy-done.1, bf16[512,4096]{1,0:T(8,128)(2,1)S(1)} %copy-done.3, ...), custom_call_target="tpu_custom_call" | custom-call | flops 2147483648 | bytes 8388608 | tf_op jit(solution)/shard_map/part_cosines/pallas_call | solution.py:443
  83.7 3.3 %weights.1 = (bf16[2048,256]{1,0:T(8,128)(2,1)S(1)}, bf16[256,2048]{1,0:T(8,128)(2,1)S(1)}, f32[2048,128]{1,0:T(8,128)S(1)}, f32[8,128]{1,0:T(8,128)S(1)}) custom-call(s32[1]{0:T(128)} %bitcast.2.delta_ref, bf16[256,1024]{1,0:T(8,128)(2,1)S(1)} %get-tuple-element.55.low_ref.refs_2_, bf16[256,1024]{1,0:T(8,128)(2,1)S(1)} %get-tuple-element.56.high_ref.refs_3_, ...), custom_call_target="tpu_custom_call" | custom-call | flops 2147483648 | bytes 8388608 | tf_op jit(solution)/shard_map/weights/pallas_call | solution.py:452
  92.5 2.0 %collective-permute-start.18 = (s32[272,256]{1,0:T(8,128)}, s32[272,256]{1,0:T(8,128)S(1)}, u32[]{:S(2)}, u32[]{:S(2)}) collective-permute-start(s32[272,256]{1,0:T(8,128)} %get-tuple-element.71.refs_5_), channel_id=1, source_target_pairs={{0,2},{2,0},{1,3},{3,1},{4,6},{6,4},{5,7},{7,5},{8,10},{10,8},{9,1... | collective-permute-start | bytes 835592 | tf_op jit(solution)/shard_map/ppermute | solution.py:320
  96.2 5.8 %finish.4 = (f32[2048,4096]{1,0:T(8,128)}, f32[8,128]{1,0:T(8,128)S(1)}) custom-call(bf16[2048,256]{1,0:T(8,128)(2,1)S(1)} %get-tuple-element.64.col_ref, bf16[2048,4096]{1,0:T(8,128)(2,1)} %decoder_ref.19, f32[2048,128]{1,0:T(8,128)S(1)} %get-tuple-element.65.factor_ref, bf16[256,1024]{1,0:T(8,128)(2,1)S(1)} %get-tuple-element.58.low_ref.refs_0_, ...), custom_call_target="tpu_custom_call" | custom-call | flops 1073741824 | bytes 12582912 | tf_op jit(solution)/shard_map/finish/pallas_call | solution.py:543
  102.5 1.5 collective-permute-start.20
  104.0 3.5 %collective-permute-done.15.refs_0_ = s32[272,256]{1,0:T(8,128)S(1)} collective-permute-done((s32[272,256]{1,0:T(8,128)S(1)}, s32[272,256]{1,0:T(8,128)S(1)}, u32[]{:S(2)}, u32[]{:S(2)}) %collective-permute-start.15) | collective-permute-done | bytes 278560 | tf_op jit(solution)/shard_map/ppermute | solution.py:320
  107.8 1.5 collective-permute-start.17
  109.3 5.8 %finish.5 = (f32[2048,4096]{1,0:T(8,128)}, f32[8,128]{1,0:T(8,128)S(1)}) custom-call(bf16[2048,256]{1,0:T(8,128)(2,1)S(1)} %get-tuple-element.64.col_ref, bf16[2048,4096]{1,0:T(8,128)(2,1)} %decoder_ref.19, f32[2048,128]{1,0:T(8,128)S(1)} %get-tuple-element.65.factor_ref, ...), custom_call_target="tpu_custom_call", output_to_operand_aliasing={{0}: (9, {})} | custom-call | flops 1073741824 | bytes 12582912 | tf_op jit(solution)/shard_map/finish/pallas_call | solution.py:543
  117.4 4.4 %finish.6 = (f32[2048,4096]{1,0:T(8,128)}, f32[8,128]{1,0:T(8,128)S(1)}) custom-call(bf16[2048,256]{1,0:T(8,128)(2,1)S(1)} %get-tuple-element.64.col_ref, bf16[2048,4096]{1,0:T(8,128)(2,1)} %decoder_ref.19, f32[2048,128]{1,0:T(8,128)S(1)} %get-tuple-element.65.factor_ref, ...), custom_call_target="tpu_custom_call", output_to_operand_aliasing={{0}: (9, {})} | custom-call | flops 536870912 | bytes 6291456 | tf_op jit(solution)/shard_map/finish/pallas_call | solution.py:543
  125.1 10.5 %collective-permute-done.26.refs_2_ = s32[272,256]{1,0:T(8,128)S(1)} collective-permute-done((s32[272,256]{1,0:T(8,128)S(1)}, s32[272,256]{1,0:T(8,128)S(1)}, u32[]{:S(2)}, u32[]{:S(2)}) %collective-permute-start.26) | collective-permute-done | bytes 278560 | tf_op jit(solution)/shard_map/ppermute | solution.py:320
  140.8 1.7 %merge.13 = (f32[256,512]{1,0:T(8,128)S(1)}, f32[8,128]{1,0:T(8,128)S(1)}, s32[272,256]{1,0:T(8,128)}) custom-call(f32[256,512]{1,0:T(8,128)S(1)} %get-tuple-element.73.kept_ref, f32[8,128]{1,0:T(8,128)S(1)} %get-tuple-element.74.penalty_ref, s32[272,256]{1,0:T(8,128)S(1)} %collective-permute-done.17.refs_0_, ...), custom_call_target="tpu_custom_call" | custom-call | flops 2621440 | bytes 1572864 | tf_op jit(solution)/shard_map/merge/pallas_call | solution.py:488
  149.3 5.9 %finish.7 = (f32[2048,4096]{1,0:T(8,128)}, f32[8,128]{1,0:T(8,128)}) custom-call(bf16[2048,256]{1,0:T(8,128)(2,1)S(1)} %get-tuple-element.64.col_ref, bf16[2048,4096]{1,0:T(8,128)(2,1)} %decoder_ref.19, f32[2048,128]{1,0:T(8,128)S(1)} %get-tuple-element.65.factor_ref, ...), custom_call_target="tpu_custom_call", output_to_operand_aliasing={{0}: (9, {})} | custom-call | flops 1073741824 | bytes 12582912 | tf_op jit(solution)/shard_map/finish/pallas_call | solution.py:543
  155.4 5.3 %finish_rows.1 = (f32[2048,4096]{1,0:T(8,128)}, f32[1]{0:T(128)}) custom-call(s32[1]{0:T(128)} %bitcast.1.owner_ref, bf16[2048,256]{1,0:T(8,128)(2,1)S(1)} %get-tuple-element.64.col_ref, bf16[2048,4096]{1,0:T(8,128)(2,1)} %decoder_ref.19, f32[2048,128]{1,0:T(8,128)S(1)} %get-tuple-element.65.factor_ref, ...), custom_call_target="tpu_custom_call", output_to_operand_aliasing={{0}: (23, {})} | custom-call | tf_op jit(solution)/shard_map/finish_rows/pallas_call | solution.py:610
  (109 shorter events, 43.8 us)
Async XLA Ops:
  4.1 11.6 %collective-permute-start.3 = (bf16[256,1024]{1,0:T(8,128)(2,1)S(1)}, bf16[256,1024]{1,0:T(8,128)(2,1)S(1)}, u32[]{:S(2)}, u32[]{:S(2)}) collective-permute-start(bf16[256,1024]{1,0:T(8,128)(2,1)S(1)} %get-tuple-element.51), channel_id=1, source_target_pairs={{0,2},{4,6},{8,10},{12,14},{16,18},{20,22},{24,26},{28,30}} | collective-permute-start | bytes 1572872 | tf_op jit(solution)/shard_map/ppermute | solution.py:320
  9.0 12.3 %collective-permute-start = (bf16[256,1024]{1,0:T(8,128)(2,1)S(1)}, bf16[256,1024]{1,0:T(8,128)(2,1)S(1)}, u32[]{:S(2)}, u32[]{:S(2)}) collective-permute-start(bf16[256,1024]{1,0:T(8,128)(2,1)S(1)} %get-tuple-element.49), channel_id=1, source_target_pairs={{0,2},{4,6},{8,10},{12,14},{16,18},{20,22},{24,26},{28,30}} | collective-permute-start | bytes 1572872 | tf_op jit(solution)/shard_map/ppermute | solution.py:320
  16.2 14.4 %collective-permute-start.4 = (bf16[256,1024]{1,0:T(8,128)(2,1)S(1)}, bf16[256,1024]{1,0:T(8,128)(2,1)S(1)}, u32[]{:S(2)}, u32[]{:S(2)}) collective-permute-start(bf16[256,1024]{1,0:T(8,128)(2,1)S(1)} %pick.12.refs_0_), channel_id=1, source_target_pairs={{0,4},{2,6},{12,8},{14,10},{16,20},{18,22},{28,24},{30,26}} | collective-permute-start | bytes 1572872 | tf_op jit(solution)/shard_map/ppermute | solution.py:320
  21.8 10.2 %collective-permute-start.1 = (bf16[256,1024]{1,0:T(8,128)(2,1)S(1)}, bf16[256,1024]{1,0:T(8,128)(2,1)S(1)}, u32[]{:S(2)}, u32[]{:S(2)}) collective-permute-start(bf16[256,1024]{1,0:T(8,128)(2,1)S(1)} %pick.10.refs_0_), channel_id=1, source_target_pairs={{0,4},{2,6},{12,8},{14,10},{16,20},{18,22},{28,24},{30,26}} | collective-permute-start | bytes 1572872 | tf_op jit(solution)/shard_map/ppermute | solution.py:320
  31.3 2.1 %collective-permute-start.5 = (bf16[256,1024]{1,0:T(8,128)(2,1)S(1)}, bf16[256,1024]{1,0:T(8,128)(2,1)S(1)}, u32[]{:S(2)}, u32[]{:S(2)}) collective-permute-start(bf16[256,1024]{1,0:T(8,128)(2,1)S(1)} %pick.13), channel_id=1, source_target_pairs={{4,8},{6,10},{8,4},{10,6},{20,24},{22,26},{24,20},{26,22}} | collective-permute-start | bytes 1572872 | tf_op jit(solution)/shard_map/ppermute | solution.py:320
  32.6 8.0 %collective-permute-start.2 = (bf16[256,1024]{1,0:T(8,128)(2,1)S(1)}, bf16[256,1024]{1,0:T(8,128)(2,1)S(1)}, u32[]{:S(2)}, u32[]{:S(2)}) collective-permute-start(bf16[256,1024]{1,0:T(8,128)(2,1)S(1)} %pick.11), channel_id=1, source_target_pairs={{4,8},{6,10},{8,4},{10,6},{20,24},{22,26},{24,20},{26,22}} | collective-permute-start | bytes 1572872 | tf_op jit(solution)/shard_map/ppermute | solution.py:320
  34.0 16.8 %collective-permute-start.10 = (bf16[256,1024]{1,0:T(8,128)(2,1)S(1)}, bf16[256,1024]{1,0:T(8,128)(2,1)S(1)}, u32[]{:S(2)}, u32[]{:S(2)}) collective-permute-start(bf16[256,1024]{1,0:T(8,128)(2,1)S(1)} %pick.14.refs_0_), channel_id=1, source_target_pairs={{8,12},{10,14},{4,0},{6,2},{24,28},{26,30},{20,16},{22,18}} | collective-permute-start | bytes 1572872 | tf_op jit(solution)/shard_map/ppermute | solution.py:320
  41.2 16.8 %collective-permute-start.6 = (bf16[256,1024]{1,0:T(8,128)(2,1)S(1)}, bf16[256,1024]{1,0:T(8,128)(2,1)S(1)}, u32[]{:S(2)}, u32[]{:S(2)}) collective-permute-start(bf16[256,1024]{1,0:T(8,128)(2,1)S(1)} %pick.15), channel_id=1, source_target_pairs={{8,12},{10,14},{4,0},{6,2},{24,28},{26,30},{20,16},{22,18}} | collective-permute-start | bytes 1572872 | tf_op jit(solution)/shard_map/ppermute | solution.py:320
  51.4 13.0 %collective-permute-start.12 = (bf16[256,1024]{1,0:T(8,128)(2,1)S(1)}, bf16[256,1024]{1,0:T(8,128)(2,1)S(1)}, u32[]{:S(2)}, u32[]{:S(2)}) collective-permute-start(bf16[256,1024]{1,0:T(8,128)(2,1)S(1)} %pick.18.refs_0_), channel_id=1, source_target_pairs={{0,2},{2,0},{4,6},{6,4},{8,10},{10,8},{12,14},{14,12},{16,18},{18,... | collective-permute-start | bytes 1572872 | tf_op jit(solution)/shard_map/ppermute | solution.py:320
  58.7 11.5 %collective-permute-start.8 = (bf16[256,1024]{1,0:T(8,128)(2,1)S(1)}, bf16[256,1024]{1,0:T(8,128)(2,1)S(1)}, u32[]{:S(2)}, u32[]{:S(2)}) collective-permute-start(bf16[256,1024]{1,0:T(8,128)(2,1)S(1)} %pick.16.refs_0_), channel_id=1, source_target_pairs={{0,2},{2,0},{4,6},{6,4},{8,10},{10,8},{12,14},{14,12},{16,18},{18,... | collective-permute-start | bytes 1572872 | tf_op jit(solution)/shard_map/ppermute | solution.py:320
  63.1 12.8 %collective-permute-start.11 = (bf16[256,1024]{1,0:T(8,128)(2,1)S(1)}, bf16[256,1024]{1,0:T(8,128)(2,1)S(1)}, u32[]{:S(2)}, u32[]{:S(2)}) collective-permute-start(bf16[256,1024]{1,0:T(8,128)(2,1)S(1)} %pick.18.refs_0_), channel_id=1, source_target_pairs={{0,1},{2,3},{4,5},{6,7},{8,9},{10,11},{12,13},{14,15},{16,17},{18,... | collective-permute-start | bytes 1572872 | tf_op jit(solution)/shard_map/ppermute | solution.py:320
  64.4 12.3 %collective-permute-start.13 = (bf16[256,1024]{1,0:T(8,128)(2,1)S(1)}, bf16[256,1024]{1,0:T(8,128)(2,1)S(1)}, u32[]{:S(2)}, u32[]{:S(2)}) collective-permute-start(bf16[256,1024]{1,0:T(8,128)(2,1)S(1)} %collective-permute-done.12.refs_2_), channel_id=1, source_target_pairs={{0,1},{2,3},{4,5},{6,7},{8,9},{10,11},{12,13},{14,15},{16,17},{18,... | collective-permute-start | bytes 1572872 | tf_op jit(solution)/shard_map/ppermute | solution.py:320
  65.8 17.2 %collective-permute-start.7 = (bf16[256,1024]{1,0:T(8,128)(2,1)S(1)}, bf16[256,1024]{1,0:T(8,128)(2,1)}, u32[]{:S(2)}, u32[]{:S(2)}) collective-permute-start(bf16[256,1024]{1,0:T(8,128)(2,1)S(1)} %pick.16.refs_0_), channel_id=1, source_target_pairs={{0,1},{2,3},{4,5},{6,7},{8,9},{10,11},{12,13},{14,15},{16,17},{18,... | collective-permute-start | bytes 1572872 | tf_op jit(solution)/shard_map/ppermute | solution.py:320
  70.2 12.8 %collective-permute-start.9 = (bf16[256,1024]{1,0:T(8,128)(2,1)S(1)}, bf16[256,1024]{1,0:T(8,128)(2,1)}, u32[]{:S(2)}, u32[]{:S(2)}) collective-permute-start(bf16[256,1024]{1,0:T(8,128)(2,1)S(1)} %collective-permute-done.8.refs_2_), channel_id=1, source_target_pairs={{0,1},{2,3},{4,5},{6,7},{8,9},{10,11},{12,13},{14,15},{16,17},{18,... | collective-permute-start | bytes 1572872 | tf_op jit(solution)/shard_map/ppermute | solution.py:320
  83.7 33.7 %copy-start.6 = (bf16[256,1024]{1,0:T(8,128)(2,1)}, bf16[256,1024]{1,0:T(8,128)(2,1)S(1)}, u32[]{:S(2)}) copy-start(bf16[256,1024]{1,0:T(8,128)(2,1)S(1)} %get-tuple-element.55.low_ref.refs_2_) | copy-start | bytes 1572868
  83.7 33.7 %copy-start.8 = (bf16[256,1024]{1,0:T(8,128)(2,1)}, bf16[256,1024]{1,0:T(8,128)(2,1)S(1)}, u32[]{:S(2)}) copy-start(bf16[256,1024]{1,0:T(8,128)(2,1)S(1)} %get-tuple-element.56.high_ref.refs_3_) | copy-start | bytes 1572868
  88.3 3.2 %collective-permute-start.16 = (f32[264,1024]{1,0:T(8,128)S(1)}, f32[264,1024]{1,0:T(8,128)S(1)}, u32[]{:S(2)}, u32[]{:S(2)}) collective-permute-start(f32[264,1024]{1,0:T(8,128)S(1)} %row_part.7), channel_id=1, source_target_pairs={{0,1},{1,0},{2,3},{3,2},{4,5},{5,4},{6,7},{7,6},{8,9},{9,8},{10,11... | collective-permute-start | bytes 3244040 | tf_op jit(solution)/shard_map/ppermute | solution.py:320
  89.6 6.1 %collective-permute-start.14 = (f32[264,1024]{1,0:T(8,128)S(1)}, f32[264,1024]{1,0:T(8,128)S(1)}, u32[]{:S(2)}, u32[]{:S(2)}) collective-permute-start(f32[264,1024]{1,0:T(8,128)S(1)} %row_part.5), channel_id=1, source_target_pairs={{0,1},{1,0},{2,3},{3,2},{4,5},{5,4},{6,7},{7,6},{8,9},{9,8},{10,11... | collective-permute-start | bytes 3244040 | tf_op jit(solution)/shard_map/ppermute | solution.py:320
  92.5 9.7 %collective-permute-start.18 = (s32[272,256]{1,0:T(8,128)}, s32[272,256]{1,0:T(8,128)S(1)}, u32[]{:S(2)}, u32[]{:S(2)}) collective-permute-start(s32[272,256]{1,0:T(8,128)} %get-tuple-element.71.refs_5_), channel_id=1, source_target_pairs={{0,2},{2,0},{1,3},{3,1},{4,6},{6,4},{5,7},{7,5},{8,10},{10,8},{9,1... | collective-permute-start | bytes 835592 | tf_op jit(solution)/shard_map/ppermute | solution.py:320
  96.1 11.4 %collective-permute-start.15 = (s32[272,256]{1,0:T(8,128)S(1)}, s32[272,256]{1,0:T(8,128)S(1)}, u32[]{:S(2)}, u32[]{:S(2)}) collective-permute-start(s32[272,256]{1,0:T(8,128)S(1)} %get-tuple-element.70.refs_4_), channel_id=1, source_target_pairs={{0,2},{2,0},{1,3},{3,1},{4,6},{6,4},{5,7},{7,5},{8,10},{10,8},{9,1... | collective-permute-start | bytes 835592 | tf_op jit(solution)/shard_map/ppermute | solution.py:320
  102.5 12.6 %collective-permute-start.20 = (s32[272,256]{1,0:T(8,128)S(1)}, s32[272,256]{1,0:T(8,128)S(1)}, u32[]{:S(2)}, u32[]{:S(2)}) collective-permute-start(s32[272,256]{1,0:T(8,128)S(1)} %get-tuple-element.78.refs_5_), channel_id=1, source_target_pairs={{0,4},{1,5},{2,6},{3,7},{12,8},{13,9},{14,10},{15,11},{16,20},{17,... | collective-permute-start | bytes 835592 | tf_op jit(solution)/shard_map/ppermute | solution.py:320
  107.8 8.5 %collective-permute-start.17 = (s32[272,256]{1,0:T(8,128)S(1)}, s32[272,256]{1,0:T(8,128)S(1)}, u32[]{:S(2)}, u32[]{:S(2)}) collective-permute-start(s32[272,256]{1,0:T(8,128)S(1)} %get-tuple-element.75.refs_4_), channel_id=1, source_target_pairs={{0,4},{1,5},{2,6},{3,7},{12,8},{13,9},{14,10},{15,11},{16,20},{17,... | collective-permute-start | bytes 835592 | tf_op jit(solution)/shard_map/ppermute | solution.py:320
  115.5 6.4 %collective-permute-start.25 = (s32[272,256]{1,0:T(8,128)S(1)}, s32[272,256]{1,0:T(8,128)S(1)}, u32[]{:S(2)}, u32[]{:S(2)}) collective-permute-start(s32[272,256]{1,0:T(8,128)S(1)} %merge.11.refs_5_), channel_id=1, source_target_pairs={{4,8},{5,9},{6,10},{7,11},{8,4},{9,5},{10,6},{11,7},{20,24},{21,25... | collective-permute-start | bytes 835592 | tf_op jit(solution)/shard_map/ppermute | solution.py:320
  116.7 6.8 %collective-permute-start.19 = (s32[272,256]{1,0:T(8,128)S(1)}, s32[272,256]{1,0:T(8,128)S(1)}, u32[]{:S(2)}, u32[]{:S(2)}) collective-permute-start(s32[272,256]{1,0:T(8,128)S(1)} %merge.10.refs_4_), channel_id=1, source_target_pairs={{4,8},{5,9},{6,10},{7,11},{8,4},{9,5},{10,6},{11,7},{20,24},{21,25... | collective-permute-start | bytes 835592 | tf_op jit(solution)/shard_map/ppermute | solution.py:320
  122.1 13.5 %collective-permute-start.26 = (s32[272,256]{1,0:T(8,128)S(1)}, s32[272,256]{1,0:T(8,128)S(1)}, u32[]{:S(2)}, u32[]{:S(2)}) collective-permute-start(s32[272,256]{1,0:T(8,128)S(1)} %merge.14), channel_id=1, source_target_pairs={{8,12},{9,13},{10,14},{11,15},{4,0},{5,1},{6,2},{7,3},{24,28},{25,... | collective-permute-start | bytes 835592 | tf_op jit(solution)/shard_map/ppermute | solution.py:320
  123.8 17.0 %collective-permute-start.21 = (s32[272,256]{1,0:T(8,128)S(1)}, s32[272,256]{1,0:T(8,128)S(1)}, u32[]{:S(2)}, u32[]{:S(2)}) collective-permute-start(s32[272,256]{1,0:T(8,128)S(1)} %merge.12), channel_id=1, source_target_pairs={{8,12},{9,13},{10,14},{11,15},{4,0},{5,1},{6,2},{7,3},{24,28},{25,... | collective-permute-start | bytes 835592 | tf_op jit(solution)/shard_map/ppermute | solution.py:320
  136.9 9.0 %collective-permute-start.29 = (s32[272,256]{1,0:T(8,128)}, s32[272,256]{1,0:T(8,128)S(1)}, u32[]{:S(2)}, u32[]{:S(2)}) collective-permute-start(s32[272,256]{1,0:T(8,128)} %get-tuple-element.89.refs_5_), channel_id=1, source_target_pairs={{3,0},{7,4},{11,8},{15,12},{19,16},{23,20},{27,24},{31,28}} | collective-permute-start | bytes 835592 | tf_op jit(solution)/shard_map/ppermute | solution.py:320
  138.2 17.0 %collective-permute-start.28 = (s32[272,256]{1,0:T(8,128)}, s32[272,256]{1,0:T(8,128)}, u32[]{:S(2)}, u32[]{:S(2)}) collective-permute-start(s32[272,256]{1,0:T(8,128)} %get-tuple-element.89.refs_5_), channel_id=1, source_target_pairs={{1,0},{5,4},{9,8},{13,12},{17,16},{21,20},{25,24},{29,28}} | collective-permute-start | bytes 835592 | tf_op jit(solution)/shard_map/ppermute | solution.py:320
  139.5 15.7 %collective-permute-start.27 = (s32[272,256]{1,0:T(8,128)}, s32[272,256]{1,0:T(8,128)}, u32[]{:S(2)}, u32[]{:S(2)}) collective-permute-start(s32[272,256]{1,0:T(8,128)} %get-tuple-element.89.refs_5_), channel_id=1, source_target_pairs={{2,0},{6,4},{10,8},{14,12},{18,16},{22,20},{26,24},{30,28}} | collective-permute-start | bytes 835592 | tf_op jit(solution)/shard_map/ppermute | solution.py:320
  143.3 11.9 %collective-permute-start.24 = (s32[272,256]{1,0:T(8,128)}, s32[272,256]{1,0:T(8,128)}, u32[]{:S(2)}, u32[]{:S(2)}) collective-permute-start(s32[272,256]{1,0:T(8,128)} %get-tuple-element.87.refs_4_), channel_id=1, source_target_pairs={{3,0},{7,4},{11,8},{15,12},{19,16},{23,20},{27,24},{31,28}} | collective-permute-start | bytes 835592 | tf_op jit(solution)/shard_map/ppermute | solution.py:320
  144.5 10.6 %collective-permute-start.23 = (s32[272,256]{1,0:T(8,128)}, s32[272,256]{1,0:T(8,128)}, u32[]{:S(2)}, u32[]{:S(2)}) collective-permute-start(s32[272,256]{1,0:T(8,128)} %get-tuple-element.87.refs_4_), channel_id=1, source_target_pairs={{1,0},{5,4},{9,8},{13,12},{17,16},{21,20},{25,24},{29,28}} | collective-permute-start | bytes 835592 | tf_op jit(solution)/shard_map/ppermute | solution.py:320
  145.9 9.6 %collective-permute-start.22 = (s32[272,256]{1,0:T(8,128)}, s32[272,256]{1,0:T(8,128)}, u32[]{:S(2)}, u32[]{:S(2)}) collective-permute-start(s32[272,256]{1,0:T(8,128)} %get-tuple-element.87.refs_4_), channel_id=1, source_target_pairs={{2,0},{6,4},{10,8},{14,12},{18,16},{22,20},{26,24},{30,28}} | collective-permute-start | bytes 835592 | tf_op jit(solution)/shard_map/ppermute | solution.py:320
  (20 other events, 102.6 us)

commit v10 on v8

--- a/solution.py
+++ b/solution.py
@@ -397,7 +397,7 @@
                 pltpu.VMEM((2, BLOCK, width), jnp.bfloat16),
                 pltpu.SemaphoreType.DMA((2,)),
             ],
-            compiler_params=params((46, 44, 40, 36)[part]),
+            compiler_params=params((37, 33, 29, 25)[part]),
             cost_estimate=cost(4 * rows * width, 4 * rows * width),
             name="units",
         )(decoder, tie)

time: 156 us -> 172 us (1.10)
  local copies, waits for them, and re-layouts: 10.7 us -> 29.6 us
  Pallas kernels: 66 us -> 62.9 us
    unnamed x40 -> x66, local copies, waits for them, and re-layouts: 10.6 us -> 29.5 us
    pallas_call x4, Pallas kernels: 13.5 us -> 9.37 us  [make_units(): pl.pallas_call(functools.partial(units_kernel, low, high - low), in_specs...]
  transfers between devices with their start and end apart: 30 -> 30, of which waited for: 8 -> 8; matrix products, arithmetic and copies ran while one was open for 0% -> 0% of each run, Pallas kernels for 34% -> 28%
where the time goes in v10:
time: 172 us; the launch traced here: 171 us
  Pallas kernels  62.9 us (37%)
  starting transfers between devices  51 us (30%)
  local copies, waits for them, and re-layouts  29.6 us (17%)
  waiting for transfers between devices  24.7 us (14%)
  between operations  2.4 us (1%)
    ppermute x30, starting transfers between devices, send(): return lax.ppermute(value, 'row', pairs)  51 us
    unnamed x66, local copies, waits for them, and re-layouts  29.5 us
    ppermute x30, waiting for transfers between devices, send(): return lax.ppermute(value, 'row', pairs)  24.7 us
    pallas_call x4, Pallas kernels, finish(): pl.pallas_call(finish_kernel, grid=(high - low,), in_specs=specs, out_spe...  21.9 us
    pallas_call x4, Pallas kernels, make_units(): pl.pallas_call(functools.partial(units_kernel, low, high - low), in_specs...  9.37 us
    pallas_call x10, Pallas kernels, pick(): pl.pallas_call(functools.partial(pick_kernel, slots, len(candidates)), in...  7.36 us
    pallas_call x1, Pallas kernels, on_device(): pl.pallas_call(functools.partial(last_kernel, DW / (ROWS * latents)), gri...  5.58 us
    pallas_call x4, Pallas kernels, row_part(): pl.pallas_call(functools.partial(row_kernel, k, parts), in_specs=[smem] +...  5.06 us
  transfers between devices with their start and end apart: 30, of which 8 were waited for; matrix products, arithmetic and copies ran while one was open for 0% of the time, Pallas kernels for 28%

profile of v10, /device:TPU:0, one launch (start us, length us, event | category | flops | bytes accessed | tf_op | source)
XLA Modules:
  0.0 170.7 jit_solution(16460371940304498001)
XLA Ops:
  1.5 2.6 %head_units.1 = (bf16[256,1024]{1,0:T(8,128)(2,1)S(1)}, bf16[256,1024]{1,0:T(8,128)(2,1)S(1)}, bf16[256,1024]{1,0:T(8,128)(2,1)S(1)}, bf16[256,1024]{1,0:T(8,128)(2,1)S(1)}) custom-call(s32[5]{0:T(128)S(1)} %stack.23.flags_ref, bf16[2048,4096]{1,0:T(8,128)(2,1)} %decoder_ref.19), custom_call_target="tpu_custom_call" | custom-call | flops 4194304 | bytes 4194304 | tf_op jit(solution)/shard_map/head_units/pallas_call | solution.py:346
  4.1 4.9 %collective-permute-start.3 = (bf16[256,1024]{1,0:T(8,128)(2,1)S(1)}, bf16[256,1024]{1,0:T(8,128)(2,1)S(1)}, u32[]{:S(2)}, u32[]{:S(2)}) collective-permute-start(bf16[256,1024]{1,0:T(8,128)(2,1)S(1)} %get-tuple-element.51), channel_id=1, source_target_pairs={{0,2},{4,6},{8,10},{12,14},{16,18},{20,22},{24,26},{28,30}} | collective-permute-start | bytes 1572872 | tf_op jit(solution)/shard_map/ppermute | solution.py:320
  10.3 3.3 %units.4 = (bf16[512,4096]{1,0:T(8,128)(2,1)S(1)}, f32[512,128]{1,0:T(8,128)S(1)}) custom-call(bf16[2048,4096]{1,0:T(8,128)(2,1)} %decoder_ref.19, bf16[256,1024]{1,0:T(8,128)(2,1)S(1)} %get-tuple-element.50.refs_0_), custom_call_target="tpu_custom_call" | custom-call | flops 8388608 | bytes 8388608 | tf_op jit(solution)/shard_map/units/pallas_call | solution.py:388
  13.6 2.0 %copy-done.3 = bf16[512,4096]{1,0:T(8,128)(2,1)} copy-done((bf16[512,4096]{1,0:T(8,128)(2,1)}, bf16[512,4096]{1,0:T(8,128)(2,1)S(1)}, u32[]{:S(2)}) %copy-start.3) | copy-done | bytes 4194328
  16.2 3.5 %collective-permute-start.4 = (bf16[256,1024]{1,0:T(8,128)(2,1)S(1)}, bf16[256,1024]{1,0:T(8,128)(2,1)S(1)}, u32[]{:S(2)}, u32[]{:S(2)}) collective-permute-start(bf16[256,1024]{1,0:T(8,128)(2,1)S(1)} %pick.12.refs_0_), channel_id=1, source_target_pairs={{0,4},{2,6},{12,8},{14,10},{16,20},{18,22},{28,24},{30,26}} | collective-permute-start | bytes 1572872 | tf_op jit(solution)/shard_map/ppermute | solution.py:320
  21.8 3.5 %collective-permute-start.1 = (bf16[256,1024]{1,0:T(8,128)(2,1)S(1)}, bf16[256,1024]{1,0:T(8,128)(2,1)S(1)}, u32[]{:S(2)}, u32[]{:S(2)}) collective-permute-start(bf16[256,1024]{1,0:T(8,128)(2,1)S(1)} %pick.10.refs_0_), channel_id=1, source_target_pairs={{0,4},{2,6},{12,8},{14,10},{16,20},{18,22},{28,24},{30,26}} | collective-permute-start | bytes 1572872 | tf_op jit(solution)/shard_map/ppermute | solution.py:320
  25.4 5.8 %copy-done = bf16[2048,4096]{1,0:T(8,128)(2,1)S(1)} copy-done((bf16[2048,4096]{1,0:T(8,128)(2,1)S(1)}, bf16[2048,4096]{1,0:T(8,128)(2,1)}, u32[]{:S(2)}) %copy-start) | copy-done | bytes 16777240
  31.1 2.0 %units.5 = (bf16[512,4096]{1,0:T(8,128)(2,1)S(1)}, f32[512,128]{1,0:T(8,128)S(1)}) custom-call(bf16[2048,4096]{1,0:T(8,128)(2,1)S(1)} %copy-done, bf16[256,1024]{1,0:T(8,128)(2,1)S(1)} %pick.10.refs_0_), custom_call_target="tpu_custom_call" | custom-call | flops 8388608 | bytes 8388608 | tf_op jit(solution)/shard_map/units/pallas_call | solution.py:388
  37.8 5.8 %copy-done.1 = bf16[2048,4096]{1,0:T(8,128)(2,1)S(1)} copy-done((bf16[2048,4096]{1,0:T(8,128)(2,1)S(1)}, bf16[2048,4096]{1,0:T(8,128)(2,1)}, u32[]{:S(2)}) %copy-start.1) | copy-done | bytes 16777240
  43.5 2.0 %units.6 = (bf16[512,4096]{1,0:T(8,128)(2,1)S(1)}, f32[512,128]{1,0:T(8,128)S(1)}) custom-call(bf16[2048,4096]{1,0:T(8,128)(2,1)S(1)} %copy-done.1, bf16[256,1024]{1,0:T(8,128)(2,1)S(1)} %pick.14.refs_0_), custom_call_target="tpu_custom_call" | custom-call | flops 8388608 | bytes 8388608 | tf_op jit(solution)/shard_map/units/pallas_call | solution.py:388
  45.6 2.0 %copy-done.7 = bf16[512,4096]{1,0:T(8,128)(2,1)} copy-done((bf16[512,4096]{1,0:T(8,128)(2,1)}, bf16[512,4096]{1,0:T(8,128)(2,1)S(1)}, u32[]{:S(2)}) %copy-start.7) | copy-done | bytes 4194328
  49.5 3.8 %collective-permute-done.10.refs_3_ = bf16[256,1024]{1,0:T(8,128)(2,1)S(1)} collective-permute-done((bf16[256,1024]{1,0:T(8,128)(2,1)S(1)}, bf16[256,1024]{1,0:T(8,128)(2,1)S(1)}, u32[]{:S(2)}, u32[]{:S(2)}) %collective-permute-start.10) | collective-permute-done | bytes 524320 | tf_op jit(solution)/shard_map/ppermute | solution.py:320
  53.9 4.4 %collective-permute-start.12 = (bf16[256,1024]{1,0:T(8,128)(2,1)S(1)}, bf16[256,1024]{1,0:T(8,128)(2,1)S(1)}, u32[]{:S(2)}, u32[]{:S(2)}) collective-permute-start(bf16[256,1024]{1,0:T(8,128)(2,1)S(1)} %pick.18.refs_0_), channel_id=1, source_target_pairs={{0,2},{2,0},{4,6},{6,4},{8,10},{10,8},{12,14},{14,12},{16,18},{18,... | collective-permute-start | bytes 1572872 | tf_op jit(solution)/shard_map/ppermute | solution.py:320
  58.3 6.7 %collective-permute-done.6.refs_3_ = bf16[256,1024]{1,0:T(8,128)(2,1)S(1)} collective-permute-done((bf16[256,1024]{1,0:T(8,128)(2,1)S(1)}, bf16[256,1024]{1,0:T(8,128)(2,1)S(1)}, u32[]{:S(2)}, u32[]{:S(2)}) %collective-permute-start.6) | collective-permute-done | bytes 524320 | tf_op jit(solution)/shard_map/ppermute | solution.py:320
  65.7 4.4 %collective-permute-start.8 = (bf16[256,1024]{1,0:T(8,128)(2,1)S(1)}, bf16[256,1024]{1,0:T(8,128)(2,1)}, u32[]{:S(2)}, u32[]{:S(2)}) collective-permute-start(bf16[256,1024]{1,0:T(8,128)(2,1)S(1)} %pick.16.refs_0_), channel_id=1, source_target_pairs={{0,2},{2,0},{4,6},{6,4},{8,10},{10,8},{12,14},{14,12},{16,18},{18,... | collective-permute-start | bytes 1572872 | tf_op jit(solution)/shard_map/ppermute | solution.py:320
  71.4 2.1 %collective-permute-start.13 = (bf16[256,1024]{1,0:T(8,128)(2,1)S(1)}, bf16[256,1024]{1,0:T(8,128)(2,1)}, u32[]{:S(2)}, u32[]{:S(2)}) collective-permute-start(bf16[256,1024]{1,0:T(8,128)(2,1)S(1)} %collective-permute-done.12.refs_2_), channel_id=1, source_target_pairs={{0,1},{2,3},{4,5},{6,7},{8,9},{10,11},{12,13},{14,15},{16,17},{18,... | collective-permute-start | bytes 1572872 | tf_op jit(solution)/shard_map/ppermute | solution.py:320
  73.5 2.1 %collective-permute-start.7 = (bf16[256,1024]{1,0:T(8,128)(2,1)S(1)}, bf16[256,1024]{1,0:T(8,128)(2,1)}, u32[]{:S(2)}, u32[]{:S(2)}) collective-permute-start(bf16[256,1024]{1,0:T(8,128)(2,1)S(1)} %pick.16.refs_0_), channel_id=1, source_target_pairs={{0,1},{2,3},{4,5},{6,7},{8,9},{10,11},{12,13},{14,15},{16,17},{18,... | collective-permute-start | bytes 1572872 | tf_op jit(solution)/shard_map/ppermute | solution.py:320
  75.6 1.7 collective-permute-done.8.refs_2_
  77.3 2.1 %collective-permute-start.9 = (bf16[256,1024]{1,0:T(8,128)(2,1)}, bf16[256,1024]{1,0:T(8,128)(2,1)}, u32[]{:S(2)}, u32[]{:S(2)}) collective-permute-start(bf16[256,1024]{1,0:T(8,128)(2,1)} %collective-permute-done.8.refs_2_), channel_id=1, source_target_pairs={{0,1},{2,3},{4,5},{6,7},{8,9},{10,11},{12,13},{14,15},{16,17},{18,... | collective-permute-start | bytes 1572872 | tf_op jit(solution)/shard_map/ppermute | solution.py:320
  79.4 5.8 %copy-done.2 = bf16[2048,4096]{1,0:T(8,128)(2,1)S(1)} copy-done((bf16[2048,4096]{1,0:T(8,128)(2,1)S(1)}, bf16[2048,4096]{1,0:T(8,128)(2,1)}, u32[]{:S(2)}) %copy-start.2) | copy-done | bytes 16777240
  85.2 2.0 %units.7 = (bf16[512,4096]{1,0:T(8,128)(2,1)S(1)}, f32[512,128]{1,0:T(8,128)S(1)}) custom-call(bf16[2048,4096]{1,0:T(8,128)(2,1)S(1)} %copy-done.2, bf16[256,1024]{1,0:T(8,128)(2,1)S(1)} %pick.16.refs_0_), custom_call_target="tpu_custom_call" | custom-call | flops 8388608 | bytes 8388608 | tf_op jit(solution)/shard_map/units/pallas_call | solution.py:388
  88.0 1.8 %copy-done.28 = bf16[256,1024]{1,0:T(8,128)(2,1)S(1)} copy-done((bf16[256,1024]{1,0:T(8,128)(2,1)S(1)}, bf16[256,1024]{1,0:T(8,128)(2,1)}, u32[]{:S(2)}) %copy-start.28) | copy-done | bytes 524312
  91.8 2.4 %part_cosines.1.partial_ref = f32[2048,256]{1,0:T(8,128)S(1)} custom-call(bf16[256,1024]{1,0:T(8,128)(2,1)S(1)} %get-tuple-element.58.low_ref.refs_0_, bf16[256,1024]{1,0:T(8,128)(2,1)S(1)} %get-tuple-element.59.high_ref.refs_1_, bf16[512,4096]{1,0:T(8,128)(2,1)S(1)} %copy-done.4, bf16[512,4096]{1,0:T(8,128)(2,1)S(1)} %copy-done.6, ...), custom_call_target="tpu_custom_call" | custom-call | flops 2147483648 | bytes 8388608 | tf_op jit(solution)/shard_map/part_cosines/pallas_call | solution.py:443
  95.9 3.3 %weights.1 = (bf16[2048,256]{1,0:T(8,128)(2,1)S(1)}, bf16[256,2048]{1,0:T(8,128)(2,1)S(1)}, f32[2048,128]{1,0:T(8,128)S(1)}, f32[8,128]{1,0:T(8,128)S(1)}) custom-call(s32[1]{0:T(128)} %bitcast.2.delta_ref, bf16[256,1024]{1,0:T(8,128)(2,1)S(1)} %get-tuple-element.55.low_ref.refs_2_, bf16[256,1024]{1,0:T(8,128)(2,1)S(1)} %get-tuple-element.56.high_ref.refs_3_, ...), custom_call_target="tpu_custom_call" | custom-call | flops 2147483648 | bytes 8388608 | tf_op jit(solution)/shard_map/weights/pallas_call | solution.py:452
  104.1 2.0 %collective-permute-start.18 = (s32[272,256]{1,0:T(8,128)S(1)}, s32[272,256]{1,0:T(8,128)S(1)}, u32[]{:S(2)}, u32[]{:S(2)}) collective-permute-start(s32[272,256]{1,0:T(8,128)S(1)} %get-tuple-element.71.refs_4_), channel_id=1, source_target_pairs={{0,2},{2,0},{1,3},{3,1},{4,6},{6,4},{5,7},{7,5},{8,10},{10,8},{9,1... | collective-permute-start | bytes 835592 | tf_op jit(solution)/shard_map/ppermute | solution.py:320
  107.8 5.8 %collective-permute-done.18.refs_0_ = s32[272,256]{1,0:T(8,128)S(1)} collective-permute-done((s32[272,256]{1,0:T(8,128)S(1)}, s32[272,256]{1,0:T(8,128)S(1)}, u32[]{:S(2)}, u32[]{:S(2)}) %collective-permute-start.18) | collective-permute-done | bytes 278560 | tf_op jit(solution)/shard_map/ppermute | solution.py:320
  118.4 5.8 %finish.4 = (f32[2048,4096]{1,0:T(8,128)}, f32[8,128]{1,0:T(8,128)S(1)}) custom-call(bf16[2048,256]{1,0:T(8,128)(2,1)S(1)} %get-tuple-element.64.col_ref, bf16[2048,4096]{1,0:T(8,128)(2,1)} %decoder_ref.19, f32[2048,128]{1,0:T(8,128)} %copy-done.10, bf16[256,1024]{1,0:T(8,128)(2,1)S(1)} %get-tuple-element.58.low_ref.refs_0_, ...), custom_call_target="tpu_custom_call" | custom-call | flops 1073741824 | bytes 12582912 | tf_op jit(solution)/shard_map/finish/pallas_call | solution.py:543
  127.1 5.8 %finish.5 = (f32[2048,4096]{1,0:T(8,128)}, f32[8,128]{1,0:T(8,128)S(1)}) custom-call(bf16[2048,256]{1,0:T(8,128)(2,1)S(1)} %get-tuple-element.64.col_ref, bf16[2048,4096]{1,0:T(8,128)(2,1)} %decoder_ref.19, f32[2048,128]{1,0:T(8,128)} %copy-done.10, bf16[256,1024]{1,0:T(8,128)(2,1)S(1)} %get-tuple-element.58.low_ref.refs_0_, ...), custom_call_target="tpu_custom_call", output_to_operand_aliasing={{0}: (8, {})} | custom-call | flops 1073741824 | bytes 12582912 | tf_op jit(solution)/shard_map/finish/pallas_call | solution.py:543
  135.5 4.5 %finish.6 = (f32[2048,4096]{1,0:T(8,128)}, f32[8,128]{1,0:T(8,128)S(1)}) custom-call(bf16[2048,256]{1,0:T(8,128)(2,1)S(1)} %get-tuple-element.64.col_ref, bf16[2048,4096]{1,0:T(8,128)(2,1)} %decoder_ref.19, f32[2048,128]{1,0:T(8,128)} %copy-done.10, bf16[256,1024]{1,0:T(8,128)(2,1)S(1)} %get-tuple-element.58.low_ref.refs_0_, ...), custom_call_target="tpu_custom_call", output_to_operand_aliasing={{0}: (8, {})} | custom-call | flops 536870912 | bytes 6291456 | tf_op jit(solution)/shard_map/finish/pallas_call | solution.py:543
  141.6 2.7 %collective-permute-done.26.refs_2_ = s32[272,256]{1,0:T(8,128)S(1)} collective-permute-done((s32[272,256]{1,0:T(8,128)S(1)}, s32[272,256]{1,0:T(8,128)S(1)}, u32[]{:S(2)}, u32[]{:S(2)}) %collective-permute-start.26) | collective-permute-done | bytes 278560 | tf_op jit(solution)/shard_map/ppermute | solution.py:320
  157.6 5.8 %finish.7 = (f32[2048,4096]{1,0:T(8,128)}, f32[8,128]{1,0:T(8,128)}) custom-call(bf16[2048,256]{1,0:T(8,128)(2,1)S(1)} %get-tuple-element.64.col_ref, bf16[2048,4096]{1,0:T(8,128)(2,1)} %decoder_ref.19, f32[2048,128]{1,0:T(8,128)} %copy-done.10, bf16[256,1024]{1,0:T(8,128)(2,1)S(1)} %get-tuple-element.58.low_ref.refs_0_, ...), custom_call_target="tpu_custom_call", output_to_operand_aliasing={{0}: (8, {})} | custom-call | flops 1073741824 | bytes 12582912 | tf_op jit(solution)/shard_map/finish/pallas_call | solution.py:543
  165.0 5.6 %finish_rows.1 = (f32[2048,4096]{1,0:T(8,128)}, f32[1]{0:T(128)}) custom-call(s32[1]{0:T(128)} %bitcast.1.owner_ref, bf16[2048,256]{1,0:T(8,128)(2,1)} %copy-done.9, bf16[2048,4096]{1,0:T(8,128)(2,1)} %decoder_ref.19, f32[2048,128]{1,0:T(8,128)} %copy-done.10, f32[8,128]{1,0:T(8,128)S(1)} %get-tuple-element.85.tile_ref, ...), custom_call_target="tpu_custom_call", output_to_operand_aliasing={{0}: (23, {})} | custom-call | tf_op jit(solution)/shard_map/finish_rows/pallas_call | solution.py:611
  (131 shorter events, 50.4 us)
Async XLA Ops:
  4.1 11.6 %collective-permute-start.3 = (bf16[256,1024]{1,0:T(8,128)(2,1)S(1)}, bf16[256,1024]{1,0:T(8,128)(2,1)S(1)}, u32[]{:S(2)}, u32[]{:S(2)}) collective-permute-start(bf16[256,1024]{1,0:T(8,128)(2,1)S(1)} %get-tuple-element.51), channel_id=1, source_target_pairs={{0,2},{4,6},{8,10},{12,14},{16,18},{20,22},{24,26},{28,30}} | collective-permute-start | bytes 1572872 | tf_op jit(solution)/shard_map/ppermute | solution.py:320
  9.0 12.3 %collective-permute-start = (bf16[256,1024]{1,0:T(8,128)(2,1)S(1)}, bf16[256,1024]{1,0:T(8,128)(2,1)S(1)}, u32[]{:S(2)}, u32[]{:S(2)}) collective-permute-start(bf16[256,1024]{1,0:T(8,128)(2,1)S(1)} %get-tuple-element.49), channel_id=1, source_target_pairs={{0,2},{4,6},{8,10},{12,14},{16,18},{20,22},{24,26},{28,30}} | collective-permute-start | bytes 1572872 | tf_op jit(solution)/shard_map/ppermute | solution.py:320
  16.2 16.9 %collective-permute-start.4 = (bf16[256,1024]{1,0:T(8,128)(2,1)S(1)}, bf16[256,1024]{1,0:T(8,128)(2,1)S(1)}, u32[]{:S(2)}, u32[]{:S(2)}) collective-permute-start(bf16[256,1024]{1,0:T(8,128)(2,1)S(1)} %pick.12.refs_0_), channel_id=1, source_target_pairs={{0,4},{2,6},{12,8},{14,10},{16,20},{18,22},{28,24},{30,26}} | collective-permute-start | bytes 1572872 | tf_op jit(solution)/shard_map/ppermute | solution.py:320
  21.8 12.7 %collective-permute-start.1 = (bf16[256,1024]{1,0:T(8,128)(2,1)S(1)}, bf16[256,1024]{1,0:T(8,128)(2,1)S(1)}, u32[]{:S(2)}, u32[]{:S(2)}) collective-permute-start(bf16[256,1024]{1,0:T(8,128)(2,1)S(1)} %pick.10.refs_0_), channel_id=1, source_target_pairs={{0,4},{2,6},{12,8},{14,10},{16,20},{18,22},{28,24},{30,26}} | collective-permute-start | bytes 1572872 | tf_op jit(solution)/shard_map/ppermute | solution.py:320
  33.8 2.0 %collective-permute-start.5 = (bf16[256,1024]{1,0:T(8,128)(2,1)S(1)}, bf16[256,1024]{1,0:T(8,128)(2,1)S(1)}, u32[]{:S(2)}, u32[]{:S(2)}) collective-permute-start(bf16[256,1024]{1,0:T(8,128)(2,1)S(1)} %pick.13), channel_id=1, source_target_pairs={{4,8},{6,10},{8,4},{10,6},{20,24},{22,26},{24,20},{26,22}} | collective-permute-start | bytes 1572872 | tf_op jit(solution)/shard_map/ppermute | solution.py:320
  35.1 12.5 %collective-permute-start.2 = (bf16[256,1024]{1,0:T(8,128)(2,1)S(1)}, bf16[256,1024]{1,0:T(8,128)(2,1)S(1)}, u32[]{:S(2)}, u32[]{:S(2)}) collective-permute-start(bf16[256,1024]{1,0:T(8,128)(2,1)S(1)} %pick.11), channel_id=1, source_target_pairs={{4,8},{6,10},{8,4},{10,6},{20,24},{22,26},{24,20},{26,22}} | collective-permute-start | bytes 1572872 | tf_op jit(solution)/shard_map/ppermute | solution.py:320
  36.5 16.8 %collective-permute-start.10 = (bf16[256,1024]{1,0:T(8,128)(2,1)S(1)}, bf16[256,1024]{1,0:T(8,128)(2,1)S(1)}, u32[]{:S(2)}, u32[]{:S(2)}) collective-permute-start(bf16[256,1024]{1,0:T(8,128)(2,1)S(1)} %pick.14.refs_0_), channel_id=1, source_target_pairs={{8,12},{10,14},{4,0},{6,2},{24,28},{26,30},{20,16},{22,18}} | collective-permute-start | bytes 1572872 | tf_op jit(solution)/shard_map/ppermute | solution.py:320
  47.6 29.8 %copy-start.23 = (f32[512,128]{1,0:T(8,128)}, f32[512,128]{1,0:T(8,128)S(1)}, u32[]{:S(2)}) copy-start(f32[512,128]{1,0:T(8,128)S(1)} %get-tuple-element.54.refs_2_.refs_6_) | copy-start | bytes 786436
  48.2 16.9 %collective-permute-start.6 = (bf16[256,1024]{1,0:T(8,128)(2,1)S(1)}, bf16[256,1024]{1,0:T(8,128)(2,1)S(1)}, u32[]{:S(2)}, u32[]{:S(2)}) collective-permute-start(bf16[256,1024]{1,0:T(8,128)(2,1)S(1)} %pick.15), channel_id=1, source_target_pairs={{8,12},{10,14},{4,0},{6,2},{24,28},{26,30},{20,16},{22,18}} | collective-permute-start | bytes 1572872 | tf_op jit(solution)/shard_map/ppermute | solution.py:320
  53.9 17.5 %collective-permute-start.12 = (bf16[256,1024]{1,0:T(8,128)(2,1)S(1)}, bf16[256,1024]{1,0:T(8,128)(2,1)S(1)}, u32[]{:S(2)}, u32[]{:S(2)}) collective-permute-start(bf16[256,1024]{1,0:T(8,128)(2,1)S(1)} %pick.18.refs_0_), channel_id=1, source_target_pairs={{0,2},{2,0},{4,6},{6,4},{8,10},{10,8},{12,14},{14,12},{16,18},{18,... | collective-permute-start | bytes 1572872 | tf_op jit(solution)/shard_map/ppermute | solution.py:320
  65.7 11.6 %collective-permute-start.8 = (bf16[256,1024]{1,0:T(8,128)(2,1)S(1)}, bf16[256,1024]{1,0:T(8,128)(2,1)}, u32[]{:S(2)}, u32[]{:S(2)}) collective-permute-start(bf16[256,1024]{1,0:T(8,128)(2,1)S(1)} %pick.16.refs_0_), channel_id=1, source_target_pairs={{0,2},{2,0},{4,6},{6,4},{8,10},{10,8},{12,14},{14,12},{16,18},{18,... | collective-permute-start | bytes 1572872 | tf_op jit(solution)/shard_map/ppermute | solution.py:320
  70.1 17.2 %collective-permute-start.11 = (bf16[256,1024]{1,0:T(8,128)(2,1)S(1)}, bf16[256,1024]{1,0:T(8,128)(2,1)S(1)}, u32[]{:S(2)}, u32[]{:S(2)}) collective-permute-start(bf16[256,1024]{1,0:T(8,128)(2,1)S(1)} %pick.18.refs_0_), channel_id=1, source_target_pairs={{0,1},{2,3},{4,5},{6,7},{8,9},{10,11},{12,13},{14,15},{16,17},{18,... | collective-permute-start | bytes 1572872 | tf_op jit(solution)/shard_map/ppermute | solution.py:320
  71.4 16.6 %collective-permute-start.13 = (bf16[256,1024]{1,0:T(8,128)(2,1)S(1)}, bf16[256,1024]{1,0:T(8,128)(2,1)}, u32[]{:S(2)}, u32[]{:S(2)}) collective-permute-start(bf16[256,1024]{1,0:T(8,128)(2,1)S(1)} %collective-permute-done.12.refs_2_), channel_id=1, source_target_pairs={{0,1},{2,3},{4,5},{6,7},{8,9},{10,11},{12,13},{14,15},{16,17},{18,... | collective-permute-start | bytes 1572872 | tf_op jit(solution)/shard_map/ppermute | solution.py:320
  73.5 20.6 %collective-permute-start.7 = (bf16[256,1024]{1,0:T(8,128)(2,1)S(1)}, bf16[256,1024]{1,0:T(8,128)(2,1)}, u32[]{:S(2)}, u32[]{:S(2)}) collective-permute-start(bf16[256,1024]{1,0:T(8,128)(2,1)S(1)} %pick.16.refs_0_), channel_id=1, source_target_pairs={{0,1},{2,3},{4,5},{6,7},{8,9},{10,11},{12,13},{14,15},{16,17},{18,... | collective-permute-start | bytes 1572872 | tf_op jit(solution)/shard_map/ppermute | solution.py:320
  77.3 16.8 %collective-permute-start.9 = (bf16[256,1024]{1,0:T(8,128)(2,1)}, bf16[256,1024]{1,0:T(8,128)(2,1)}, u32[]{:S(2)}, u32[]{:S(2)}) collective-permute-start(bf16[256,1024]{1,0:T(8,128)(2,1)} %collective-permute-done.8.refs_2_), channel_id=1, source_target_pairs={{0,1},{2,3},{4,5},{6,7},{8,9},{10,11},{12,13},{14,15},{16,17},{18,... | collective-permute-start | bytes 1572872 | tf_op jit(solution)/shard_map/ppermute | solution.py:320
  99.2 58.3 %copy-start.9 = (bf16[2048,256]{1,0:T(8,128)(2,1)}, bf16[2048,256]{1,0:T(8,128)(2,1)S(1)}, u32[]{:S(2)}) copy-start(bf16[2048,256]{1,0:T(8,128)(2,1)S(1)} %get-tuple-element.64.col_ref) | copy-start | bytes 3145732
  100.5 3.2 %collective-permute-start.16 = (f32[264,1024]{1,0:T(8,128)S(1)}, f32[264,1024]{1,0:T(8,128)S(1)}, u32[]{:S(2)}, u32[]{:S(2)}) collective-permute-start(f32[264,1024]{1,0:T(8,128)S(1)} %row_part.7), channel_id=1, source_target_pairs={{0,1},{1,0},{2,3},{3,2},{4,5},{5,4},{6,7},{7,6},{8,9},{9,8},{10,11... | collective-permute-start | bytes 3244040 | tf_op jit(solution)/shard_map/ppermute | solution.py:320
  101.8 5.5 %collective-permute-start.14 = (f32[264,1024]{1,0:T(8,128)S(1)}, f32[264,1024]{1,0:T(8,128)S(1)}, u32[]{:S(2)}, u32[]{:S(2)}) collective-permute-start(f32[264,1024]{1,0:T(8,128)S(1)} %row_part.5), channel_id=1, source_target_pairs={{0,1},{1,0},{2,3},{3,2},{4,5},{5,4},{6,7},{7,6},{8,9},{9,8},{10,11... | collective-permute-start | bytes 3244040 | tf_op jit(solution)/shard_map/ppermute | solution.py:320
  104.1 9.6 %collective-permute-start.18 = (s32[272,256]{1,0:T(8,128)S(1)}, s32[272,256]{1,0:T(8,128)S(1)}, u32[]{:S(2)}, u32[]{:S(2)}) collective-permute-start(s32[272,256]{1,0:T(8,128)S(1)} %get-tuple-element.71.refs_4_), channel_id=1, source_target_pairs={{0,2},{2,0},{1,3},{3,1},{4,6},{6,4},{5,7},{7,5},{8,10},{10,8},{9,1... | collective-permute-start | bytes 835592 | tf_op jit(solution)/shard_map/ppermute | solution.py:320
  107.7 16.5 %collective-permute-start.15 = (s32[272,256]{1,0:T(8,128)S(1)}, s32[272,256]{1,0:T(8,128)S(1)}, u32[]{:S(2)}, u32[]{:S(2)}) collective-permute-start(s32[272,256]{1,0:T(8,128)S(1)} %get-tuple-element.70), channel_id=1, source_target_pairs={{0,2},{2,0},{1,3},{3,1},{4,6},{6,4},{5,7},{7,5},{8,10},{10,8},{9,1... | collective-permute-start | bytes 835592 | tf_op jit(solution)/shard_map/ppermute | solution.py:320
  113.9 11.9 %collective-permute-start.20 = (s32[272,256]{1,0:T(8,128)S(1)}, s32[272,256]{1,0:T(8,128)S(1)}, u32[]{:S(2)}, u32[]{:S(2)}) collective-permute-start(s32[272,256]{1,0:T(8,128)S(1)} %get-tuple-element.78.refs_4_), channel_id=1, source_target_pairs={{0,4},{1,5},{2,6},{3,7},{12,8},{13,9},{14,10},{15,11},{16,20},{17,... | collective-permute-start | bytes 835592 | tf_op jit(solution)/shard_map/ppermute | solution.py:320
  124.5 8.3 %collective-permute-start.17 = (s32[272,256]{1,0:T(8,128)S(1)}, s32[272,256]{1,0:T(8,128)S(1)}, u32[]{:S(2)}, u32[]{:S(2)}) collective-permute-start(s32[272,256]{1,0:T(8,128)S(1)} %get-tuple-element.75), channel_id=1, source_target_pairs={{0,4},{1,5},{2,6},{3,7},{12,8},{13,9},{14,10},{15,11},{16,20},{17,... | collective-permute-start | bytes 835592 | tf_op jit(solution)/shard_map/ppermute | solution.py:320
  126.2 7.7 %collective-permute-start.25 = (s32[272,256]{1,0:T(8,128)S(1)}, s32[272,256]{1,0:T(8,128)S(1)}, u32[]{:S(2)}, u32[]{:S(2)}) collective-permute-start(s32[272,256]{1,0:T(8,128)S(1)} %merge.11.refs_4_), channel_id=1, source_target_pairs={{4,8},{5,9},{6,10},{7,11},{8,4},{9,5},{10,6},{11,7},{20,24},{21,25... | collective-permute-start | bytes 835592 | tf_op jit(solution)/shard_map/ppermute | solution.py:320
  133.2 6.8 %collective-permute-start.19 = (s32[272,256]{1,0:T(8,128)S(1)}, s32[272,256]{1,0:T(8,128)S(1)}, u32[]{:S(2)}, u32[]{:S(2)}) collective-permute-start(s32[272,256]{1,0:T(8,128)S(1)} %merge.10), channel_id=1, source_target_pairs={{4,8},{5,9},{6,10},{7,11},{8,4},{9,5},{10,6},{11,7},{20,24},{21,25... | collective-permute-start | bytes 835592 | tf_op jit(solution)/shard_map/ppermute | solution.py:320
  134.2 10.1 %collective-permute-start.26 = (s32[272,256]{1,0:T(8,128)S(1)}, s32[272,256]{1,0:T(8,128)S(1)}, u32[]{:S(2)}, u32[]{:S(2)}) collective-permute-start(s32[272,256]{1,0:T(8,128)S(1)} %merge.14), channel_id=1, source_target_pairs={{8,12},{9,13},{10,14},{11,15},{4,0},{5,1},{6,2},{7,3},{24,28},{25,... | collective-permute-start | bytes 835592 | tf_op jit(solution)/shard_map/ppermute | solution.py:320
  140.3 10.2 %collective-permute-start.21 = (s32[272,256]{1,0:T(8,128)S(1)}, s32[272,256]{1,0:T(8,128)S(1)}, u32[]{:S(2)}, u32[]{:S(2)}) collective-permute-start(s32[272,256]{1,0:T(8,128)S(1)} %merge.12), channel_id=1, source_target_pairs={{8,12},{9,13},{10,14},{11,15},{4,0},{5,1},{6,2},{7,3},{24,28},{25,... | collective-permute-start | bytes 835592 | tf_op jit(solution)/shard_map/ppermute | solution.py:320
  145.6 9.9 %collective-permute-start.29 = (s32[272,256]{1,0:T(8,128)}, s32[272,256]{1,0:T(8,128)S(1)}, u32[]{:S(2)}, u32[]{:S(2)}) collective-permute-start(s32[272,256]{1,0:T(8,128)} %get-tuple-element.89.refs_4_), channel_id=1, source_target_pairs={{3,0},{7,4},{11,8},{15,12},{19,16},{23,20},{27,24},{31,28}} | collective-permute-start | bytes 835592 | tf_op jit(solution)/shard_map/ppermute | solution.py:320
  146.9 16.5 %collective-permute-start.28 = (s32[272,256]{1,0:T(8,128)}, s32[272,256]{1,0:T(8,128)}, u32[]{:S(2)}, u32[]{:S(2)}) collective-permute-start(s32[272,256]{1,0:T(8,128)} %get-tuple-element.89.refs_4_), channel_id=1, source_target_pairs={{1,0},{5,4},{9,8},{13,12},{17,16},{21,20},{25,24},{29,28}} | collective-permute-start | bytes 835592 | tf_op jit(solution)/shard_map/ppermute | solution.py:320
  148.2 15.2 %collective-permute-start.27 = (s32[272,256]{1,0:T(8,128)}, s32[272,256]{1,0:T(8,128)}, u32[]{:S(2)}, u32[]{:S(2)}) collective-permute-start(s32[272,256]{1,0:T(8,128)} %get-tuple-element.89.refs_4_), channel_id=1, source_target_pairs={{2,0},{6,4},{10,8},{14,12},{18,16},{22,20},{26,24},{30,28}} | collective-permute-start | bytes 835592 | tf_op jit(solution)/shard_map/ppermute | solution.py:320
  152.9 10.5 %collective-permute-start.24 = (s32[272,256]{1,0:T(8,128)}, s32[272,256]{1,0:T(8,128)}, u32[]{:S(2)}, u32[]{:S(2)}) collective-permute-start(s32[272,256]{1,0:T(8,128)} %get-tuple-element.87), channel_id=1, source_target_pairs={{3,0},{7,4},{11,8},{15,12},{19,16},{23,20},{27,24},{31,28}} | collective-permute-start | bytes 835592 | tf_op jit(solution)/shard_map/ppermute | solution.py:320
  154.2 9.2 %collective-permute-start.23 = (s32[272,256]{1,0:T(8,128)}, s32[272,256]{1,0:T(8,128)}, u32[]{:S(2)}, u32[]{:S(2)}) collective-permute-start(s32[272,256]{1,0:T(8,128)} %get-tuple-element.87), channel_id=1, source_target_pairs={{1,0},{5,4},{9,8},{13,12},{17,16},{21,20},{25,24},{29,28}} | collective-permute-start | bytes 835592 | tf_op jit(solution)/shard_map/ppermute | solution.py:320
  156.2 8.7 %collective-permute-start.22 = (s32[272,256]{1,0:T(8,128)}, s32[272,256]{1,0:T(8,128)}, u32[]{:S(2)}, u32[]{:S(2)}) collective-permute-start(s32[272,256]{1,0:T(8,128)} %get-tuple-element.87), channel_id=1, source_target_pairs={{2,0},{6,4},{10,8},{14,12},{18,16},{22,20},{26,24},{30,28}} | collective-permute-start | bytes 835592 | tf_op jit(solution)/shard_map/ppermute | solution.py:320
  (31 other events, 171.9 us)

commit v11 on v10

--- a/solution.py
+++ b/solution.py
@@ -56,9 +56,18 @@
                 ref[rows, t : t + 128] = (v * inverse).astype(jnp.bfloat16)
 
 
-def units_kernel(low, count, decoder_ref, *refs):
-    units_ref, inverse_ref, held, sems = refs[-4:]
+def units_kernel(low, count, away, decoder_ref, *refs):
     strip = 64
+    if away:
+        _, target_ref, inverse_ref, held, sems, units_ref, out_sems = refs
+    else:
+        _, units_ref, inverse_ref, held, sems = refs
+
+    def leave(j):
+        rows = pl.ds(j * BLOCK, BLOCK)
+        return pltpu.make_async_copy(
+            units_ref.at[rows, :], target_ref.at[rows, :], out_sems.at[j]
+        )
 
     def fetch(j):
         return pltpu.make_async_copy(
@@ -79,6 +88,11 @@
             for t in range(0, block.shape[1], 128):
                 v = block[rows, t : t + 128].astype(jnp.float32)
                 units_ref[to, t : t + 128] = (v * inverse).astype(jnp.bfloat16)
+        if away:
+            leave(j).start()
+    if away:
+        for j in range(count):
+            leave(j).wait()
 
 
 def pair_cosines(k, units_ref, rows, low_ref, high_ref):
@@ -385,10 +399,15 @@
         if high == low:
             return []
         rows = (high - low) * BLOCK
+        away = part < 3
+        extra = [
+            pltpu.VMEM((rows, width), jnp.bfloat16),
+            pltpu.SemaphoreType.DMA((high - low,)),
+        ]
         made = pl.pallas_call(
-            functools.partial(units_kernel, low, high - low),
+            functools.partial(units_kernel, low, high - low, away),
             in_specs=[pinned, any_spec],
-            out_specs=[vmem, vmem],
+            out_specs=[pl.BlockSpec(memory_space=pltpu.HBM) if away else vmem, vmem],
             out_shape=[
                 jax.ShapeDtypeStruct((rows, width), jnp.bfloat16),
                 jax.ShapeDtypeStruct((rows, 128), jnp.float32),
@@ -396,8 +415,9 @@
             scratch_shapes=[
                 pltpu.VMEM((2, BLOCK, width), jnp.bfloat16),
                 pltpu.SemaphoreType.DMA((2,)),
-            ],
-            compiler_params=params((37, 33, 29, 25)[part]),
+            ]
+            + (extra if away else []),
+            compiler_params=params((50, 50, 50, 36)[part]),
             cost_estimate=cost(4 * rows * width, 4 * rows * width),
             name="units",
         )(decoder, tie)

time: 172 us -> 154 us (0.90)
  local copies, waits for them, and re-layouts: 29.6 us -> 4.73 us
  Pallas kernels: 62.9 us -> 70.1 us
    unnamed x66 -> x34, local copies, waits for them, and re-layouts: 29.5 us -> 4.64 us
    pallas_call x4, Pallas kernels: 9.37 us -> 17.6 us  [make_units(): pl.pallas_call(functools.partial(units_kernel, low, high - low, away), in...]
  transfers between devices with their start and end apart: 30 -> 30, of which waited for: 8 -> 10; matrix products, arithmetic and copies ran while one was open for 0% -> 0% of each run, Pallas kernels for 28% -> 37%
where the time goes in v11:
time: 154 us
  Pallas kernels  70.1 us (46%)
  starting transfers between devices  50.2 us (33%)
  waiting for transfers between devices  26.4 us (17%)
  local copies, waits for them, and re-layouts  4.73 us (3%)
  between operations  2.24 us (1%)
    ppermute x30, starting transfers between devices, send(): return lax.ppermute(value, 'row', pairs)  50.2 us
    ppermute x30, waiting for transfers between devices, send(): return lax.ppermute(value, 'row', pairs)  26.4 us
    pallas_call x4, Pallas kernels, finish(): pl.pallas_call(finish_kernel, grid=(high - low,), in_specs=specs, out_spe...  21.8 us
    pallas_call x4, Pallas kernels, make_units(): pl.pallas_call(functools.partial(units_kernel, low, high - low, away), in...  17.6 us
    pallas_call x10, Pallas kernels, pick(): pl.pallas_call(functools.partial(pick_kernel, slots, len(candidates)), in...  6.39 us
    pallas_call x1, Pallas kernels, on_device(): pl.pallas_call(functools.partial(last_kernel, DW / (ROWS * latents)), gri...  5.58 us
    pallas_call x4, Pallas kernels, row_part(): pl.pallas_call(functools.partial(row_kernel, k, parts), in_specs=[smem] +...  5.02 us
    pallas_call x8, Pallas kernels, merge(): pl.pallas_call(functools.partial(merge_kernel, len(arrived), keep), in_sp...  4.72 us
  transfers between devices with their start and end apart: 30, of which 10 were waited for; matrix products, arithmetic and copies ran while one was open for 0% of the time, Pallas kernels for 37%

profile of v11, /device:TPU:0, one launch (start us, length us, event | category | flops | bytes accessed | tf_op | source)
XLA Modules:
  0.0 153.7 jit_solution(8873190199131832866)
XLA Ops:
  1.5 2.6 %head_units.1 = (bf16[256,1024]{1,0:T(8,128)(2,1)S(1)}, bf16[256,1024]{1,0:T(8,128)(2,1)S(1)}, bf16[256,1024]{1,0:T(8,128)(2,1)S(1)}, bf16[256,1024]{1,0:T(8,128)(2,1)S(1)}) custom-call(s32[5]{0:T(128)S(1)} %stack.23.flags_ref, bf16[2048,4096]{1,0:T(8,128)(2,1)} %decoder_ref.19), custom_call_target="tpu_custom_call" | custom-call | flops 4194304 | bytes 4194304 | tf_op jit(solution)/shard_map/head_units/pallas_call | solution.py:360
  4.1 4.9 %collective-permute-start.3 = (bf16[256,1024]{1,0:T(8,128)(2,1)S(1)}, bf16[256,1024]{1,0:T(8,128)(2,1)S(1)}, u32[]{:S(2)}, u32[]{:S(2)}) collective-permute-start(bf16[256,1024]{1,0:T(8,128)(2,1)S(1)} %get-tuple-element.51), channel_id=1, source_target_pairs={{0,2},{4,6},{8,10},{12,14},{16,18},{20,22},{24,26},{28,30}} | collective-permute-start | bytes 1572872 | tf_op jit(solution)/shard_map/ppermute | solution.py:334
  9.0 1.3 collective-permute-start
  10.3 4.7 %units.4 = (bf16[512,4096]{1,0:T(8,128)(2,1)}, f32[512,128]{1,0:T(8,128)S(1)}) custom-call(bf16[2048,4096]{1,0:T(8,128)(2,1)} %decoder_ref.19, bf16[256,1024]{1,0:T(8,128)(2,1)S(1)} %get-tuple-element.50.refs_0_), custom_call_target="tpu_custom_call" | custom-call | flops 8388608 | bytes 8388608 | tf_op jit(solution)/shard_map/units/pallas_call | solution.py:407
  16.2 3.5 %collective-permute-start.4 = (bf16[256,1024]{1,0:T(8,128)(2,1)S(1)}, bf16[256,1024]{1,0:T(8,128)(2,1)S(1)}, u32[]{:S(2)}, u32[]{:S(2)}) collective-permute-start(bf16[256,1024]{1,0:T(8,128)(2,1)S(1)} %pick.12.refs_0_), channel_id=1, source_target_pairs={{0,4},{2,6},{12,8},{14,10},{16,20},{18,22},{28,24},{30,26}} | collective-permute-start | bytes 1572872 | tf_op jit(solution)/shard_map/ppermute | solution.py:334
  19.7 1.5 collective-permute-done.refs_1_
  21.8 3.5 %collective-permute-start.1 = (bf16[256,1024]{1,0:T(8,128)(2,1)S(1)}, bf16[256,1024]{1,0:T(8,128)(2,1)S(1)}, u32[]{:S(2)}, u32[]{:S(2)}) collective-permute-start(bf16[256,1024]{1,0:T(8,128)(2,1)S(1)} %pick.10.refs_0_), channel_id=1, source_target_pairs={{0,4},{2,6},{12,8},{14,10},{16,20},{18,22},{28,24},{30,26}} | collective-permute-start | bytes 1572872 | tf_op jit(solution)/shard_map/ppermute | solution.py:334
  25.4 4.7 %units.5 = (bf16[512,4096]{1,0:T(8,128)(2,1)}, f32[512,128]{1,0:T(8,128)S(1)}) custom-call(bf16[2048,4096]{1,0:T(8,128)(2,1)} %decoder_ref.19, bf16[256,1024]{1,0:T(8,128)(2,1)S(1)} %pick.10.refs_0_), custom_call_target="tpu_custom_call" | custom-call | flops 8388608 | bytes 8388608 | tf_op jit(solution)/shard_map/units/pallas_call | solution.py:407
  35.2 4.7 %units.6 = (bf16[512,4096]{1,0:T(8,128)(2,1)}, f32[512,128]{1,0:T(8,128)S(1)}) custom-call(bf16[2048,4096]{1,0:T(8,128)(2,1)} %decoder_ref.19, bf16[256,1024]{1,0:T(8,128)(2,1)S(1)} %pick.14.refs_0_), custom_call_target="tpu_custom_call" | custom-call | flops 8388608 | bytes 8388608 | tf_op jit(solution)/shard_map/units/pallas_call | solution.py:407
  41.9 8.3 %collective-permute-done.10.refs_3_ = bf16[256,1024]{1,0:T(8,128)(2,1)S(1)} collective-permute-done((bf16[256,1024]{1,0:T(8,128)(2,1)S(1)}, bf16[256,1024]{1,0:T(8,128)(2,1)S(1)}, u32[]{:S(2)}, u32[]{:S(2)}) %collective-permute-start.10) | collective-permute-done | bytes 524320 | tf_op jit(solution)/shard_map/ppermute | solution.py:334
  50.8 4.4 %collective-permute-start.12 = (bf16[256,1024]{1,0:T(8,128)(2,1)S(1)}, bf16[256,1024]{1,0:T(8,128)(2,1)S(1)}, u32[]{:S(2)}, u32[]{:S(2)}) collective-permute-start(bf16[256,1024]{1,0:T(8,128)(2,1)S(1)} %pick.18.refs_0_), channel_id=1, source_target_pairs={{0,2},{2,0},{4,6},{6,4},{8,10},{10,8},{12,14},{14,12},{16,18},{18,... | collective-permute-start | bytes 1572872 | tf_op jit(solution)/shard_map/ppermute | solution.py:334
  55.2 1.7 %collective-permute-done.6.refs_3_ = bf16[256,1024]{1,0:T(8,128)(2,1)S(1)} collective-permute-done((bf16[256,1024]{1,0:T(8,128)(2,1)S(1)}, bf16[256,1024]{1,0:T(8,128)(2,1)S(1)}, u32[]{:S(2)}, u32[]{:S(2)}) %collective-permute-start.6) | collective-permute-done | bytes 524320 | tf_op jit(solution)/shard_map/ppermute | solution.py:334
  57.5 4.4 %collective-permute-start.8 = (bf16[256,1024]{1,0:T(8,128)(2,1)S(1)}, bf16[256,1024]{1,0:T(8,128)(2,1)S(1)}, u32[]{:S(2)}, u32[]{:S(2)}) collective-permute-start(bf16[256,1024]{1,0:T(8,128)(2,1)S(1)} %pick.16.refs_0_), channel_id=1, source_target_pairs={{0,2},{2,0},{4,6},{6,4},{8,10},{10,8},{12,14},{14,12},{16,18},{18,... | collective-permute-start | bytes 1572872 | tf_op jit(solution)/shard_map/ppermute | solution.py:334
  61.9 1.3 collective-permute-start.11
  63.2 1.3 collective-permute-start.13
  64.6 2.1 %collective-permute-start.7 = (bf16[256,1024]{1,0:T(8,128)(2,1)S(1)}, bf16[256,1024]{1,0:T(8,128)(2,1)}, u32[]{:S(2)}, u32[]{:S(2)}) collective-permute-start(bf16[256,1024]{1,0:T(8,128)(2,1)S(1)} %pick.16.refs_0_), channel_id=1, source_target_pairs={{0,1},{2,3},{4,5},{6,7},{8,9},{10,11},{12,13},{14,15},{16,17},{18,... | collective-permute-start | bytes 1572872 | tf_op jit(solution)/shard_map/ppermute | solution.py:334
  66.7 2.4 %collective-permute-done.8.refs_2_ = bf16[256,1024]{1,0:T(8,128)(2,1)S(1)} collective-permute-done((bf16[256,1024]{1,0:T(8,128)(2,1)S(1)}, bf16[256,1024]{1,0:T(8,128)(2,1)S(1)}, u32[]{:S(2)}, u32[]{:S(2)}) %collective-permute-start.8) | collective-permute-done | bytes 524320 | tf_op jit(solution)/shard_map/ppermute | solution.py:334
  69.0 2.1 %collective-permute-start.9 = (bf16[256,1024]{1,0:T(8,128)(2,1)S(1)}, bf16[256,1024]{1,0:T(8,128)(2,1)}, u32[]{:S(2)}, u32[]{:S(2)}) collective-permute-start(bf16[256,1024]{1,0:T(8,128)(2,1)S(1)} %collective-permute-done.8.refs_2_), channel_id=1, source_target_pairs={{0,1},{2,3},{4,5},{6,7},{8,9},{10,11},{12,13},{14,15},{16,17},{18,... | collective-permute-start | bytes 1572872 | tf_op jit(solution)/shard_map/ppermute | solution.py:334
  71.1 3.5 %units.7 = (bf16[512,4096]{1,0:T(8,128)(2,1)S(1)}, f32[512,128]{1,0:T(8,128)S(1)}) custom-call(bf16[2048,4096]{1,0:T(8,128)(2,1)} %decoder_ref.19, bf16[256,1024]{1,0:T(8,128)(2,1)S(1)} %pick.16.refs_0_), custom_call_target="tpu_custom_call" | custom-call | flops 8388608 | bytes 8388608 | tf_op jit(solution)/shard_map/units/pallas_call | solution.py:407
  79.4 2.4 %part_cosines.1.partial_ref = f32[2048,256]{1,0:T(8,128)S(1)} custom-call(bf16[256,1024]{1,0:T(8,128)(2,1)S(1)} %get-tuple-element.58.low_ref.refs_0_, bf16[256,1024]{1,0:T(8,128)(2,1)S(1)} %get-tuple-element.59.high_ref.refs_1_, bf16[512,4096]{1,0:T(8,128)(2,1)S(1)} %copy-done, bf16[512,4096]{1,0:T(8,128)(2,1)S(1)} %copy-done.1, ...), custom_call_target="tpu_custom_call" | custom-call | flops 2147483648 | bytes 8388608 | tf_op jit(solution)/shard_map/part_cosines/pallas_call | solution.py:463
  82.5 3.3 %weights.1 = (bf16[2048,256]{1,0:T(8,128)(2,1)S(1)}, bf16[256,2048]{1,0:T(8,128)(2,1)S(1)}, f32[2048,128]{1,0:T(8,128)S(1)}, f32[8,128]{1,0:T(8,128)S(1)}) custom-call(s32[1]{0:T(128)} %bitcast.2.delta_ref, bf16[256,1024]{1,0:T(8,128)(2,1)S(1)} %get-tuple-element.55.low_ref.refs_2_, bf16[256,1024]{1,0:T(8,128)(2,1)S(1)} %get-tuple-element.56.high_ref.refs_3_, ...), custom_call_target="tpu_custom_call" | custom-call | flops 2147483648 | bytes 8388608 | tf_op jit(solution)/shard_map/weights/pallas_call | solution.py:472
  90.6 2.1 %collective-permute-start.18 = (s32[272,256]{1,0:T(8,128)S(1)}, s32[272,256]{1,0:T(8,128)S(1)}, u32[]{:S(2)}, u32[]{:S(2)}) collective-permute-start(s32[272,256]{1,0:T(8,128)S(1)} %get-tuple-element.71.refs_4_), channel_id=1, source_target_pairs={{0,2},{2,0},{1,3},{3,1},{4,6},{6,4},{5,7},{7,5},{8,10},{10,8},{9,1... | collective-permute-start | bytes 835592 | tf_op jit(solution)/shard_map/ppermute | solution.py:334
  94.4 5.8 %collective-permute-done.18.refs_0_ = s32[272,256]{1,0:T(8,128)S(1)} collective-permute-done((s32[272,256]{1,0:T(8,128)S(1)}, s32[272,256]{1,0:T(8,128)S(1)}, u32[]{:S(2)}, u32[]{:S(2)}) %collective-permute-start.18) | collective-permute-done | bytes 278560 | tf_op jit(solution)/shard_map/ppermute | solution.py:334
  100.5 1.5 collective-permute-start.20
  102.0 5.8 %finish.4 = (f32[2048,4096]{1,0:T(8,128)}, f32[8,128]{1,0:T(8,128)S(1)}) custom-call(bf16[2048,256]{1,0:T(8,128)(2,1)S(1)} %get-tuple-element.64.col_ref, bf16[2048,4096]{1,0:T(8,128)(2,1)} %decoder_ref.19, f32[2048,128]{1,0:T(8,128)} %copy-done.4, bf16[256,1024]{1,0:T(8,128)(2,1)S(1)} %get-tuple-element.58.low_ref.refs_0_, ...), custom_call_target="tpu_custom_call" | custom-call | flops 1073741824 | bytes 12582912 | tf_op jit(solution)/shard_map/finish/pallas_call | solution.py:563
  110.6 5.8 %finish.5 = (f32[2048,4096]{1,0:T(8,128)}, f32[8,128]{1,0:T(8,128)S(1)}) custom-call(bf16[2048,256]{1,0:T(8,128)(2,1)S(1)} %get-tuple-element.64.col_ref, bf16[2048,4096]{1,0:T(8,128)(2,1)} %decoder_ref.19, f32[2048,128]{1,0:T(8,128)} %copy-done.4, bf16[256,1024]{1,0:T(8,128)(2,1)S(1)} %get-tuple-element.58.low_ref.refs_0_, ...), custom_call_target="tpu_custom_call", output_to_operand_aliasing={{0}: (8, {})} | custom-call | flops 1073741824 | bytes 12582912 | tf_op jit(solution)/shard_map/finish/pallas_call | solution.py:563
  119.0 4.4 %finish.6 = (f32[2048,4096]{1,0:T(8,128)}, f32[8,128]{1,0:T(8,128)S(1)}) custom-call(bf16[2048,256]{1,0:T(8,128)(2,1)S(1)} %get-tuple-element.64.col_ref, bf16[2048,4096]{1,0:T(8,128)(2,1)} %decoder_ref.19, f32[2048,128]{1,0:T(8,128)} %copy-done.4, bf16[256,1024]{1,0:T(8,128)(2,1)S(1)} %get-tuple-element.58.low_ref.refs_0_, ...), custom_call_target="tpu_custom_call", output_to_operand_aliasing={{0}: (8, {})} | custom-call | flops 536870912 | bytes 6291456 | tf_op jit(solution)/shard_map/finish/pallas_call | solution.py:563
  125.1 3.0 %collective-permute-done.26.refs_2_ = s32[272,256]{1,0:T(8,128)S(1)} collective-permute-done((s32[272,256]{1,0:T(8,128)S(1)}, s32[272,256]{1,0:T(8,128)S(1)}, u32[]{:S(2)}, u32[]{:S(2)}) %collective-permute-start.26) | collective-permute-done | bytes 278560 | tf_op jit(solution)/shard_map/ppermute | solution.py:334
  134.1 1.6 %merge.13 = (f32[256,512]{1,0:T(8,128)S(1)}, f32[8,128]{1,0:T(8,128)S(1)}, s32[272,256]{1,0:T(8,128)}) custom-call(f32[256,512]{1,0:T(8,128)S(1)} %get-tuple-element.73.kept_ref, f32[8,128]{1,0:T(8,128)S(1)} %get-tuple-element.74.penalty_ref, s32[272,256]{1,0:T(8,128)S(1)} %collective-permute-done.17.refs_0_, ...), custom_call_target="tpu_custom_call" | custom-call | flops 2621440 | bytes 1572864 | tf_op jit(solution)/shard_map/merge/pallas_call | solution.py:508
  140.5 5.8 %finish.7 = (f32[2048,4096]{1,0:T(8,128)}, f32[8,128]{1,0:T(8,128)}) custom-call(bf16[2048,256]{1,0:T(8,128)(2,1)S(1)} %get-tuple-element.64.col_ref, bf16[2048,4096]{1,0:T(8,128)(2,1)} %decoder_ref.19, f32[2048,128]{1,0:T(8,128)} %copy-done.4, bf16[256,1024]{1,0:T(8,128)(2,1)S(1)} %get-tuple-element.58.low_ref.refs_0_, ...), custom_call_target="tpu_custom_call", output_to_operand_aliasing={{0}: (8, {})} | custom-call | flops 1073741824 | bytes 12582912 | tf_op jit(solution)/shard_map/finish/pallas_call | solution.py:563
  146.3 1.6 %collective-permute-done.22.refs_5_.refs_6_ = s32[272,256]{1,0:T(8,128)} collective-permute-done((s32[272,256]{1,0:T(8,128)}, s32[272,256]{1,0:T(8,128)}, u32[]{:S(2)}, u32[]{:S(2)}) %collective-permute-start.22) | collective-permute-done | bytes 278560 | tf_op jit(solution)/shard_map/ppermute | solution.py:334
  147.9 5.6 %finish_rows.1 = (f32[2048,4096]{1,0:T(8,128)}, f32[1]{0:T(128)}) custom-call(s32[1]{0:T(128)} %bitcast.1.owner_ref, bf16[2048,256]{1,0:T(8,128)(2,1)} %copy-done.3, bf16[2048,4096]{1,0:T(8,128)(2,1)} %decoder_ref.19, f32[2048,128]{1,0:T(8,128)} %copy-done.4, f32[8,128]{1,0:T(8,128)S(1)} %get-tuple-element.85.tile_ref, ...), custom_call_target="tpu_custom_call", output_to_operand_aliasing={{0}: (23, {})} | custom-call | tf_op jit(solution)/shard_map/finish_rows/pallas_call | solution.py:631
  (99 shorter events, 40.0 us)
Async XLA Ops:
  4.1 11.5 %collective-permute-start.3 = (bf16[256,1024]{1,0:T(8,128)(2,1)S(1)}, bf16[256,1024]{1,0:T(8,128)(2,1)S(1)}, u32[]{:S(2)}, u32[]{:S(2)}) collective-permute-start(bf16[256,1024]{1,0:T(8,128)(2,1)S(1)} %get-tuple-element.51), channel_id=1, source_target_pairs={{0,2},{4,6},{8,10},{12,14},{16,18},{20,22},{24,26},{28,30}} | collective-permute-start | bytes 1572872 | tf_op jit(solution)/shard_map/ppermute | solution.py:334
  9.0 12.3 %collective-permute-start = (bf16[256,1024]{1,0:T(8,128)(2,1)S(1)}, bf16[256,1024]{1,0:T(8,128)(2,1)S(1)}, u32[]{:S(2)}, u32[]{:S(2)}) collective-permute-start(bf16[256,1024]{1,0:T(8,128)(2,1)S(1)} %get-tuple-element.49), channel_id=1, source_target_pairs={{0,2},{4,6},{8,10},{12,14},{16,18},{20,22},{24,26},{28,30}} | collective-permute-start | bytes 1572872 | tf_op jit(solution)/shard_map/ppermute | solution.py:334
  16.2 13.9 %collective-permute-start.4 = (bf16[256,1024]{1,0:T(8,128)(2,1)S(1)}, bf16[256,1024]{1,0:T(8,128)(2,1)S(1)}, u32[]{:S(2)}, u32[]{:S(2)}) collective-permute-start(bf16[256,1024]{1,0:T(8,128)(2,1)S(1)} %pick.12.refs_0_), channel_id=1, source_target_pairs={{0,4},{2,6},{12,8},{14,10},{16,20},{18,22},{28,24},{30,26}} | collective-permute-start | bytes 1572872 | tf_op jit(solution)/shard_map/ppermute | solution.py:334
  21.8 10.2 %collective-permute-start.1 = (bf16[256,1024]{1,0:T(8,128)(2,1)S(1)}, bf16[256,1024]{1,0:T(8,128)(2,1)S(1)}, u32[]{:S(2)}, u32[]{:S(2)}) collective-permute-start(bf16[256,1024]{1,0:T(8,128)(2,1)S(1)} %pick.10.refs_0_), channel_id=1, source_target_pairs={{0,4},{2,6},{12,8},{14,10},{16,20},{18,22},{28,24},{30,26}} | collective-permute-start | bytes 1572872 | tf_op jit(solution)/shard_map/ppermute | solution.py:334
  30.7 2.6 %collective-permute-start.5 = (bf16[256,1024]{1,0:T(8,128)(2,1)S(1)}, bf16[256,1024]{1,0:T(8,128)(2,1)S(1)}, u32[]{:S(2)}, u32[]{:S(2)}) collective-permute-start(bf16[256,1024]{1,0:T(8,128)(2,1)S(1)} %pick.13), channel_id=1, source_target_pairs={{4,8},{6,10},{8,4},{10,6},{20,24},{22,26},{24,20},{26,22}} | collective-permute-start | bytes 1572872 | tf_op jit(solution)/shard_map/ppermute | solution.py:334
  32.6 7.4 %collective-permute-start.2 = (bf16[256,1024]{1,0:T(8,128)(2,1)S(1)}, bf16[256,1024]{1,0:T(8,128)(2,1)S(1)}, u32[]{:S(2)}, u32[]{:S(2)}) collective-permute-start(bf16[256,1024]{1,0:T(8,128)(2,1)S(1)} %pick.11), channel_id=1, source_target_pairs={{4,8},{6,10},{8,4},{10,6},{20,24},{22,26},{24,20},{26,22}} | collective-permute-start | bytes 1572872 | tf_op jit(solution)/shard_map/ppermute | solution.py:334
  33.9 16.2 %collective-permute-start.10 = (bf16[256,1024]{1,0:T(8,128)(2,1)S(1)}, bf16[256,1024]{1,0:T(8,128)(2,1)S(1)}, u32[]{:S(2)}, u32[]{:S(2)}) collective-permute-start(bf16[256,1024]{1,0:T(8,128)(2,1)S(1)} %pick.14.refs_0_), channel_id=1, source_target_pairs={{8,12},{10,14},{4,0},{6,2},{24,28},{26,30},{20,16},{22,18}} | collective-permute-start | bytes 1572872 | tf_op jit(solution)/shard_map/ppermute | solution.py:334
  40.0 29.1 %copy-start.7 = (f32[512,128]{1,0:T(8,128)}, f32[512,128]{1,0:T(8,128)S(1)}, u32[]{:S(2)}) copy-start(f32[512,128]{1,0:T(8,128)S(1)} %get-tuple-element.54.refs_2_.refs_6_) | copy-start | bytes 786436
  40.6 16.3 %collective-permute-start.6 = (bf16[256,1024]{1,0:T(8,128)(2,1)S(1)}, bf16[256,1024]{1,0:T(8,128)(2,1)S(1)}, u32[]{:S(2)}, u32[]{:S(2)}) collective-permute-start(bf16[256,1024]{1,0:T(8,128)(2,1)S(1)} %pick.15), channel_id=1, source_target_pairs={{8,12},{10,14},{4,0},{6,2},{24,28},{26,30},{20,16},{22,18}} | collective-permute-start | bytes 1572872 | tf_op jit(solution)/shard_map/ppermute | solution.py:334
  50.8 12.4 %collective-permute-start.12 = (bf16[256,1024]{1,0:T(8,128)(2,1)S(1)}, bf16[256,1024]{1,0:T(8,128)(2,1)S(1)}, u32[]{:S(2)}, u32[]{:S(2)}) collective-permute-start(bf16[256,1024]{1,0:T(8,128)(2,1)S(1)} %pick.18.refs_0_), channel_id=1, source_target_pairs={{0,2},{2,0},{4,6},{6,4},{8,10},{10,8},{12,14},{14,12},{16,18},{18,... | collective-permute-start | bytes 1572872 | tf_op jit(solution)/shard_map/ppermute | solution.py:334
  57.5 11.5 %collective-permute-start.8 = (bf16[256,1024]{1,0:T(8,128)(2,1)S(1)}, bf16[256,1024]{1,0:T(8,128)(2,1)S(1)}, u32[]{:S(2)}, u32[]{:S(2)}) collective-permute-start(bf16[256,1024]{1,0:T(8,128)(2,1)S(1)} %pick.16.refs_0_), channel_id=1, source_target_pairs={{0,2},{2,0},{4,6},{6,4},{8,10},{10,8},{12,14},{14,12},{16,18},{18,... | collective-permute-start | bytes 1572872 | tf_op jit(solution)/shard_map/ppermute | solution.py:334
  61.9 12.8 %collective-permute-start.11 = (bf16[256,1024]{1,0:T(8,128)(2,1)S(1)}, bf16[256,1024]{1,0:T(8,128)(2,1)S(1)}, u32[]{:S(2)}, u32[]{:S(2)}) collective-permute-start(bf16[256,1024]{1,0:T(8,128)(2,1)S(1)} %pick.18.refs_0_), channel_id=1, source_target_pairs={{0,1},{2,3},{4,5},{6,7},{8,9},{10,11},{12,13},{14,15},{16,17},{18,... | collective-permute-start | bytes 1572872 | tf_op jit(solution)/shard_map/ppermute | solution.py:334
  63.2 12.2 %collective-permute-start.13 = (bf16[256,1024]{1,0:T(8,128)(2,1)S(1)}, bf16[256,1024]{1,0:T(8,128)(2,1)S(1)}, u32[]{:S(2)}, u32[]{:S(2)}) collective-permute-start(bf16[256,1024]{1,0:T(8,128)(2,1)S(1)} %collective-permute-done.12.refs_2_), channel_id=1, source_target_pairs={{0,1},{2,3},{4,5},{6,7},{8,9},{10,11},{12,13},{14,15},{16,17},{18,... | collective-permute-start | bytes 1572872 | tf_op jit(solution)/shard_map/ppermute | solution.py:334
  64.6 17.2 %collective-permute-start.7 = (bf16[256,1024]{1,0:T(8,128)(2,1)S(1)}, bf16[256,1024]{1,0:T(8,128)(2,1)}, u32[]{:S(2)}, u32[]{:S(2)}) collective-permute-start(bf16[256,1024]{1,0:T(8,128)(2,1)S(1)} %pick.16.refs_0_), channel_id=1, source_target_pairs={{0,1},{2,3},{4,5},{6,7},{8,9},{10,11},{12,13},{14,15},{16,17},{18,... | collective-permute-start | bytes 1572872 | tf_op jit(solution)/shard_map/ppermute | solution.py:334
  69.0 12.8 %collective-permute-start.9 = (bf16[256,1024]{1,0:T(8,128)(2,1)S(1)}, bf16[256,1024]{1,0:T(8,128)(2,1)}, u32[]{:S(2)}, u32[]{:S(2)}) collective-permute-start(bf16[256,1024]{1,0:T(8,128)(2,1)S(1)} %collective-permute-done.8.refs_2_), channel_id=1, source_target_pairs={{0,1},{2,3},{4,5},{6,7},{8,9},{10,11},{12,13},{14,15},{16,17},{18,... | collective-permute-start | bytes 1572872 | tf_op jit(solution)/shard_map/ppermute | solution.py:334
  85.8 54.7 %copy-start.3 = (bf16[2048,256]{1,0:T(8,128)(2,1)}, bf16[2048,256]{1,0:T(8,128)(2,1)S(1)}, u32[]{:S(2)}) copy-start(bf16[2048,256]{1,0:T(8,128)(2,1)S(1)} %get-tuple-element.64.col_ref) | copy-start | bytes 3145732
  87.1 3.2 %collective-permute-start.16 = (f32[264,1024]{1,0:T(8,128)S(1)}, f32[264,1024]{1,0:T(8,128)S(1)}, u32[]{:S(2)}, u32[]{:S(2)}) collective-permute-start(f32[264,1024]{1,0:T(8,128)S(1)} %row_part.7), channel_id=1, source_target_pairs={{0,1},{1,0},{2,3},{3,2},{4,5},{5,4},{6,7},{7,6},{8,9},{9,8},{10,11... | collective-permute-start | bytes 3244040 | tf_op jit(solution)/shard_map/ppermute | solution.py:334
  88.5 5.5 %collective-permute-start.14 = (f32[264,1024]{1,0:T(8,128)S(1)}, f32[264,1024]{1,0:T(8,128)S(1)}, u32[]{:S(2)}, u32[]{:S(2)}) collective-permute-start(f32[264,1024]{1,0:T(8,128)S(1)} %row_part.5), channel_id=1, source_target_pairs={{0,1},{1,0},{2,3},{3,2},{4,5},{5,4},{6,7},{7,6},{8,9},{9,8},{10,11... | collective-permute-start | bytes 3244040 | tf_op jit(solution)/shard_map/ppermute | solution.py:334
  90.6 9.6 %collective-permute-start.18 = (s32[272,256]{1,0:T(8,128)S(1)}, s32[272,256]{1,0:T(8,128)S(1)}, u32[]{:S(2)}, u32[]{:S(2)}) collective-permute-start(s32[272,256]{1,0:T(8,128)S(1)} %get-tuple-element.71.refs_4_), channel_id=1, source_target_pairs={{0,2},{2,0},{1,3},{3,1},{4,6},{6,4},{5,7},{7,5},{8,10},{10,8},{9,1... | collective-permute-start | bytes 835592 | tf_op jit(solution)/shard_map/ppermute | solution.py:334
  94.3 13.4 %collective-permute-start.15 = (s32[272,256]{1,0:T(8,128)S(1)}, s32[272,256]{1,0:T(8,128)S(1)}, u32[]{:S(2)}, u32[]{:S(2)}) collective-permute-start(s32[272,256]{1,0:T(8,128)S(1)} %get-tuple-element.70), channel_id=1, source_target_pairs={{0,2},{2,0},{1,3},{3,1},{4,6},{6,4},{5,7},{7,5},{8,10},{10,8},{9,1... | collective-permute-start | bytes 835592 | tf_op jit(solution)/shard_map/ppermute | solution.py:334
  100.5 8.9 %collective-permute-start.20 = (s32[272,256]{1,0:T(8,128)S(1)}, s32[272,256]{1,0:T(8,128)S(1)}, u32[]{:S(2)}, u32[]{:S(2)}) collective-permute-start(s32[272,256]{1,0:T(8,128)S(1)} %get-tuple-element.78.refs_4_), channel_id=1, source_target_pairs={{0,4},{1,5},{2,6},{3,7},{12,8},{13,9},{14,10},{15,11},{16,20},{17,... | collective-permute-start | bytes 835592 | tf_op jit(solution)/shard_map/ppermute | solution.py:334
  108.1 8.3 %collective-permute-start.17 = (s32[272,256]{1,0:T(8,128)S(1)}, s32[272,256]{1,0:T(8,128)S(1)}, u32[]{:S(2)}, u32[]{:S(2)}) collective-permute-start(s32[272,256]{1,0:T(8,128)S(1)} %get-tuple-element.75), channel_id=1, source_target_pairs={{0,4},{1,5},{2,6},{3,7},{12,8},{13,9},{14,10},{15,11},{16,20},{17,... | collective-permute-start | bytes 835592 | tf_op jit(solution)/shard_map/ppermute | solution.py:334
  109.7 7.7 %collective-permute-start.25 = (s32[272,256]{1,0:T(8,128)S(1)}, s32[272,256]{1,0:T(8,128)S(1)}, u32[]{:S(2)}, u32[]{:S(2)}) collective-permute-start(s32[272,256]{1,0:T(8,128)S(1)} %merge.11.refs_4_), channel_id=1, source_target_pairs={{4,8},{5,9},{6,10},{7,11},{8,4},{9,5},{10,6},{11,7},{20,24},{21,25... | collective-permute-start | bytes 835592 | tf_op jit(solution)/shard_map/ppermute | solution.py:334
  116.7 6.7 %collective-permute-start.19 = (s32[272,256]{1,0:T(8,128)S(1)}, s32[272,256]{1,0:T(8,128)S(1)}, u32[]{:S(2)}, u32[]{:S(2)}) collective-permute-start(s32[272,256]{1,0:T(8,128)S(1)} %merge.10), channel_id=1, source_target_pairs={{4,8},{5,9},{6,10},{7,11},{8,4},{9,5},{10,6},{11,7},{20,24},{21,25... | collective-permute-start | bytes 835592 | tf_op jit(solution)/shard_map/ppermute | solution.py:334
  117.7 10.3 %collective-permute-start.26 = (s32[272,256]{1,0:T(8,128)S(1)}, s32[272,256]{1,0:T(8,128)S(1)}, u32[]{:S(2)}, u32[]{:S(2)}) collective-permute-start(s32[272,256]{1,0:T(8,128)S(1)} %merge.14), channel_id=1, source_target_pairs={{8,12},{9,13},{10,14},{11,15},{4,0},{5,1},{6,2},{7,3},{24,28},{25,... | collective-permute-start | bytes 835592 | tf_op jit(solution)/shard_map/ppermute | solution.py:334
  123.8 10.4 %collective-permute-start.21 = (s32[272,256]{1,0:T(8,128)S(1)}, s32[272,256]{1,0:T(8,128)S(1)}, u32[]{:S(2)}, u32[]{:S(2)}) collective-permute-start(s32[272,256]{1,0:T(8,128)S(1)} %merge.12), channel_id=1, source_target_pairs={{8,12},{9,13},{10,14},{11,15},{4,0},{5,1},{6,2},{7,3},{24,28},{25,... | collective-permute-start | bytes 835592 | tf_op jit(solution)/shard_map/ppermute | solution.py:334
  129.3 9.8 %collective-permute-start.29 = (s32[272,256]{1,0:T(8,128)}, s32[272,256]{1,0:T(8,128)S(1)}, u32[]{:S(2)}, u32[]{:S(2)}) collective-permute-start(s32[272,256]{1,0:T(8,128)} %get-tuple-element.89.refs_4_), channel_id=1, source_target_pairs={{3,0},{7,4},{11,8},{15,12},{19,16},{23,20},{27,24},{31,28}} | collective-permute-start | bytes 835592 | tf_op jit(solution)/shard_map/ppermute | solution.py:334
  130.6 15.7 %collective-permute-start.28 = (s32[272,256]{1,0:T(8,128)}, s32[272,256]{1,0:T(8,128)}, u32[]{:S(2)}, u32[]{:S(2)}) collective-permute-start(s32[272,256]{1,0:T(8,128)} %get-tuple-element.89.refs_4_), channel_id=1, source_target_pairs={{1,0},{5,4},{9,8},{13,12},{17,16},{21,20},{25,24},{29,28}} | collective-permute-start | bytes 835592 | tf_op jit(solution)/shard_map/ppermute | solution.py:334
  131.9 14.4 %collective-permute-start.27 = (s32[272,256]{1,0:T(8,128)}, s32[272,256]{1,0:T(8,128)}, u32[]{:S(2)}, u32[]{:S(2)}) collective-permute-start(s32[272,256]{1,0:T(8,128)} %get-tuple-element.89.refs_4_), channel_id=1, source_target_pairs={{2,0},{6,4},{10,8},{14,12},{18,16},{22,20},{26,24},{30,28}} | collective-permute-start | bytes 835592 | tf_op jit(solution)/shard_map/ppermute | solution.py:334
  136.6 9.7 %collective-permute-start.24 = (s32[272,256]{1,0:T(8,128)}, s32[272,256]{1,0:T(8,128)}, u32[]{:S(2)}, u32[]{:S(2)}) collective-permute-start(s32[272,256]{1,0:T(8,128)} %get-tuple-element.87), channel_id=1, source_target_pairs={{3,0},{7,4},{11,8},{15,12},{19,16},{23,20},{27,24},{31,28}} | collective-permute-start | bytes 835592 | tf_op jit(solution)/shard_map/ppermute | solution.py:334
  137.9 8.5 %collective-permute-start.23 = (s32[272,256]{1,0:T(8,128)}, s32[272,256]{1,0:T(8,128)}, u32[]{:S(2)}, u32[]{:S(2)}) collective-permute-start(s32[272,256]{1,0:T(8,128)} %get-tuple-element.87), channel_id=1, source_target_pairs={{1,0},{5,4},{9,8},{13,12},{17,16},{21,20},{25,24},{29,28}} | collective-permute-start | bytes 835592 | tf_op jit(solution)/shard_map/ppermute | solution.py:334
  139.2 8.8 %collective-permute-start.22 = (s32[272,256]{1,0:T(8,128)}, s32[272,256]{1,0:T(8,128)}, u32[]{:S(2)}, u32[]{:S(2)}) collective-permute-start(s32[272,256]{1,0:T(8,128)} %get-tuple-element.87), channel_id=1, source_target_pairs={{2,0},{6,4},{10,8},{14,12},{18,16},{22,20},{26,24},{30,28}} | collective-permute-start | bytes 835592 | tf_op jit(solution)/shard_map/ppermute | solution.py:334
  (15 other events, 58.0 us)

commit v12 on v11

--- a/solution.py
+++ b/solution.py
@@ -399,7 +399,7 @@
         if high == low:
             return []
         rows = (high - low) * BLOCK
-        away = part < 3
+        away = part < 4
         extra = [
             pltpu.VMEM((rows, width), jnp.bfloat16),
             pltpu.SemaphoreType.DMA((high - low,)),
@@ -417,7 +417,7 @@
                 pltpu.SemaphoreType.DMA((2,)),
             ]
             + (extra if away else []),
-            compiler_params=params((50, 50, 50, 36)[part]),
+            compiler_params=params(50),
             cost_estimate=cost(4 * rows * width, 4 * rows * width),
             name="units",
         )(decoder, tie)

time: 154 us -> 162 us (1.052)
  Pallas kernels: 70.1 us -> 74.3 us
  local copies, waits for them, and re-layouts: 4.73 us -> 8.27 us
  waiting for transfers between devices: 26.4 us -> 24.3 us
    unnamed x34 -> x62, local copies, waits for them, and re-layouts: 4.64 us -> 8.19 us
    pallas_call x10, Pallas kernels: 6.39 us -> 9 us  [pick(): pl.pallas_call(functools.partial(pick_kernel, slots, len(candidates)), in...]
    ppermute x30, waiting for transfers between devices: 26.4 us -> 24.3 us  [send(): return lax.ppermute(value, 'row', pairs)]
where the time goes in v12:
time: 162 us; the launch traced here: 161 us
  Pallas kernels  74.3 us (46%)
  starting transfers between devices  51.8 us (32%)
  waiting for transfers between devices  24.3 us (15%)
  local copies, waits for them, and re-layouts  8.27 us (5%)
  between operations  2.4 us (1%)
    ppermute x30, starting transfers between devices, send(): return lax.ppermute(value, 'row', pairs)  51.8 us
    ppermute x30, waiting for transfers between devices, send(): return lax.ppermute(value, 'row', pairs)  24.3 us
    pallas_call x4, Pallas kernels, finish(): pl.pallas_call(finish_kernel, grid=(high - low,), in_specs=specs, out_spe...  22 us
    pallas_call x4, Pallas kernels, make_units(): pl.pallas_call(functools.partial(units_kernel, low, high - low, away), in...  19.1 us
    pallas_call x10, Pallas kernels, pick(): pl.pallas_call(functools.partial(pick_kernel, slots, len(candidates)), in...  9 us
    unnamed x62, local copies, waits for them, and re-layouts  8.19 us
    pallas_call x1, Pallas kernels, on_device(): pl.pallas_call(functools.partial(last_kernel, DW / (ROWS * latents)), gri...  5.58 us
    pallas_call x4, Pallas kernels, row_part(): pl.pallas_call(functools.partial(row_kernel, k, parts), in_specs=[smem] +...  5.06 us
  transfers between devices with their start and end apart: 30, of which 10 were waited for; matrix products, arithmetic and copies ran while one was open for 0% of the time, Pallas kernels for 37%

profile of v12, /device:TPU:0, one launch (start us, length us, event | category | flops | bytes accessed | tf_op | source)
XLA Modules:
  0.0 161.1 jit_solution(1004327972447686203)
XLA Ops:
  1.5 2.6 %head_units.1 = (bf16[256,1024]{1,0:T(8,128)(2,1)S(1)}, bf16[256,1024]{1,0:T(8,128)(2,1)S(1)}, bf16[256,1024]{1,0:T(8,128)(2,1)S(1)}, bf16[256,1024]{1,0:T(8,128)(2,1)S(1)}) custom-call(s32[5]{0:T(128)S(1)} %stack.23.flags_ref, bf16[2048,4096]{1,0:T(8,128)(2,1)} %decoder_ref.19), custom_call_target="tpu_custom_call" | custom-call | flops 4194304 | bytes 4194304 | tf_op jit(solution)/shard_map/head_units/pallas_call | solution.py:360
  4.1 4.9 %collective-permute-start.3 = (bf16[256,1024]{1,0:T(8,128)(2,1)S(1)}, bf16[256,1024]{1,0:T(8,128)(2,1)S(1)}, u32[]{:S(2)}, u32[]{:S(2)}) collective-permute-start(bf16[256,1024]{1,0:T(8,128)(2,1)S(1)} %get-tuple-element.51), channel_id=1, source_target_pairs={{0,2},{4,6},{8,10},{12,14},{16,18},{20,22},{24,26},{28,30}} | collective-permute-start | bytes 1572872 | tf_op jit(solution)/shard_map/ppermute | solution.py:334
  10.3 4.7 %units.4 = (bf16[512,4096]{1,0:T(8,128)(2,1)}, f32[512,128]{1,0:T(8,128)S(1)}) custom-call(bf16[2048,4096]{1,0:T(8,128)(2,1)} %decoder_ref.19, bf16[256,1024]{1,0:T(8,128)(2,1)S(1)} %get-tuple-element.50.refs_0_), custom_call_target="tpu_custom_call" | custom-call | flops 8388608 | bytes 8388608 | tf_op jit(solution)/shard_map/units/pallas_call | solution.py:407
  16.2 3.5 %collective-permute-start.4 = (bf16[256,1024]{1,0:T(8,128)(2,1)S(1)}, bf16[256,1024]{1,0:T(8,128)(2,1)S(1)}, u32[]{:S(2)}, u32[]{:S(2)}) collective-permute-start(bf16[256,1024]{1,0:T(8,128)(2,1)S(1)} %pick.12.refs_0_), channel_id=1, source_target_pairs={{0,4},{2,6},{12,8},{14,10},{16,20},{18,22},{28,24},{30,26}} | collective-permute-start | bytes 1572872 | tf_op jit(solution)/shard_map/ppermute | solution.py:334
  19.7 1.5 collective-permute-done.refs_1_
  21.8 3.5 %collective-permute-start.1 = (bf16[256,1024]{1,0:T(8,128)(2,1)S(1)}, bf16[256,1024]{1,0:T(8,128)(2,1)S(1)}, u32[]{:S(2)}, u32[]{:S(2)}) collective-permute-start(bf16[256,1024]{1,0:T(8,128)(2,1)S(1)} %pick.10.refs_0_), channel_id=1, source_target_pairs={{0,4},{2,6},{12,8},{14,10},{16,20},{18,22},{28,24},{30,26}} | collective-permute-start | bytes 1572872 | tf_op jit(solution)/shard_map/ppermute | solution.py:334
  25.4 4.7 %units.5 = (bf16[512,4096]{1,0:T(8,128)(2,1)}, f32[512,128]{1,0:T(8,128)S(1)}) custom-call(bf16[2048,4096]{1,0:T(8,128)(2,1)} %decoder_ref.19, bf16[256,1024]{1,0:T(8,128)(2,1)S(1)} %pick.10.refs_0_), custom_call_target="tpu_custom_call" | custom-call | flops 8388608 | bytes 8388608 | tf_op jit(solution)/shard_map/units/pallas_call | solution.py:407
  35.2 4.7 %units.6 = (bf16[512,4096]{1,0:T(8,128)(2,1)}, f32[512,128]{1,0:T(8,128)S(1)}) custom-call(bf16[2048,4096]{1,0:T(8,128)(2,1)} %decoder_ref.19, bf16[256,1024]{1,0:T(8,128)(2,1)S(1)} %pick.14.refs_0_), custom_call_target="tpu_custom_call" | custom-call | flops 8388608 | bytes 8388608 | tf_op jit(solution)/shard_map/units/pallas_call | solution.py:407
  41.9 8.3 %collective-permute-done.10.refs_3_ = bf16[256,1024]{1,0:T(8,128)(2,1)S(1)} collective-permute-done((bf16[256,1024]{1,0:T(8,128)(2,1)S(1)}, bf16[256,1024]{1,0:T(8,128)(2,1)S(1)}, u32[]{:S(2)}, u32[]{:S(2)}) %collective-permute-start.10) | collective-permute-done | bytes 524320 | tf_op jit(solution)/shard_map/ppermute | solution.py:334
  50.8 4.4 %collective-permute-start.12 = (bf16[256,1024]{1,0:T(8,128)(2,1)S(1)}, bf16[256,1024]{1,0:T(8,128)(2,1)}, u32[]{:S(2)}, u32[]{:S(2)}) collective-permute-start(bf16[256,1024]{1,0:T(8,128)(2,1)S(1)} %pick.18.refs_0_), channel_id=1, source_target_pairs={{0,2},{2,0},{4,6},{6,4},{8,10},{10,8},{12,14},{14,12},{16,18},{18,... | collective-permute-start | bytes 1572872 | tf_op jit(solution)/shard_map/ppermute | solution.py:334
  55.2 1.7 %collective-permute-done.6.refs_3_ = bf16[256,1024]{1,0:T(8,128)(2,1)S(1)} collective-permute-done((bf16[256,1024]{1,0:T(8,128)(2,1)S(1)}, bf16[256,1024]{1,0:T(8,128)(2,1)S(1)}, u32[]{:S(2)}, u32[]{:S(2)}) %collective-permute-start.6) | collective-permute-done | bytes 524320 | tf_op jit(solution)/shard_map/ppermute | solution.py:334
  57.5 4.4 %collective-permute-start.8 = (bf16[256,1024]{1,0:T(8,128)(2,1)S(1)}, bf16[256,1024]{1,0:T(8,128)(2,1)}, u32[]{:S(2)}, u32[]{:S(2)}) collective-permute-start(bf16[256,1024]{1,0:T(8,128)(2,1)S(1)} %pick.16.refs_0_), channel_id=1, source_target_pairs={{0,2},{2,0},{4,6},{6,4},{8,10},{10,8},{12,14},{14,12},{16,18},{18,... | collective-permute-start | bytes 1572872 | tf_op jit(solution)/shard_map/ppermute | solution.py:334
  61.9 2.1 %collective-permute-start.11 = (bf16[256,1024]{1,0:T(8,128)(2,1)S(1)}, bf16[256,1024]{1,0:T(8,128)(2,1)}, u32[]{:S(2)}, u32[]{:S(2)}) collective-permute-start(bf16[256,1024]{1,0:T(8,128)(2,1)S(1)} %pick.18.refs_0_), channel_id=1, source_target_pairs={{0,1},{2,3},{4,5},{6,7},{8,9},{10,11},{12,13},{14,15},{16,17},{18,... | collective-permute-start | bytes 1572872 | tf_op jit(solution)/shard_map/ppermute | solution.py:334
  64.0 2.1 %collective-permute-start.13 = (bf16[256,1024]{1,0:T(8,128)(2,1)}, bf16[256,1024]{1,0:T(8,128)(2,1)}, u32[]{:S(2)}, u32[]{:S(2)}) collective-permute-start(bf16[256,1024]{1,0:T(8,128)(2,1)} %collective-permute-done.12.refs_2_), channel_id=1, source_target_pairs={{0,1},{2,3},{4,5},{6,7},{8,9},{10,11},{12,13},{14,15},{16,17},{18,... | collective-permute-start | bytes 1572872 | tf_op jit(solution)/shard_map/ppermute | solution.py:334
  66.1 2.1 %collective-permute-start.7 = (bf16[256,1024]{1,0:T(8,128)(2,1)S(1)}, bf16[256,1024]{1,0:T(8,128)(2,1)}, u32[]{:S(2)}, u32[]{:S(2)}) collective-permute-start(bf16[256,1024]{1,0:T(8,128)(2,1)S(1)} %pick.16.refs_0_), channel_id=1, source_target_pairs={{0,1},{2,3},{4,5},{6,7},{8,9},{10,11},{12,13},{14,15},{16,17},{18,... | collective-permute-start | bytes 1572872 | tf_op jit(solution)/shard_map/ppermute | solution.py:334
  69.2 2.1 %collective-permute-start.9 = (bf16[256,1024]{1,0:T(8,128)(2,1)}, bf16[256,1024]{1,0:T(8,128)(2,1)}, u32[]{:S(2)}, u32[]{:S(2)}) collective-permute-start(bf16[256,1024]{1,0:T(8,128)(2,1)} %collective-permute-done.8.refs_2_), channel_id=1, source_target_pairs={{0,1},{2,3},{4,5},{6,7},{8,9},{10,11},{12,13},{14,15},{16,17},{18,... | collective-permute-start | bytes 1572872 | tf_op jit(solution)/shard_map/ppermute | solution.py:334
  71.3 4.9 %units.7 = (bf16[512,4096]{1,0:T(8,128)(2,1)}, f32[512,128]{1,0:T(8,128)S(1)}) custom-call(bf16[2048,4096]{1,0:T(8,128)(2,1)} %decoder_ref.19, bf16[256,1024]{1,0:T(8,128)(2,1)S(1)} %pick.16.refs_0_), custom_call_target="tpu_custom_call" | custom-call | flops 8388608 | bytes 8388608 | tf_op jit(solution)/shard_map/units/pallas_call | solution.py:407
  76.3 2.5 %pick.19 = (bf16[256,1024]{1,0:T(8,128)(2,1)S(1)}, bf16[256,1024]{1,0:T(8,128)(2,1)S(1)}) custom-call(s32[5]{0:T(128)S(1)} %stack.23.flags_ref, bf16[256,1024]{1,0:T(8,128)(2,1)S(1)} %pick.18.refs_0_, bf16[256,1024]{1,0:T(8,128)(2,1)} %collective-permute-done.11.refs_1_, bf16[256,1024]{1,0:T(8,128)(2,1)} %collective-permute-done.12.refs_2_, ...), custom_call_target="tpu_custom_call" | custom-call | flops 262144 | bytes 1048576 | tf_op jit(solution)/shard_map/pick/pallas_call | solution.py:383
  78.8 2.5 %copy-done.3 = bf16[512,4096]{1,0:T(8,128)(2,1)S(1)} copy-done((bf16[512,4096]{1,0:T(8,128)(2,1)S(1)}, bf16[512,4096]{1,0:T(8,128)(2,1)}, u32[]{:S(2)}) %copy-start.3) | copy-done | bytes 4194328
  81.4 2.4 %part_cosines.1.partial_ref = f32[2048,256]{1,0:T(8,128)S(1)} custom-call(bf16[256,1024]{1,0:T(8,128)(2,1)S(1)} %get-tuple-element.58.low_ref.refs_0_, bf16[256,1024]{1,0:T(8,128)(2,1)S(1)} %get-tuple-element.59.high_ref.refs_1_, bf16[512,4096]{1,0:T(8,128)(2,1)S(1)} %copy-done, bf16[512,4096]{1,0:T(8,128)(2,1)S(1)} %copy-done.1, ...), custom_call_target="tpu_custom_call" | custom-call | flops 2147483648 | bytes 8388608 | tf_op jit(solution)/shard_map/part_cosines/pallas_call | solution.py:463
  83.8 1.7 %pick.17 = (bf16[256,1024]{1,0:T(8,128)(2,1)S(1)}, bf16[256,1024]{1,0:T(8,128)(2,1)S(1)}) custom-call(s32[5]{0:T(128)S(1)} %stack.23.flags_ref, bf16[256,1024]{1,0:T(8,128)(2,1)S(1)} %pick.16.refs_0_, bf16[256,1024]{1,0:T(8,128)(2,1)} %collective-permute-done.7.refs_1_, bf16[256,1024]{1,0:T(8,128)(2,1)} %collective-permute-done.8.refs_2_, ...), custom_call_target="tpu_custom_call" | custom-call | flops 262144 | bytes 1048576 | tf_op jit(solution)/shard_map/pick/pallas_call | solution.py:383
  85.5 3.3 %weights.1 = (bf16[2048,256]{1,0:T(8,128)(2,1)S(1)}, bf16[256,2048]{1,0:T(8,128)(2,1)S(1)}, f32[2048,128]{1,0:T(8,128)S(1)}, f32[8,128]{1,0:T(8,128)S(1)}) custom-call(s32[1]{0:T(128)} %bitcast.2.delta_ref, bf16[256,1024]{1,0:T(8,128)(2,1)S(1)} %get-tuple-element.55.low_ref.refs_2_, bf16[256,1024]{1,0:T(8,128)(2,1)S(1)} %get-tuple-element.56.high_ref.refs_3_, ...), custom_call_target="tpu_custom_call" | custom-call | flops 2147483648 | bytes 8388608 | tf_op jit(solution)/shard_map/weights/pallas_call | solution.py:472
  93.7 1.9 %collective-permute-start.18 = (s32[272,256]{1,0:T(8,128)S(1)}, s32[272,256]{1,0:T(8,128)S(1)}, u32[]{:S(2)}, u32[]{:S(2)}) collective-permute-start(s32[272,256]{1,0:T(8,128)S(1)} %get-tuple-element.71.refs_4_), channel_id=1, source_target_pairs={{0,2},{2,0},{1,3},{3,1},{4,6},{6,4},{5,7},{7,5},{8,10},{10,8},{9,1... | collective-permute-start | bytes 835592 | tf_op jit(solution)/shard_map/ppermute | solution.py:334
  97.5 5.8 %collective-permute-done.18.refs_0_ = s32[272,256]{1,0:T(8,128)S(1)} collective-permute-done((s32[272,256]{1,0:T(8,128)S(1)}, s32[272,256]{1,0:T(8,128)S(1)}, u32[]{:S(2)}, u32[]{:S(2)}) %collective-permute-start.18) | collective-permute-done | bytes 278560 | tf_op jit(solution)/shard_map/ppermute | solution.py:334
  109.1 5.8 %finish.4 = (f32[2048,4096]{1,0:T(8,128)}, f32[8,128]{1,0:T(8,128)S(1)}) custom-call(bf16[2048,256]{1,0:T(8,128)(2,1)S(1)} %get-tuple-element.64.col_ref, bf16[2048,4096]{1,0:T(8,128)(2,1)} %decoder_ref.19, f32[2048,128]{1,0:T(8,128)} %copy-done.6, bf16[256,1024]{1,0:T(8,128)(2,1)S(1)} %copy-done.8, bf16[256,1024]{1,0:T(8,128)(2,1)S(1)} %copy-done.11, ...), custom_call_target="tpu_custom_call" | custom-call | flops 1073741824 | bytes 12582912 | tf_op jit(solution)/shard_map/finish/pallas_call | solution.py:563
  117.7 5.8 %finish.5 = (f32[2048,4096]{1,0:T(8,128)}, f32[8,128]{1,0:T(8,128)S(1)}) custom-call(bf16[2048,256]{1,0:T(8,128)(2,1)S(1)} %get-tuple-element.64.col_ref, bf16[2048,4096]{1,0:T(8,128)(2,1)} %decoder_ref.19, f32[2048,128]{1,0:T(8,128)} %copy-done.6, bf16[256,1024]{1,0:T(8,128)(2,1)S(1)} %copy-done.8, ...), custom_call_target="tpu_custom_call", output_to_operand_aliasing={{0}: (8, {})} | custom-call | flops 1073741824 | bytes 12582912 | tf_op jit(solution)/shard_map/finish/pallas_call | solution.py:563
  126.2 4.5 %finish.6 = (f32[2048,4096]{1,0:T(8,128)}, f32[8,128]{1,0:T(8,128)S(1)}) custom-call(bf16[2048,256]{1,0:T(8,128)(2,1)S(1)} %get-tuple-element.64.col_ref, bf16[2048,4096]{1,0:T(8,128)(2,1)} %decoder_ref.19, f32[2048,128]{1,0:T(8,128)} %copy-done.6, bf16[256,1024]{1,0:T(8,128)(2,1)S(1)} %copy-done.8, ...), custom_call_target="tpu_custom_call", output_to_operand_aliasing={{0}: (8, {})} | custom-call | flops 536870912 | bytes 6291456 | tf_op jit(solution)/shard_map/finish/pallas_call | solution.py:563
  132.4 2.3 %collective-permute-done.26.refs_2_ = s32[272,256]{1,0:T(8,128)S(1)} collective-permute-done((s32[272,256]{1,0:T(8,128)S(1)}, s32[272,256]{1,0:T(8,128)S(1)}, u32[]{:S(2)}, u32[]{:S(2)}) %collective-permute-start.26) | collective-permute-done | bytes 278560 | tf_op jit(solution)/shard_map/ppermute | solution.py:334
  140.9 1.6 %merge.13 = (f32[256,512]{1,0:T(8,128)S(1)}, f32[8,128]{1,0:T(8,128)S(1)}, s32[272,256]{1,0:T(8,128)}) custom-call(f32[256,512]{1,0:T(8,128)S(1)} %get-tuple-element.73.kept_ref, f32[8,128]{1,0:T(8,128)S(1)} %get-tuple-element.74.penalty_ref, s32[272,256]{1,0:T(8,128)S(1)} %collective-permute-done.17.refs_0_, ...), custom_call_target="tpu_custom_call" | custom-call | flops 2621440 | bytes 1572864 | tf_op jit(solution)/shard_map/merge/pallas_call | solution.py:508
  148.0 5.8 %finish.7 = (f32[2048,4096]{1,0:T(8,128)}, f32[8,128]{1,0:T(8,128)}) custom-call(bf16[2048,256]{1,0:T(8,128)(2,1)S(1)} %get-tuple-element.64.col_ref, bf16[2048,4096]{1,0:T(8,128)(2,1)} %decoder_ref.19, f32[2048,128]{1,0:T(8,128)} %copy-done.6, bf16[256,1024]{1,0:T(8,128)(2,1)S(1)} %copy-done.9, ...), custom_call_target="tpu_custom_call", output_to_operand_aliasing={{0}: (8, {})} | custom-call | flops 1073741824 | bytes 12582912 | tf_op jit(solution)/shard_map/finish/pallas_call | solution.py:563
  153.8 1.5 collective-permute-done.22.refs_5_.refs_6_
  155.4 5.6 %finish_rows.1 = (f32[2048,4096]{1,0:T(8,128)}, f32[1]{0:T(128)}) custom-call(s32[1]{0:T(128)} %bitcast.1.owner_ref, bf16[2048,256]{1,0:T(8,128)(2,1)} %copy-done.5, bf16[2048,4096]{1,0:T(8,128)(2,1)} %decoder_ref.19, f32[2048,128]{1,0:T(8,128)} %copy-done.6, f32[8,128]{1,0:T(8,128)S(1)} %get-tuple-element.85.tile_ref, ...), custom_call_target="tpu_custom_call", output_to_operand_aliasing={{0}: (23, {})} | custom-call | tf_op jit(solution)/shard_map/finish_rows/pallas_call | solution.py:631
  (127 shorter events, 43.6 us)
Async XLA Ops:
  4.1 11.5 %collective-permute-start.3 = (bf16[256,1024]{1,0:T(8,128)(2,1)S(1)}, bf16[256,1024]{1,0:T(8,128)(2,1)S(1)}, u32[]{:S(2)}, u32[]{:S(2)}) collective-permute-start(bf16[256,1024]{1,0:T(8,128)(2,1)S(1)} %get-tuple-element.51), channel_id=1, source_target_pairs={{0,2},{4,6},{8,10},{12,14},{16,18},{20,22},{24,26},{28,30}} | collective-permute-start | bytes 1572872 | tf_op jit(solution)/shard_map/ppermute | solution.py:334
  9.0 12.3 %collective-permute-start = (bf16[256,1024]{1,0:T(8,128)(2,1)S(1)}, bf16[256,1024]{1,0:T(8,128)(2,1)S(1)}, u32[]{:S(2)}, u32[]{:S(2)}) collective-permute-start(bf16[256,1024]{1,0:T(8,128)(2,1)S(1)} %get-tuple-element.49), channel_id=1, source_target_pairs={{0,2},{4,6},{8,10},{12,14},{16,18},{20,22},{24,26},{28,30}} | collective-permute-start | bytes 1572872 | tf_op jit(solution)/shard_map/ppermute | solution.py:334
  16.2 13.9 %collective-permute-start.4 = (bf16[256,1024]{1,0:T(8,128)(2,1)S(1)}, bf16[256,1024]{1,0:T(8,128)(2,1)S(1)}, u32[]{:S(2)}, u32[]{:S(2)}) collective-permute-start(bf16[256,1024]{1,0:T(8,128)(2,1)S(1)} %pick.12.refs_0_), channel_id=1, source_target_pairs={{0,4},{2,6},{12,8},{14,10},{16,20},{18,22},{28,24},{30,26}} | collective-permute-start | bytes 1572872 | tf_op jit(solution)/shard_map/ppermute | solution.py:334
  21.8 10.2 %collective-permute-start.1 = (bf16[256,1024]{1,0:T(8,128)(2,1)S(1)}, bf16[256,1024]{1,0:T(8,128)(2,1)S(1)}, u32[]{:S(2)}, u32[]{:S(2)}) collective-permute-start(bf16[256,1024]{1,0:T(8,128)(2,1)S(1)} %pick.10.refs_0_), channel_id=1, source_target_pairs={{0,4},{2,6},{12,8},{14,10},{16,20},{18,22},{28,24},{30,26}} | collective-permute-start | bytes 1572872 | tf_op jit(solution)/shard_map/ppermute | solution.py:334
  30.7 2.6 %collective-permute-start.5 = (bf16[256,1024]{1,0:T(8,128)(2,1)S(1)}, bf16[256,1024]{1,0:T(8,128)(2,1)S(1)}, u32[]{:S(2)}, u32[]{:S(2)}) collective-permute-start(bf16[256,1024]{1,0:T(8,128)(2,1)S(1)} %pick.13), channel_id=1, source_target_pairs={{4,8},{6,10},{8,4},{10,6},{20,24},{22,26},{24,20},{26,22}} | collective-permute-start | bytes 1572872 | tf_op jit(solution)/shard_map/ppermute | solution.py:334
  32.6 7.4 %collective-permute-start.2 = (bf16[256,1024]{1,0:T(8,128)(2,1)S(1)}, bf16[256,1024]{1,0:T(8,128)(2,1)S(1)}, u32[]{:S(2)}, u32[]{:S(2)}) collective-permute-start(bf16[256,1024]{1,0:T(8,128)(2,1)S(1)} %pick.11), channel_id=1, source_target_pairs={{4,8},{6,10},{8,4},{10,6},{20,24},{22,26},{24,20},{26,22}} | collective-permute-start | bytes 1572872 | tf_op jit(solution)/shard_map/ppermute | solution.py:334
  33.9 16.2 %collective-permute-start.10 = (bf16[256,1024]{1,0:T(8,128)(2,1)S(1)}, bf16[256,1024]{1,0:T(8,128)(2,1)S(1)}, u32[]{:S(2)}, u32[]{:S(2)}) collective-permute-start(bf16[256,1024]{1,0:T(8,128)(2,1)S(1)} %pick.14.refs_0_), channel_id=1, source_target_pairs={{8,12},{10,14},{4,0},{6,2},{24,28},{26,30},{20,16},{22,18}} | collective-permute-start | bytes 1572872 | tf_op jit(solution)/shard_map/ppermute | solution.py:334
  40.0 29.2 %copy-start.25 = (f32[512,128]{1,0:T(8,128)}, f32[512,128]{1,0:T(8,128)S(1)}, u32[]{:S(2)}) copy-start(f32[512,128]{1,0:T(8,128)S(1)} %get-tuple-element.54.refs_2_.refs_6_) | copy-start | bytes 786436
  40.6 16.3 %collective-permute-start.6 = (bf16[256,1024]{1,0:T(8,128)(2,1)S(1)}, bf16[256,1024]{1,0:T(8,128)(2,1)S(1)}, u32[]{:S(2)}, u32[]{:S(2)}) collective-permute-start(bf16[256,1024]{1,0:T(8,128)(2,1)S(1)} %pick.15), channel_id=1, source_target_pairs={{8,12},{10,14},{4,0},{6,2},{24,28},{26,30},{20,16},{22,18}} | collective-permute-start | bytes 1572872 | tf_op jit(solution)/shard_map/ppermute | solution.py:334
  50.8 13.2 %collective-permute-start.12 = (bf16[256,1024]{1,0:T(8,128)(2,1)S(1)}, bf16[256,1024]{1,0:T(8,128)(2,1)}, u32[]{:S(2)}, u32[]{:S(2)}) collective-permute-start(bf16[256,1024]{1,0:T(8,128)(2,1)S(1)} %pick.18.refs_0_), channel_id=1, source_target_pairs={{0,2},{2,0},{4,6},{6,4},{8,10},{10,8},{12,14},{14,12},{16,18},{18,... | collective-permute-start | bytes 1572872 | tf_op jit(solution)/shard_map/ppermute | solution.py:334
  57.5 11.6 %collective-permute-start.8 = (bf16[256,1024]{1,0:T(8,128)(2,1)S(1)}, bf16[256,1024]{1,0:T(8,128)(2,1)}, u32[]{:S(2)}, u32[]{:S(2)}) collective-permute-start(bf16[256,1024]{1,0:T(8,128)(2,1)S(1)} %pick.16.refs_0_), channel_id=1, source_target_pairs={{0,2},{2,0},{4,6},{6,4},{8,10},{10,8},{12,14},{14,12},{16,18},{18,... | collective-permute-start | bytes 1572872 | tf_op jit(solution)/shard_map/ppermute | solution.py:334
  61.9 14.3 %collective-permute-start.11 = (bf16[256,1024]{1,0:T(8,128)(2,1)S(1)}, bf16[256,1024]{1,0:T(8,128)(2,1)}, u32[]{:S(2)}, u32[]{:S(2)}) collective-permute-start(bf16[256,1024]{1,0:T(8,128)(2,1)S(1)} %pick.18.refs_0_), channel_id=1, source_target_pairs={{0,1},{2,3},{4,5},{6,7},{8,9},{10,11},{12,13},{14,15},{16,17},{18,... | collective-permute-start | bytes 1572872 | tf_op jit(solution)/shard_map/ppermute | solution.py:334
  64.0 12.2 %collective-permute-start.13 = (bf16[256,1024]{1,0:T(8,128)(2,1)}, bf16[256,1024]{1,0:T(8,128)(2,1)}, u32[]{:S(2)}, u32[]{:S(2)}) collective-permute-start(bf16[256,1024]{1,0:T(8,128)(2,1)} %collective-permute-done.12.refs_2_), channel_id=1, source_target_pairs={{0,1},{2,3},{4,5},{6,7},{8,9},{10,11},{12,13},{14,15},{16,17},{18,... | collective-permute-start | bytes 1572872 | tf_op jit(solution)/shard_map/ppermute | solution.py:334
  66.1 17.6 %collective-permute-start.7 = (bf16[256,1024]{1,0:T(8,128)(2,1)S(1)}, bf16[256,1024]{1,0:T(8,128)(2,1)}, u32[]{:S(2)}, u32[]{:S(2)}) collective-permute-start(bf16[256,1024]{1,0:T(8,128)(2,1)S(1)} %pick.16.refs_0_), channel_id=1, source_target_pairs={{0,1},{2,3},{4,5},{6,7},{8,9},{10,11},{12,13},{14,15},{16,17},{18,... | collective-permute-start | bytes 1572872 | tf_op jit(solution)/shard_map/ppermute | solution.py:334
  69.2 14.6 %collective-permute-start.9 = (bf16[256,1024]{1,0:T(8,128)(2,1)}, bf16[256,1024]{1,0:T(8,128)(2,1)}, u32[]{:S(2)}, u32[]{:S(2)}) collective-permute-start(bf16[256,1024]{1,0:T(8,128)(2,1)} %collective-permute-done.8.refs_2_), channel_id=1, source_target_pairs={{0,1},{2,3},{4,5},{6,7},{8,9},{10,11},{12,13},{14,15},{16,17},{18,... | collective-permute-start | bytes 1572872 | tf_op jit(solution)/shard_map/ppermute | solution.py:334
  88.8 59.1 %copy-start.5 = (bf16[2048,256]{1,0:T(8,128)(2,1)}, bf16[2048,256]{1,0:T(8,128)(2,1)S(1)}, u32[]{:S(2)}) copy-start(bf16[2048,256]{1,0:T(8,128)(2,1)S(1)} %get-tuple-element.64.col_ref) | copy-start | bytes 3145732
  90.1 3.2 %collective-permute-start.16 = (f32[264,1024]{1,0:T(8,128)S(1)}, f32[264,1024]{1,0:T(8,128)S(1)}, u32[]{:S(2)}, u32[]{:S(2)}) collective-permute-start(f32[264,1024]{1,0:T(8,128)S(1)} %row_part.7), channel_id=1, source_target_pairs={{0,1},{1,0},{2,3},{3,2},{4,5},{5,4},{6,7},{7,6},{8,9},{9,8},{10,11... | collective-permute-start | bytes 3244040 | tf_op jit(solution)/shard_map/ppermute | solution.py:334
  91.4 5.4 %collective-permute-start.14 = (f32[264,1024]{1,0:T(8,128)S(1)}, f32[264,1024]{1,0:T(8,128)S(1)}, u32[]{:S(2)}, u32[]{:S(2)}) collective-permute-start(f32[264,1024]{1,0:T(8,128)S(1)} %row_part.5), channel_id=1, source_target_pairs={{0,1},{1,0},{2,3},{3,2},{4,5},{5,4},{6,7},{7,6},{8,9},{9,8},{10,11... | collective-permute-start | bytes 3244040 | tf_op jit(solution)/shard_map/ppermute | solution.py:334
  93.7 9.6 %collective-permute-start.18 = (s32[272,256]{1,0:T(8,128)S(1)}, s32[272,256]{1,0:T(8,128)S(1)}, u32[]{:S(2)}, u32[]{:S(2)}) collective-permute-start(s32[272,256]{1,0:T(8,128)S(1)} %get-tuple-element.71.refs_4_), channel_id=1, source_target_pairs={{0,2},{2,0},{1,3},{3,1},{4,6},{6,4},{5,7},{7,5},{8,10},{10,8},{9,1... | collective-permute-start | bytes 835592 | tf_op jit(solution)/shard_map/ppermute | solution.py:334
  97.2 17.7 %collective-permute-start.15 = (s32[272,256]{1,0:T(8,128)S(1)}, s32[272,256]{1,0:T(8,128)S(1)}, u32[]{:S(2)}, u32[]{:S(2)}) collective-permute-start(s32[272,256]{1,0:T(8,128)S(1)} %get-tuple-element.70), channel_id=1, source_target_pairs={{0,2},{2,0},{1,3},{3,1},{4,6},{6,4},{5,7},{7,5},{8,10},{10,8},{9,1... | collective-permute-start | bytes 835592 | tf_op jit(solution)/shard_map/ppermute | solution.py:334
  103.6 13.0 %collective-permute-start.20 = (s32[272,256]{1,0:T(8,128)S(1)}, s32[272,256]{1,0:T(8,128)S(1)}, u32[]{:S(2)}, u32[]{:S(2)}) collective-permute-start(s32[272,256]{1,0:T(8,128)S(1)} %get-tuple-element.78.refs_4_), channel_id=1, source_target_pairs={{0,4},{1,5},{2,6},{3,7},{12,8},{13,9},{14,10},{15,11},{16,20},{17,... | collective-permute-start | bytes 835592 | tf_op jit(solution)/shard_map/ppermute | solution.py:334
  115.2 8.3 %collective-permute-start.17 = (s32[272,256]{1,0:T(8,128)S(1)}, s32[272,256]{1,0:T(8,128)S(1)}, u32[]{:S(2)}, u32[]{:S(2)}) collective-permute-start(s32[272,256]{1,0:T(8,128)S(1)} %get-tuple-element.75), channel_id=1, source_target_pairs={{0,4},{1,5},{2,6},{3,7},{12,8},{13,9},{14,10},{15,11},{16,20},{17,... | collective-permute-start | bytes 835592 | tf_op jit(solution)/shard_map/ppermute | solution.py:334
  116.8 7.7 %collective-permute-start.25 = (s32[272,256]{1,0:T(8,128)S(1)}, s32[272,256]{1,0:T(8,128)S(1)}, u32[]{:S(2)}, u32[]{:S(2)}) collective-permute-start(s32[272,256]{1,0:T(8,128)S(1)} %merge.11.refs_4_), channel_id=1, source_target_pairs={{4,8},{5,9},{6,10},{7,11},{8,4},{9,5},{10,6},{11,7},{20,24},{21,25... | collective-permute-start | bytes 835592 | tf_op jit(solution)/shard_map/ppermute | solution.py:334
  123.9 6.9 %collective-permute-start.19 = (s32[272,256]{1,0:T(8,128)S(1)}, s32[272,256]{1,0:T(8,128)S(1)}, u32[]{:S(2)}, u32[]{:S(2)}) collective-permute-start(s32[272,256]{1,0:T(8,128)S(1)} %merge.10), channel_id=1, source_target_pairs={{4,8},{5,9},{6,10},{7,11},{8,4},{9,5},{10,6},{11,7},{20,24},{21,25... | collective-permute-start | bytes 835592 | tf_op jit(solution)/shard_map/ppermute | solution.py:334
  124.9 9.8 %collective-permute-start.26 = (s32[272,256]{1,0:T(8,128)S(1)}, s32[272,256]{1,0:T(8,128)S(1)}, u32[]{:S(2)}, u32[]{:S(2)}) collective-permute-start(s32[272,256]{1,0:T(8,128)S(1)} %merge.14), channel_id=1, source_target_pairs={{8,12},{9,13},{10,14},{11,15},{4,0},{5,1},{6,2},{7,3},{24,28},{25,... | collective-permute-start | bytes 835592 | tf_op jit(solution)/shard_map/ppermute | solution.py:334
  131.1 9.8 %collective-permute-start.21 = (s32[272,256]{1,0:T(8,128)S(1)}, s32[272,256]{1,0:T(8,128)S(1)}, u32[]{:S(2)}, u32[]{:S(2)}) collective-permute-start(s32[272,256]{1,0:T(8,128)S(1)} %merge.12), channel_id=1, source_target_pairs={{8,12},{9,13},{10,14},{11,15},{4,0},{5,1},{6,2},{7,3},{24,28},{25,... | collective-permute-start | bytes 835592 | tf_op jit(solution)/shard_map/ppermute | solution.py:334
  135.9 10.0 %collective-permute-start.29 = (s32[272,256]{1,0:T(8,128)}, s32[272,256]{1,0:T(8,128)S(1)}, u32[]{:S(2)}, u32[]{:S(2)}) collective-permute-start(s32[272,256]{1,0:T(8,128)} %get-tuple-element.89.refs_4_), channel_id=1, source_target_pairs={{3,0},{7,4},{11,8},{15,12},{19,16},{23,20},{27,24},{31,28}} | collective-permute-start | bytes 835592 | tf_op jit(solution)/shard_map/ppermute | solution.py:334
  137.2 16.6 %collective-permute-start.28 = (s32[272,256]{1,0:T(8,128)}, s32[272,256]{1,0:T(8,128)}, u32[]{:S(2)}, u32[]{:S(2)}) collective-permute-start(s32[272,256]{1,0:T(8,128)} %get-tuple-element.89.refs_4_), channel_id=1, source_target_pairs={{1,0},{5,4},{9,8},{13,12},{17,16},{21,20},{25,24},{29,28}} | collective-permute-start | bytes 835592 | tf_op jit(solution)/shard_map/ppermute | solution.py:334
  138.5 15.3 %collective-permute-start.27 = (s32[272,256]{1,0:T(8,128)}, s32[272,256]{1,0:T(8,128)}, u32[]{:S(2)}, u32[]{:S(2)}) collective-permute-start(s32[272,256]{1,0:T(8,128)} %get-tuple-element.89.refs_4_), channel_id=1, source_target_pairs={{2,0},{6,4},{10,8},{14,12},{18,16},{22,20},{26,24},{30,28}} | collective-permute-start | bytes 835592 | tf_op jit(solution)/shard_map/ppermute | solution.py:334
  143.3 10.5 %collective-permute-start.24 = (s32[272,256]{1,0:T(8,128)}, s32[272,256]{1,0:T(8,128)}, u32[]{:S(2)}, u32[]{:S(2)}) collective-permute-start(s32[272,256]{1,0:T(8,128)} %get-tuple-element.87), channel_id=1, source_target_pairs={{3,0},{7,4},{11,8},{15,12},{19,16},{23,20},{27,24},{31,28}} | collective-permute-start | bytes 835592 | tf_op jit(solution)/shard_map/ppermute | solution.py:334
  144.6 9.2 %collective-permute-start.23 = (s32[272,256]{1,0:T(8,128)}, s32[272,256]{1,0:T(8,128)}, u32[]{:S(2)}, u32[]{:S(2)}) collective-permute-start(s32[272,256]{1,0:T(8,128)} %get-tuple-element.87), channel_id=1, source_target_pairs={{1,0},{5,4},{9,8},{13,12},{17,16},{21,20},{25,24},{29,28}} | collective-permute-start | bytes 835592 | tf_op jit(solution)/shard_map/ppermute | solution.py:334
  146.6 8.7 %collective-permute-start.22 = (s32[272,256]{1,0:T(8,128)}, s32[272,256]{1,0:T(8,128)}, u32[]{:S(2)}, u32[]{:S(2)}) collective-permute-start(s32[272,256]{1,0:T(8,128)} %get-tuple-element.87), channel_id=1, source_target_pairs={{2,0},{6,4},{10,8},{14,12},{18,16},{22,20},{26,24},{30,28}} | collective-permute-start | bytes 835592 | tf_op jit(solution)/shard_map/ppermute | solution.py:334
  (29 other events, 202.3 us)
